TPU v7x, 32 devices: a whole 2x2x4 slice. The times are simulated.
32 devices in a mesh: ctx: 16 (over z, y, core), fsdp: 2 (over x).
Axes of the slice: x: 2, y: 2, z: 4, core: 2. Of those that a mesh axis runs over, the one named last changes fastest.
Arguments:
- tokens: bfloat16 [6144, 2048], P(('ctx', 'fsdp')), may hold values from -6 to 6
- cotangent: bfloat16 [6144, 2048], P(('ctx', 'fsdp')), may hold values from -6 to 6
- expert_ids: int32 [6144, 8], P(('ctx', 'fsdp')), may hold values from 0 to 15, all different within a row; in each aligned block of 192 rows (0 to 191, 192 to 383, ...) at most 120 rows name the same one
- attention_gain: float32 [2048], replicated, may hold values from 0.5 to 1.5
- ffn_gain: float32 [2048], replicated, may hold values from 0.5 to 1.5
- query_gain: float32 [128], replicated, may hold values from 0.5 to 1.5
- key_gain: float32 [128], replicated, may hold values from 0.5 to 1.5
- w_query: bfloat16 [2048, 4096], P(('ctx', 'fsdp')), may hold values from -0.125 to 0.125
- key_weight: bfloat16 [2048, 512], P(('ctx', 'fsdp')), may hold values from -0.125 to 0.125
- value_weight: bfloat16 [2048, 512], P(('ctx', 'fsdp')), may hold values from -0.125 to 0.125
- w_output: bfloat16 [4096, 2048], P(('ctx', 'fsdp')), may hold values from -2 to 2
- w_router: bfloat16 [2048, 16], P(('ctx', 'fsdp')), may hold values from -0.0625 to 0.0625
- w_gate: bfloat16 [16, 2048, 768], P('ctx', 'fsdp'), may hold values from -0.125 to 0.125
- w_up: bfloat16 [16, 2048, 768], P('ctx', 'fsdp'), may hold values from -0.125 to 0.125
- w_down: bfloat16 [16, 768, 2048], P('ctx', 'fsdp'), may hold values from -1 to 1
Outputs:
- mixed: bfloat16 [6144, 2048], P(('ctx', 'fsdp'))
- d_tokens: bfloat16 [6144, 2048], P(('ctx', 'fsdp'))
- attention_gain_grad: float32 [2048], replicated
- ffn_gain_grad: float32 [2048], replicated
- query_gain_grad: float32 [128], replicated
- key_gain_grad: float32 [128], replicated
- query_grad: float32 [2048, 4096], P(('ctx', 'fsdp'))
- key_grad: float32 [2048, 512], P(('ctx', 'fsdp'))
- value_grad: float32 [2048, 512], P(('ctx', 'fsdp'))
- output_grad: float32 [4096, 2048], P(('ctx', 'fsdp'))
- router_grad: float32 [2048, 16], P(('ctx', 'fsdp'))
- gate_grad: float32 [16, 2048, 768], P('ctx', 'fsdp')
- up_grad: float32 [16, 2048, 768], P('ctx', 'fsdp')
- down_grad: float32 [16, 768, 2048], P('ctx', 'fsdp')
Inputs may be any that keep to these rules, and one draw needn't show every extreme that they name: `expert_ids`: among the rows of one device no expert is named more than 120 times, a bound that some block reaches.
All inputs are finite; a program needn't handle non-finite values.
Results may differ from a plain program's by a relative error of at most 0.024.
Values may be sent and summed in bfloat16 or wider, within the bound.
No kernel may reach another device: no remote copies, remote signals or barrier semaphores. Data moves between devices by JAX's collectives and lax.ppermute only.
A program may use at most 320 MiB of HBM per device.

v0:
```python
import math

import jax
import jax.numpy as jnp
from jax import lax
from jax.sharding import PartitionSpec as P

QUERY_HEADS = 32
KEY_VALUE_HEADS = 4
HEAD_SIZE = 128
TOP = 8
LOCAL_SEQUENCES = 3


EPS = 1e-06
THETA = 1000000.0
NEGATIVE_LIMIT = -1e30


def shard_positions(device, context_count, block_len):
    within = jnp.arange(2 * block_len, dtype=jnp.int32)
    lower_pos = device * block_len + within
    upper_pos = (2 * context_count - 1 - device) * block_len + within - block_len
    return jnp.where(within < block_len, lower_pos, upper_pos)


def group_positions(first_dev, query_group_size, context_count, block_len):
    devices = first_dev + jnp.arange(query_group_size, dtype=jnp.int32)
    return jax.vmap(lambda device: shard_positions(device, context_count, block_len))(
        devices
    ).reshape(-1)


def rotary(positions, head_width):
    half_width = head_width // 2
    frequency = jnp.exp(
        -math.log(THETA) * (2.0 * jnp.arange(half_width, dtype=jnp.float32)) / head_width
    )
    angles = positions.astype(jnp.float32)[:, None] * frequency[None, :]
    angles = jnp.concatenate([angles, angles], -1)
    return (jnp.cos(angles)[:, None, :], jnp.sin(angles)[:, None, :])


def rope_apply(value_rows_list, cosine, sine_tab):
    half_width = value_rows_list.shape[-1] // 2
    turned = jnp.concatenate(
        [-value_rows_list[..., half_width:], value_rows_list[..., :half_width]], -1
    )
    return value_rows_list * cosine + turned * sine_tab


def rope_back(upstream, cosine, sine_tab):
    half_width = upstream.shape[-1] // 2
    moved_part = upstream * sine_tab
    return upstream * cosine + jnp.concatenate(
        [moved_part[..., half_width:], -moved_part[..., :half_width]], -1
    )


def rms_apply(value_rows_list, gain_vec):
    inverse = lax.rsqrt(jnp.mean(value_rows_list * value_rows_list, -1, keepdims=True) + EPS)
    return (value_rows_list * inverse * gain_vec, inverse)


def rms_back(value_rows_list, inverse, gain_vec, upstream):
    normalized_input = value_rows_list * inverse
    gain_part = jnp.sum((upstream * normalized_input).reshape(-1, value_rows_list.shape[-1]), 0)
    scaled = upstream * gain_vec
    back_part = inverse * (
        scaled - normalized_input * jnp.mean(scaled * normalized_input, -1, keepdims=True)
    )
    return (back_part, gain_part)


def arrange(blocks):
    query_group_size, seq_count, paired_rows, heads_kv, head_dim = blocks.shape
    return blocks.transpose(1, 0, 2, 3, 4).reshape(
        seq_count, query_group_size * paired_rows, heads_kv, head_dim
    )


def unarrange(rows_all, query_group_size):
    seq_count, width_all, heads_kv, head_dim = rows_all.shape
    return rows_all.reshape(
        seq_count, query_group_size, width_all // query_group_size, heads_kv, head_dim
    ).transpose(1, 0, 2, 3, 4)


def attend_group(state_now, queries, key_row_matrix, value_rows, query_pos, key_pos, score_scale):
    run_max, run_sum, run_acc = state_now
    scores = (
        jnp.einsum("skgqd,swkd->skgqw", queries, key_row_matrix, preferred_element_type=jnp.float32)
        * score_scale
    )
    allowed = key_pos[None, :] <= query_pos[:, None]
    new_max = jnp.maximum(run_max, jnp.max(jnp.where(allowed, scores, NEGATIVE_LIMIT), -1))
    weights_now = jnp.where(allowed, jnp.exp(scores - new_max[..., None]), 0.0)
    factor = jnp.exp(run_max - new_max)
    new_sum = run_sum * factor + jnp.sum(weights_now, -1)
    update = jnp.einsum(
        "skgqw,swkd->skgqd",
        weights_now.astype(jnp.bfloat16),
        value_rows,
        preferred_element_type=jnp.float32,
    )
    return (new_max, new_sum, run_acc * factor[..., None] + update)


def local(
    tokens,
    cotangent,
    expert_ids,
    attention_gain,
    ffn_gain,
    query_gain,
    key_gain,
    w_query,
    key_weight,
    value_weight,
    w_output,
    w_router,
    w_gate,
    w_up,
    w_down,
):
    context_count = lax.axis_size("ctx")
    ctx_here = lax.axis_index("ctx")
    token_per_device = tokens.shape[0]
    block_len = token_per_device // (2 * LOCAL_SEQUENCES)
    paired_rows = 2 * block_len
    query_groups = QUERY_HEADS // KEY_VALUE_HEADS
    score_scale = 1.0 / math.sqrt(HEAD_SIZE)
    experts_all = w_router.shape[1]
    exp_dev = w_gate.shape[0]
    cap_rows = token_per_device * TOP * 5 // (4 * experts_all)
    routes = token_per_device * TOP
    inputs = tokens.astype(jnp.float32)
    normed_attn, inverse_attn = rms_apply(inputs, attention_gain)
    normed_low = normed_attn.astype(jnp.bfloat16)
    query_all, key_all, value_all, output_all, router_all = (
        lax.all_gather(w_query, ("ctx", "fsdp"), axis=0, tiled=True),
        lax.all_gather(key_weight, ("ctx", "fsdp"), axis=0, tiled=True),
        lax.all_gather(value_weight, ("ctx", "fsdp"), axis=0, tiled=True),
        lax.all_gather(w_output, ("ctx", "fsdp"), axis=0, tiled=True),
        lax.all_gather(w_router, ("ctx", "fsdp"), axis=0, tiled=True),
    )
    local_pos = shard_positions(ctx_here, context_count, block_len)
    row_pos = jnp.tile(local_pos, LOCAL_SEQUENCES)
    cosine, sine_tab = rotary(row_pos, HEAD_SIZE)
    query_proj = jnp.dot(normed_low, query_all, preferred_element_type=jnp.float32).reshape(
        token_per_device, QUERY_HEADS, HEAD_SIZE
    )
    key_proj = jnp.dot(normed_low, key_all, preferred_element_type=jnp.float32).reshape(
        token_per_device, KEY_VALUE_HEADS, HEAD_SIZE
    )
    value_proj = jnp.dot(normed_low, value_all, preferred_element_type=jnp.float32).reshape(
        token_per_device, KEY_VALUE_HEADS, HEAD_SIZE
    )
    query_normed, query_inverse = rms_apply(query_proj, query_gain)
    key_normed, key_inverse = rms_apply(key_proj, key_gain)
    query_lower = rope_apply(query_normed, cosine, sine_tab).astype(jnp.bfloat16)
    key_low = rope_apply(key_normed, cosine, sine_tab).astype(jnp.bfloat16)
    value_low = value_proj.astype(jnp.bfloat16)
    query_head_rows = query_lower.reshape(
        LOCAL_SEQUENCES, paired_rows, KEY_VALUE_HEADS, query_groups, HEAD_SIZE
    ).transpose(0, 2, 3, 1, 4)
    initial = (
        jnp.full(
            (LOCAL_SEQUENCES, KEY_VALUE_HEADS, query_groups, paired_rows),
            NEGATIVE_LIMIT,
            jnp.float32,
        ),
        jnp.zeros((LOCAL_SEQUENCES, KEY_VALUE_HEADS, query_groups, paired_rows), jnp.float32),
        jnp.zeros(
            (LOCAL_SEQUENCES, KEY_VALUE_HEADS, query_groups, paired_rows, HEAD_SIZE), jnp.float32
        ),
    )
    key_every, value_every = (
        lax.all_gather(key_low, "ctx", axis=0, tiled=True),
        lax.all_gather(value_low, "ctx", axis=0, tiled=True),
    )
    shard_total_count = key_every.shape[0] // token_per_device
    fold_query_group_size = 4
    key_block_list = key_every.reshape(
        shard_total_count // fold_query_group_size,
        fold_query_group_size,
        LOCAL_SEQUENCES,
        paired_rows,
        KEY_VALUE_HEADS,
        HEAD_SIZE,
    )
    value_block_list = value_every.reshape(
        shard_total_count // fold_query_group_size,
        fold_query_group_size,
        LOCAL_SEQUENCES,
        paired_rows,
        KEY_VALUE_HEADS,
        HEAD_SIZE,
    )
    first_devs = 0 // token_per_device + fold_query_group_size * jnp.arange(
        shard_total_count // fold_query_group_size, dtype=jnp.int32
    )

    def one_group(state_in, loop_item):
        key_group, value_group, first_dev = loop_item
        key_pos = group_positions(first_dev, fold_query_group_size, context_count, block_len)
        return (
            attend_group(
                state_in,
                query_head_rows,
                arrange(key_group),
                arrange(value_group),
                local_pos,
                key_pos,
                score_scale,
            ),
            None,
        )

    state_out, unused = lax.scan(one_group, initial, (key_block_list, value_block_list, first_devs))
    run_max, run_sum, run_acc = state_out
    log_sum = run_max + jnp.log(run_sum)
    attended = run_acc / run_sum[..., None]
    attended_low = (
        attended.transpose(0, 3, 1, 2, 4)
        .reshape(token_per_device, QUERY_HEADS * HEAD_SIZE)
        .astype(jnp.bfloat16)
    )
    mixed_attn = inputs + jnp.dot(attended_low, output_all, preferred_element_type=jnp.float32)
    normed_ffn, inverse_ffn = rms_apply(mixed_attn, ffn_gain)
    ffn_low = normed_ffn.astype(jnp.bfloat16)
    logits = jnp.dot(ffn_low, router_all, preferred_element_type=jnp.float32)
    chosen = (expert_ids[..., None] == jnp.arange(experts_all, dtype=jnp.int32)).astype(jnp.float32)
    picked = jnp.einsum("tje,te->tj", chosen, logits, precision=lax.Precision.HIGHEST)
    gate_probs = jax.nn.softmax(picked, -1)
    flat_ids = expert_ids.reshape(-1)
    route_marks = (flat_ids[:, None] == jnp.arange(experts_all, dtype=jnp.int32)).astype(jnp.int32)
    route_ranks = jnp.sum((jnp.cumsum(route_marks, 0) - 1) * route_marks, -1)
    slot_of_route = flat_ids * cap_rows + route_ranks
    route_of_slot = (
        jnp.full((experts_all * cap_rows,), routes, jnp.int32)
        .at[slot_of_route]
        .set(jnp.arange(routes, dtype=jnp.int32))
    )
    padded = jnp.concatenate([ffn_low, jnp.zeros((1, ffn_low.shape[1]), jnp.bfloat16)], 0)
    outgoing = padded[route_of_slot // TOP].reshape(experts_all, cap_rows, -1)
    arrived = lax.all_to_all(outgoing, "ctx", split_axis=0, concat_axis=0, tiled=True)

    def to_experts(buffer):
        return (
            buffer.reshape(context_count, exp_dev, cap_rows, -1)
            .transpose(1, 0, 2, 3)
            .reshape(exp_dev, context_count * cap_rows, -1)
        )

    def from_experts(buffer):
        return (
            buffer.reshape(exp_dev, context_count, cap_rows, -1)
            .transpose(1, 0, 2, 3)
            .reshape(context_count * exp_dev, cap_rows, -1)
        )

    expert_rows = to_experts(arrived)
    gate_all, up_all, down_all = (
        lax.all_gather(w_gate, "fsdp", axis=1, tiled=True),
        lax.all_gather(w_up, "fsdp", axis=1, tiled=True),
        lax.all_gather(w_down, "fsdp", axis=1, tiled=True),
    )
    gate_part = jnp.einsum(
        "esd,edf->esf", expert_rows, gate_all, preferred_element_type=jnp.float32
    )
    up_part = jnp.einsum("esd,edf->esf", expert_rows, up_all, preferred_element_type=jnp.float32)
    sigmoid_gate = jax.nn.sigmoid(gate_part)
    silu_gate = gate_part * sigmoid_gate
    hidden_low = (silu_gate * up_part).astype(jnp.bfloat16)
    results = jnp.einsum(
        "esf,efd->esd", hidden_low, down_all, preferred_element_type=jnp.float32
    ).astype(jnp.bfloat16)
    returned = lax.all_to_all(from_experts(results), "ctx", split_axis=0, concat_axis=0, tiled=True)
    route_out = returned.reshape(experts_all * cap_rows, -1)[slot_of_route].reshape(
        token_per_device, TOP, -1
    )
    mixed = (mixed_attn + jnp.sum(gate_probs[..., None] * route_out, 1)).astype(jnp.bfloat16)
    query_back, key_back, value_back, output_back, router_back = (
        lax.all_gather(w_query, ("ctx", "fsdp"), axis=0, tiled=True),
        lax.all_gather(key_weight, ("ctx", "fsdp"), axis=0, tiled=True),
        lax.all_gather(value_weight, ("ctx", "fsdp"), axis=0, tiled=True),
        lax.all_gather(w_output, ("ctx", "fsdp"), axis=0, tiled=True),
        lax.all_gather(w_router, ("ctx", "fsdp"), axis=0, tiled=True),
    )
    upstream = cotangent.astype(jnp.float32)
    dgates = jnp.sum(upstream[:, None, :] * route_out, -1)
    dpicked = gate_probs * (dgates - jnp.sum(gate_probs * dgates, -1, keepdims=True))
    dlogits_low = jnp.einsum("tj,tje->te", dpicked, chosen, precision=lax.Precision.HIGHEST).astype(
        jnp.bfloat16
    )
    router_grad = jnp.einsum("td,te->de", ffn_low, dlogits_low, preferred_element_type=jnp.float32)
    dresults = (
        (gate_probs[..., None] * upstream[:, None, :]).astype(jnp.bfloat16).reshape(routes, -1)
    )
    dresults = jnp.concatenate([dresults, jnp.zeros((1, dresults.shape[1]), jnp.bfloat16)], 0)
    dreturned = lax.all_to_all(
        dresults[route_of_slot].reshape(experts_all, cap_rows, -1),
        "ctx",
        split_axis=0,
        concat_axis=0,
        tiled=True,
    )
    dresult_rows = to_experts(dreturned)
    dhidden = jnp.einsum("esd,efd->esf", dresult_rows, down_all, preferred_element_type=jnp.float32)
    down_grad = jnp.einsum(
        "esf,esd->efd", hidden_low, dresult_rows, preferred_element_type=jnp.float32
    )
    dsilu_gate = sigmoid_gate * (1.0 + gate_part * (1.0 - sigmoid_gate))
    dgate_low = (dhidden * up_part * dsilu_gate).astype(jnp.bfloat16)
    dup_low = (dhidden * silu_gate).astype(jnp.bfloat16)
    gate_grad = jnp.einsum(
        "esd,esf->edf", expert_rows, dgate_low, preferred_element_type=jnp.float32
    )
    up_grad = jnp.einsum("esd,esf->edf", expert_rows, dup_low, preferred_element_type=jnp.float32)
    dexpert_rows = (
        jnp.einsum("esf,edf->esd", dgate_low, gate_all, preferred_element_type=jnp.float32)
        + jnp.einsum("esf,edf->esd", dup_low, up_all, preferred_element_type=jnp.float32)
    ).astype(jnp.bfloat16)
    dsent_rows = lax.all_to_all(
        from_experts(dexpert_rows), "ctx", split_axis=0, concat_axis=0, tiled=True
    )
    droutes = dsent_rows.reshape(experts_all * cap_rows, -1)[slot_of_route].reshape(
        token_per_device, TOP, -1
    )
    dffn_rows = jnp.sum(droutes.astype(jnp.float32), 1) + jnp.einsum(
        "te,de->td", dlogits_low, router_back, preferred_element_type=jnp.float32
    )
    expert_sums = (
        lax.psum_scatter(
            gate_grad.astype(jnp.bfloat16), "fsdp", scatter_dimension=1, tiled=True
        ).astype(jnp.float32),
        lax.psum_scatter(
            up_grad.astype(jnp.bfloat16), "fsdp", scatter_dimension=1, tiled=True
        ).astype(jnp.float32),
        lax.psum_scatter(
            down_grad.astype(jnp.bfloat16), "fsdp", scatter_dimension=1, tiled=True
        ).astype(jnp.float32),
    )
    dmixed_norm, ffn_gain_part = rms_back(mixed_attn, inverse_ffn, ffn_gain, dffn_rows)
    dmixed_attn = upstream + dmixed_norm
    dattn_low = dmixed_attn.astype(jnp.bfloat16)
    output_grad = jnp.einsum(
        "tc,td->cd", attended_low, dattn_low, preferred_element_type=jnp.float32
    )
    attended_lower_grad = jnp.einsum(
        "td,cd->tc", dattn_low, output_back, preferred_element_type=jnp.float32
    ).astype(jnp.bfloat16)
    output_heads_grad = attended_lower_grad.reshape(
        LOCAL_SEQUENCES, paired_rows, KEY_VALUE_HEADS, query_groups, HEAD_SIZE
    ).transpose(0, 2, 3, 1, 4)
    delta_row = jnp.sum(output_heads_grad.astype(jnp.float32) * attended, -1)
    key_recomputed, value_recomputed = (key_every, value_every)

    def score_grads(key_group, value_group, first_dev, query_group_size):
        key_row_matrix = arrange(key_group)
        value_rows = arrange(value_group)
        key_pos = group_positions(first_dev, query_group_size, context_count, block_len)
        scores = (
            jnp.einsum(
                "skgqd,swkd->skgqw",
                query_head_rows,
                key_row_matrix,
                preferred_element_type=jnp.float32,
            )
            * score_scale
        )
        allowed = key_pos[None, :] <= local_pos[:, None]
        weights_now = jnp.where(allowed, jnp.exp(scores - log_sum[..., None]), 0.0)
        dweights = jnp.einsum(
            "skgqd,swkd->skgqw", output_heads_grad, value_rows, preferred_element_type=jnp.float32
        )
        dscores = (weights_now * (dweights - delta_row[..., None])).astype(jnp.bfloat16)
        return (key_row_matrix, weights_now, dscores)

    def key_terms(weights_now, dscores, query_group_size):
        dkey_rows = jnp.einsum(
            "skgqw,skgqd->swkd", dscores, query_head_rows, preferred_element_type=jnp.float32
        )
        dvalue_rows = jnp.einsum(
            "skgqw,skgqd->swkd",
            weights_now.astype(jnp.bfloat16),
            output_heads_grad,
            preferred_element_type=jnp.float32,
        )
        return (unarrange(dkey_rows, query_group_size), unarrange(dvalue_rows, query_group_size))

    query_group_size = 4
    loop_step_count = context_count // query_group_size
    key_block_list = key_recomputed.reshape(
        loop_step_count, query_group_size, LOCAL_SEQUENCES, paired_rows, KEY_VALUE_HEADS, HEAD_SIZE
    )
    value_block_list = value_recomputed.reshape(
        loop_step_count, query_group_size, LOCAL_SEQUENCES, paired_rows, KEY_VALUE_HEADS, HEAD_SIZE
    )
    first_devs = query_group_size * jnp.arange(loop_step_count, dtype=jnp.int32)

    def back_group(dquery_acc, loop_item):
        key_group, value_group, first_dev = loop_item
        key_row_matrix, weights_now, dscores = score_grads(
            key_group, value_group, first_dev, query_group_size
        )
        dquery_acc = dquery_acc + jnp.einsum(
            "skgqw,swkd->skgqd", dscores, key_row_matrix, preferred_element_type=jnp.float32
        )
        return (dquery_acc, key_terms(weights_now, dscores, query_group_size))

    dquery_heads, key_value_pieces = lax.scan(
        back_group,
        jnp.zeros(query_head_rows.shape, jnp.float32),
        (key_block_list, value_block_list, first_devs),
    )
    key_grad_every = key_value_pieces[0].reshape(
        context_count * token_per_device, KEY_VALUE_HEADS, HEAD_SIZE
    )
    value_grad_every = key_value_pieces[1].reshape(
        context_count * token_per_device, KEY_VALUE_HEADS, HEAD_SIZE
    )
    dkey_own, value_local_grad = (
        lax.psum_scatter(key_grad_every, "ctx", scatter_dimension=0, tiled=True),
        lax.psum_scatter(value_grad_every, "ctx", scatter_dimension=0, tiled=True),
    )
    dquery = (
        (dquery_heads * score_scale)
        .transpose(0, 3, 1, 2, 4)
        .reshape(token_per_device, QUERY_HEADS, HEAD_SIZE)
    )
    dquery_proj, query_gain_part = rms_back(
        query_proj, query_inverse, query_gain, rope_back(dquery, cosine, sine_tab)
    )
    key_projection_grad, key_gain_part = rms_back(
        key_proj, key_inverse, key_gain, rope_back(dkey_own * score_scale, cosine, sine_tab)
    )
    dquery_low = dquery_proj.reshape(token_per_device, QUERY_HEADS * HEAD_SIZE).astype(jnp.bfloat16)
    key_lower_grad = key_projection_grad.reshape(
        token_per_device, KEY_VALUE_HEADS * HEAD_SIZE
    ).astype(jnp.bfloat16)
    value_lower_grad = value_local_grad.reshape(
        token_per_device, KEY_VALUE_HEADS * HEAD_SIZE
    ).astype(jnp.bfloat16)
    query_grad = jnp.einsum("td,tc->dc", normed_low, dquery_low, preferred_element_type=jnp.float32)
    key_grad = jnp.einsum(
        "td,tc->dc", normed_low, key_lower_grad, preferred_element_type=jnp.float32
    )
    value_grad = jnp.einsum(
        "td,tc->dc", normed_low, value_lower_grad, preferred_element_type=jnp.float32
    )
    dnormed = jnp.einsum("tc,dc->td", dquery_low, query_back, preferred_element_type=jnp.float32)
    dnormed = dnormed + jnp.einsum(
        "tc,dc->td", key_lower_grad, key_back, preferred_element_type=jnp.float32
    )
    dnormed = dnormed + jnp.einsum(
        "tc,dc->td", value_lower_grad, value_back, preferred_element_type=jnp.float32
    )
    dinput_norm, attention_gain_part = rms_back(inputs, inverse_attn, attention_gain, dnormed)
    d_tokens = (dmixed_attn + dinput_norm).astype(jnp.bfloat16)
    gain_sums = lax.psum(
        (attention_gain_part, ffn_gain_part, query_gain_part, key_gain_part), ("ctx", "fsdp")
    )
    layer_sums = (
        lax.psum_scatter(query_grad, ("ctx", "fsdp"), scatter_dimension=0, tiled=True),
        lax.psum_scatter(key_grad, ("ctx", "fsdp"), scatter_dimension=0, tiled=True),
        lax.psum_scatter(value_grad, ("ctx", "fsdp"), scatter_dimension=0, tiled=True),
        lax.psum_scatter(output_grad, ("ctx", "fsdp"), scatter_dimension=0, tiled=True),
        lax.psum_scatter(router_grad, ("ctx", "fsdp"), scatter_dimension=0, tiled=True),
    )
    return (
        mixed,
        d_tokens,
        gain_sums[0],
        gain_sums[1],
        gain_sums[2],
        gain_sums[3],
        layer_sums[0],
        layer_sums[1],
        layer_sums[2],
        layer_sums[3],
        layer_sums[4],
        expert_sums[0],
        expert_sums[1],
        expert_sums[2],
    )


def solution(mesh):
    return jax.shard_map(
        local,
        mesh=mesh,
        in_specs=(
            P(("ctx", "fsdp"), None),
            P(("ctx", "fsdp"), None),
            P(("ctx", "fsdp"), None),
            P(),
            P(),
            P(),
            P(),
            P(("ctx", "fsdp"), None),
            P(("ctx", "fsdp"), None),
            P(("ctx", "fsdp"), None),
            P(("ctx", "fsdp"), None),
            P(("ctx", "fsdp"), None),
            P("ctx", "fsdp", None),
            P("ctx", "fsdp", None),
            P("ctx", "fsdp", None),
        ),
        out_specs=(
            P(("ctx", "fsdp"), None),
            P(("ctx", "fsdp"), None),
            P(),
            P(),
            P(),
            P(),
            P(("ctx", "fsdp"), None),
            P(("ctx", "fsdp"), None),
            P(("ctx", "fsdp"), None),
            P(("ctx", "fsdp"), None),
            P(("ctx", "fsdp"), None),
            P("ctx", "fsdp", None),
            P("ctx", "fsdp", None),
            P("ctx", "fsdp", None),
        ),
        check_vma=False,
    )
```

profile of v0, /device:TPU:0, one launch (start us, length us, event | category | flops | bytes accessed | tf_op | source)
XLA Modules:
  0.0 3552.5 jit_solution(13697605618941445234)
XLA Ops:
  12.4 58.7 %all-gather.11.cloned.1.call-done = bf16[2048,512]{1,0:T(8,128)(2,1)} async-done(((bf16[64,512]{1,0:T(8,128)(2,1)}), bf16[2048,512]{1,0:T(8,128)(2,1)}) %all-gather.11.cloned.1.call-update) | async-done | bytes 2097168 | tf_op jit(solution)/shard_map/all_gather | solution.py:142
  75.5 53.9 %all-gather.17.cloned.1.call-done = bf16[2048,512]{1,0:T(8,128)(2,1)} async-done(((bf16[64,512]{1,0:T(8,128)(2,1)}), bf16[2048,512]{1,0:T(8,128)(2,1)}) %all-gather.17.cloned.1.call-update) | async-done | bytes 2097168 | tf_op jit(solution)/shard_map/all_gather | solution.py:143
  147.4 29.2 all-gather.13.cloned.1.call-done
  181.3 42.1 %all-gather.19.cloned.1.call-done = bf16[3072,4,128]{2,0,1:T(8,128)(2,1)} async-done(((bf16[192,4,128]{2,0,1:T(8,128)(2,1)}), bf16[3072,4,128]{2,0,1:T(8,128)(2,1)}) %all-gather.19.cloned.1.call-update) | async-done | bytes 3145744 | tf_op jit(solution)/shard_map/all_gather | solution.py:180
  228.0 111.9 %all-gather.15.cloned.1.call-done = bf16[2048,4096]{1,0:T(8,128)(2,1)} async-done(((bf16[64,4096]{1,0:T(8,128)(2,1)}), bf16[2048,4096]{1,0:T(8,128)(2,1)}) %all-gather.15.cloned.1.call-update) | async-done | bytes 16777232 | tf_op jit(solution)/shard_map/all_gather | solution.py:141
  340.0 8.1 fusion.116
  362.3 67.7 %while.34 = (s32[]{:T(128)}, f32[3,4,8,64]{3,2,1,0:T(8,128)S(1)}, f32[3,4,8,64]{3,2,1,0:T(8,128)S(1)}, f32[3,4,8,64,128]{4,3,2,1,0:T(8,128)}, s32[4]{0:T(128)S(1...) while((s32[]{:T(128)}, f32[3,4,8,64]{3,2,1,0:T(8,128)S(1)}, ...), condition=%wide.region_6.7_spmd.clone, body=%wide.region_3.6_spmd.clone.sunk | while | flops 825015680 | bytes 57086840 | solution.py:220
  439.1 16.8 all-gather.21.cloned.1.call-done
  455.9 8.3 multiply_reduce_fusion.6
  465.7 8.8 gather_fusion
  479.4 190.9 %all-gather = bf16[32,64,16]{1,2,0:T(8,128)(2,1)S(1)} all-gather(bf16[1,64,16]{1,2,0:T(8,128)(2,1)S(1)} %bitcast.408), channel_id=1, replica_groups=mesh['ctx'=16,'fsdp'=2] {'ctx','fsdp'}, dimensions={0}, use_global_device_ids=true | all-gather | bytes 67584 | tf_op jit(solution)/shard_map/all_gather | solution.py:145
  677.2 19.9 gather_fusion.2
  697.2 30.5 all-to-all-start.2
  729.5 45.6 %all-gather.25.cloned.1.call-done = bf16[1,2048,768]{2,1,0:T(8,128)(2,1)} async-done(((bf16[1,1024,768]{2,1,0:T(8,128)(2,1)}), bf16[1,2048,768]{2,1,0:T(8,128)(2,1)}) %all-gather.25.cloned.1.call-update) | async-done | bytes 3145744 | tf_op jit(solution)/shard_map/all_gather | solution.py:266
  775.0 11.4 fusion.47
  786.4 34.9 all-gather.23.cloned.1.call-done
  821.2 11.2 fusion.51
  832.4 35.0 all-gather.27.cloned.1.call-done
  869.3 15.6 multiply_convert_fusion
  884.9 8.5 convolution_convert_fusion
  893.4 34.9 all-to-all-start.1
  928.4 12.0 fusion.49
  940.4 11.8 add_convert_fusion
  952.2 117.7 %all-to-all-done.1 = bf16[16,120,2048]{2,1,0:T(8,128)(2,1)} async-done(((bf16[16,120,2048]{2,1,0:T(8,128)(2,1)}), bf16[16,120,2048]{2,1,0:T(8,128)(2,1)}, u32[]{:S(2)}, u32[]{:S(2)}) %all-to-all-start.1) | async-done | bytes 7864352 | tf_op jit(solution)/shard_map/all_to_all | solution.py:279
  1069.9 34.6 all-to-all-start.3
  1105.2 17.0 gather_fusion.1
  1130.0 116.1 %all-to-all-done.3 = bf16[16,120,2048]{2,1,0:T(8,128)(2,1)} async-done(((bf16[16,120,2048]{2,1,0:T(8,128)(2,1)}), bf16[16,120,2048]{2,1,0:T(8,128)(2,1)}, u32[]{:S(2)}, u32[]{:S(2)}) %all-to-all-start.3) | async-done | bytes 7864352 | tf_op jit(solution)/shard_map/all_to_all | solution.py:325
  1246.1 17.1 gather_fusion.3
  1263.2 7.9 convert_reduce_fusion
  1273.8 12.0 fusion.69
  1291.6 76.5 %while.35 = (s32[]{:T(128)}, f32[3,4,8,64,128]{4,3,2,1,0:T(8,128)}, f32[4,4,3,64,4,128]{5,3,2,1,0,4:T(8,128)}, f32[4,4,3,64,4,128]{5,3,2,1,0,4:T(8,128)}, s32[4]...) while((s32[]{:T(128)}, f32[3,4,8,64,128]{4,3,2,1,0:T(8,128)}, ...), condition=%wide.region_21.22_spmd.clone, body=%wide.region_20.21_spmd.clone.sunk | while | flops 2030585216 | bytes 74839472 | solution.py:413
  1370.0 10.2 fusion.55
  1382.0 10.7 fusion.53
  1394.6 10.3 fusion.54
  1407.6 74.7 %reduce-scatter.13.cloned.1.call-done = f32[192,4,128]{2,0,1:T(8,128)} async-done(((f32[3072,4,128]{2,0,1:T(8,128)}), f32[192,4,128]{2,0,1:T(8,128)}) %reduce-scatter.13.cloned.1.call-update) | async-done | bytes 393232 | tf_op jit(solution)/shard_map/reduce_scatter | solution.py:425
  1488.3 82.9 %reduce-scatter.15.cloned.1.call-done = f32[192,4,128]{2,0,1:T(8,128)} async-done(((f32[3072,4,128]{2,0,1:T(8,128)}), f32[192,4,128]{2,0,1:T(8,128)}) %reduce-scatter.15.cloned.1.call-update) | async-done | bytes 393232 | tf_op jit(solution)/shard_map/reduce_scatter | solution.py:426
  1604.8 11.5 fusion.39
  1616.3 14.3 fusion.113
  1632.1 14.7 fusion.75
  1650.3 11.4 reduce-scatter.25.cloned.1.call-done
  1665.0 42.3 %reduce-scatter.27.cloned.1.call-done = bf16[1,1024,768]{2,1,0:T(8,128)(2,1)} async-done(((bf16[1,2048,768]{2,1,0:T(8,128)(2,1)}), bf16[1,1024,768]{2,1,0:T(8,128)(2,1)}) %reduce-scatter.27.cloned.1.call-update) | async-done | bytes 1572880 | tf_op jit(solution)/shard_map/reduce_scatter | solution.py:338
  1710.6 13.1 fusion.125
  1723.8 121.3 %reduce-scatter.31.cloned.1.call-done = f32[64,16]{1,0:T(8,128)} async-done(((f32[2048,16]{1,0:T(8,128)}), f32[64,16]{1,0:T(8,128)}) %reduce-scatter.31.cloned.1.call-update) | async-done | bytes 4112
  1851.7 37.9 %all-reduce.2 = (f32[2048]{0:T(1024)}, f32[2048]{0:T(1024)}, f32[128]{0:T(128)}, f32[128]{0:T(128)}) all-reduce(f32[2048]{0:T(1024)S(1)} %get-tuple-element.490, f32[2048]{0:T(1024)S(1)} %copy-done.60, f32[128]{0:T(128)S(1)} %get-tuple-element.484, f32[128]{0:T(128)S(1)} %get-tuple-element.492), channel_id=1, replica_groups=mesh['ctx'=16,'fsdp'=2] {'ctx','fsdp'}, use_global_device_ids=true, to_apply=%region_28.29 | all-reduce | flops 4352 | bytes 34816 | tf_op jit(solution)/shard_map/psum | solution.py:462
  1892.3 94.0 %reduce-scatter.19.cloned.1.call-done = f32[64,512]{1,0:T(8,128)} async-done(((f32[2048,512]{1,0:T(8,128)}), f32[64,512]{1,0:T(8,128)}) %reduce-scatter.19.cloned.1.call-update) | async-done | bytes 131088 | tf_op jit(solution)/shard_map/reduce_scatter | solution.py:467
  1986.3 141.9 %reduce-scatter.21.cloned.1.call-done = f32[64,512]{1,0:T(8,128)} async-done(((f32[2048,512]{1,0:T(8,128)}), f32[64,512]{1,0:T(8,128)}) %reduce-scatter.21.cloned.1.call-update) | async-done | bytes 131088 | tf_op jit(solution)/shard_map/reduce_scatter | solution.py:468
  2128.2 705.3 %reduce-scatter.17.cloned.1.call-done = f32[64,4096]{1,0:T(8,128)} async-done(((f32[2048,4096]{1,0:T(8,128)}), f32[64,4096]{1,0:T(8,128)}) %reduce-scatter.17.cloned.1.call-update) | async-done | bytes 1048592 | tf_op jit(solution)/shard_map/reduce_scatter | solution.py:466
  2833.5 711.5 %reduce-scatter.23.cloned.1.call-done = f32[128,2048]{1,0:T(8,128)} async-done(((f32[4096,2048]{1,0:T(8,128)}), f32[128,2048]{1,0:T(8,128)}) %reduce-scatter.23.cloned.1.call-update) | async-done | bytes 1048592 | tf_op jit(solution)/shard_map/reduce_scatter | solution.py:469
  (457 shorter events, 304.0 us)
Async XLA Ops:
  8.0 63.0 %all-gather.11.cloned.1.call-start = ((), (), s32[]{:S(2)}) async-start(), calls=%async_computation.14 | async-start | bytes 2162688 | tf_op jit(solution)/shard_map/all_gather | solution.py:142
  8.7 120.7 %all-gather.17.cloned.1.call-start = ((), (), s32[]{:S(2)}) async-start(), calls=%async_computation.17 | async-start | bytes 2162688 | tf_op jit(solution)/shard_map/all_gather | solution.py:143
  9.5 167.1 %all-gather.13.cloned.1.call-start = ((), (), s32[]{:S(2)}) async-start(), calls=%async_computation.15 | async-start | bytes 3342336 | tf_op jit(solution)/shard_map/all_gather | solution.py:179
  9.8 64.3 %copy-start.66 = (f32[128]{0:T(128)S(1)}, f32[128]{0:T(128)}, u32[]{:S(2)}) copy-start(f32[128]{0:T(128)} %param.25) | copy-start | bytes 1540
  10.9 63.6 %copy-start.40 = (f32[192,128]{1,0:T(8,128)}, f32[192,128]{1,0:T(8,128)S(1)}, u32[]{:S(2)}) copy-start(f32[192,128]{1,0:T(8,128)S(1)} %get-tuple-element.573) | copy-start | bytes 294916
  10.9 63.6 %copy-start.44 = (f32[192,128]{1,0:T(8,128)}, f32[192,128]{1,0:T(8,128)S(1)}, u32[]{:S(2)}) copy-start(f32[192,128]{1,0:T(8,128)S(1)} %get-tuple-element.572) | copy-start | bytes 294916
  12.3 327.6 %copy-start.57 = (f32[192]{0:T(256)}, f32[192]{0:T(256)S(1)}, u32[]{:S(2)}) copy-start(f32[192]{0:T(256)S(1)} %add_rsqrt_fusion.3) | copy-start | bytes 2308
  73.5 58.1 %copy-start.24 = (f32[192,512]{1,0:T(8,128)}, f32[192,512]{1,0:T(8,128)S(1)}, u32[]{:S(2)}) copy-start(f32[192,512]{1,0:T(8,128)S(1)} %fusion.118) | copy-start | bytes 1179652
  73.5 55.9 %copy-start.7 = (bf16[192,2048]{1,0:T(8,128)(2,1)S(1)}, bf16[192,2048]{1,0:T(8,128)(2,1)}, u32[]{:S(2)}) copy-start(bf16[192,2048]{1,0:T(8,128)(2,1)} %param.19) | copy-start | bytes 2359300
  73.6 55.9 %copy-start.48 = (f32[2048]{0:T(1024)S(1)}, f32[2048]{0:T(1024)}, u32[]{:S(2)}) copy-start(f32[2048]{0:T(1024)} %param.22) | copy-start | bytes 24580
  75.4 58.2 %copy-start.63 = (s32[192,8]{0,1:T(8,128)S(1)}, s32[192,8]{0,1:T(8,128)}, u32[]{:S(2)}) copy-start(s32[192,8]{0,1:T(8,128)} %param.21) | copy-start | bytes 18436
  75.5 147.9 %all-gather.19.cloned.1.call-start = ((), (), s32[]{:S(2)}) async-start(), calls=%async_computation.18 | async-start | bytes 3342336 | tf_op jit(solution)/shard_map/all_gather | solution.py:180
  132.4 207.6 %all-gather.15.cloned.1.call-start = ((), (), s32[]{:S(2)}) async-start(), calls=%async_computation.16 | async-start | bytes 17301504 | tf_op jit(solution)/shard_map/all_gather | solution.py:141
  133.0 322.9 %all-gather.21.cloned.1.call-start = ((), (), s32[]{:S(2)}) async-start(), calls=%async_computation.19 | async-start | bytes 17301504 | tf_op jit(solution)/shard_map/all_gather | solution.py:144
  147.4 212.2 %copy-start.38 = (f32[3,64,128]{2,1,0:T(8,128)}, f32[3,64,128]{2,1,0:T(8,128)S(1)}, u32[]{:S(2)}) copy-start(f32[3,64,128]{2,1,0:T(8,128)S(1)} %get-tuple-element.574) | copy-start | bytes 294916
  433.1 22.8 copy-start.8
  439.1 26.3 copy-start.55
  465.6 205.1 %copy-start.19 = (bf16[192,2048]{1,0:T(8,128)(2,1)}, bf16[192,2048]{1,0:T(8,128)(2,1)S(1)}, u32[]{:S(2)}) copy-start(bf16[192,2048]{1,0:T(8,128)(2,1)S(1)} %multiply_convert_fusion.3) | copy-start | bytes 2359300
  474.5 196.0 %copy-start.33 = (bf16[192,2048]{1,0:T(8,128)(2,1)S(1)}, bf16[192,2048]{1,0:T(8,128)(2,1)}, u32[]{:S(2)}) copy-start(bf16[192,2048]{1,0:T(8,128)(2,1)} %param.20) | copy-start | bytes 2359300
  474.5 222.6 %all-to-all-start = ((bf16[16,120,2048]{2,1,0:T(8,128)(2,1)}), bf16[16,120,2048]{2,1,0:T(8,128)(2,1)}, u32[]{:S(2)}, u32[]{:S(2)}) async-start(bf16[16,120,2048]{2,1,0:T(8,128)(2,1)} %bitcast.374), calls=%async_computation | async-start | bytes 15728640 | tf_op jit(solution)/shard_map/all_to_all | solution.py:247
  697.2 172.1 %all-to-all-start.2 = ((bf16[16,120,2048]{2,1,0:T(8,128)(2,1)}), bf16[16,120,2048]{2,1,0:T(8,128)(2,1)}, u32[]{:S(2)}, u32[]{:S(2)}) async-start(bf16[16,120,2048]{2,1,0:T(8,128)(2,1)} %bitcast.373), calls=%async_computation.2 | async-start | bytes 15728640 | tf_op jit(solution)/shard_map/all_to_all | solution.py:302
  727.7 47.3 %all-gather.25.cloned.1.call-start = ((), (), s32[]{:S(2)}) async-start(), calls=%async_computation.21 | async-start | bytes 4718592 | tf_op jit(solution)/shard_map/all_gather | solution.py:266
  728.3 92.9 %all-gather.23.cloned.1.call-start = ((), (), s32[]{:S(2)}) async-start(), calls=%async_computation.20 | async-start | bytes 4718592 | tf_op jit(solution)/shard_map/all_gather | solution.py:265
  728.9 138.6 %all-gather.27.cloned.1.call-start = ((), (), s32[]{:S(2)}) async-start(), calls=%async_computation.22 | async-start | bytes 4718592 | tf_op jit(solution)/shard_map/all_gather | solution.py:267
  893.4 176.5 %all-to-all-start.1 = ((bf16[16,120,2048]{2,1,0:T(8,128)(2,1)}), bf16[16,120,2048]{2,1,0:T(8,128)(2,1)}, u32[]{:S(2)}, u32[]{:S(2)}) async-start(bf16[16,120,2048]{2,1,0:T(8,128)(2,1)} %bitcast.390), calls=%async_computation.1 | async-start | bytes 15728640 | tf_op jit(solution)/shard_map/all_to_all | solution.py:279
  1069.9 34.6 copy-start.62
  1069.9 34.7 copy-start.28
  1069.9 34.7 copy-start.32
  1069.9 176.1 %all-to-all-start.3 = ((bf16[16,120,2048]{2,1,0:T(8,128)(2,1)}), bf16[16,120,2048]{2,1,0:T(8,128)(2,1)}, u32[]{:S(2)}, u32[]{:S(2)}) async-start(bf16[16,120,2048]{2,1,0:T(8,128)(2,1)} %bitcast.389), calls=%async_computation.3 | async-start | bytes 15728640 | tf_op jit(solution)/shard_map/all_to_all | solution.py:325
  1104.5 377.9 %reduce-scatter.13.cloned.1.call-start = ((), (), s32[]{:S(2)}) async-start(), calls=%async_computation.23 | async-start | bytes 6684672 | tf_op jit(solution)/shard_map/reduce_scatter | solution.py:425
  1368.1 203.2 %reduce-scatter.15.cloned.1.call-start = ((), (), s32[]{:S(2)}) async-start(), calls=%async_computation.24 | async-start | bytes 6684672 | tf_op jit(solution)/shard_map/reduce_scatter | solution.py:426
  1368.8 278.0 %reduce-scatter.29.cloned.1.call-start = ((), (), s32[]{:S(2)}) async-start(), calls=%async_computation.31 | async-start | bytes 4718592 | tf_op jit(solution)/shard_map/reduce_scatter | solution.py:341
  1380.2 281.4 %reduce-scatter.25.cloned.1.call-start = ((), (), s32[]{:S(2)}) async-start(), calls=%async_computation.29 | async-start | bytes 4718592 | tf_op jit(solution)/shard_map/reduce_scatter | solution.py:335
  1392.8 314.5 %reduce-scatter.27.cloned.1.call-start = ((), (), s32[]{:S(2)}) async-start(), calls=%async_computation.30 | async-start | bytes 4718592 | tf_op jit(solution)/shard_map/reduce_scatter | solution.py:338
  1404.9 77.5 %copy-start.52 = (f32[192,128]{1,0:T(8,128)S(1)}, f32[192,128]{1,0:T(8,128)}, u32[]{:S(2)}) copy-start(f32[192,128]{1,0:T(8,128)} %get-tuple-element.571) | copy-start | bytes 294916
  1404.9 78.6 %copy-start.25 = (f32[192,512]{1,0:T(8,128)S(1)}, f32[192,512]{1,0:T(8,128)}, u32[]{:S(2)}) copy-start(f32[192,512]{1,0:T(8,128)} %copy-done.24) | copy-start | bytes 1179652
  1404.9 78.6 %copy-start.51 = (f32[192,128]{1,0:T(8,128)S(1)}, f32[192,128]{1,0:T(8,128)}, u32[]{:S(2)}) copy-start(f32[192,128]{1,0:T(8,128)} %get-tuple-element.570) | copy-start | bytes 294916
  1405.0 78.6 %copy-start.54 = (f32[192,4]{0,1:T(4,128)S(1)}, f32[192,4]{0,1:T(4,128)}, u32[]{:S(2)}) copy-start(f32[192,4]{0,1:T(4,128)} %copy-done.53) | copy-start | bytes 9220
  1405.0 78.6 %copy-start.67 = (f32[128]{0:T(128)S(1)}, f32[128]{0:T(128)}, u32[]{:S(2)}) copy-start(f32[128]{0:T(128)} %param.25) | copy-start | bytes 1540
  1405.0 440.1 %reduce-scatter.31.cloned.1.call-start = ((), (), s32[]{:S(2)}) async-start(), calls=%async_computation.32 | async-start | bytes 1081344
  1407.6 77.8 %copy-start.9 = (bf16[192,2048]{1,0:T(8,128)(2,1)S(1)}, bf16[192,2048]{1,0:T(8,128)(2,1)}, u32[]{:S(2)}) copy-start(bf16[192,2048]{1,0:T(8,128)(2,1)} %param.19) | copy-start | bytes 2359300
  1407.6 77.8 %copy-start.49 = (f32[2048]{0:T(1024)S(1)}, f32[2048]{0:T(1024)}, u32[]{:S(2)}) copy-start(f32[2048]{0:T(1024)} %param.22) | copy-start | bytes 24580
  1407.6 77.8 %copy-start.58 = (f32[192]{0:T(256)S(1)}, f32[192]{0:T(256)}, u32[]{:S(2)}) copy-start(f32[192]{0:T(256)} %copy-done.57) | copy-start | bytes 2308
  1407.6 578.7 %reduce-scatter.19.cloned.1.call-start = ((), (), s32[]{:S(2)}) async-start(), calls=%async_computation.26 | async-start | bytes 4325376 | tf_op jit(solution)/shard_map/reduce_scatter | solution.py:467
  1488.3 639.9 %reduce-scatter.21.cloned.1.call-start = ((), (), s32[]{:S(2)}) async-start(), calls=%async_computation.27 | async-start | bytes 4325376 | tf_op jit(solution)/shard_map/reduce_scatter | solution.py:468
  1575.1 1258.3 %reduce-scatter.17.cloned.1.call-start = ((), (), s32[]{:S(2)}) async-start(), calls=%async_computation.25 | async-start | bytes 34603008 | tf_op jit(solution)/shard_map/reduce_scatter | solution.py:466
  1630.7 1914.3 %reduce-scatter.23.cloned.1.call-start = ((), (), s32[]{:S(2)}) async-start(), calls=%async_computation.28 | async-start | bytes 34603008 | tf_op jit(solution)/shard_map/reduce_scatter | solution.py:469
  1723.8 125.8 %copy-start.36 = (f32[192,4,128]{2,0,1:T(8,128)S(1)}, f32[192,4,128]{2,0,1:T(8,128)}, u32[]{:S(2)}) copy-start(f32[192,4,128]{2,0,1:T(8,128)} %reduce-scatter.15.cloned.1.call-done) | copy-start | bytes 1179652
  (64 other events, 285.2 us)
Sparse Core Ops, SparseCore 0:
  11.8 59.1 all-gather.10
  74.0 55.3 all-gather.16
  132.3 44.3 all-gather.12
  179.3 44.0 all-gather.18
  226.2 113.6 all-gather.14
  342.8 113.0 all-gather.20
  1368.2 114.1 reduce-scatter.12
  1486.8 84.3 reduce-scatter.14
  1573.5 42.5 reduce-scatter.28
  1618.3 43.3 reduce-scatter.24
  1663.9 43.3 reduce-scatter.26
  1709.5 135.5 reduce-scatter.30
  1847.9 138.3 reduce-scatter.18
  1989.0 139.1 reduce-scatter.20
  2130.9 702.5 reduce-scatter.16
  2836.2 708.7 reduce-scatter.22
Sparse Core Ops, SparseCore 1:
  729.7 45.2 all-gather.24
  776.4 44.7 all-gather.22
  822.7 44.7 all-gather.26
where the time goes:
time: 3560 us; the launch traced here: 3550 us
  waiting for transfers between devices  2650 us (74%)
  matrix products  275 us (8%)
  blocking collectives  229 us (6%)
  local copies, waits for them, and re-layouts  160 us (4%)
  other arithmetic  112 us (3%)
  starting transfers between devices  106 us (3%)
    reduce_scatter x1, waiting for transfers between devices, local(): lax.psum_scatter(output_grad, ('ctx', 'fsdp'), scatter_dimension=0, tiled...  711 us
    reduce_scatter x1, waiting for transfers between devices, local(): lax.psum_scatter(query_grad, ('ctx', 'fsdp'), scatter_dimension=0, tiled=...  705 us
    all_gather x1, blocking collectives, local(): lax.all_gather(w_router, ('ctx', 'fsdp'), axis=0, tiled=True)  191 us
    reduce_scatter x1, waiting for transfers between devices, local(): lax.psum_scatter(value_grad, ('ctx', 'fsdp'), scatter_dimension=0, tiled=...  142 us
    unnamed x20, waiting for transfers between devices  126 us
    all_to_all x1, waiting for transfers between devices, local(): lax.all_to_all(from_experts(results), 'ctx', split_axis=0, concat_axis=0,...  118 us
    all_to_all x1, waiting for transfers between devices, local(): lax.all_to_all(from_experts(dexpert_rows), 'ctx', split_axis=0, concat_ax...  116 us
    all_gather x1, waiting for transfers between devices, local(): lax.all_gather(w_query, ('ctx', 'fsdp'), axis=0, tiled=True)  112 us
  transfers between devices with their start and end apart: 23, of which 21 were waited for; matrix products, arithmetic and copies ran while one was open for 10% of the time, Pallas kernels for 0%

commit v1 on v0

--- a/solution.py
+++ b/solution.py
@@ -3,6 +3,9 @@
 import jax
 import jax.numpy as jnp
 from jax import lax
+from jax.experimental import pallas as pl
+from jax.experimental.pallas import tpu as pltpu
+from jax.sharding import Mesh
 from jax.sharding import PartitionSpec as P
 
 QUERY_HEADS = 32
@@ -106,7 +109,7 @@
     return (new_max, new_sum, run_acc * factor[..., None] + update)
 
 
-def local(
+def routed_layer(
     tokens,
     cotangent,
     expert_ids,
@@ -487,42 +490,544 @@
     )
 
 
+MEMBERS = 4
+
+
+def shift(block, axis, step):
+    count = lax.axis_size(axis)
+    return lax.ppermute(block, axis, [(i, (i + step) % count) for i in range(count)])
+
+
+def swap(block, axis):
+    return lax.ppermute(block, axis, [(0, 1), (1, 0)])
+
+
+def after(block, *earlier):
+    return lax.optimization_barrier((block,) + earlier)[0]
+
+
+def gather_members(block):
+    other = swap(block, "y")
+    near = swap(jnp.stack([block, other]), "c")
+    return jnp.stack([block, near[0], other, near[1]])
+
+
+def scatter_members(parts):
+    low = jnp.bfloat16
+    near = swap(jnp.stack([parts[1].astype(low), parts[3].astype(low)]), "c")
+    own = parts[0].astype(jnp.float32) + near[0].astype(jnp.float32)
+    other = (parts[2].astype(jnp.float32) + near[1].astype(jnp.float32)).astype(low)
+    return own + swap(other, "y").astype(jnp.float32)
+
+
+def exchange_members(blocks):
+    far = swap(jnp.stack([blocks[2], blocks[3]]), "y")
+    near = swap(jnp.stack([blocks[1], far[1]]), "c")
+    return [blocks[0], near[0], far[0], near[1]]
+
+
+def pick(stack, index):
+    return lax.dynamic_index_in_dim(stack, index, 0, keepdims=False)
+
+
+def roped(raw, gain, cosine, sine):
+    inverse = lax.rsqrt(jnp.mean(raw * raw, -1, keepdims=True) + EPS)
+    scaled = raw * inverse * gain
+    return scaled * cosine + pltpu.roll(scaled, HEAD_SIZE // 2, 1) * sine
+
+
+def attend_kernel(heads_ref, q_ref, k_ref, v_ref, cos_ref, sin_ref, gain_ref, mask_ref, out_ref):
+    queries = q_ref.shape[0] * q_ref.shape[2]
+    keys = k_ref.shape[0] * k_ref.shape[1] * k_ref.shape[3]
+    exponent = math.log2(math.e) / math.sqrt(HEAD_SIZE)
+    q = roped(
+        q_ref[...].reshape(queries, HEAD_SIZE), gain_ref[...], cos_ref[...], sin_ref[...]
+    ).astype(jnp.bfloat16)
+    k = k_ref[...].reshape(keys, HEAD_SIZE)
+    v = v_ref[...].reshape(keys, HEAD_SIZE)
+    scores = lax.dot_general(k, q, (((1,), (1,)), ((), ())), preferred_element_type=jnp.float32)
+    weights = jnp.exp2(scores * exponent) * mask_ref[...]
+    total = jnp.sum(weights, 0, keepdims=True)
+    mixed = lax.dot_general(
+        v,
+        weights.astype(jnp.bfloat16),
+        (((0,), (0,)), ((), ())),
+        preferred_element_type=jnp.float32,
+    )
+    mixed = (mixed / total).T
+    out_ref[...] = mixed.astype(jnp.bfloat16).reshape(out_ref.shape)
+
+
+def attend_back_kernel(
+    heads_ref,
+    q_ref,
+    up_ref,
+    k_ref,
+    v_ref,
+    cos_ref,
+    sin_ref,
+    gain_ref,
+    mask_ref,
+    dq_ref,
+    dkv_ref,
+    dgain_ref,
+):
+    queries = q_ref.shape[0] * q_ref.shape[2]
+    keys = k_ref.shape[0] * k_ref.shape[1] * k_ref.shape[3]
+    score_scale = 1.0 / math.sqrt(HEAD_SIZE)
+    exponent = math.log2(math.e) * score_scale
+    cosine, sine, gain = cos_ref[...], sin_ref[...], gain_ref[...]
+    raw = q_ref[...].reshape(queries, HEAD_SIZE)
+    inverse = lax.rsqrt(jnp.mean(raw * raw, -1, keepdims=True) + EPS)
+    unit = raw * inverse
+    scaled = unit * gain
+    q = (scaled * cosine + pltpu.roll(scaled, HEAD_SIZE // 2, 1) * sine).astype(jnp.bfloat16)
+    up = up_ref[...].reshape(queries, HEAD_SIZE)
+    k = k_ref[...].reshape(keys, HEAD_SIZE)
+    v = v_ref[...].reshape(keys, HEAD_SIZE)
+    across = (((1,), (1,)), ((), ()))
+    down = (((0,), (0,)), ((), ()))
+    scores = lax.dot_general(k, q, across, preferred_element_type=jnp.float32)
+    weights = jnp.exp2(scores * exponent) * mask_ref[...]
+    probs = weights * (1.0 / jnp.sum(weights, 0, keepdims=True))
+    dprobs = lax.dot_general(v, up, across, preferred_element_type=jnp.float32)
+    delta = jnp.sum(probs * dprobs, 0, keepdims=True)
+    dscores = (probs * (dprobs - delta)).astype(jnp.bfloat16)
+    dv = jnp.dot(probs.astype(jnp.bfloat16), up, preferred_element_type=jnp.float32)
+    dk = jnp.dot(dscores, q, preferred_element_type=jnp.float32) * score_scale
+    dq = lax.dot_general(k, dscores, down, preferred_element_type=jnp.float32).T * score_scale
+    dkv = jnp.concatenate([dk, dv], 1).reshape(dkv_ref.shape)
+
+    @pl.when(pl.program_id(1) == 0)
+    def _():
+        dkv_ref[...] = dkv
+
+    @pl.when(pl.program_id(1) != 0)
+    def _():
+        dkv_ref[...] += dkv
+
+    turned = dq * cosine - pltpu.roll(dq, HEAD_SIZE // 2, 1) * sine
+    part = jnp.sum(turned * unit, 0, keepdims=True)
+    part = jnp.concatenate([part, jnp.zeros((7, HEAD_SIZE), jnp.float32)], 0)
+    first = (pl.program_id(0) == 0) & (pl.program_id(1) == 0)
+
+    @pl.when(first)
+    def _():
+        dgain_ref[...] = part
+
+    @pl.when(jnp.logical_not(first))
+    def _():
+        dgain_ref[...] += part
+
+    turned = turned * gain
+    back = inverse * (turned - unit * jnp.mean(turned * unit, -1, keepdims=True))
+    dq_ref[...] = back.astype(jnp.bfloat16).reshape(dq_ref.shape)
+
+
+def attention_specs(q, kv):
+    nz, members, sequences, paired, _ = kv.shape
+    q_block = (members, 1, paired, HEAD_SIZE)
+    kv_block = (nz, members, 1, paired, HEAD_SIZE)
+    keys, queries = nz * members * paired, members * paired
+    own = pl.BlockSpec(q_block, lambda s, r, heads: (0, s, 0, heads[r]))
+    relative = pl.BlockSpec(q_block, lambda s, r, heads: (0, s, 0, r))
+    key = pl.BlockSpec(kv_block, lambda s, r, heads: (0, 0, s, 0, 0))
+    value = pl.BlockSpec(kv_block, lambda s, r, heads: (0, 0, s, 0, 1))
+    both = pl.BlockSpec(
+        (nz, members, 1, paired, 2 * HEAD_SIZE), lambda s, r, heads: (0, 0, s, 0, 0)
+    )
+    fixed = lambda shape: pl.BlockSpec(shape, lambda s, r, heads: (0, 0))
+    tables = [
+        fixed((queries, HEAD_SIZE)),
+        fixed((queries, HEAD_SIZE)),
+        fixed((1, HEAD_SIZE)),
+        fixed((keys, queries)),
+    ]
+    return own, relative, key, value, both, fixed, tables
+
+
+def attend(heads, q, kv, cosine, sine, gain, mask):
+    members, sequences, paired, width = q.shape
+    own, relative, key, value, both, fixed, tables = attention_specs(q, kv)
+    count = heads.shape[0]
+    elements = sequences * count * mask.size
+    return pl.pallas_call(
+        attend_kernel,
+        grid_spec=pltpu.PrefetchScalarGridSpec(
+            num_scalar_prefetch=1,
+            grid=(sequences, count),
+            in_specs=[own, key, value] + tables,
+            out_specs=relative,
+        ),
+        out_shape=jax.ShapeDtypeStruct(
+            (members, sequences, paired, count * HEAD_SIZE), jnp.bfloat16
+        ),
+        compiler_params=pltpu.CompilerParams(vmem_limit_bytes=40 * 2**20),
+        cost_estimate=pl.CostEstimate(
+            flops=4 * elements * HEAD_SIZE, bytes_accessed=8 * 2**20, transcendentals=elements
+        ),
+    )(heads, q, kv, kv, cosine, sine, gain, mask)
+
+
+def attend_back(heads, q, up, kv, cosine, sine, gain, mask):
+    members, sequences, paired, width = q.shape
+    own, relative, key, value, both, fixed, tables = attention_specs(q, kv)
+    count = heads.shape[0]
+    elements = sequences * count * mask.size
+    return pl.pallas_call(
+        attend_back_kernel,
+        grid_spec=pltpu.PrefetchScalarGridSpec(
+            num_scalar_prefetch=1,
+            grid=(sequences, count),
+            in_specs=[own, relative, key, value] + tables,
+            out_specs=(own, both, fixed((8, HEAD_SIZE))),
+        ),
+        out_shape=(
+            jax.ShapeDtypeStruct((members, sequences, paired, count * HEAD_SIZE), jnp.bfloat16),
+            jax.ShapeDtypeStruct(kv.shape, jnp.float32),
+            jax.ShapeDtypeStruct((8, HEAD_SIZE), jnp.float32),
+        ),
+        compiler_params=pltpu.CompilerParams(vmem_limit_bytes=40 * 2**20),
+        cost_estimate=pl.CostEstimate(
+            flops=10 * elements * HEAD_SIZE, bytes_accessed=16 * 2**20, transcendentals=elements
+        ),
+    )(heads, q, up, kv, kv, cosine, sine, gain, mask)
+
+
+def dot32(subscripts, left, right):
+    return jnp.einsum(subscripts, left, right, preferred_element_type=jnp.float32)
+
+
+def member_layer(
+    tokens,
+    cotangent,
+    expert_ids,
+    attention_gain,
+    ffn_gain,
+    query_gain,
+    key_gain,
+    w_query,
+    key_weight,
+    value_weight,
+    w_output,
+    w_router,
+    w_gate,
+    w_up,
+    w_down,
+):
+    low, wide = jnp.bfloat16, jnp.float32
+    nz = lax.axis_size("z")
+    zi, yi, ci, xi = (lax.axis_index(axis) for axis in ("z", "y", "c", "x"))
+    member = 2 * yi + ci
+    context_count = nz * MEMBERS
+    rows, model = tokens.shape
+    paired = rows // LOCAL_SEQUENCES
+    block_len = paired // 2
+    groups = QUERY_HEADS // KEY_VALUE_HEADS
+    experts_all = w_router.shape[1]
+    relative = jnp.arange(MEMBERS, dtype=jnp.int32)
+    from_z = (zi - jnp.arange(nz, dtype=jnp.int32)) % nz
+    members = member ^ relative
+
+    inputs = tokens.astype(wide)
+    normed_attn, inverse_attn = rms_apply(inputs, attention_gain)
+    normed_low = normed_attn.astype(low)
+    normed_all = gather_members(normed_low).reshape(MEMBERS * rows, model)
+
+    piece = w_query.shape[0]
+    columns = jnp.concatenate(
+        [w.reshape(piece, KEY_VALUE_HEADS, -1) for w in (w_query, key_weight, value_weight)], -1
+    ).transpose(1, 0, 2)
+    width = columns.shape[-1]
+    parts = exchange_members([pick(columns, members[j]) for j in range(MEMBERS)])
+    ordered = jnp.stack(parts)[members]
+    qkv_weight = jnp.zeros((nz, MEMBERS, 2, piece, width), low)
+    last = None
+    for k in range(nz):
+        held = ordered if k == 0 else shift(ordered, "z", k)
+        crossed = swap(held, "x")
+        qkv_weight = lax.dynamic_update_slice(
+            qkv_weight, held[None, :, None], (from_z[k], 0, xi, 0, 0)
+        )
+        qkv_weight = lax.dynamic_update_slice(
+            qkv_weight, crossed[None, :, None], (from_z[k], 0, 1 - xi, 0, 0)
+        )
+        last = held
+    qkv_weight = qkv_weight.reshape(model, width)
+
+    router = jnp.stack([w_router] + [shift(w_router, "z", k) for k in range(1, nz)])
+    for axis in ("y", "c", "x"):
+        router = jnp.stack([router, swap(router, axis)], 1)
+    router = router.reshape(nz, 2, 2, 2, piece, experts_all)
+    order_z = from_z_index = (zi - jnp.arange(nz, dtype=jnp.int32)) % nz
+    router = router[order_z]
+    two = jnp.arange(2, dtype=jnp.int32)
+    router = router[:, two ^ xi][:, :, two ^ ci][:, :, :, two ^ yi]
+    router_all = router.transpose(0, 3, 2, 1, 4, 5).reshape(model, experts_all)
+    ids = expert_ids.T
+    ids_all = jnp.stack([ids] + [shift(ids, "z", k) for k in range(1, nz)])
+    ids_all = jnp.stack([ids_all, swap(ids_all, "y")], 1)
+    near = swap(ids_all, "c")
+    ids_all = jnp.stack([ids_all, near], 2).reshape(nz, MEMBERS, TOP, rows)
+    own_expert = zi * MEMBERS + member
+    named = jnp.any(ids_all == own_expert, 2)
+    before = (
+        jnp.arange(rows, dtype=jnp.int32)[:, None] <= jnp.arange(rows, dtype=jnp.int32)[None, :]
+    )
+    ranks = dot32("kjs,st->kjt", named.astype(low), before.astype(low)).astype(jnp.int32) - 1
+    cap_rows = rows * TOP * 5 // (4 * experts_all)
+    slots = -(-cap_rows // 16) * 16
+    places = (
+        (ranks[:, :, None, :] == jnp.arange(slots, dtype=jnp.int32)[:, None])
+        & named[:, :, None, :]
+    ).astype(low)
+
+    qkv = jnp.dot(normed_all, qkv_weight, preferred_element_type=wide)
+    qkv = qkv.reshape(MEMBERS, LOCAL_SEQUENCES, paired, width)
+    all_pos = jax.vmap(lambda device: shard_positions(device, context_count, block_len))(
+        (from_z[:, None] * MEMBERS + members[None, :]).reshape(-1)
+    )
+    own_pos = all_pos[:MEMBERS].reshape(-1)
+    mask = (all_pos.reshape(-1)[:, None] <= own_pos[None, :]).astype(wide)
+    cosine, sine_tab = rotary(own_pos, HEAD_SIZE)
+    cosine, sine_tab = cosine[:, 0], sine_tab[:, 0]
+    half = HEAD_SIZE // 2
+    sine = jnp.concatenate([-sine_tab[:, :half], sine_tab[:, half:]], -1)
+    row_cosine = cosine.reshape(MEMBERS, 1, paired, HEAD_SIZE)
+    row_sine = sine_tab.reshape(MEMBERS, 1, paired, HEAD_SIZE)
+    query_width = groups * HEAD_SIZE
+    key_proj = qkv[..., query_width : query_width + HEAD_SIZE]
+    key_normed, key_inverse = rms_apply(key_proj, key_gain)
+    key_low = rope_apply(key_normed, row_cosine, row_sine).astype(low)
+    key_value = jnp.concatenate([key_low, qkv[..., query_width + HEAD_SIZE :].astype(low)], -1)
+    key_value = jnp.stack([key_value] + [shift(key_value, "z", k) for k in range(1, nz)])
+
+    relative_heads = jnp.arange(groups, dtype=jnp.int32)
+    heads = ((relative_heads & 3) ^ member) * 2 + ((relative_heads >> 2) ^ xi)
+    gain_row = query_gain[None]
+    attended = attend(heads, qkv, key_value, cosine, sine, gain_row, mask)
+    attended = attended.reshape(MEMBERS * rows, query_width)
+
+    head_rows = w_output.shape[0]
+    behind = after(w_output, last)
+    planes = jnp.stack([behind] + [shift(behind, "z", k) for k in range(1, nz)])
+    wanted = exchange_members([pick(planes, (zi - members[j]) % nz) for j in range(MEMBERS)])
+    wanted = jnp.stack(wanted)
+    output_weight = jnp.stack([wanted, swap(wanted, "x")]).reshape(query_width, model)
+    mixed_part = jnp.dot(attended, output_weight, preferred_element_type=wide)
+    mixed_attn = inputs + scatter_members(mixed_part.reshape(MEMBERS, rows, model))
+    normed_ffn, inverse_ffn = rms_apply(mixed_attn, ffn_gain)
+    ffn_low = normed_ffn.astype(low)
+
+    logits = dot32("de,td->et", router_all, ffn_low)
+    chosen = jnp.any(
+        ids[:, None, :] == jnp.arange(experts_all, dtype=jnp.int32)[None, :, None], 0
+    )
+    highest = jnp.max(jnp.where(chosen, logits, NEGATIVE_LIMIT), 0, keepdims=True)
+    raised = jnp.where(chosen, jnp.exp(jnp.where(chosen, logits, highest) - highest), 0.0)
+    gates = raised / jnp.sum(raised, 0, keepdims=True)
+    gates_all = jnp.stack([gates] + [shift(gates, "z", k) for k in range(1, nz)])
+    gates_all = jnp.stack([gates_all, swap(gates_all, "y")], 1)
+    near = swap(gates_all, "c")
+    gates_all = jnp.stack([gates_all, near], 2).reshape(nz, MEMBERS, experts_all, rows)
+    own_gates = lax.dynamic_index_in_dim(gates_all, own_expert, 2, keepdims=False)
+
+    def whole(part, earlier):
+        part = after(part, earlier)
+        other = swap(part, "x")
+        full = jnp.zeros((2,) + part.shape[1:], low)
+        full = lax.dynamic_update_slice(full, part, (xi, 0, 0))
+        full = lax.dynamic_update_slice(full, other, (1 - xi, 0, 0))
+        return full.reshape(2 * part.shape[1], part.shape[2])
+
+    gate_all, up_all, down_all = (
+        whole(w_gate, last),
+        whole(w_up, last),
+        whole(w_down, last),
+    )
+
+    def spread(block):
+        return [gather_members(block if k == 0 else shift(block, "z", k)) for k in range(nz)]
+
+    cotangents = spread(after(cotangent, last))
+    arrived = spread(ffn_low)
+    sent, dsent, dgates, kept = [], [], [], []
+    for k in range(nz):
+        place, gate_col = places[k], own_gates[k][..., None]
+        upstream = cotangents[k]
+        expert_rows = dot32("jst,jtd->jsd", place, arrived[k]).astype(low)
+        expert_rows = expert_rows.reshape(MEMBERS * slots, model)
+        gate_part = jnp.dot(expert_rows, gate_all, preferred_element_type=wide)
+        up_part = jnp.dot(expert_rows, up_all, preferred_element_type=wide)
+        sigmoid_gate = jax.nn.sigmoid(gate_part)
+        silu_gate = gate_part * sigmoid_gate
+        hidden_low = (silu_gate * up_part).astype(low)
+        results = jnp.dot(hidden_low, down_all, preferred_element_type=wide).astype(low)
+        token_results = dot32(
+            "jst,jsd->jtd", place, results.reshape(MEMBERS, slots, model)
+        ).astype(low)
+        sent.append((gate_col * token_results).astype(low))
+        dgates.append(jnp.sum(upstream.astype(wide) * token_results.astype(wide), -1))
+        dresults = dot32("jst,jtd->jsd", place, (gate_col * upstream).astype(low)).astype(low)
+        dresults = dresults.reshape(MEMBERS * slots, model)
+        dhidden = dot32("sd,fd->sf", dresults, down_all)
+        dsilu_gate = sigmoid_gate * (1.0 + gate_part * (1.0 - sigmoid_gate))
+        dgate_low = (dhidden * up_part * dsilu_gate).astype(low)
+        dup_low = (dhidden * silu_gate).astype(low)
+        dexpert_rows = (
+            dot32("sf,df->sd", dgate_low, gate_all) + dot32("sf,df->sd", dup_low, up_all)
+        ).astype(low)
+        dsent.append(
+            dot32("jst,jsd->jtd", place, dexpert_rows.reshape(MEMBERS, slots, model)).astype(low)
+        )
+        kept.append((expert_rows, hidden_low, dresults, dgate_low, dup_low))
+
+    def collect(parts):
+        total = None
+        for k in range(nz):
+            mine = scatter_members(parts[k])
+            if k == 0:
+                total = mine
+            else:
+                total = total + shift(mine.astype(low), "z", -k).astype(wide)
+        return total
+
+    dffn_routed = collect(dsent)
+    mixed = (mixed_attn + collect(sent)).astype(low)
+    returned = jnp.stack(dgates)
+    near = swap(returned[:, 1::2], "c")
+    returned = jnp.stack([returned[:, 0::2], near], 2)
+    far = swap(returned[:, 1], "y")
+    returned = jnp.stack([returned[:, 0], far], 1)
+    returned = jnp.stack([returned[0]] + [shift(returned[k], "z", -k) for k in range(1, nz)])
+    returned = returned.reshape(context_count, rows)
+    expert_index = jnp.arange(context_count, dtype=jnp.int32)
+    dgates_own = returned[
+        ((expert_index // MEMBERS - zi) % nz) * MEMBERS + ((expert_index % MEMBERS) ^ member)
+    ]
+    dlogits = gates * (dgates_own - jnp.sum(gates * dgates_own, 0, keepdims=True))
+    dlogits_low = dlogits.astype(low)
+    router_grad = dot32("et,td->ed", dlogits_low, ffn_low)
+
+    expert_rows, hidden_low, dresults, dgate_low, dup_low = (
+        jnp.concatenate(column, 0) for column in zip(*kept)
+    )
+
+    def halves(grad):
+        rows_half = grad.shape[0] // 2
+        own = lax.dynamic_slice_in_dim(grad, xi * rows_half, rows_half, 0)
+        other = lax.dynamic_slice_in_dim(grad, (1 - xi) * rows_half, rows_half, 0)
+        return (own + swap(other.astype(low), "x").astype(wide))[None]
+
+    gate_grad = halves(dot32("sd,sf->df", expert_rows, dgate_low))
+    up_grad = halves(dot32("sd,sf->df", expert_rows, dup_low))
+    down_grad = halves(dot32("sf,sd->fd", hidden_low, dresults))
+
+    upstream = cotangent.astype(wide)
+    dffn_rows = dffn_routed + dot32("et,de->td", dlogits_low, router_all)
+    dmixed_norm, ffn_gain_part = rms_back(mixed_attn, inverse_ffn, ffn_gain, dffn_rows)
+    dmixed_attn = upstream + dmixed_norm
+    dattn_all = gather_members(dmixed_attn.astype(low)).reshape(MEMBERS * rows, model)
+    attended_grad = dot32("td,cd->tc", dattn_all, output_weight).astype(low)
+    attended_grad = attended_grad.reshape(MEMBERS, LOCAL_SEQUENCES, paired, query_width)
+    dquery_low, dkey_value, query_gain_part = attend_back(
+        heads, qkv, attended_grad, key_value, cosine, sine, gain_row, mask
+    )
+    query_gain_part = query_gain_part[0]
+    dquery_low = dquery_low.reshape(MEMBERS * rows, query_width)
+    dkey_value_own = dkey_value[0]
+    for k in range(1, nz):
+        dkey_value_own = dkey_value_own + shift(dkey_value[k].astype(low), "z", -k).astype(wide)
+
+    output_part = dot32("tc,td->cd", attended, dattn_all).astype(low)
+    output_part = output_part.reshape(2, MEMBERS, head_rows, model)
+    output_part = (
+        output_part[0].astype(wide) + swap(output_part[1], "x").astype(wide)
+    ).astype(low)
+    output_part = exchange_members([output_part[j] for j in range(MEMBERS)])
+    output_part = jnp.stack(output_part)[members]
+    output_grad = pick(output_part, zi).astype(wide)
+    for k in range(1, nz):
+        sending = pick(output_part, (zi + k) % nz)
+        output_grad = output_grad + shift(sending, "z", k).astype(wide)
+
+    def weight_grad(grad_low):
+        part = dot32("td,tc->dc", normed_all, grad_low)
+        part = part.reshape(nz, MEMBERS, 2, piece, grad_low.shape[1])
+        total = None
+        for k in range(nz):
+            plane = pick(part, (zi + k) % nz)
+            own = lax.dynamic_index_in_dim(plane, xi, 1, keepdims=False)
+            other = lax.dynamic_index_in_dim(plane, 1 - xi, 1, keepdims=False)
+            summed = own + swap(other.astype(low), "x").astype(wide)
+            if k == 0:
+                total = summed
+            else:
+                total = total + shift(summed.astype(low), "z", k).astype(wide)
+        total = total.astype(low)
+        pieces = exchange_members([pick(total, members[j]) for j in range(MEMBERS)])
+        return jnp.stack(pieces)[members].astype(wide)
+
+    query_grad = weight_grad(dquery_low).transpose(1, 0, 2).reshape(piece, -1)
+    dkey, dvalue = dkey_value_own[..., :HEAD_SIZE], dkey_value_own[..., HEAD_SIZE:]
+    dkey_proj, key_gain_part = rms_back(
+        key_proj, key_inverse, key_gain, rope_back(dkey, row_cosine, row_sine)
+    )
+    dkey_value_low = jnp.concatenate([dkey_proj, dvalue], -1).astype(low)
+    dkey_value_low = dkey_value_low.reshape(MEMBERS * rows, 2 * HEAD_SIZE)
+    key_value_grad = weight_grad(dkey_value_low)
+    key_grad = key_value_grad[..., :HEAD_SIZE].transpose(1, 0, 2).reshape(piece, -1)
+    value_grad = key_value_grad[..., HEAD_SIZE:].transpose(1, 0, 2).reshape(piece, -1)
+    dnormed = dot32("tc,dc->td", dquery_low, qkv_weight[:, :query_width])
+    dnormed = dnormed + dot32("tc,dc->td", dkey_value_low, qkv_weight[:, query_width:])
+    dnormed = scatter_members(dnormed.reshape(MEMBERS, rows, model))
+    dinput_norm, attention_gain_part = rms_back(inputs, inverse_attn, attention_gain, dnormed)
+    d_tokens = (dmixed_attn + dinput_norm).astype(low)
+
+    def everywhere(part):
+        for axis in ("x", "y", "c"):
+            part = part + swap(part, axis)
+        return part + sum(shift(part, "z", k) for k in range(1, nz))
+
+    early = everywhere(jnp.concatenate([router_grad, ffn_gain_part[None]], 0))
+    device = (zi * MEMBERS + member) * 2 + xi
+    router_own = lax.dynamic_slice_in_dim(early[:experts_all], device * piece, piece, 1).T
+    gains = everywhere(
+        jnp.concatenate([attention_gain_part, query_gain_part, key_gain_part]).reshape(-1, 128)
+    ).reshape(-1)
+    return (
+        mixed,
+        d_tokens,
+        gains[:model],
+        early[experts_all],
+        gains[model : model + HEAD_SIZE],
+        gains[model + HEAD_SIZE :],
+        query_grad,
+        key_grad,
+        value_grad,
+        output_grad,
+        router_own,
+        gate_grad,
+        up_grad,
+        down_grad,
+    )
+
+
 def solution(mesh):
+    contexts, pairs = mesh.shape["ctx"], mesh.shape["fsdp"]
+    planes = contexts // MEMBERS
+    if planes == KEY_VALUE_HEADS and pairs * MEMBERS * KEY_VALUE_HEADS == QUERY_HEADS:
+        layer, every, split = member_layer, ("z", "y", "c", "x"), ("z", "y", "c")
+        pair = "x"
+        mesh = Mesh(mesh.devices.reshape(planes, 2, 2, pairs), every)
+    else:
+        layer, every, split, pair = routed_layer, ("ctx", "fsdp"), "ctx", "fsdp"
+    by_row = P(every, None)
+    by_expert = P(split, pair, None)
     return jax.shard_map(
-        local,
+        layer,
         mesh=mesh,
-        in_specs=(
-            P(("ctx", "fsdp"), None),
-            P(("ctx", "fsdp"), None),
-            P(("ctx", "fsdp"), None),
-            P(),
-            P(),
-            P(),
-            P(),
-            P(("ctx", "fsdp"), None),
-            P(("ctx", "fsdp"), None),
-            P(("ctx", "fsdp"), None),
-            P(("ctx", "fsdp"), None),
-            P(("ctx", "fsdp"), None),
-            P("ctx", "fsdp", None),
-            P("ctx", "fsdp", None),
-            P("ctx", "fsdp", None),
-        ),
-        out_specs=(
-            P(("ctx", "fsdp"), None),
-            P(("ctx", "fsdp"), None),
-            P(),
-            P(),
-            P(),
-            P(),
-            P(("ctx", "fsdp"), None),
-            P(("ctx", "fsdp"), None),
-            P(("ctx", "fsdp"), None),
-            P(("ctx", "fsdp"), None),
-            P(("ctx", "fsdp"), None),
-            P("ctx", "fsdp", None),
-            P("ctx", "fsdp", None),
-            P("ctx", "fsdp", None),
-        ),
+        in_specs=(by_row,) * 3 + (P(),) * 4 + (by_row,) * 5 + (by_expert,) * 3,
+        out_specs=(by_row,) * 2 + (P(),) * 4 + (by_row,) * 5 + (by_expert,) * 3,
         check_vma=False,
     )

time: 3560 us -> 1270 us (0.36)
  waiting for transfers between devices: 2650 us -> 640 us
  blocking collectives: 229 us -> 0 us
  matrix products: 275 us -> 177 us
  local copies, waits for them, and re-layouts: 160 us -> 74 us
  starting transfers between devices: 106 us -> 176 us
  Pallas kernels: 0 us -> 63.4 us
    reduce_scatter x9 -> x0, waiting for transfers between devices: 1860 us -> none  [the longest x1 711 us: local(): lax.psum_scatter(output_grad, ('ctx', 'fsdp'), scatter_dimension=0, tiled...]
    ppermute x0 -> x136, waiting for transfers between devices: none -> 640 us  [the longest x85 340 us: swap(): return lax.ppermute(block, axis, [(0, 1), (1, 0)])]
    all_gather x9 -> x0, waiting for transfers between devices: 428 us -> none  [the longest x1 112 us: local(): lax.all_gather(w_query, ('ctx', 'fsdp'), axis=0, tiled=True)]
    all_to_all x4 -> x0, waiting for transfers between devices: 236 us -> none  [the longest x1 118 us: local(): lax.all_to_all(from_experts(results), 'ctx', split_axis=0, concat_axis=0,...]
    all_gather x1 -> x0, blocking collectives: 191 us -> none  [local(): lax.all_gather(w_router, ('ctx', 'fsdp'), axis=0, tiled=True)]
    ppermute x0 -> x136, starting transfers between devices: none -> 176 us  [the longest x51 112 us: shift(): lax.ppermute(block, axis, [(i, (i + step) % count) for i in range(count)])]
    unnamed x20 -> x0, waiting for transfers between devices: 126 us -> none
    all_to_all x4 -> x0, starting transfers between devices: 105 us -> none  [the longest x1 34.9 us: local(): lax.all_to_all(from_experts(results), 'ctx', split_axis=0, concat_axis=0,...]
  transfers between devices with their start and end apart: 23 -> 136, of which waited for: 21 -> 54; matrix products, arithmetic and copies ran while one was open for 10% -> 18% of each run, Pallas kernels for 0% -> 2%
where the time goes in v1:
time: 1270 us; the launch traced here: 1260 us
  waiting for transfers between devices  640 us (50%)
  matrix products  177 us (14%)
  starting transfers between devices  176 us (14%)
  other arithmetic  103 us (8%)
  local copies, waits for them, and re-layouts  74 us (6%)
  Pallas kernels  63.4 us (5%)
  between operations  22.5 us (2%)
    ppermute x85, waiting for transfers between devices, swap(): return lax.ppermute(block, axis, [(0, 1), (1, 0)])  340 us
    ppermute x51, waiting for transfers between devices, shift(): lax.ppermute(block, axis, [(i, (i + step) % count) for i in range(count)])  300 us
    dot_general x41, matrix products, dot32(): jnp.einsum(subscripts, left, right, preferred_element_type=jnp.float32)  139 us
    ppermute x51, starting transfers between devices, shift(): lax.ppermute(block, axis, [(i, (i + step) % count) for i in range(count)])  112 us
    ppermute x85, starting transfers between devices, swap(): return lax.ppermute(block, axis, [(0, 1), (1, 0)])  63.4 us
    pallas_call x1, Pallas kernels, attend_back(): pl.pallas_call(attend_back_kernel, grid_spec=pltpu.PrefetchScalarGridSpec...  42.3 us
  transfers between devices with their start and end apart: 136, of which 54 were waited for; matrix products, arithmetic and copies ran while one was open for 18% of the time, Pallas kernels for 2%

profile of v1, /device:TPU:0, one launch (start us, length us, event | category | flops | bytes accessed | tf_op | source)
XLA Modules:
  0.0 1255.2 jit_solution(3782051530677418929)
XLA Ops:
  53.1 13.9 %collective-permute-done.25 = bf16[4,64,16]{1,2,0:T(8,128)(2,1)S(1)} collective-permute-done((bf16[4,64,16]{1,2,0:T(8,128)(2,1)S(1)}, bf16[4,64,16]{1,2,0:T(8,128)(2,1)S(1)}, u32[]{:S(2)}, u32[]{:S(2)}) %collective-permute-start.25) | collective-permute-done | bytes 8224 | tf_op jit(solution)/shard_map/ppermute | solution.py:502
  80.3 24.9 %collective-permute-done.9 = bf16[4,64,1280]{2,1,0:T(8,128)(2,1)S(1)} collective-permute-done((bf16[4,64,1280]{2,1,0:T(8,128)(2,1)}, bf16[4,64,1280]{2,1,0:T(8,128)(2,1)S(1)}, u32[]{:S(2)}, u32[]{:S(2)}) %collective-permute-start.9) | collective-permute-done | bytes 655392 | tf_op jit(solution)/shard_map/ppermute | solution.py:498
  110.5 8.8 collective-permute-done.16
  121.2 45.7 %collective-permute-done.15 = bf16[128,2048]{1,0:T(8,128)(2,1)S(1)} collective-permute-done((bf16[128,2048]{1,0:T(8,128)(2,1)S(1)}, bf16[128,2048]{1,0:T(8,128)(2,1)S(1)}, u32[]{:S(2)}, u32[]{:S(2)}) %collective-permute-start.15) | collective-permute-done | bytes 524320 | tf_op jit(solution)/shard_map/ppermute | solution.py:498
  169.0 10.4 collective-permute-done.7
  186.6 25.5 %collective-permute-done.8 = bf16[4,64,1280]{2,1,0:T(8,128)(2,1)S(1)} collective-permute-done((bf16[4,64,1280]{2,1,0:T(8,128)(2,1)S(1)}, bf16[4,64,1280]{2,1,0:T(8,128)(2,1)S(1)}, u32[]{:S(2)}, u32[]{:S(2)}) %collective-permute-start.8) | collective-permute-done | bytes 655392 | tf_op jit(solution)/shard_map/ppermute | solution.py:502
  213.8 23.2 %collective-permute-done.17 = bf16[2,128,2048]{2,1,0:T(8,128)(2,1)S(1)} collective-permute-done((bf16[2,128,2048]{2,1,0:T(8,128)(2,1)S(1)}, bf16[2,128,2048]{2,1,0:T(8,128)(2,1)S(1)}, u32[]{:S(2)}, u32[]{:S(2)}) %collective-permute-start.17) | collective-permute-done | bytes 1048608 | tf_op jit(solution)/shard_map/ppermute | solution.py:502
  237.3 5.4 fusion.34.q_ref
  260.3 16.3 %collective-permute-done.12 = bf16[4,3,64,256]{3,2,1,0:T(8,128)(2,1)} collective-permute-done((bf16[4,3,64,256]{3,2,1,0:T(8,128)(2,1)}, bf16[4,3,64,256]{3,2,1,0:T(8,128)(2,1)}, u32[]{:S(2)}, u32[]{:S(2)}) %collective-permute-start.12) | collective-permute-done | bytes 393248 | tf_op jit(solution)/shard_map/ppermute | solution.py:498
  276.5 42.2 %collective-permute-start.67 = (bf16[192,2048]{1,0:T(8,128)(2,1)}, bf16[192,2048]{1,0:T(8,128)(2,1)}, u32[]{:S(2)}, u32[]{:S(2)}) collective-permute-start(bf16[192,2048]{1,0:T(8,128)(2,1)} %param.16), channel_id=1, source_target_pairs={{0,8},{8,16},{16,24},{24,0},{1,9},{9,17},{17,25},{25,1},{2,10},{10... | collective-permute-start | bytes 2359304 | tf_op jit(solution)/shard_map/ppermute | solution.py:498
  324.1 21.1 %shard_map.254 = bf16[4,3,64,1024]{3,2,1,0:T(8,128)(2,1)S(1)} custom-call(s32[8]{0:T(128)S(1)} %xor_add_fusion.heads_ref, f32[4,3,64,1280]{3,2,1,0:T(8,128)S(1)} %copy-done.3, bf16[4,4,3,64,256]{4,3,2,1,0:T(8,128)(2,1)S(1)} %pad_maximum_fusion.12.k_ref.v_ref, bf16[4,4,3,64,256]{4,3,2,1,0:T(8,128)(2,1)S(1)} %pad_maximum_fusion.12.k_ref.v_ref, ...), custom_call_target="tpu_custom_call" | custom-call | flops 3221225472 | bytes 8388608 | tf_op jit(solution)/shard_map/pallas_call | solution.py:654
  361.0 12.4 collective-permute-done.68
  375.3 14.6 %collective-permute-done.74 = bf16[192,2048]{1,0:T(8,128)(2,1)S(1)} collective-permute-done((bf16[192,2048]{1,0:T(8,128)(2,1)}, bf16[192,2048]{1,0:T(8,128)(2,1)S(1)}, u32[]{:S(2)}, u32[]{:S(2)}) %collective-permute-start.74) | collective-permute-done | bytes 786464 | tf_op jit(solution)/shard_map/ppermute | solution.py:502
  392.4 16.9 %collective-permute-done.80 = bf16[192,2048]{1,0:T(8,128)(2,1)S(1)} collective-permute-done((bf16[192,2048]{1,0:T(8,128)(2,1)}, bf16[192,2048]{1,0:T(8,128)(2,1)S(1)}, u32[]{:S(2)}, u32[]{:S(2)}) %collective-permute-start.80) | collective-permute-done | bytes 786464 | tf_op jit(solution)/shard_map/ppermute | solution.py:502
  411.7 17.0 %collective-permute-done.41 = bf16[1,1024,768]{2,1,0:T(8,128)(2,1)S(1)} collective-permute-done((bf16[1,1024,768]{2,1,0:T(8,128)(2,1)S(1)}, bf16[1,1024,768]{2,1,0:T(8,128)(2,1)S(1)}, u32[]{:S(2)}, u32[]{:S(2)}) %collective-permute-start.41) | collective-permute-done | bytes 1572896 | tf_op jit(solution)/shard_map/ppermute | solution.py:502
  428.9 32.5 %collective-permute-done.42 = bf16[1,384,2048]{2,1,0:T(8,128)(2,1)S(1)} collective-permute-done((bf16[1,384,2048]{2,1,0:T(8,128)(2,1)S(1)}, bf16[1,384,2048]{2,1,0:T(8,128)(2,1)S(1)}, u32[]{:S(2)}, u32[]{:S(2)}) %collective-permute-start.42) | collective-permute-done | bytes 1572896 | tf_op jit(solution)/shard_map/ppermute | solution.py:502
  468.2 14.4 %collective-permute-done.38 = bf16[192,2048]{1,0:T(8,128)(2,1)S(1)} collective-permute-done((bf16[192,2048]{1,0:T(8,128)(2,1)S(1)}, bf16[192,2048]{1,0:T(8,128)(2,1)S(1)}, u32[]{:S(2)}, u32[]{:S(2)}) %collective-permute-start.38) | collective-permute-done | bytes 786464 | tf_op jit(solution)/shard_map/ppermute | solution.py:502
  486.7 49.4 %collective-permute-done.51 = bf16[192,2048]{1,0:T(8,128)(2,1)S(1)} collective-permute-done((bf16[192,2048]{1,0:T(8,128)(2,1)S(1)}, bf16[192,2048]{1,0:T(8,128)(2,1)S(1)}, u32[]{:S(2)}, u32[]{:S(2)}) %collective-permute-start.51) | collective-permute-done | bytes 786464 | tf_op jit(solution)/shard_map/ppermute | solution.py:498
  538.9 17.7 %collective-permute-done.52 = bf16[192,2048]{1,0:T(8,128)(2,1)S(1)} collective-permute-done((bf16[192,2048]{1,0:T(8,128)(2,1)S(1)}, bf16[192,2048]{1,0:T(8,128)(2,1)S(1)}, u32[]{:S(2)}, u32[]{:S(2)}) %collective-permute-start.52) | collective-permute-done | bytes 786464 | tf_op jit(solution)/shard_map/ppermute | solution.py:502
  556.9 15.0 %collective-permute-done.46 = bf16[192,2048]{1,0:T(8,128)(2,1)S(1)} collective-permute-done((bf16[192,2048]{1,0:T(8,128)(2,1)S(1)}, bf16[192,2048]{1,0:T(8,128)(2,1)S(1)}, u32[]{:S(2)}, u32[]{:S(2)}) %collective-permute-start.46) | collective-permute-done | bytes 786464 | tf_op jit(solution)/shard_map/ppermute | solution.py:502
  626.8 4.6 copy.117
  677.6 11.7 fusion
  689.3 4.9 multiply_convert_fusion.1
  709.5 12.3 fusion.82
  754.6 11.8 fusion.74
  766.5 5.2 add_convert_fusion.3
  797.6 30.3 %collective-permute-done.133 = bf16[1024,768]{1,0:T(8,128)(2,1)S(1)} collective-permute-done((bf16[1024,768]{1,0:T(8,128)(2,1)S(1)}, bf16[1024,768]{1,0:T(8,128)(2,1)S(1)}, u32[]{:S(2)}, u32[]{:S(2)}) %collective-permute-start.133) | collective-permute-done | bytes 1572896 | tf_op jit(solution)/shard_map/ppermute | solution.py:502
  839.9 9.7 collective-permute-done.77
  851.8 8.7 collective-permute-done.134
  873.6 33.6 %collective-permute-done.78 = bf16[192,2048]{1,0:T(8,128)(2,1)S(1)} collective-permute-done((bf16[192,2048]{1,0:T(8,128)(2,1)S(1)}, bf16[192,2048]{1,0:T(8,128)(2,1)S(1)}, u32[]{:S(2)}, u32[]{:S(2)}) %collective-permute-start.78) | collective-permute-done | bytes 786464 | tf_op jit(solution)/shard_map/ppermute | solution.py:498
  919.9 18.3 %collective-permute-done.104 = f32[17,2048]{1,0:T(8,128)S(1)} collective-permute-done((f32[17,2048]{1,0:T(8,128)S(1)}, f32[17,2048]{1,0:T(8,128)S(1)}, u32[]{:S(2)}, u32[]{:S(2)}) %collective-permute-start.104) | collective-permute-done | bytes 139296 | tf_op jit(solution)/shard_map/ppermute | solution.py:502
  948.8 12.2 collective-permute-done.107
  968.2 5.1 convolution_convert_fusion
  973.3 42.3 %shard_map.255 = (bf16[4,3,64,1024]{3,2,1,0:T(8,128)(2,1)S(1)}, f32[4,4,3,64,256]{4,3,2,1,0:T(8,128)S(1)}, f32[8,128]{1,0:T(8,128)S(1)}) custom-call(s32[8]{0:T(128)S(1)} %xor_add_fusion.heads_ref, f32[4,3,64,1280]{3,2,1,0:T(8,128)S(1)} %copy-done.4, bf16[4,3,64,1024]{3,2,1,0:T(8,128)(2,1)S(1)} %bitcast.567, bf16[4,4,3,64,256]{4,3,2,1,0:T(8,128)(2,1)S(1)} %copy-done.1, ...), custom_call_target="tpu_custom_call" | custom-call | flops 8053063680 | bytes 16777216 | tf_op jit(solution)/shard_map/pallas_call | solution.py:677
  1019.7 5.6 fusion.312
  1037.5 14.6 %collective-permute-done.93 = bf16[4,3,64,256]{3,2,1,0:T(8,128)(2,1)S(1)} collective-permute-done((bf16[4,3,64,256]{3,2,1,0:T(8,128)(2,1)S(1)}, bf16[4,3,64,256]{3,2,1,0:T(8,128)(2,1)S(1)}, u32[]{:S(2)}, u32[]{:S(2)}) %collective-permute-start.93) | collective-permute-done | bytes 393248 | tf_op jit(solution)/shard_map/ppermute | solution.py:498
  1058.2 5.4 fusion.301
  1063.6 5.7 collective-permute-done.119
  1090.9 6.9 collective-permute-done.122
  1104.2 7.3 collective-permute-done.115
  1111.5 21.9 %collective-permute-done.113 = bf16[4,64,1024]{2,1,0:T(8,128)(2,1)S(1)} collective-permute-done((bf16[4,64,1024]{2,1,0:T(8,128)(2,1)S(1)}, bf16[4,64,1024]{2,1,0:T(8,128)(2,1)S(1)}, u32[]{:S(2)}, u32[]{:S(2)}) %collective-permute-start.113) | collective-permute-done | bytes 524320 | tf_op jit(solution)/shard_map/ppermute | solution.py:498
  1136.1 6.3 collective-permute-done.116
  1154.3 15.6 %collective-permute-done.96 = bf16[192,2048]{1,0:T(8,128)(2,1)S(1)} collective-permute-done((bf16[192,2048]{1,0:T(8,128)(2,1)S(1)}, bf16[192,2048]{1,0:T(8,128)(2,1)S(1)}, u32[]{:S(2)}, u32[]{:S(2)}) %collective-permute-start.96) | collective-permute-done | bytes 786464 | tf_op jit(solution)/shard_map/ppermute | solution.py:502
  1177.4 14.3 %collective-permute-done.128 = bf16[2,128,2048]{2,1,0:T(8,128)(2,1)S(1)} collective-permute-done((bf16[2,128,2048]{2,1,0:T(8,128)(2,1)S(1)}, bf16[2,128,2048]{2,1,0:T(8,128)(2,1)S(1)}, u32[]{:S(2)}, u32[]{:S(2)}) %collective-permute-start.128) | collective-permute-done | bytes 1048608 | tf_op jit(solution)/shard_map/ppermute | solution.py:502
  1198.6 5.0 fusion.134
  1203.7 7.4 collective-permute-start.102
  1222.4 10.9 collective-permute-done.130
  1233.3 20.4 %collective-permute-done.131 = bf16[128,2048]{1,0:T(8,128)(2,1)S(1)} collective-permute-done((bf16[128,2048]{1,0:T(8,128)(2,1)S(1)}, bf16[128,2048]{1,0:T(8,128)(2,1)S(1)}, u32[]{:S(2)}, u32[]{:S(2)}) %collective-permute-start.131) | collective-permute-done | bytes 524320 | tf_op jit(solution)/shard_map/ppermute | solution.py:498
  (852 shorter events, 447.0 us)
Async XLA Ops:
  0.6 44.5 %collective-permute-start.22 = (bf16[64,16]{0,1:T(8,128)(2,1)}, bf16[64,16]{0,1:T(8,128)(2,1)S(1)}, u32[]{:S(2)}, u32[]{:S(2)}) collective-permute-start(bf16[64,16]{0,1:T(8,128)(2,1)} %param.26), channel_id=1, source_target_pairs={{0,8},{8,16},{16,24},{24,0},{1,9},{9,17},{17,25},{25,1},{2,10},{10... | collective-permute-start | bytes 6152 | tf_op jit(solution)/shard_map/ppermute | solution.py:498
  3.7 41.5 %collective-permute-start.24 = (bf16[64,16]{0,1:T(8,128)(2,1)}, bf16[64,16]{0,1:T(8,128)(2,1)S(1)}, u32[]{:S(2)}, u32[]{:S(2)}) collective-permute-start(bf16[64,16]{0,1:T(8,128)(2,1)} %param.26), channel_id=1, source_target_pairs={{0,24},{8,0},{16,8},{24,16},{1,25},{9,1},{17,9},{25,17},{2,26},{10... | collective-permute-start | bytes 6152 | tf_op jit(solution)/shard_map/ppermute | solution.py:498
  5.8 43.2 %collective-permute-start.23 = (bf16[64,16]{0,1:T(8,128)(2,1)}, bf16[64,16]{0,1:T(8,128)(2,1)S(1)}, u32[]{:S(2)}, u32[]{:S(2)}) collective-permute-start(bf16[64,16]{0,1:T(8,128)(2,1)} %param.26), channel_id=1, source_target_pairs={{0,16},{8,24},{16,0},{24,8},{1,17},{9,25},{17,1},{25,9},{2,18},{10... | collective-permute-start | bytes 6152 | tf_op jit(solution)/shard_map/ppermute | solution.py:498
  6.8 60.3 %collective-permute-start.34 = (s32[8,192]{1,0:T(8,128)}, s32[8,192]{1,0:T(8,128)S(1)}, u32[]{:S(2)}, u32[]{:S(2)}) collective-permute-start(s32[8,192]{1,0:T(8,128)} %bitcast.669), channel_id=1, source_target_pairs={{0,16},{8,24},{16,0},{24,8},{1,17},{9,25},{17,1},{25,9},{2,18},{10... | collective-permute-start | bytes 18440 | tf_op jit(solution)/shard_map/ppermute | solution.py:498
  68.3 182.1 %collective-permute-start.36 = (s32[4,8,192]{2,1,0:T(8,128)}, s32[4,8,192]{2,1,0:T(8,128)}, u32[]{:S(2)}, u32[]{:S(2)}) collective-permute-start(s32[4,8,192]{2,1,0:T(8,128)} %get-tuple-element.183), channel_id=1, source_target_pairs={{0,4},{4,0},{1,5},{5,1},{2,6},{6,2},{3,7},{7,3},{8,12},{12,8},{9,1... | collective-permute-start | bytes 73736 | tf_op jit(solution)/shard_map/ppermute | solution.py:502
  106.1 60.8 %collective-permute-start.15 = (bf16[128,2048]{1,0:T(8,128)(2,1)S(1)}, bf16[128,2048]{1,0:T(8,128)(2,1)S(1)}, u32[]{:S(2)}, u32[]{:S(2)}) collective-permute-start(bf16[128,2048]{1,0:T(8,128)(2,1)S(1)} %copy-done.91), channel_id=1, source_target_pairs={{0,16},{8,24},{16,0},{24,8},{1,17},{9,25},{17,1},{25,9},{2,18},{10... | collective-permute-start | bytes 1572872 | tf_op jit(solution)/shard_map/ppermute | solution.py:498
  106.3 60.6 %collective-permute-start.14 = (bf16[128,2048]{1,0:T(8,128)(2,1)S(1)}, bf16[128,2048]{1,0:T(8,128)(2,1)S(1)}, u32[]{:S(2)}, u32[]{:S(2)}) collective-permute-start(bf16[128,2048]{1,0:T(8,128)(2,1)S(1)} %copy-done.91), channel_id=1, source_target_pairs={{0,8},{8,16},{16,24},{24,0},{1,9},{9,17},{17,25},{25,1},{2,10},{10... | collective-permute-start | bytes 1572872 | tf_op jit(solution)/shard_map/ppermute | solution.py:498
  108.9 145.1 %collective-permute-start.27 = (bf16[4,2,2,64,16]{3,4,0,2,1:T(8,128)(2,1)}, bf16[4,2,2,64,16]{3,4,0,2,1:T(8,128)(2,1)S(1)}, u32[]{:S(2)}, u32[]{:S(2)}) collective-permute-start(bf16[4,2,2,64,16]{3,4,0,2,1:T(8,128)(2,1)} %get-tuple-element.177), channel_id=1, source_target_pairs={{0,1},{1,0},{2,3},{3,2},{4,5},{5,4},{6,7},{7,6},{8,9},{9,8},{10,11... | collective-permute-start | bytes 98312 | tf_op jit(solution)/shard_map/ppermute | solution.py:502
  119.3 60.1 %collective-permute-start.7 = (bf16[4,64,1280]{2,1,0:T(8,128)(2,1)S(1)}, bf16[4,64,1280]{2,1,0:T(8,128)(2,1)S(1)}, u32[]{:S(2)}, u32[]{:S(2)}) collective-permute-start(bf16[4,64,1280]{2,1,0:T(8,128)(2,1)S(1)} %copy-done.47), channel_id=1, source_target_pairs={{0,16},{8,24},{16,0},{24,8},{1,17},{9,25},{17,1},{25,9},{2,18},{10... | collective-permute-start | bytes 1966088 | tf_op jit(solution)/shard_map/ppermute | solution.py:498
  166.9 46.6 %collective-permute-start.1 = (bf16[2,192,2048]{2,1,0:T(8,128)(2,1)S(1)}, bf16[2,192,2048]{2,1,0:T(8,128)(2,1)S(1)}, u32[]{:S(2)}, u32[]{:S(2)}) collective-permute-start(bf16[2,192,2048]{2,1,0:T(8,128)(2,1)S(1)} %pad_maximum_fusion.11), channel_id=1, source_target_pairs={{0,2},{2,0},{1,3},{3,1},{4,6},{6,4},{5,7},{7,5},{8,10},{10,8},{9,1... | collective-permute-start | bytes 4718600 | tf_op jit(solution)/shard_map/ppermute | solution.py:502
  245.5 99.7 %collective-permute-start.19 = (bf16[4,128,2048]{2,1,0:T(8,128)(2,1)}, bf16[4,128,2048]{2,1,0:T(8,128)(2,1)}, u32[]{:S(2)}, u32[]{:S(2)}) collective-permute-start(bf16[4,128,2048]{2,1,0:T(8,128)(2,1)} %get-tuple-element.92), channel_id=1, source_target_pairs={{0,1},{1,0},{2,3},{3,2},{4,5},{5,4},{6,7},{7,6},{8,9},{9,8},{10,11... | collective-permute-start | bytes 6291464 | tf_op jit(solution)/shard_map/ppermute | solution.py:502
  250.4 68.4 %collective-permute-start.13 = (bf16[4,3,64,256]{3,2,1,0:T(8,128)(2,1)}, bf16[4,3,64,256]{3,2,1,0:T(8,128)(2,1)}, u32[]{:S(2)}, u32[]{:S(2)}) collective-permute-start(bf16[4,3,64,256]{3,2,1,0:T(8,128)(2,1)} %get-tuple-element.141), channel_id=1, source_target_pairs={{0,24},{8,0},{16,8},{24,16},{1,25},{9,1},{17,9},{25,17},{2,26},{10... | collective-permute-start | bytes 1179656 | tf_op jit(solution)/shard_map/ppermute | solution.py:498
  259.8 97.9 %collective-permute-start.79 = (bf16[192,2048]{1,0:T(8,128)(2,1)}, bf16[192,2048]{1,0:T(8,128)(2,1)}, u32[]{:S(2)}, u32[]{:S(2)}) collective-permute-start(bf16[192,2048]{1,0:T(8,128)(2,1)} %param.16), channel_id=1, source_target_pairs={{0,24},{8,0},{16,8},{24,16},{1,25},{9,1},{17,9},{25,17},{2,26},{10... | collective-permute-start | bytes 2359304 | tf_op jit(solution)/shard_map/ppermute | solution.py:498
  276.5 79.2 %collective-permute-start.73 = (bf16[192,2048]{1,0:T(8,128)(2,1)}, bf16[192,2048]{1,0:T(8,128)(2,1)}, u32[]{:S(2)}, u32[]{:S(2)}) collective-permute-start(bf16[192,2048]{1,0:T(8,128)(2,1)} %param.16), channel_id=1, source_target_pairs={{0,16},{8,24},{16,0},{24,8},{1,17},{9,25},{17,1},{25,9},{2,18},{10... | collective-permute-start | bytes 2359304 | tf_op jit(solution)/shard_map/ppermute | solution.py:498
  276.5 76.3 %collective-permute-start.67 = (bf16[192,2048]{1,0:T(8,128)(2,1)}, bf16[192,2048]{1,0:T(8,128)(2,1)}, u32[]{:S(2)}, u32[]{:S(2)}) collective-permute-start(bf16[192,2048]{1,0:T(8,128)(2,1)} %param.16), channel_id=1, source_target_pairs={{0,8},{8,16},{16,24},{24,0},{1,9},{9,17},{17,25},{25,1},{2,10},{10... | collective-permute-start | bytes 2359304 | tf_op jit(solution)/shard_map/ppermute | solution.py:498
  357.6 53.8 %collective-permute-start.40 = (bf16[1,1024,768]{2,1,0:T(8,128)(2,1)S(1)}, bf16[1,1024,768]{2,1,0:T(8,128)(2,1)S(1)}, u32[]{:S(2)}, u32[]{:S(2)}) collective-permute-start(bf16[1,1024,768]{2,1,0:T(8,128)(2,1)S(1)} %copy-done.49), channel_id=1, source_target_pairs={{0,1},{1,0},{2,3},{3,2},{4,5},{5,4},{6,7},{7,6},{8,9},{9,8},{10,11... | collective-permute-start | bytes 4718600 | tf_op jit(solution)/shard_map/ppermute | solution.py:502
  358.3 70.4 %collective-permute-start.41 = (bf16[1,1024,768]{2,1,0:T(8,128)(2,1)S(1)}, bf16[1,1024,768]{2,1,0:T(8,128)(2,1)S(1)}, u32[]{:S(2)}, u32[]{:S(2)}) collective-permute-start(bf16[1,1024,768]{2,1,0:T(8,128)(2,1)S(1)} %copy-done.50), channel_id=1, source_target_pairs={{0,1},{1,0},{2,3},{3,2},{4,5},{5,4},{6,7},{7,6},{8,9},{9,8},{10,11... | collective-permute-start | bytes 4718600 | tf_op jit(solution)/shard_map/ppermute | solution.py:502
  373.5 87.9 %collective-permute-start.42 = (bf16[1,384,2048]{2,1,0:T(8,128)(2,1)S(1)}, bf16[1,384,2048]{2,1,0:T(8,128)(2,1)S(1)}, u32[]{:S(2)}, u32[]{:S(2)}) collective-permute-start(bf16[1,384,2048]{2,1,0:T(8,128)(2,1)S(1)} %copy-done.51), channel_id=1, source_target_pairs={{0,1},{1,0},{2,3},{3,2},{4,5},{5,4},{6,7},{7,6},{8,9},{9,8},{10,11... | collective-permute-start | bytes 4718600 | tf_op jit(solution)/shard_map/ppermute | solution.py:502
  392.1 71.7 %collective-permute-start.64 = (bf16[2,192,2048]{2,1,0:T(8,128)(2,1)S(1)}, bf16[2,192,2048]{2,1,0:T(8,128)(2,1)S(1)}, u32[]{:S(2)}, u32[]{:S(2)}) collective-permute-start(bf16[2,192,2048]{2,1,0:T(8,128)(2,1)S(1)} %pad_maximum_fusion.22), channel_id=1, source_target_pairs={{0,2},{2,0},{1,3},{3,1},{4,6},{6,4},{5,7},{7,5},{8,10},{10,8},{9,1... | collective-permute-start | bytes 4718600 | tf_op jit(solution)/shard_map/ppermute | solution.py:502
  409.3 52.4 %collective-permute-start.21 = (bf16[192,2048]{1,0:T(8,128)(2,1)S(1)}, bf16[192,2048]{1,0:T(8,128)(2,1)S(1)}, u32[]{:S(2)}, u32[]{:S(2)}) collective-permute-start(bf16[192,2048]{1,0:T(8,128)(2,1)S(1)} %fusion.139), channel_id=1, source_target_pairs={{0,4},{4,0},{1,5},{5,1},{2,6},{6,2},{3,7},{7,3},{8,12},{12,8},{9,1... | collective-permute-start | bytes 2359304 | tf_op jit(solution)/shard_map/ppermute | solution.py:502
  411.4 54.2 %collective-permute-start.81 = (bf16[2,192,2048]{2,1,0:T(8,128)(2,1)S(1)}, bf16[2,192,2048]{2,1,0:T(8,128)(2,1)S(1)}, u32[]{:S(2)}, u32[]{:S(2)}) collective-permute-start(bf16[2,192,2048]{2,1,0:T(8,128)(2,1)S(1)} %pad_maximum_fusion.28), channel_id=1, source_target_pairs={{0,2},{2,0},{1,3},{3,1},{4,6},{6,4},{5,7},{7,5},{8,10},{10,8},{9,1... | collective-permute-start | bytes 4718600 | tf_op jit(solution)/shard_map/ppermute | solution.py:502
  428.7 56.7 %collective-permute-start.75 = (bf16[2,192,2048]{2,1,0:T(8,128)(2,1)S(1)}, bf16[2,192,2048]{2,1,0:T(8,128)(2,1)S(1)}, u32[]{:S(2)}, u32[]{:S(2)}) collective-permute-start(bf16[2,192,2048]{2,1,0:T(8,128)(2,1)S(1)} %pad_maximum_fusion.26), channel_id=1, source_target_pairs={{0,2},{2,0},{1,3},{3,1},{4,6},{6,4},{5,7},{7,5},{8,10},{10,8},{9,1... | collective-permute-start | bytes 4718600 | tf_op jit(solution)/shard_map/ppermute | solution.py:502
  461.4 77.1 %collective-permute-start.69 = (bf16[2,192,2048]{2,1,0:T(8,128)(2,1)S(1)}, bf16[2,192,2048]{2,1,0:T(8,128)(2,1)S(1)}, u32[]{:S(2)}, u32[]{:S(2)}) collective-permute-start(bf16[2,192,2048]{2,1,0:T(8,128)(2,1)S(1)} %pad_maximum_fusion.24), channel_id=1, source_target_pairs={{0,2},{2,0},{1,3},{3,1},{4,6},{6,4},{5,7},{7,5},{8,10},{10,8},{9,1... | collective-permute-start | bytes 4718600 | tf_op jit(solution)/shard_map/ppermute | solution.py:502
  465.6 70.6 %collective-permute-start.51 = (bf16[192,2048]{1,0:T(8,128)(2,1)S(1)}, bf16[192,2048]{1,0:T(8,128)(2,1)S(1)}, u32[]{:S(2)}, u32[]{:S(2)}) collective-permute-start(bf16[192,2048]{1,0:T(8,128)(2,1)S(1)} %multiply_convert_fusion.12), channel_id=1, source_target_pairs={{0,16},{8,24},{16,0},{24,8},{1,17},{9,25},{17,1},{25,9},{2,18},{10... | collective-permute-start | bytes 2359304 | tf_op jit(solution)/shard_map/ppermute | solution.py:498
  482.6 54.7 %collective-permute-start.45 = (bf16[192,2048]{1,0:T(8,128)(2,1)S(1)}, bf16[192,2048]{1,0:T(8,128)(2,1)S(1)}, u32[]{:S(2)}, u32[]{:S(2)}) collective-permute-start(bf16[192,2048]{1,0:T(8,128)(2,1)S(1)} %multiply_convert_fusion.12), channel_id=1, source_target_pairs={{0,8},{8,16},{16,24},{24,0},{1,9},{9,17},{17,25},{25,1},{2,10},{10... | collective-permute-start | bytes 2359304 | tf_op jit(solution)/shard_map/ppermute | solution.py:498
  485.4 86.7 %collective-permute-start.39 = (bf16[2,192,2048]{2,1,0:T(8,128)(2,1)S(1)}, bf16[2,192,2048]{2,1,0:T(8,128)(2,1)S(1)}, u32[]{:S(2)}, u32[]{:S(2)}) collective-permute-start(bf16[2,192,2048]{2,1,0:T(8,128)(2,1)S(1)} %pad_maximum_fusion.14), channel_id=1, source_target_pairs={{0,2},{2,0},{1,3},{3,1},{4,6},{6,4},{5,7},{7,5},{8,10},{10,8},{9,1... | collective-permute-start | bytes 4718600 | tf_op jit(solution)/shard_map/ppermute | solution.py:502
  485.5 53.2 %collective-permute-start.58 = (bf16[192,2048]{1,0:T(8,128)(2,1)S(1)}, bf16[192,2048]{1,0:T(8,128)(2,1)S(1)}, u32[]{:S(2)}, u32[]{:S(2)}) collective-permute-start(bf16[192,2048]{1,0:T(8,128)(2,1)S(1)} %collective-permute-done.57), channel_id=1, source_target_pairs={{0,4},{4,0},{1,5},{5,1},{2,6},{6,2},{3,7},{7,3},{8,12},{12,8},{9,1... | collective-permute-start | bytes 2359304 | tf_op jit(solution)/shard_map/ppermute | solution.py:502
  538.8 49.9 %collective-permute-start.59 = (bf16[2,192,2048]{2,1,0:T(8,128)(2,1)S(1)}, bf16[2,192,2048]{2,1,0:T(8,128)(2,1)S(1)}, u32[]{:S(2)}, u32[]{:S(2)}) collective-permute-start(bf16[2,192,2048]{2,1,0:T(8,128)(2,1)S(1)} %pad_maximum_fusion.20), channel_id=1, source_target_pairs={{0,2},{2,0},{1,3},{3,1},{4,6},{6,4},{5,7},{7,5},{8,10},{10,8},{9,1... | collective-permute-start | bytes 4718600 | tf_op jit(solution)/shard_map/ppermute | solution.py:502
  731.9 48.6 %collective-permute-start.43 = (bf16[2,192,2048]{2,1,0:T(8,128)(2,1)}, bf16[2,192,2048]{2,1,0:T(8,128)(2,1)}, u32[]{:S(2)}, u32[]{:S(2)}) collective-permute-start(bf16[2,192,2048]{2,1,0:T(8,128)(2,1)} %pad_maximum_fusion.15), channel_id=1, source_target_pairs={{0,2},{2,0},{1,3},{3,1},{4,6},{6,4},{5,7},{7,5},{8,10},{10,8},{9,1... | collective-permute-start | bytes 4718600 | tf_op jit(solution)/shard_map/ppermute | solution.py:502
  733.3 49.5 %collective-permute-start.54 = (bf16[2,192,2048]{2,1,0:T(8,128)(2,1)}, bf16[2,192,2048]{2,1,0:T(8,128)(2,1)}, u32[]{:S(2)}, u32[]{:S(2)}) collective-permute-start(bf16[2,192,2048]{2,1,0:T(8,128)(2,1)} %pad_maximum_fusion.19), channel_id=1, source_target_pairs={{0,2},{2,0},{1,3},{3,1},{4,6},{6,4},{5,7},{7,5},{8,10},{10,8},{9,1... | collective-permute-start | bytes 4718600 | tf_op jit(solution)/shard_map/ppermute | solution.py:502
  735.0 50.7 %collective-permute-start.48 = (bf16[2,192,2048]{2,1,0:T(8,128)(2,1)}, bf16[2,192,2048]{2,1,0:T(8,128)(2,1)}, u32[]{:S(2)}, u32[]{:S(2)}) collective-permute-start(bf16[2,192,2048]{2,1,0:T(8,128)(2,1)} %pad_maximum_fusion.17), channel_id=1, source_target_pairs={{0,2},{2,0},{1,3},{3,1},{4,6},{6,4},{5,7},{7,5},{8,10},{10,8},{9,1... | collective-permute-start | bytes 4718600 | tf_op jit(solution)/shard_map/ppermute | solution.py:502
  736.5 51.7 %collective-permute-start.60 = (bf16[2,192,2048]{2,1,0:T(8,128)(2,1)}, bf16[2,192,2048]{2,1,0:T(8,128)(2,1)}, u32[]{:S(2)}, u32[]{:S(2)}) collective-permute-start(bf16[2,192,2048]{2,1,0:T(8,128)(2,1)} %pad_maximum_fusion.21), channel_id=1, source_target_pairs={{0,2},{2,0},{1,3},{3,1},{4,6},{6,4},{5,7},{7,5},{8,10},{10,8},{9,1... | collective-permute-start | bytes 4718600 | tf_op jit(solution)/shard_map/ppermute | solution.py:502
  740.4 124.8 %collective-permute-start.135 = (bf16[384,2048]{1,0:T(8,128)(2,1)}, bf16[384,2048]{1,0:T(8,128)(2,1)}, u32[]{:S(2)}, u32[]{:S(2)}) collective-permute-start(bf16[384,2048]{1,0:T(8,128)(2,1)} %dynamic-slice_convert_fusion), channel_id=1, source_target_pairs={{0,1},{1,0},{2,3},{3,2},{4,5},{5,4},{6,7},{7,6},{8,9},{9,8},{10,11... | collective-permute-start | bytes 4718600 | tf_op jit(solution)/shard_map/ppermute | solution.py:502
  793.2 67.3 %collective-permute-start.134 = (bf16[1024,768]{1,0:T(8,128)(2,1)S(1)}, bf16[1024,768]{1,0:T(8,128)(2,1)}, u32[]{:S(2)}, u32[]{:S(2)}) collective-permute-start(bf16[1024,768]{1,0:T(8,128)(2,1)S(1)} %dynamic-slice_convert_fusion.1), channel_id=1, source_target_pairs={{0,1},{1,0},{2,3},{3,2},{4,5},{5,4},{6,7},{7,6},{8,9},{9,8},{10,11... | collective-permute-start | bytes 4718600 | tf_op jit(solution)/shard_map/ppermute | solution.py:502
  796.1 40.8 %collective-permute-start.71 = (bf16[192,2048]{1,0:T(8,128)(2,1)}, bf16[192,2048]{1,0:T(8,128)(2,1)S(1)}, u32[]{:S(2)}, u32[]{:S(2)}) collective-permute-start(bf16[192,2048]{1,0:T(8,128)(2,1)} %fusion.178), channel_id=1, source_target_pairs={{0,4},{4,0},{1,5},{5,1},{2,6},{6,2},{3,7},{7,3},{8,12},{12,8},{9,1... | collective-permute-start | bytes 2359304 | tf_op jit(solution)/shard_map/ppermute | solution.py:502
  860.6 46.7 %collective-permute-start.78 = (bf16[192,2048]{1,0:T(8,128)(2,1)S(1)}, bf16[192,2048]{1,0:T(8,128)(2,1)S(1)}, u32[]{:S(2)}, u32[]{:S(2)}) collective-permute-start(bf16[192,2048]{1,0:T(8,128)(2,1)S(1)} %fusion.142), channel_id=1, source_target_pairs={{0,16},{8,24},{16,0},{24,8},{1,17},{9,25},{17,1},{25,9},{2,18},{10... | collective-permute-start | bytes 2359304 | tf_op jit(solution)/shard_map/ppermute | solution.py:498
  865.2 52.3 %collective-permute-start.55 = (bf16[192,2048]{1,0:T(8,128)(2,1)S(1)}, bf16[192,2048]{1,0:T(8,128)(2,1)S(1)}, u32[]{:S(2)}, u32[]{:S(2)}) collective-permute-start(bf16[192,2048]{1,0:T(8,128)(2,1)S(1)} %copy-done.88), channel_id=1, source_target_pairs={{0,4},{4,0},{1,5},{5,1},{2,6},{6,2},{3,7},{7,3},{8,12},{12,8},{9,1... | collective-permute-start | bytes 2359304 | tf_op jit(solution)/shard_map/ppermute | solution.py:502
  870.2 68.9 %collective-permute-start.49 = (bf16[192,2048]{1,0:T(8,128)(2,1)S(1)}, bf16[192,2048]{1,0:T(8,128)(2,1)S(1)}, u32[]{:S(2)}, u32[]{:S(2)}) collective-permute-start(bf16[192,2048]{1,0:T(8,128)(2,1)S(1)} %copy-done.87), channel_id=1, source_target_pairs={{0,4},{4,0},{1,5},{5,1},{2,6},{6,2},{3,7},{7,3},{8,12},{12,8},{9,1... | collective-permute-start | bytes 2359304 | tf_op jit(solution)/shard_map/ppermute | solution.py:502
  871.3 74.1 %collective-permute-start.61 = (bf16[192,2048]{1,0:T(8,128)(2,1)S(1)}, bf16[192,2048]{1,0:T(8,128)(2,1)S(1)}, u32[]{:S(2)}, u32[]{:S(2)}) collective-permute-start(bf16[192,2048]{1,0:T(8,128)(2,1)S(1)} %fusion.176), channel_id=1, source_target_pairs={{0,4},{4,0},{1,5},{5,1},{2,6},{6,2},{3,7},{7,3},{8,12},{12,8},{9,1... | collective-permute-start | bytes 2359304 | tf_op jit(solution)/shard_map/ppermute | solution.py:502
  1028.9 48.4 %collective-permute-start.110 = (bf16[4,64,1024]{2,1,0:T(8,128)(2,1)}, bf16[4,64,1024]{2,1,0:T(8,128)(2,1)S(1)}, u32[]{:S(2)}, u32[]{:S(2)}) collective-permute-start(bf16[4,64,1024]{2,1,0:T(8,128)(2,1)} %get-tuple-element.43), channel_id=1, source_target_pairs={{0,1},{1,0},{2,3},{3,2},{4,5},{5,4},{6,7},{7,6},{8,9},{9,8},{10,11... | collective-permute-start | bytes 1572872 | tf_op jit(solution)/shard_map/ppermute | solution.py:502
  1030.4 47.9 %collective-permute-start.114 = (bf16[4,64,1024]{2,1,0:T(8,128)(2,1)}, bf16[4,64,1024]{2,1,0:T(8,128)(2,1)S(1)}, u32[]{:S(2)}, u32[]{:S(2)}) collective-permute-start(bf16[4,64,1024]{2,1,0:T(8,128)(2,1)} %get-tuple-element.44), channel_id=1, source_target_pairs={{0,1},{1,0},{2,3},{3,2},{4,5},{5,4},{6,7},{7,6},{8,9},{9,8},{10,11... | collective-permute-start | bytes 1572872 | tf_op jit(solution)/shard_map/ppermute | solution.py:502
  1033.7 47.6 %collective-permute-start.112 = (bf16[4,64,1024]{2,1,0:T(8,128)(2,1)S(1)}, bf16[4,64,1024]{2,1,0:T(8,128)(2,1)S(1)}, u32[]{:S(2)}, u32[]{:S(2)}) collective-permute-start(bf16[4,64,1024]{2,1,0:T(8,128)(2,1)S(1)} %get-tuple-element.45), channel_id=1, source_target_pairs={{0,1},{1,0},{2,3},{3,2},{4,5},{5,4},{6,7},{7,6},{8,9},{9,8},{10,11... | collective-permute-start | bytes 1572872 | tf_op jit(solution)/shard_map/ppermute | solution.py:502
  1090.9 42.4 %collective-permute-start.113 = (bf16[4,64,1024]{2,1,0:T(8,128)(2,1)S(1)}, bf16[4,64,1024]{2,1,0:T(8,128)(2,1)S(1)}, u32[]{:S(2)}, u32[]{:S(2)}) collective-permute-start(bf16[4,64,1024]{2,1,0:T(8,128)(2,1)S(1)} %get-tuple-element.48), channel_id=1, source_target_pairs={{0,16},{8,24},{16,0},{24,8},{1,17},{9,25},{17,1},{25,9},{2,18},{10... | collective-permute-start | bytes 1572872 | tf_op jit(solution)/shard_map/ppermute | solution.py:498
  1103.1 92.3 %collective-permute-start.44 = (bf16[192,2048]{1,0:T(8,128)(2,1)}, bf16[192,2048]{1,0:T(8,128)(2,1)}, u32[]{:S(2)}, u32[]{:S(2)}) collective-permute-start(bf16[192,2048]{1,0:T(8,128)(2,1)} %fusion.173), channel_id=1, source_target_pairs={{0,4},{4,0},{1,5},{5,1},{2,6},{6,2},{3,7},{7,3},{8,12},{12,8},{9,1... | collective-permute-start | bytes 2359304 | tf_op jit(solution)/shard_map/ppermute | solution.py:502
  1104.0 46.4 %collective-permute-start.127 = (bf16[4,128,2048]{2,1,0:T(8,128)(2,1)}, bf16[4,128,2048]{2,1,0:T(8,128)(2,1)}, u32[]{:S(2)}, u32[]{:S(2)}) collective-permute-start(bf16[4,128,2048]{2,1,0:T(8,128)(2,1)} %bitcast.198), channel_id=1, source_target_pairs={{0,1},{1,0},{2,3},{3,2},{4,5},{5,4},{6,7},{7,6},{8,9},{9,8},{10,11... | collective-permute-start | bytes 6291464 | tf_op jit(solution)/shard_map/ppermute | solution.py:502
  1104.1 43.5 %collective-permute-start.95 = (bf16[2,192,2048]{2,1,0:T(8,128)(2,1)}, bf16[2,192,2048]{2,1,0:T(8,128)(2,1)}, u32[]{:S(2)}, u32[]{:S(2)}) collective-permute-start(bf16[2,192,2048]{2,1,0:T(8,128)(2,1)} %pad_maximum_fusion.31), channel_id=1, source_target_pairs={{0,2},{2,0},{1,3},{3,1},{4,6},{6,4},{5,7},{7,5},{8,10},{10,8},{9,1... | collective-permute-start | bytes 4718600 | tf_op jit(solution)/shard_map/ppermute | solution.py:502
  1136.1 59.9 %collective-permute-start.56 = (bf16[192,2048]{1,0:T(8,128)(2,1)}, bf16[192,2048]{1,0:T(8,128)(2,1)}, u32[]{:S(2)}, u32[]{:S(2)}) collective-permute-start(bf16[192,2048]{1,0:T(8,128)(2,1)} %fusion.149), channel_id=1, source_target_pairs={{0,16},{8,24},{16,0},{24,8},{1,17},{9,25},{17,1},{25,9},{2,18},{10... | collective-permute-start | bytes 2359304 | tf_op jit(solution)/shard_map/ppermute | solution.py:498
  1144.6 54.1 %collective-permute-start.50 = (bf16[192,2048]{1,0:T(8,128)(2,1)}, bf16[192,2048]{1,0:T(8,128)(2,1)}, u32[]{:S(2)}, u32[]{:S(2)}) collective-permute-start(bf16[192,2048]{1,0:T(8,128)(2,1)} %fusion.150), channel_id=1, source_target_pairs={{0,24},{8,0},{16,8},{24,16},{1,25},{9,1},{17,9},{25,17},{2,26},{10... | collective-permute-start | bytes 2359304 | tf_op jit(solution)/shard_map/ppermute | solution.py:498
  (237 other events, 5382.4 us)

commit v2 on v0

--- a/solution.py
+++ b/solution.py
@@ -1,8 +1,12 @@
+import functools
 import math
 
 import jax
 import jax.numpy as jnp
 from jax import lax
+from jax.experimental import pallas as pl
+from jax.experimental.pallas import tpu as pltpu
+from jax.sharding import Mesh
 from jax.sharding import PartitionSpec as P
 
 QUERY_HEADS = 32
@@ -106,7 +110,7 @@
     return (new_max, new_sum, run_acc * factor[..., None] + update)
 
 
-def local(
+def routed_layer(
     tokens,
     cotangent,
     expert_ids,
@@ -487,42 +491,1090 @@
     )
 
 
+MEMBERS = 4
+
+
+def shift(block, axis, step):
+    count = lax.axis_size(axis)
+    return lax.ppermute(block, axis, [(i, (i + step) % count) for i in range(count)])
+
+
+def swap(block, axis):
+    return lax.ppermute(block, axis, [(0, 1), (1, 0)])
+
+
+def after(block, *earlier):
+    return lax.optimization_barrier((block,) + earlier)[0]
+
+
+class Steps:
+    def __init__(self):
+        self.mark = None
+
+    def __call__(self, sends, work=None, given=(), join=()):
+        blocks = tuple(send[0] for send in sends)
+        mark = () if self.mark is None else (self.mark,)
+        blocks, given, mark = lax.optimization_barrier((blocks, tuple(given), mark))
+        moved = tuple(
+            swap(block, send[1]) if len(send) == 2 else shift(block, send[1], send[2])
+            for block, send in zip(blocks, sends)
+        )
+        done = () if work is None else work(*given)
+        moved, done, join, mark = lax.optimization_barrier((moved, done, tuple(join), mark))
+        self.mark = jax.tree.leaves((moved, done, join))[0]
+        return moved, done, join
+
+    def start(self, block, axis):
+        return swap(after(block, self.mark), axis)
+
+
+def scatter_members(parts):
+    low, wide = jnp.bfloat16, jnp.float32
+    near = swap(parts[1].astype(low), "c")
+    far = swap((parts[0, 1] + near[1].astype(wide)).astype(low), "y")
+    return parts[0, 0] + near[0].astype(wide) + far.astype(wide)
+
+
+def pick(stack, index):
+    return lax.dynamic_index_in_dim(stack, index, 0, keepdims=False)
+
+
+def roped(raw, gain, cosine, sine):
+    inverse = lax.rsqrt(jnp.mean(raw * raw, -1, keepdims=True) + EPS)
+    scaled = raw * inverse * gain
+    return scaled * cosine + pltpu.roll(scaled, HEAD_SIZE // 2, 1) * sine
+
+
+def split_heads(ref, start, heads):
+    size = ref.shape[2] // 2
+    rows = ref[:, 0, start * size : (start + 1) * size, :]
+    rows = rows.reshape(ref.shape[0] * size, ref.shape[3])
+    return jnp.concatenate(
+        [rows[:, i * HEAD_SIZE : (i + 1) * HEAD_SIZE] for i in range(heads)], 0
+    )
+
+
+def key_half(ref, k, start):
+    size = ref.shape[3] // 2
+    rows = ref[k, :, 0, start * size : (start + 1) * size, :]
+    return rows.reshape(ref.shape[1] * size, HEAD_SIZE)
+
+
+def twice(rows):
+    return jnp.concatenate([rows, rows], 0)
+
+
+ACROSS = (((1,), (1,)), ((), ()))
+DOWN = (((0,), (0,)), ((), ()))
+
+
+def score_blocks(z_here, queries, k_ref):
+    nz = k_ref.shape[0]
+    low_q, high_q = queries
+    low_keys = jnp.concatenate([key_half(k_ref, k, 0) for k in range(nz)], 0)
+    blocks = [(low_keys, high_q, None)]
+    for k in range(1, nz):
+        before = z_here >= k
+        keys = jnp.where(before, key_half(k_ref, k, 0), key_half(k_ref, k, 1))
+        blocks.append((keys, jnp.where(before, low_q, high_q), before))
+    blocks.append((key_half(k_ref, 0, 0), low_q, None))
+    blocks.append((key_half(k_ref, 0, 1), high_q, None))
+    return blocks
+
+
+def value_blocks(z_here, ref):
+    nz = ref.shape[0]
+    blocks = [jnp.concatenate([key_half(ref, k, 0) for k in range(nz)], 0)]
+    for k in range(1, nz):
+        blocks.append(jnp.where(z_here >= k, key_half(ref, k, 0), key_half(ref, k, 1)))
+    return blocks + [key_half(ref, 0, 0), key_half(ref, 0, 1)]
+
+
+def to_halves(parts, blocks):
+    low_sum, high_sum = parts[-2], parts[0] + parts[-1]
+    for part, (_, _, before) in zip(parts[1:-2], blocks[1:-2]):
+        low_sum = low_sum + jnp.where(before, part, 0.0)
+        high_sum = high_sum + jnp.where(before, 0.0, part)
+    return low_sum, high_sum
+
+
+def of_halves(low_row, high_row, blocks):
+    rows = [high_row]
+    rows += [jnp.where(before, low_row, high_row) for _, _, before in blocks[1:-2]]
+    return rows + [low_row, high_row]
+
+
+def weigh(blocks, mask_ref):
+    exponent = math.log2(math.e) / math.sqrt(HEAD_SIZE)
+    weights = []
+    for keys, queries, _ in blocks:
+        scores = lax.dot_general(keys, queries, ACROSS, preferred_element_type=jnp.float32)
+        weights.append(jnp.exp2(scores * exponent))
+    weights[-2] = weights[-2] * mask_ref[0]
+    weights[-1] = weights[-1] * mask_ref[1]
+    return weights
+
+
+def attend_kernel(places_ref, q_ref, k_ref, v_ref, cos_ref, sin_ref, gain_ref, mask_ref, out_ref):
+    count = q_ref.shape[3] // HEAD_SIZE
+    size = q_ref.shape[2] // 2
+    queries = []
+    for half in range(2):
+        raw = split_heads(q_ref, half, count)
+        queries.append(
+            roped(raw, gain_ref[...], twice(cos_ref[half]), twice(sin_ref[half])).astype(
+                jnp.bfloat16
+            )
+        )
+    z_here = places_ref[1]
+    blocks = score_blocks(z_here, queries, k_ref)
+    weights = weigh(blocks, mask_ref)
+    totals = to_halves([jnp.sum(weight, 0, keepdims=True) for weight in weights], blocks)
+    mixed = [
+        lax.dot_general(
+            values, weight.astype(jnp.bfloat16), DOWN, preferred_element_type=jnp.float32
+        )
+        for values, weight in zip(value_blocks(z_here, v_ref), weights)
+    ]
+    mixed = to_halves(mixed, blocks)
+    for half in range(2):
+        out = (mixed[half] / totals[half]).T.astype(jnp.bfloat16)
+        rows = out.shape[0] // count
+        for i in range(count):
+            out_ref[:, 0, half * size : (half + 1) * size, i * HEAD_SIZE : (i + 1) * HEAD_SIZE] = (
+                out[i * rows : (i + 1) * rows].reshape(-1, size, HEAD_SIZE)
+            )
+
+
+def attend_back_kernel(
+    places_ref,
+    q_ref,
+    up_ref,
+    k_ref,
+    v_ref,
+    cos_ref,
+    sin_ref,
+    gain_ref,
+    mask_ref,
+    dq_ref,
+    dkv_ref,
+    dgain_ref,
+):
+    nz = k_ref.shape[0]
+    count = q_ref.shape[3] // HEAD_SIZE
+    size = q_ref.shape[2] // 2
+    low = jnp.bfloat16
+    score_scale = 1.0 / math.sqrt(HEAD_SIZE)
+    gain = gain_ref[...]
+    z_here = places_ref[1]
+    raws, queries, ups = [], [], []
+    for half in range(2):
+        raw = split_heads(q_ref, half, count)
+        raws.append(raw)
+        queries.append(roped(raw, gain, twice(cos_ref[half]), twice(sin_ref[half])).astype(low))
+        ups.append(split_heads(up_ref, half, count))
+    blocks = score_blocks(z_here, queries, k_ref)
+    weights = weigh(blocks, mask_ref)
+    totals = to_halves([jnp.sum(weight, 0, keepdims=True) for weight in weights], blocks)
+    inverses = [1.0 / total for total in totals]
+    block_ups = [ups[1]]
+    block_ups += [jnp.where(before, ups[0], ups[1]) for _, _, before in blocks[1:-2]]
+    block_ups += ups
+    dprobs = [
+        lax.dot_general(values, up, ACROSS, preferred_element_type=jnp.float32)
+        for values, up in zip(value_blocks(z_here, v_ref), block_ups)
+    ]
+    probs = [
+        weight * inverse
+        for weight, inverse in zip(weights, of_halves(inverses[0], inverses[1], blocks))
+    ]
+    deltas = to_halves(
+        [jnp.sum(p * d, 0, keepdims=True) for p, d in zip(probs, dprobs)], blocks
+    )
+    dscores = [
+        (p * (d - delta)).astype(low)
+        for p, d, delta in zip(probs, dprobs, of_halves(deltas[0], deltas[1], blocks))
+    ]
+    dvs = [
+        jnp.dot(p.astype(low), up, preferred_element_type=jnp.float32)
+        for p, up in zip(probs, block_ups)
+    ]
+    dks = [
+        jnp.dot(d, block[1], preferred_element_type=jnp.float32) * score_scale
+        for d, block in zip(dscores, blocks)
+    ]
+    dqs = [
+        lax.dot_general(block[0], d, DOWN, preferred_element_type=jnp.float32)
+        for d, block in zip(dscores, blocks)
+    ]
+    dqs = to_halves(dqs, blocks)
+    each = dks[-1].shape[0]
+    fresh = pl.program_id(1) == 0
+    for k in range(nz):
+        both = [
+            jnp.concatenate([dk, dv], 1)
+            for dk, dv in (
+                (dks[0][k * each : (k + 1) * each], dvs[0][k * each : (k + 1) * each]),
+                (dks[k], dvs[k]) if k > 0 else (dks[-2], dvs[-2]),
+            )
+        ]
+        if k == 0:
+            halves = (both[0] + both[1], jnp.concatenate([dks[-1], dvs[-1]], 1))
+        else:
+            before = z_here >= k
+            halves = (
+                both[0] + jnp.where(before, both[1], 0.0),
+                jnp.where(before, 0.0, both[1]),
+            )
+        for half in range(2):
+            part = slice(half * size, (half + 1) * size)
+            earlier = jnp.where(fresh, 0.0, dkv_ref[k, :, 0, part, :])
+            dkv_ref[k, :, 0, part, :] = earlier + halves[half].reshape(-1, size, 2 * HEAD_SIZE)
+
+    gain_part = jnp.zeros((1, HEAD_SIZE), jnp.float32)
+    for half in range(2):
+        cosine, sine = twice(cos_ref[half]), twice(sin_ref[half])
+        raw = raws[half]
+        inverse = lax.rsqrt(jnp.mean(raw * raw, -1, keepdims=True) + EPS)
+        unit = raw * inverse
+        dq = dqs[half].T * score_scale
+        turned = dq * cosine - pltpu.roll(dq, HEAD_SIZE // 2, 1) * sine
+        gain_part = gain_part + jnp.sum(turned * unit, 0, keepdims=True)
+        turned = turned * gain
+        back = inverse * (turned - unit * jnp.mean(turned * unit, -1, keepdims=True))
+        back = back.astype(low)
+        rows = back.shape[0] // count
+        for i in range(count):
+            dq_ref[:, 0, half * size : (half + 1) * size, i * HEAD_SIZE : (i + 1) * HEAD_SIZE] = (
+                back[i * rows : (i + 1) * rows].reshape(-1, size, HEAD_SIZE)
+            )
+    gain_part = jnp.concatenate([gain_part, jnp.zeros((7, HEAD_SIZE), jnp.float32)], 0)
+    first = fresh & (pl.program_id(0) == 0)
+    dgain_ref[...] = jnp.where(first, 0.0, dgain_ref[...]) + gain_part
+
+
+def attention_specs(q, kv, mask):
+    nz, members, sequences, paired, _ = kv.shape
+    pair = q.shape[-1] // MEMBERS
+    q_block = (members, 1, paired, pair)
+    kv_block = (nz, members, 1, paired, HEAD_SIZE)
+    own = pl.BlockSpec(q_block, lambda s, r, places: (0, s, 0, r ^ places[0]))
+    relative = pl.BlockSpec(q_block, lambda s, r, places: (0, s, 0, r))
+    key = pl.BlockSpec(kv_block, lambda s, r, places: (0, 0, s, 0, 0))
+    value = pl.BlockSpec(kv_block, lambda s, r, places: (0, 0, s, 0, 1))
+    both = pl.BlockSpec(
+        (nz, members, 1, paired, 2 * HEAD_SIZE), lambda s, r, places: (0, 0, s, 0, 0)
+    )
+    fixed = lambda shape: pl.BlockSpec(shape, lambda s, r, places: (0,) * len(shape))
+    table = fixed((2, members * paired // 2, HEAD_SIZE))
+    tables = [table, table, fixed((1, HEAD_SIZE)), fixed(mask.shape)]
+    return own, relative, key, value, both, fixed, tables
+
+
+def attend(places, q, kv, cosine, sine, gain, mask):
+    members, sequences, paired, width = q.shape
+    own, relative, key, value, both, fixed, tables = attention_specs(q, kv, mask)
+    elements = sequences * width // HEAD_SIZE * members * paired * kv.shape[0] * members * paired
+    return pl.pallas_call(
+        attend_kernel,
+        grid_spec=pltpu.PrefetchScalarGridSpec(
+            num_scalar_prefetch=1,
+            grid=(sequences, MEMBERS),
+            in_specs=[own, key, value] + tables,
+            out_specs=relative,
+        ),
+        out_shape=jax.ShapeDtypeStruct(q.shape, jnp.bfloat16),
+        compiler_params=pltpu.CompilerParams(vmem_limit_bytes=40 * 2**20),
+        cost_estimate=pl.CostEstimate(
+            flops=4 * elements * HEAD_SIZE, bytes_accessed=8 * 2**20, transcendentals=elements
+        ),
+    )(places, q, kv, kv, cosine, sine, gain, mask)
+
+
+def attend_back(places, q, up, kv, cosine, sine, gain, mask):
+    members, sequences, paired, width = q.shape
+    own, relative, key, value, both, fixed, tables = attention_specs(q, kv, mask)
+    elements = sequences * width // HEAD_SIZE * members * paired * kv.shape[0] * members * paired
+    return pl.pallas_call(
+        attend_back_kernel,
+        grid_spec=pltpu.PrefetchScalarGridSpec(
+            num_scalar_prefetch=1,
+            grid=(sequences, MEMBERS),
+            in_specs=[own, relative, key, value] + tables,
+            out_specs=(own, both, fixed((8, HEAD_SIZE))),
+        ),
+        out_shape=(
+            jax.ShapeDtypeStruct(q.shape, jnp.bfloat16),
+            jax.ShapeDtypeStruct(kv.shape, jnp.float32),
+            jax.ShapeDtypeStruct((8, HEAD_SIZE), jnp.float32),
+        ),
+        compiler_params=pltpu.CompilerParams(vmem_limit_bytes=40 * 2**20),
+        cost_estimate=pl.CostEstimate(
+            flops=10 * elements * HEAD_SIZE, bytes_accessed=16 * 2**20, transcendentals=elements
+        ),
+    )(places, q, up, kv, kv, cosine, sine, gain, mask)
+
+
+def dot32(subscripts, left, right):
+    return jnp.einsum(subscripts, left, right, preferred_element_type=jnp.float32)
+
+
+def expert_kernel(*refs):
+    scalars_ref, x_refs = refs[0], refs[1:5]
+    c_ref, rank_ref, chosen_ref, router_ref, gate_ref, up_ref, down_ref = refs[5:12]
+    rows_ref, hidden_ref, dresults_ref, dgate_ref, dup_ref = refs[-9:-4]
+    sent_refs, back_refs = refs[-4:-2], refs[-2:]
+    low, wide = jnp.bfloat16, jnp.float32
+    blocks = 2
+    tokens, model = x_refs[0].shape
+    opening = pl.program_id(0) == 0
+    slots = rows_ref.shape[2]
+    experts_all = router_ref.shape[0]
+    across = (((1,), (1,)), ((), ()))
+    down = (((0,), (0,)), ((), ()))
+    own_expert = scalars_ref[3]
+    places, picked, upstream, gates = [], [], [], []
+    for block in range(blocks):
+        rows = jnp.where(opening, x_refs[block][...], x_refs[2 + block][...])
+        slot = lax.broadcasted_iota(jnp.int32, (slots, tokens), 0)
+        place = jnp.where(slot == rank_ref[0, block], 1.0, 0.0)
+        chosen = chosen_ref[0, block] > 0.5
+        logits = lax.dot_general(router_ref[...], rows, across, preferred_element_type=wide)
+        highest = jnp.max(jnp.where(chosen, logits, NEGATIVE_LIMIT), 0, keepdims=True)
+        raised = jnp.where(chosen, jnp.exp(jnp.minimum(logits - highest, 0.0)), 0.0)
+        expert = lax.broadcasted_iota(jnp.int32, (experts_all, tokens), 0)
+        mine = jnp.sum(jnp.where(expert == own_expert, raised, 0.0), 0, keepdims=True)
+        gate_row = mine / jnp.sum(raised, 0, keepdims=True)
+        gates.append(jnp.sum(place * gate_row, 1, keepdims=True))
+        place = place.astype(low)
+        places.append(place)
+        picked.append(jnp.dot(place, rows, preferred_element_type=wide).astype(low))
+        cotangent = c_ref[0, block ^ scalars_ref[2]]
+        upstream.append(jnp.dot(place, cotangent, preferred_element_type=wide))
+    rows = jnp.concatenate(picked, 0)
+    upstream = jnp.concatenate(upstream, 0)
+    gates = jnp.concatenate(gates, 0)
+    gate_part = jnp.dot(rows, gate_ref[...], preferred_element_type=wide)
+    up_part = jnp.dot(rows, up_ref[...], preferred_element_type=wide)
+    sigmoid_gate = 1.0 / (1.0 + jnp.exp(-gate_part))
+    silu_gate = gate_part * sigmoid_gate
+    hidden = (silu_gate * up_part).astype(low)
+    results = jnp.dot(hidden, down_ref[...], preferred_element_type=wide).astype(low).astype(wide)
+    dgates = jnp.sum(upstream * results, 1, keepdims=True)
+    scaled = (gates * results).astype(low)
+    dresults = (gates * upstream).astype(low)
+    dhidden = lax.dot_general(dresults, down_ref[...], across, preferred_element_type=wide)
+    dsilu_gate = sigmoid_gate * (1.0 + gate_part * (1.0 - sigmoid_gate))
+    dgate_low = (dhidden * up_part * dsilu_gate).astype(low)
+    dup_low = (dhidden * silu_gate).astype(low)
+    drows = lax.dot_general(dgate_low, gate_ref[...], across, preferred_element_type=wide)
+    drows = drows + lax.dot_general(dup_low, up_ref[...], across, preferred_element_type=wide)
+    drows = drows.astype(low)
+    lane = lax.broadcasted_iota(jnp.int32, (blocks * slots, 128), 1)
+    coarse = dgates.astype(low).astype(wide)
+    extra = jnp.where(lane == own_expert, coarse, 0.0)
+    extra = extra + jnp.where(lane == own_expert + experts_all, dgates - coarse, 0.0)
+    extra = extra.astype(low)
+    for block in range(blocks):
+        part = slice(block * slots, (block + 1) * slots)
+        sent_refs[block][0] = lax.dot_general(
+            places[block], scaled[part], down, preferred_element_type=wide
+        ).astype(low)
+        back_refs[block][0, :, :model] = lax.dot_general(
+            places[block], drows[part], down, preferred_element_type=wide
+        ).astype(low)
+        back_refs[block][0, :, model:] = lax.dot_general(
+            places[block], extra[part], down, preferred_element_type=wide
+        ).astype(low)
+        rows_ref[0, block] = rows[part]
+        hidden_ref[0, block] = hidden[part]
+        dresults_ref[0, block] = dresults[part]
+        dgate_ref[0, block] = dgate_low[part]
+        dup_ref[0, block] = dup_low[part]
+
+
+def experts(scalars, x_blocks, cotangents, ranks, chosen, router, gate, up, down, slots, earlier):
+    tokens, model = x_blocks[0].shape
+    nz, members = cotangents.shape[:2]
+    hidden = gate.shape[1]
+    low = jnp.bfloat16
+    pair = members // 2
+    experts_all = router.shape[0]
+    whole = lambda array: pl.BlockSpec(
+        array.shape, lambda a, s: (0, 0), pipeline_mode=pl.Buffered(1)
+    )
+    by_plane = pl.BlockSpec(
+        (1, pair, tokens, model), lambda a, s: (s[0], a ^ s[1], 0, 0)
+    )
+    turn = lambda *tail: pl.BlockSpec((1, pair) + tail, lambda a, s: (s[4], a, 0, 0))
+    in_specs = [
+        *[whole(block) for block in x_blocks],
+        by_plane,
+        turn(1, tokens),
+        turn(experts_all, tokens),
+        whole(router),
+        whole(gate),
+        whole(up),
+        whole(down),
+    ]
+    shapes = [(slots, model), (slots, hidden), (slots, model)]
+    shapes += [(slots, hidden), (slots, hidden)]
+    out_shape = [jax.ShapeDtypeStruct((nz, members) + shape, low) for shape in shapes]
+    out_specs = [turn(*shape) for shape in shapes]
+    wide_model = model + 128
+    for columns in (model, wide_model):
+        out_shape += [jax.ShapeDtypeStruct((2, tokens, columns), low)] * 2
+        out_specs += [pl.BlockSpec((1, tokens, columns), lambda a, s: (a, 0, 0))] * 2
+    aliases = {}
+    if earlier:
+        in_specs = in_specs + [pl.BlockSpec(memory_space=pl.ANY)] * len(earlier)
+        aliases = {12 + i: i for i in range(len(earlier))}
+    return pl.pallas_call(
+        expert_kernel,
+        grid_spec=pltpu.PrefetchScalarGridSpec(
+            num_scalar_prefetch=1, grid=(2,), in_specs=in_specs, out_specs=out_specs
+        ),
+        out_shape=out_shape,
+        input_output_aliases=aliases,
+        compiler_params=pltpu.CompilerParams(vmem_limit_bytes=58 * 2**20),
+        cost_estimate=pl.CostEstimate(
+            flops=12 * members * slots * model * hidden,
+            bytes_accessed=40 * 2**20,
+            transcendentals=2 * members * slots * hidden,
+        ),
+    )(scalars, *x_blocks, cotangents, ranks, chosen, router, gate, up, down, *earlier)
+
+
+def dot32(subscripts, left, right):
+    return jnp.einsum(subscripts, left, right, preferred_element_type=jnp.float32)
+
+
+def member_layer(
+    tokens,
+    cotangent,
+    expert_ids,
+    attention_gain,
+    ffn_gain,
+    query_gain,
+    key_gain,
+    w_query,
+    key_weight,
+    value_weight,
+    w_output,
+    w_router,
+    w_gate,
+    w_up,
+    w_down,
+):
+    low, wide = jnp.bfloat16, jnp.float32
+    nz = lax.axis_size("z")
+    zi, yi, ci, xi = (lax.axis_index(axis) for axis in ("z", "y", "c", "x"))
+    member = 2 * yi + ci
+    context_count = nz * MEMBERS
+    rows, model = tokens.shape
+    paired = rows // LOCAL_SEQUENCES
+    block_len = paired // 2
+    groups = QUERY_HEADS // KEY_VALUE_HEADS
+    experts_all = w_router.shape[1]
+    around = lambda k: lax.rem(zi + (k % nz), jnp.int32(nz))
+    from_z = [around(-k) for k in range(nz)]
+    crossed = [member ^ r for r in range(MEMBERS)]
+    token_members = member ^ jnp.array([0, 2, 1, 3], jnp.int32)
+
+    def uncrossed(blocks):
+        for bit, odd in ((1, ci), (2, yi)):
+            blocks = [jnp.where(odd == 0, blocks[r], blocks[r ^ bit]) for r in range(MEMBERS)]
+        return jnp.stack(blocks)
+
+    own_expert = zi * MEMBERS + member
+    step = Steps()
+
+    piece = w_query.shape[0]
+    head_rows = w_output.shape[0]
+    query_width = groups * HEAD_SIZE
+    third = w_down.shape[1] // 3
+
+    def prepare(w_query, key_weight, value_weight, w_router, expert_ids):
+        columns = jnp.concatenate(
+            [w.reshape(piece, KEY_VALUE_HEADS, -1) for w in (w_query, key_weight, value_weight)],
+            -1,
+        ).transpose(1, 0, 2)
+        packed = jnp.concatenate([w_router.T.reshape(-1), expert_ids.T.astype(low).reshape(-1)])
+        parts = [pick(columns, crossed[r]) for r in range(MEMBERS)]
+        return parts[0], parts[1], jnp.stack(parts[2:]), packed.reshape(-1, 128)
+
+    (plane1,), (part0, part1, parts_far, packed), _ = step(
+        [(w_output, "z", 1)],
+        prepare,
+        (w_query, key_weight, value_weight, w_router, expert_ids),
+    )
+    width = part0.shape[-1]
+    inputs = tokens.astype(wide)
+    (far, plane3, down0, *small), (normed_attn, inverse_attn), _ = step(
+        [(parts_far, "y"), (w_output, "z", 3), (w_down[0, :third], "x")]
+        + [(packed, "z", k) for k in range(1, nz)],
+        lambda tokens: rms_apply(tokens.astype(wide), attention_gain),
+        (tokens,),
+    )
+    packed = jnp.stack([packed] + small)
+    normed_low = normed_attn.astype(low)
+    (near, other), _, _ = step([(jnp.stack([part1, far[1]]), "c"), (packed, "y")])
+    packed = jnp.stack([packed, other], 1)
+    ordered = uncrossed([part0, near[0], far[0], near[1]])
+    held = [ordered]
+    over_x = []
+    (moved, cross, other, near, packed_near), _, _ = step(
+        [
+            (ordered, "z", 1),
+            (ordered, "x"),
+            (normed_low, "y"),
+            (normed_low, "c"),
+            (packed, "c"),
+        ]
+    )
+    held.append(moved)
+    over_x.append(cross)
+    packed = jnp.stack([packed, packed_near], 1)
+    (moved, cross, other_near, packed_cross, down1), _, _ = step(
+        [
+            (ordered, "z", 2),
+            (held[1], "x"),
+            (other, "c"),
+            (packed, "x"),
+            (w_down[0, third : 2 * third], "x"),
+        ]
+    )
+    held.append(moved)
+    over_x.append(cross)
+    normed_all = jnp.concatenate([normed_low, other, near, other_near])
+    packed = jnp.stack([packed, packed_cross], 1)
+    (moved, cross), _, _ = step([(ordered, "z", 3), (held[2], "x")])
+    held.append(moved)
+    over_x.append(cross)
+    middle = head_rows // 2
+    (cross, plane2_low), _, _ = step([(held[3], "x"), (w_output[:middle], "z", 2)])
+    over_x.append(cross)
+
+    def assemble(start, stop):
+        full = jnp.zeros((nz, MEMBERS, 2, piece, stop - start), low)
+        for k in range(nz):
+            full = lax.dynamic_update_slice(
+                full, held[k][None, :, None, :, start:stop], (from_z[k], 0, xi, 0, 0)
+            )
+            full = lax.dynamic_update_slice(
+                full, over_x[k][None, :, None, :, start:stop], (from_z[k], 0, 1 - xi, 0, 0)
+            )
+        return full.reshape(model, stop - start)
+
+    query_weight = assemble(0, query_width)
+    key_value_weight = assemble(query_width, width)
+
+    own_pos = jax.vmap(lambda device: shard_positions(device, context_count, block_len))(
+        zi * MEMBERS + token_members
+    )
+    cosine, sine_tab = rotary(own_pos.reshape(-1), HEAD_SIZE)
+    row_cosine = cosine.reshape(MEMBERS, 1, paired, HEAD_SIZE)
+    row_sine = sine_tab.reshape(MEMBERS, 1, paired, HEAD_SIZE)
+
+    def halves(table):
+        table = table.reshape(MEMBERS, 2, block_len, HEAD_SIZE).transpose(1, 0, 2, 3)
+        return table.reshape(2, MEMBERS * block_len, HEAD_SIZE)
+
+    half = HEAD_SIZE // 2
+    signs = jnp.where(jnp.arange(HEAD_SIZE) < half, -1.0, 1.0)
+    kernel_cosine, kernel_sine = halves(row_cosine), halves(row_sine * signs)
+    half_pos = own_pos.reshape(MEMBERS, 2, block_len).transpose(1, 0, 2).reshape(2, -1)
+    mask = (half_pos[:, :, None] <= half_pos[:, None, :]).astype(wide)
+    mask = jnp.concatenate([mask, mask], 2)
+
+    width_small = piece * experts_all
+    flat = packed.reshape(nz * 8, -1)
+    device = jnp.arange(nz * 8, dtype=jnp.int32)
+    source = ((zi - device // 8) % nz) * 8 + ((device & 1) ^ xi) * 4
+    source = source + (((device >> 1) & 1) ^ ci) * 2 + (((device >> 2) & 1) ^ yi)
+    router = flat[:, :width_small][source].reshape(nz * 8, experts_all, piece)
+    router = router.transpose(1, 0, 2).reshape(experts_all, model)
+    ids_all = packed.reshape(nz, 2, 2, 2, -1)[:, 0, :, :, width_small:].transpose(0, 2, 1, 3)
+    ids_all = ids_all.reshape(nz, MEMBERS, TOP, rows).astype(jnp.int32)
+    named = jnp.any(ids_all == own_expert, 2)
+    before = (
+        jnp.arange(rows, dtype=jnp.int32)[:, None] <= jnp.arange(rows, dtype=jnp.int32)[None, :]
+    )
+    ranks = dot32("kjs,st->kjt", named.astype(low), before.astype(low)).astype(jnp.int32) - 1
+    ranks = jnp.where(named, ranks, -1)[:, :, None, :]
+    expert_column = jnp.arange(experts_all, dtype=jnp.int32)[:, None]
+    chosen_all = jnp.any(ids_all[:, :, :, None, :] == expert_column, 2).astype(wide)
+    cap_rows = rows * TOP * 5 // (4 * experts_all)
+    slots = -(-cap_rows // 16) * 16
+
+    def project_keys(normed_all, key_value_weight):
+        raw = jnp.dot(normed_all, key_value_weight, preferred_element_type=wide)
+        raw = raw.reshape(MEMBERS, LOCAL_SEQUENCES, paired, 2 * HEAD_SIZE)
+        key_proj = raw[..., :HEAD_SIZE]
+        key_normed, key_inverse = rms_apply(key_proj, key_gain)
+        key_low = rope_apply(key_normed, row_cosine, row_sine).astype(low)
+        value_low = raw[..., HEAD_SIZE:].astype(low)
+        return key_proj, key_inverse, jnp.concatenate([key_low, value_low], -1)
+
+    gate_cut = w_gate.shape[1] * 5 // 8
+    (plane2_high, down2), (key_proj, key_inverse, key_value), _ = step(
+        [(w_output[middle:], "z", 2), (w_down[0, 2 * third :], "x")],
+        project_keys,
+        (normed_all, key_value_weight),
+    )
+    planes = jnp.stack([w_output, plane1, jnp.concatenate([plane2_low, plane2_high]), plane3])
+    wanted = [pick(planes, lax.rem(zi + nz - crossed[r], jnp.int32(nz))) for r in range(MEMBERS)]
+    (key_value1, key_value3, far, gate0), queries, _ = step(
+        [
+            (key_value, "z", 1),
+            (key_value, "z", 3),
+            (jnp.stack(wanted[2:]), "y"),
+            (w_gate[0, :gate_cut], "x"),
+        ],
+        lambda normed_all, query_weight: jnp.dot(
+            normed_all, query_weight, preferred_element_type=wide
+        ),
+        (normed_all, query_weight),
+    )
+    queries = queries.reshape(MEMBERS, LOCAL_SEQUENCES, paired, query_width)
+    cotangents = lax.all_gather(
+        after(cotangent, step.mark), ("z", "y", "c"), axis=0, tiled=True
+    ).reshape(nz, MEMBERS, rows, model)
+    mine = jnp.stack([wanted[0], far[0]])
+    (key_value2, near, cross_mine), _, _ = step(
+        [(key_value, "z", 2), (jnp.stack([wanted[1], far[1]]), "c"), (mine, "x")]
+    )
+    key_value = jnp.stack([key_value, key_value1, key_value2, key_value3])
+
+    places = jnp.stack([member, zi]).astype(jnp.int32)
+    gain_row = query_gain[None]
+    (cross_near,), attended, _ = step(
+        [(near, "x")],
+        attend,
+        (places, queries, key_value, kernel_cosine, kernel_sine, gain_row, mask),
+    )
+    attended = attended.reshape(MEMBERS * rows, query_width)
+    own_heads = jnp.stack([mine[0], near[0], mine[1], near[1]])
+    other_heads = jnp.stack([cross_mine[0], cross_near[0], cross_mine[1], cross_near[1]])
+    output_weight = jnp.where(
+        xi == 0, jnp.stack([own_heads, other_heads], 1), jnp.stack([other_heads, own_heads], 1)
+    ).reshape(query_width, model)
+
+    mixed_part = jnp.dot(attended, output_weight, preferred_element_type=wide)
+    mixed_part = mixed_part.reshape(2, 2, rows, model)
+    (near,), _, _ = step([(mixed_part[1].astype(low), "c")])
+    summed_far = (mixed_part[0, 1] + near[1].astype(wide)).astype(low)
+    (other, gate1), _, _ = step([(summed_far, "y"), (w_gate[0, gate_cut:], "x")])
+    mixed_attn = inputs + (mixed_part[0, 0] + near[0].astype(wide) + other.astype(wide))
+    normed_ffn, inverse_ffn = rms_apply(mixed_attn, ffn_gain)
+    ffn_low = normed_ffn.astype(low)
+
+    logits = dot32("td,ed->te", ffn_low, router)
+    chosen = jnp.any(
+        expert_ids[:, :, None] == jnp.arange(experts_all, dtype=jnp.int32)[None, None, :], 1
+    )
+    highest = jnp.max(jnp.where(chosen, logits, NEGATIVE_LIMIT), 1, keepdims=True)
+    raised = jnp.where(chosen, jnp.exp(jnp.minimum(logits - highest, 0.0)), 0.0)
+    gates = raised / jnp.sum(raised, 1, keepdims=True)
+
+    def whole(own, others):
+        full = jnp.zeros((2,) + own.shape, low)
+        full = lax.dynamic_update_slice(full, own[None], (xi, 0, 0))
+        start = 0
+        for other in others:
+            full = lax.dynamic_update_slice(full, other[None], (1 - xi, start, 0))
+            start += other.shape[0]
+        return full.reshape(2 * own.shape[0], own.shape[1])
+
+    def run_experts(k, x_blocks, kept, weights):
+        scalars = jnp.stack([from_z[k], yi, ci, own_expert, jnp.int32(k)]).astype(jnp.int32)
+        out = experts(
+            scalars, x_blocks, cotangents, ranks, chosen_all, router, *weights, slots, kept
+        )
+        return tuple(out[:-4]), out[-4:-2], out[-2:]
+
+    def added(pair, back, a):
+        return pair[0][a].astype(wide) + back[a].astype(wide)
+
+    def assemble_experts(*pieces):
+        gates_part, ups_part, downs_part = pieces
+        return (
+            whole(w_gate[0], gates_part),
+            whole(w_up[0], ups_part),
+            whole(w_down[0], downs_part),
+        )
+
+    (x2, y0, n0, up_other), _, _ = step(
+        [(ffn_low, "z", 2), (ffn_low, "y"), (ffn_low, "c"), (w_up[0], "x")]
+    )
+    (x1, y2, ny0, n2), weights, _ = step(
+        [(ffn_low, "z", 1), (x2, "y"), (y0, "c"), (x2, "c")],
+        assemble_experts,
+        ([gate0, gate1], [up_other], [down0, down1, down2]),
+    )
+    (x3, y1, ny2, n1), (kept, mixed0, rows0), _ = step(
+        [(ffn_low, "z", 3), (x1, "y"), (y2, "c"), (x1, "c")],
+        functools.partial(run_experts, 0),
+        ([ffn_low, n0, y0, ny0], (), weights),
+    )
+    (y3, ny1, n3, back0, mixed_back0), (kept, mixed2, rows2), _ = step(
+        [(x3, "y"), (y1, "c"), (x3, "c"), (rows0[1], "c"), (mixed0[1], "c")],
+        functools.partial(run_experts, 2),
+        ([x2, n2, y2, ny2], kept, weights),
+    )
+    (ny3, back2, mixed_back2, far0), (kept, mixed1, rows1), _ = step(
+        [
+            (y3, "c"),
+            (rows2[1], "c"),
+            (mixed2[1], "c"),
+            (added(rows0, back0, 1).astype(low), "y"),
+        ],
+        functools.partial(run_experts, 1),
+        ([x1, n1, y1, ny1], kept, weights),
+    )
+    (back1, mixed_back1, far2), (kept, mixed3, rows3), _ = step(
+        [(rows1[1], "c"), (mixed1[1], "c"), (added(rows2, back2, 1).astype(low), "y")],
+        functools.partial(run_experts, 3),
+        ([x3, n3, y3, ny3], kept, weights),
+    )
+    expert_rows, hidden_low, dresults, dgate_low, dup_low = (
+        block.reshape(context_count * slots, -1) for block in kept
+    )
+
+    def halved(grad, cuts):
+        size = grad.shape[0] // 2
+        own = lax.dynamic_slice_in_dim(grad, xi * size, size, 0)
+        other = lax.dynamic_slice_in_dim(grad, (1 - xi) * size, size, 0).astype(low)
+        cut = size // cuts
+        return own, [other[i * cut : (i + 1) * cut] for i in range(cuts)]
+
+    def joined(own, moved):
+        return (own + jnp.concatenate(moved, 0).astype(wide))[None]
+
+    total2 = (added(rows2, back2, 0) + far2.astype(wide)).astype(low)
+    cut = rows // 2
+    (z2_low, far1, back3, mixed_back3), down_grad, _ = step(
+        [
+            (total2[:cut], "z", -2),
+            (added(rows1, back1, 1).astype(low), "y"),
+            (rows3[1], "c"),
+            (mixed3[1], "c"),
+        ],
+        functools.partial(dot32, "sf,sd->fd"),
+        (hidden_low, dresults),
+    )
+    down_grad, down_sends = halved(down_grad, 2)
+    (z2_high, far3, down0), gate_grad, _ = step(
+        [
+            (total2[cut:], "z", -2),
+            (added(rows3, back3, 1).astype(low), "y"),
+            (down_sends[0], "x"),
+        ],
+        functools.partial(dot32, "sd,sf->df"),
+        (expert_rows, dgate_low),
+    )
+    total1 = (added(rows1, back1, 0) + far1.astype(wide)).astype(low)
+    total3 = (added(rows3, back3, 0) + far3.astype(wide)).astype(low)
+    (z1, down1, mixed_far2), up_grad, _ = step(
+        [
+            (total1, "z", -1),
+            (down_sends[1], "x"),
+            (added(mixed2, mixed_back2, 1).astype(low), "y"),
+        ],
+        functools.partial(dot32, "sd,sf->df"),
+        (expert_rows, dup_low),
+    )
+    gate_grad, gate_sends = halved(gate_grad, 2)
+    (z3, gate0, mixed_far1), (down_grad, mixed_send2), _ = step(
+        [
+            (total3, "z", -3),
+            (gate_sends[0], "x"),
+            (added(mixed1, mixed_back1, 1).astype(low), "y"),
+        ],
+        lambda own, moved, pair, back, far: (
+            joined(own, moved),
+            (added(pair, back, 0) + far.astype(wide)).astype(low),
+        ),
+        (down_grad, [down0, down1], mixed2, mixed_back2, mixed_far2),
+    )
+    returned = added(rows0, back0, 0) + far0.astype(wide) + z1.astype(wide) + z3.astype(wide)
+    returned = returned + jnp.concatenate([z2_low, z2_high], 0).astype(wide)
+    dffn_routed = returned[:, :model]
+    dgates = returned[:, model : model + experts_all]
+    dgates = dgates + returned[:, model + experts_all : model + 2 * experts_all]
+    dlogits = gates * (dgates - jnp.sum(gates * dgates, 1, keepdims=True))
+    dlogits_low = dlogits.astype(low)
+    router_grad = dot32("te,td->ed", dlogits_low, ffn_low)
+
+    upstream = cotangent.astype(wide)
+    dffn_rows = dffn_routed + dot32("te,ed->td", dlogits_low, router)
+    dmixed_norm, ffn_gain_part = rms_back(mixed_attn, inverse_ffn, ffn_gain, dffn_rows)
+    dmixed_attn = upstream + dmixed_norm
+    dattn_low = dmixed_attn.astype(low)
+    (other, near, gate1, mixed_z2_low), (mixed_send1, up_grad, up_sends), _ = step(
+        [
+            (dattn_low, "y"),
+            (dattn_low, "c"),
+            (gate_sends[1], "x"),
+            (mixed_send2[:cut], "z", -2),
+        ],
+        lambda pair, back, far, grad: (
+            (added(pair, back, 0) + far.astype(wide)).astype(low),
+            *halved(grad, 2),
+        ),
+        (mixed1, mixed_back1, mixed_far1, up_grad),
+    )
+    (other_near,), _, _ = step([(other, "c")])
+    dattn_all = jnp.concatenate([dattn_low, other, near, other_near])
+
+    def through_output(dattn_all, output_weight, attended):
+        attended_grad = dot32("td,cd->tc", dattn_all, output_weight).astype(low)
+        output_part = dot32("tc,td->cd", attended, dattn_all).astype(low)
+        output_part = output_part.reshape(MEMBERS, 2, head_rows, model)
+        own = lax.dynamic_index_in_dim(output_part, xi, 1, keepdims=False)
+        other = lax.dynamic_index_in_dim(output_part, 1 - xi, 1, keepdims=False)
+        return attended_grad, own[:2], own[2:], other[:1], other[1:]
+
+    (mixed_far3, up0), (attended_grad, own_near, own_far, cross_first, cross_rest), _ = step(
+        [(added(mixed3, mixed_back3, 1).astype(low), "y"), (up_sends[0], "x")],
+        through_output,
+        (dattn_all, output_weight, attended),
+    )
+    attended_grad = attended_grad.reshape(MEMBERS, LOCAL_SEQUENCES, paired, query_width)
+    early = jnp.concatenate([router_grad, ffn_gain_part[None]], 0)
+    moved, (dquery_low, dkey_value, query_gain_part), _ = step(
+        [
+            (cross_rest, "x"),
+            (early, "x"),
+            (mixed_send1, "z", -1),
+            (mixed_send2[cut:], "z", -2),
+        ],
+        attend_back,
+        (
+            places,
+            queries,
+            attended_grad,
+            key_value,
+            kernel_cosine,
+            kernel_sine,
+            gain_row,
+            mask,
+        ),
+    )
+    cross, early_x, mixed_z1, mixed_z2_high = moved
+    early = early + early_x
+    output_far = (own_far.astype(wide) + cross[1:].astype(wide)).astype(low)
+    query_gain_part = query_gain_part[0]
+    dquery_low = dquery_low.reshape(MEMBERS * rows, query_width)
+
+    def planes_of(part):
+        own = lax.dynamic_index_in_dim(part, xi, 2, keepdims=False)
+        other = lax.dynamic_index_in_dim(part, 1 - xi, 2, keepdims=False)
+        return [(pick(own, around(k)), pick(other, around(k))) for k in range(nz)]
+
+    query_part = dot32("td,tc->dc", normed_all, dquery_low).astype(low)
+    query_planes = planes_of(query_part.reshape(nz, MEMBERS, 2, piece, query_width))
+    near_rest = cross[:1]
+    moved, (dnormed, mixed_send3, gate_grad), _ = step(
+        [(dkey_value[k].astype(low), "z", -k) for k in range(1, nz)]
+        + [(query_planes[2][1], "x"), (cross_first, "x"), (output_far, "y")],
+        lambda grad, weight, pair, back, far, own, moved: (
+            dot32("tc,dc->td", grad, weight),
+            (added(pair, back, 0) + far.astype(wide)).astype(low),
+            joined(own, moved),
+        ),
+        (
+            dquery_low,
+            query_weight,
+            mixed3,
+            mixed_back3,
+            mixed_far3,
+            gate_grad,
+            [gate0, gate1],
+        ),
+    )
+    cross, near_first, output_far = moved[nz - 1 :]
+    output_cross = jnp.concatenate([near_first, near_rest])
+    query_sum2 = (query_planes[2][0].astype(wide) + cross.astype(wide)).astype(low)
+    output_near = (own_near.astype(wide) + output_cross.astype(wide)).astype(low)
+
+    def project_keys_back(dnormed, dkey_value_own, moved, key_value_weight):
+        dkey_value_own = dkey_value_own + sum(block.astype(wide) for block in moved)
+        dkey, dvalue = dkey_value_own[..., :HEAD_SIZE], dkey_value_own[..., HEAD_SIZE:]
+        dkey_proj, key_gain_part = rms_back(
+            key_proj, key_inverse, key_gain, rope_back(dkey, row_cosine, row_sine)
+        )
+        dkey_value_low = jnp.concatenate([dkey_proj, dvalue], -1).astype(low)
+        dkey_value_low = dkey_value_low.reshape(MEMBERS * rows, 2 * HEAD_SIZE)
+        dnormed = dnormed + dot32("tc,dc->td", dkey_value_low, key_value_weight)
+        dnormed = scatter_members(dnormed.reshape(2, 2, rows, model))
+        key_part = dot32("td,tc->dc", normed_all, dkey_value_low).astype(low)
+        key_part = key_part.reshape(nz, MEMBERS, 2, piece, 2 * HEAD_SIZE)
+        key_own = lax.dynamic_index_in_dim(key_part, xi, 2, keepdims=False)
+        key_other = lax.dynamic_index_in_dim(key_part, 1 - xi, 2, keepdims=False)
+        return dnormed, key_own, key_other, key_gain_part
+
+    moved_z, (dnormed, key_own, key_other, key_gain_part), _ = step(
+        [
+            (query_sum2, "z", 2),
+            (mixed_send3[:cut], "z", -3),
+            (jnp.stack([query_planes[1][1], query_planes[3][1]]), "x"),
+            (jnp.stack([output_near[1], output_far[1]]), "c"),
+        ],
+        project_keys_back,
+        (dnormed, dkey_value[0], moved[: nz - 1], key_value_weight),
+    )
+    query_z2, mixed_z3_low, cross, output_back = moved_z
+    query_sum1 = (query_planes[1][0].astype(wide) + cross[0].astype(wide)).astype(low)
+    query_sum3 = (query_planes[3][0].astype(wide) + cross[1].astype(wide)).astype(low)
+    dinput_norm, attention_gain_part = rms_back(inputs, inverse_attn, attention_gain, dnormed)
+    late = jnp.concatenate([attention_gain_part, query_gain_part, key_gain_part])
+    small = jnp.concatenate([early.reshape(-1, 128), late.reshape(-1, 128)], 0)
+    output_blocks = [output_near[0], output_back[0], output_far[0], output_back[1]]
+
+    def order_output(blocks, dmixed_attn, dinput_norm):
+        blocks = uncrossed(blocks)
+        sends = [pick(blocks, around(k)) for k in range(nz)]
+        return sends, (dmixed_attn + dinput_norm).astype(low)
+
+    (query_z1, query_z3, cross, key_cross, late_x), (output_sends, d_tokens), _ = step(
+        [
+            (query_sum1, "z", 1),
+            (query_sum3, "z", 3),
+            (query_planes[0][1], "x"),
+            (key_other, "x"),
+            (late.reshape(-1, 128), "x"),
+        ],
+        order_output,
+        (output_blocks, dmixed_attn, dinput_norm),
+    )
+    early_rows = early.size // 128
+    small = jnp.concatenate([small[:early_rows], small[early_rows:] + late_x], 0)
+    key_sum = (key_own.astype(wide) + key_cross.astype(wide)).astype(low)
+
+    def total_queries(own, cross, *moved):
+        total = own.astype(wide) + cross.astype(wide) + sum(m.astype(wide) for m in moved)
+        total = total.astype(low)
+        parts = [pick(total, crossed[r]) for r in range(MEMBERS)]
+        return parts[0], parts[1], jnp.stack(parts[2:])
+
+    query_parts = total_queries(query_planes[0][0], cross, query_z1, query_z2, query_z3)
+    (output_z1, query_far, small_y, mixed_far0, mixed_z3_high, *key_moves), _, _ = step(
+        [
+            (output_sends[1], "z", 1),
+            (query_parts[2], "y"),
+            (small, "y"),
+            (added(mixed0, mixed_back0, 1).astype(low), "y"),
+            (mixed_send3[cut:], "z", -3),
+        ]
+        + [(pick(key_sum, around(k)), "z", k) for k in range(1, nz)],
+    )
+    small = small + small_y
+    key_total = pick(key_sum, zi).astype(wide)
+    key_total = (key_total + sum(m.astype(wide) for m in key_moves)).astype(low)
+    key_parts = [pick(key_total, crossed[r]) for r in range(MEMBERS)]
+
+    def member_columns(part0, near, far):
+        grads = uncrossed([part0, near[0], far[0], near[1]])
+        return grads.astype(wide).transpose(1, 0, 2)
+
+    (output_z2, up1, key_far, query_near, small_c), (mixed,), _ = step(
+        [
+            (output_sends[2], "z", 2),
+            (up_sends[1], "x"),
+            (jnp.stack(key_parts[2:]), "y"),
+            (jnp.stack([query_parts[1], query_far[1]]), "c"),
+            (small, "c"),
+        ],
+        lambda base, pair, back, far, z1, *halves: (
+            (
+                base
+                + added(pair, back, 0)
+                + far.astype(wide)
+                + z1.astype(wide)
+                + jnp.concatenate(halves[:2], 0).astype(wide)
+                + jnp.concatenate(halves[2:], 0).astype(wide)
+            ).astype(low),
+        ),
+        (
+            mixed_attn,
+            mixed0,
+            mixed_back0,
+            mixed_far0,
+            mixed_z1,
+            mixed_z2_low,
+            mixed_z2_high,
+            mixed_z3_low,
+            mixed_z3_high,
+        ),
+    )
+    small = small + small_c
+
+    def finish(own, moved, output_own, z1, z2, parts, near, far):
+        output = output_own.astype(wide) + z1.astype(wide) + z2.astype(wide)
+        return joined(own, moved), output, member_columns(parts, near, far)
+
+    (output_z3, key_near, *small_z), (up_grad, output_grad, query_grad), _ = step(
+        [
+            (output_sends[3], "z", 3),
+            (jnp.stack([key_parts[1], key_far[1]]), "c"),
+        ]
+        + [(small, "z", k) for k in range(1, nz)],
+        finish,
+        (
+            up_grad,
+            [up0, up1],
+            output_sends[0],
+            output_z1,
+            output_z2,
+            query_parts[0],
+            query_near,
+            query_far,
+        ),
+    )
+    query_grad = query_grad.reshape(piece, -1)
+    output_grad = output_grad + output_z3.astype(wide)
+    small = small + sum(small_z)
+    early = small[:early_rows].reshape(early.shape)
+    gains = small[early_rows:].reshape(-1)
+    key_grads = member_columns(key_parts[0], key_near, key_far)
+    key_grad = key_grads[..., :HEAD_SIZE].reshape(piece, -1)
+    value_grad = key_grads[..., HEAD_SIZE:].reshape(piece, -1)
+    device = own_expert * 2 + xi
+    router_own = lax.dynamic_slice_in_dim(early[:experts_all], device * piece, piece, 1).T
+    return (
+        mixed,
+        d_tokens,
+        gains[:model],
+        early[experts_all],
+        gains[model : model + HEAD_SIZE],
+        gains[model + HEAD_SIZE :],
+        query_grad,
+        key_grad,
+        value_grad,
+        output_grad,
+        router_own,
+        gate_grad,
+        up_grad,
+        down_grad,
+    )
+
+
 def solution(mesh):
+    contexts, pairs = mesh.shape["ctx"], mesh.shape["fsdp"]
+    planes = contexts // MEMBERS
+    if planes == KEY_VALUE_HEADS and pairs * MEMBERS * KEY_VALUE_HEADS == QUERY_HEADS:
+        layer, every, split = member_layer, ("z", "y", "c", "x"), ("z", "y", "c")
+        pair = "x"
+        mesh = Mesh(mesh.devices.reshape(planes, 2, 2, pairs), every)
+    else:
+        layer, every, split, pair = routed_layer, ("ctx", "fsdp"), "ctx", "fsdp"
+    by_row = P(every, None)
+    by_expert = P(split, pair, None)
     return jax.shard_map(
-        local,
+        layer,
         mesh=mesh,
-        in_specs=(
-            P(("ctx", "fsdp"), None),
-            P(("ctx", "fsdp"), None),
-            P(("ctx", "fsdp"), None),
-            P(),
-            P(),
-            P(),
-            P(),
-            P(("ctx", "fsdp"), None),
-            P(("ctx", "fsdp"), None),
-            P(("ctx", "fsdp"), None),
-            P(("ctx", "fsdp"), None),
-            P(("ctx", "fsdp"), None),
-            P("ctx", "fsdp", None),
-            P("ctx", "fsdp", None),
-            P("ctx", "fsdp", None),
-        ),
-        out_specs=(
-            P(("ctx", "fsdp"), None),
-            P(("ctx", "fsdp"), None),
-            P(),
-            P(),
-            P(),
-            P(),
-            P(("ctx", "fsdp"), None),
-            P(("ctx", "fsdp"), None),
-            P(("ctx", "fsdp"), None),
-            P(("ctx", "fsdp"), None),
-            P(("ctx", "fsdp"), None),
-            P("ctx", "fsdp", None),
-            P("ctx", "fsdp", None),
-            P("ctx", "fsdp", None),
-        ),
+        in_specs=(by_row,) * 3 + (P(),) * 4 + (by_row,) * 5 + (by_expert,) * 3,
+        out_specs=(by_row,) * 2 + (P(),) * 4 + (by_row,) * 5 + (by_expert,) * 3,
         check_vma=False,
     )

time: 3560 us -> 928 us (0.26)
  waiting for transfers between devices: 2650 us -> 415 us
  blocking collectives: 229 us -> 0 us
  matrix products: 275 us -> 54.8 us
  Pallas kernels: 0 us -> 126 us
  local copies, waits for them, and re-layouts: 160 us -> 93.5 us
    reduce_scatter x9 -> x0, waiting for transfers between devices: 1860 us -> none  [the longest x1 711 us: local(): lax.psum_scatter(output_grad, ('ctx', 'fsdp'), scatter_dimension=0, tiled...]
    all_gather x9 -> x1, waiting for transfers between devices: 428 us -> 0.01 us  [member_layer(): lax.all_gather(after(cotangent, step.mark), ('z', 'y', 'c'), axis=0, tile...]
    ppermute x0 -> x119, waiting for transfers between devices: none -> 415 us  [the longest x40 257 us: shift(): lax.ppermute(block, axis, [(i, (i + step) % count) for i in range(count)])]
    all_to_all x4 -> x0, waiting for transfers between devices: 236 us -> none  [the longest x1 118 us: local(): lax.all_to_all(from_experts(results), 'ctx', split_axis=0, concat_axis=0,...]
    dot_general x53 -> x16, matrix products: 273 us -> 54.8 us  [the longest x13 47 us: dot32(): jnp.einsum(subscripts, left, right, preferred_element_type=jnp.float32)]
    all_gather x1 -> x0, blocking collectives: 191 us -> none  [local(): lax.all_gather(w_router, ('ctx', 'fsdp'), axis=0, tiled=True)]
    unnamed x20 -> x1, waiting for transfers between devices: 126 us -> 0.02 us
    pallas_call x0 -> x6, Pallas kernels: none -> 126 us  [the longest x4 92.7 us: experts(): pl.pallas_call(expert_kernel, grid_spec=pltpu.PrefetchScalarGridSpec(num_...]
  transfers between devices with their start and end apart: 23 -> 120, of which waited for: 21 -> 50; matrix products, arithmetic and copies ran while one was open for 10% -> 17% of each run, Pallas kernels for 0% -> 14%
where the time goes in v2:
time: 928 us; the launch traced here: 919 us
  waiting for transfers between devices  415 us (45%)
  Pallas kernels  126 us (14%)
  starting transfers between devices  119 us (13%)
  other arithmetic  93.6 us (10%)
  local copies, waits for them, and re-layouts  93.5 us (10%)
  matrix products  54.8 us (6%)
  between operations  17 us (2%)
    ppermute x40, waiting for transfers between devices, shift(): lax.ppermute(block, axis, [(i, (i + step) % count) for i in range(count)])  257 us
    ppermute x79, waiting for transfers between devices, swap(): return lax.ppermute(block, axis, [(0, 1), (1, 0)])  157 us
    pallas_call x4, Pallas kernels, experts(): pl.pallas_call(expert_kernel, grid_spec=pltpu.PrefetchScalarGridSpec(num_...  92.7 us
    ppermute x40, starting transfers between devices, shift(): lax.ppermute(block, axis, [(i, (i + step) % count) for i in range(count)])  62.9 us
    ppermute x79, starting transfers between devices, swap(): return lax.ppermute(block, axis, [(0, 1), (1, 0)])  56.5 us
    dot_general x13, matrix products, dot32(): jnp.einsum(subscripts, left, right, preferred_element_type=jnp.float32)  47 us
    pallas_call x1, Pallas kernels, attend_back(): pl.pallas_call(attend_back_kernel, grid_spec=pltpu.PrefetchScalarGridSpec...  20.8 us
    unnamed x348, local copies, waits for them, and re-layouts  19.3 us
  transfers between devices with their start and end apart: 120, of which 50 were waited for; matrix products, arithmetic and copies ran while one was open for 17% of the time, Pallas kernels for 14%

profile of v2, /device:TPU:0, one launch (start us, length us, event | category | flops | bytes accessed | tf_op | source)
XLA Modules:
  0.0 918.5 jit_solution(6825210003418671212)
XLA Ops:
  19.3 5.2 collective-permute-done
  30.6 7.5 collective-permute-done.4
  56.9 10.3 %collective-permute-done.10 = bf16[4,64,1280]{2,1,0:T(8,128)(2,1)} collective-permute-done((bf16[4,64,1280]{2,1,0:T(8,128)(2,1)S(1)}, bf16[4,64,1280]{2,1,0:T(8,128)(2,1)}, u32[]{:S(2)}, u32[]{:S(2)}) %collective-permute-start.10) | collective-permute-done | bytes 655392 | tf_op jit(solution)/shard_map/ppermute | solution.py:503
  78.2 23.4 %collective-permute-done.17 = bf16[4,2,2,20,128]{4,3,2,1,0:T(8,128)(2,1)S(1)} collective-permute-done((bf16[4,2,2,20,128]{4,3,2,1,0:T(8,128)(2,1)S(1)}, bf16[4,2,2,20,128]{4,3,2,1,0:T(8,128)(2,1)S(1)}, u32[]{:S(2)}, u32[]{:S(2)}) %collective-permute-start.17) | collective-permute-done | bytes 81952 | tf_op jit(solution)/shard_map/ppermute | solution.py:503
  105.6 13.4 %collective-permute-done.19 = bf16[4,64,1280]{2,1,0:T(8,128)(2,1)S(1)} collective-permute-done((bf16[4,64,1280]{2,1,0:T(8,128)(2,1)S(1)}, bf16[4,64,1280]{2,1,0:T(8,128)(2,1)S(1)}, u32[]{:S(2)}, u32[]{:S(2)}) %collective-permute-start.19) | collective-permute-done | bytes 655392 | tf_op jit(solution)/shard_map/ppermute | solution.py:499
  121.8 11.4 %collective-permute-done.22 = bf16[64,2048]{1,0:T(8,128)(2,1)S(1)} collective-permute-done((bf16[64,2048]{1,0:T(8,128)(2,1)S(1)}, bf16[64,2048]{1,0:T(8,128)(2,1)S(1)}, u32[]{:S(2)}, u32[]{:S(2)}) %collective-permute-start.22) | collective-permute-done | bytes 262176 | tf_op jit(solution)/shard_map/ppermute | solution.py:499
  140.2 11.4 %collective-permute-done.23 = bf16[64,2048]{1,0:T(8,128)(2,1)S(1)} collective-permute-done((bf16[64,2048]{1,0:T(8,128)(2,1)S(1)}, bf16[64,2048]{1,0:T(8,128)(2,1)S(1)}, u32[]{:S(2)}, u32[]{:S(2)}) %collective-permute-start.23) | collective-permute-done | bytes 262176 | tf_op jit(solution)/shard_map/ppermute | solution.py:499
  155.8 4.1 collective-permute-start.26
  163.3 6.3 collective-permute-done.25
  169.6 4.9 collective-permute-done.26
  193.2 36.7 %collective-permute-done.29 = bf16[4,3,64,256]{3,2,1,0:T(8,128)(2,1)} collective-permute-done((bf16[4,3,64,256]{3,2,1,0:T(8,128)(2,1)S(1)}, bf16[4,3,64,256]{3,2,1,0:T(8,128)(2,1)}, u32[]{:S(2)}, u32[]{:S(2)}) %collective-permute-start.29) | collective-permute-done | bytes 393248 | tf_op jit(solution)/shard_map/ppermute | solution.py:499
  234.4 12.2 %shard_map.263 = bf16[4,3,64,1024]{3,2,1,0:T(8,128)(2,1)S(1)} custom-call(s32[2]{0:T(128)S(1)} %pad_add_fusion.places_ref, f32[4,3,64,1024]{3,2,1,0:T(8,128)S(1)} %bitcast.548, bf16[4,4,3,64,256]{4,3,2,1,0:T(8,128)(2,1)S(1)} %pad_maximum_fusion.4.k_ref.v_ref, bf16[4,4,3,64,256]{4,3,2,1,0:T(8,128)(2,1)S(1)} %pad_maximum_fusion.4.k_ref.v_ref, ...), custom_call_target="tpu_custom_call" | custom-call | flops 3221225472 | bytes 8388608 | tf_op jit(solution)/shard_map/pallas_call | solution.py:778
  248.5 7.9 collective-permute-done.32
  269.3 13.4 %collective-permute-done.35 = bf16[384,768]{1,0:T(8,128)(2,1)} collective-permute-done((bf16[384,768]{1,0:T(8,128)(2,1)}, bf16[384,768]{1,0:T(8,128)(2,1)}, u32[]{:S(2)}, u32[]{:S(2)}) %collective-permute-start.35) | collective-permute-done | bytes 589856 | tf_op jit(solution)/shard_map/ppermute | solution.py:503
  282.6 6.3 collective-permute-done.34
  311.1 29.2 %collective-permute-done.36.refs_1_ = bf16[192,2048]{1,0:T(8,128)(2,1)} collective-permute-done((bf16[192,2048]{1,0:T(8,128)(2,1)}, bf16[192,2048]{1,0:T(8,128)(2,1)}, u32[]{:S(2)}, u32[]{:S(2)}) %collective-permute-start.36) | collective-permute-done | bytes 786464 | tf_op jit(solution)/shard_map/ppermute | solution.py:499
  351.2 10.5 %collective-permute-done.40.refs_1_ = bf16[192,2048]{1,0:T(8,128)(2,1)} collective-permute-done((bf16[192,2048]{1,0:T(8,128)(2,1)}, bf16[192,2048]{1,0:T(8,128)(2,1)}, u32[]{:S(2)}, u32[]{:S(2)}) %collective-permute-start.40) | collective-permute-done | bytes 786464 | tf_op jit(solution)/shard_map/ppermute | solution.py:499
  364.6 23.3 %shard_map.264 = (bf16[4,4,128,2048]{3,2,1,0:T(8,128)(2,1)}, bf16[4,4,128,768]{3,2,1,0:T(8,128)(2,1)}, bf16[4,4,128,2048]{3,2,1,0:T(8,128)(2,1)}, bf16[4,4,128,7...) custom-call(s32[5]{0:T(128)} %stack.308.refs_0_, ...), custom_call_target="tpu_custom_call" | custom-call | flops 9663676416 | bytes 41943040 | tf_op jit(solution)/shard_map/pallas_call | solution.py:932
  391.1 23.1 %shard_map.265 = (bf16[4,4,128,2048]{3,2,1,0:T(8,128)(2,1)}, bf16[4,4,128,768]{3,2,1,0:T(8,128)(2,1)}, bf16[4,4,128,2048]{3,2,1,0:T(8,128)(2,1)}, bf16[4,4,128,7...) custom-call(s32[5]{0:T(128)} %stack.322.refs_0_, ...), custom_call_target="tpu_custom_call", output_to_operand_aliasing={{0}: (12, {}), {1}: (13, {}), {2}: (14, {}), {3}: (15, {}),... | custom-call | flops 9663676416 | bytes 41943040 | tf_op jit(solution)/shard_map/pallas_call | solution.py:932
  419.2 23.1 %shard_map.266 = (bf16[4,4,128,2048]{3,2,1,0:T(8,128)(2,1)}, bf16[4,4,128,768]{3,2,1,0:T(8,128)(2,1)}, bf16[4,4,128,2048]{3,2,1,0:T(8,128)(2,1)}, bf16[4,4,128,7...) custom-call(s32[5]{0:T(128)} %stack.324.refs_0_, ...), custom_call_target="tpu_custom_call", output_to_operand_aliasing={{0}: (12, {}), {1}: (13, {}), {2}: (14, {}), {3}: (15, {}),... | custom-call | flops 9663676416 | bytes 41943040 | tf_op jit(solution)/shard_map/pallas_call | solution.py:932
  451.3 23.2 %shard_map.267 = (bf16[4,4,128,2048]{3,2,1,0:T(8,128)(2,1)}, bf16[4,4,128,768]{3,2,1,0:T(8,128)(2,1)}, bf16[4,4,128,2048]{3,2,1,0:T(8,128)(2,1)}, bf16[4,4,128,7...) custom-call(s32[5]{0:T(128)} %stack.326.refs_0_, ...), custom_call_target="tpu_custom_call", output_to_operand_aliasing={{0}: (12, {}), {1}: (13, {}), {2}: (14, {}), {3}: (15, {}),... | custom-call | flops 9663676416 | bytes 41943040 | tf_op jit(solution)/shard_map/pallas_call | solution.py:932
  480.0 10.1 %fusion.103 = f32[768,2048]{1,0:T(8,128)S(1)} fusion(bf16[2048,768]{1,0:T(8,128)(2,1)S(1)} %bitcast.568, bf16[2048,2048]{1,0:T(8,128)(2,1)} %bitcast.563), kind=kOutput, calls=%fused_computation.382 | convolution fusion | flops 6442450944 | bytes 17825792 | tf_op jit(solution)/shard_map/sf,sd->fd/dot_general | solution.py:949
  492.4 8.4 collective-permute-done.60
  508.2 7.4 fusion.104
  518.9 9.3 %collective-permute-done.64 = bf16[96,2176]{1,0:T(8,128)(2,1)} collective-permute-done((bf16[96,2176]{1,0:T(8,128)(2,1)}, bf16[96,2176]{1,0:T(8,128)(2,1)}, u32[]{:S(2)}, u32[]{:S(2)}) %collective-permute-start.64) | collective-permute-done | bytes 417824 | tf_op jit(solution)/shard_map/ppermute | solution.py:499
  532.7 7.3 fusion.105
  541.7 9.3 %collective-permute-done.68 = bf16[192,2048]{1,0:T(8,128)(2,1)} collective-permute-done((bf16[192,2048]{1,0:T(8,128)(2,1)}, bf16[192,2048]{1,0:T(8,128)(2,1)}, u32[]{:S(2)}, u32[]{:S(2)}) %collective-permute-start.68) | collective-permute-done | bytes 786464 | tf_op jit(solution)/shard_map/ppermute | solution.py:503
  559.1 10.6 %collective-permute-done.71 = bf16[512,768]{1,0:T(8,128)(2,1)S(1)} collective-permute-done((bf16[512,768]{1,0:T(8,128)(2,1)S(1)}, bf16[512,768]{1,0:T(8,128)(2,1)S(1)}, u32[]{:S(2)}, u32[]{:S(2)}) %collective-permute-start.71) | collective-permute-done | bytes 786464 | tf_op jit(solution)/shard_map/ppermute | solution.py:503
  587.1 12.5 %collective-permute-done.76 = bf16[96,2048]{1,0:T(8,128)(2,1)S(1)} collective-permute-done((bf16[96,2048]{1,0:T(8,128)(2,1)S(1)}, bf16[96,2048]{1,0:T(8,128)(2,1)S(1)}, u32[]{:S(2)}, u32[]{:S(2)}) %collective-permute-start.76) | collective-permute-done | bytes 393248 | tf_op jit(solution)/shard_map/ppermute | solution.py:499
  613.1 4.6 convolution_convert_fusion.3
  617.7 12.6 %collective-permute-done.78 = bf16[192,2048]{1,0:T(8,128)(2,1)} collective-permute-done((bf16[192,2048]{1,0:T(8,128)(2,1)S(1)}, bf16[192,2048]{1,0:T(8,128)(2,1)}, u32[]{:S(2)}, u32[]{:S(2)}) %collective-permute-start.78) | collective-permute-done | bytes 786464 | tf_op jit(solution)/shard_map/ppermute | solution.py:503
  639.6 20.8 %shard_map.268 = (bf16[4,3,64,1024]{3,2,1,0:T(8,128)(2,1)S(1)}, f32[4,4,3,64,256]{4,3,2,1,0:T(8,128)S(1)}, f32[8,128]{1,0:T(8,128)S(1)}) custom-call(s32[2]{0:T(128)S(1)} %copy-done.14, f32[4,3,64,1024]{3,2,1,0:T(8,128)S(1)} %bitcast.549, bf16[4,3,64,1024]{3,2,1,0:T(8,128)(2,1)S(1)} %bitcast.554, bf16[4,4,3,64,256]{4,3,2,1,0:T(8,128)(2,1)S(1)} %copy-done.1, ...), custom_call_target="tpu_custom_call" | custom-call | flops 8053063680 | bytes 16777216 | tf_op jit(solution)/shard_map/pallas_call | solution.py:798
  660.5 11.9 %collective-permute-done.81 = f32[17,2048]{1,0:T(8,128)S(1)} collective-permute-done((f32[17,2048]{1,0:T(8,128)S(1)}, f32[17,2048]{1,0:T(8,128)S(1)}, u32[]{:S(2)}, u32[]{:S(2)}) %collective-permute-start.81) | collective-permute-done | bytes 139296 | tf_op jit(solution)/shard_map/ppermute | solution.py:503
  693.7 4.5 collective-permute-done.84
  698.3 17.0 %collective-permute-start.86 = (bf16[4,3,64,256]{3,2,1,0:T(8,128)(2,1)S(1)}, bf16[4,3,64,256]{3,2,1,0:T(8,128)(2,1)S(1)}, u32[]{:S(2)}, u32[]{:S(2)}) collective-permute-start(bf16[4,3,64,256]{3,2,1,0:T(8,128)(2,1)S(1)} %get-tuple-element.853), channel_id=1, source_target_pairs={{0,8},{8,16},{16,24},{24,0},{1,9},{9,17},{17,25},{25,1},{2,10},{10... | collective-permute-start | bytes 1179656 | tf_op jit(solution)/shard_map/ppermute | solution.py:499
  743.6 11.1 %collective-permute-done.95 = bf16[192,2048]{1,0:T(8,128)(2,1)} collective-permute-done((bf16[192,2048]{1,0:T(8,128)(2,1)}, bf16[192,2048]{1,0:T(8,128)(2,1)}, u32[]{:S(2)}, u32[]{:S(2)}) %collective-permute-start.95) | collective-permute-done | bytes 786464 | tf_op jit(solution)/shard_map/ppermute | solution.py:503
  756.6 8.2 collective-permute-done.91
  764.8 9.2 %collective-permute-done.90 = bf16[4,64,1024]{2,1,0:T(8,128)(2,1)S(1)} collective-permute-done((bf16[4,64,1024]{2,1,0:T(8,128)(2,1)}, bf16[4,64,1024]{2,1,0:T(8,128)(2,1)S(1)}, u32[]{:S(2)}, u32[]{:S(2)}) %collective-permute-start.90) | collective-permute-done | bytes 524320 | tf_op jit(solution)/shard_map/ppermute | solution.py:499
  777.0 3.8 collective-permute-start.97
  786.3 19.0 %collective-permute-done.100 = f32[18,128]{1,0:T(8,128)S(1)} collective-permute-done((f32[18,128]{1,0:T(8,128)S(1)}, f32[18,128]{1,0:T(8,128)S(1)}, u32[]{:S(2)}, u32[]{:S(2)}) %collective-permute-start.100) | collective-permute-done | bytes 9248 | tf_op jit(solution)/shard_map/ppermute | solution.py:503
  810.2 4.1 collective-permute-start.107
  814.4 15.4 %collective-permute-done.106 = bf16[4,64,256]{2,1,0:T(8,128)(2,1)S(1)} collective-permute-done((bf16[4,64,256]{2,1,0:T(8,128)(2,1)S(1)}, bf16[4,64,256]{2,1,0:T(8,128)(2,1)S(1)}, u32[]{:S(2)}, u32[]{:S(2)}) %collective-permute-start.106) | collective-permute-done | bytes 131104 | tf_op jit(solution)/shard_map/ppermute | solution.py:499
  829.9 10.8 %collective-permute-done.107 = bf16[4,64,256]{2,1,0:T(8,128)(2,1)S(1)} collective-permute-done((bf16[4,64,256]{2,1,0:T(8,128)(2,1)S(1)}, bf16[4,64,256]{2,1,0:T(8,128)(2,1)S(1)}, u32[]{:S(2)}, u32[]{:S(2)}) %collective-permute-start.107) | collective-permute-done | bytes 131104 | tf_op jit(solution)/shard_map/ppermute | solution.py:499
  844.0 8.4 collective-permute-done.103
  860.5 4.2 fusion.28
  864.8 16.8 %collective-permute-done.109 = bf16[128,2048]{1,0:T(8,128)(2,1)S(1)} collective-permute-done((bf16[128,2048]{1,0:T(8,128)(2,1)}, bf16[128,2048]{1,0:T(8,128)(2,1)S(1)}, u32[]{:S(2)}, u32[]{:S(2)}) %collective-permute-start.109) | collective-permute-done | bytes 524320 | tf_op jit(solution)/shard_map/ppermute | solution.py:499
  889.3 9.6 %collective-permute-done.116 = f32[290,128]{1,0:T(8,128)S(1)} collective-permute-done((f32[290,128]{1,0:T(8,128)S(1)}, f32[290,128]{1,0:T(8,128)S(1)}, u32[]{:S(2)}, u32[]{:S(2)}) %collective-permute-start.116) | collective-permute-done | bytes 148512 | tf_op jit(solution)/shard_map/ppermute | solution.py:499
  898.9 4.9 collective-permute-done.117
  (806 shorter events, 323.0 us)
Async XLA Ops:
  7.2 357.4 %all-gather.2.cloned.1.call-start = ((), (), s32[]{:S(2)}) async-start(), calls=%async_computation | async-start | bytes 13369344 | tf_op jit(solution)/shard_map/all_gather | solution.py:1140
  70.9 31.5 %collective-permute-start.16 = (bf16[192,2048]{1,0:T(8,128)(2,1)S(1)}, bf16[192,2048]{1,0:T(8,128)(2,1)S(1)}, u32[]{:S(2)}, u32[]{:S(2)}) collective-permute-start(bf16[192,2048]{1,0:T(8,128)(2,1)S(1)} %collective-permute-done.11), channel_id=1, source_target_pairs={{0,2},{2,0},{1,3},{3,1},{4,6},{6,4},{5,7},{7,5},{8,10},{10,8},{9,1... | collective-permute-start | bytes 2359304 | tf_op jit(solution)/shard_map/ppermute | solution.py:503
  70.9 31.3 %collective-permute-start.14 = (bf16[4,64,1280]{2,1,0:T(8,128)(2,1)S(1)}, bf16[4,64,1280]{2,1,0:T(8,128)(2,1)S(1)}, u32[]{:S(2)}, u32[]{:S(2)}) collective-permute-start(bf16[4,64,1280]{2,1,0:T(8,128)(2,1)S(1)} %pad_maximum_fusion.10), channel_id=1, source_target_pairs={{0,16},{8,24},{16,0},{24,8},{1,17},{9,25},{17,1},{25,9},{2,18},{10... | collective-permute-start | bytes 1966088 | tf_op jit(solution)/shard_map/ppermute | solution.py:499
  70.9 31.3 %collective-permute-start.15 = (bf16[4,64,1280]{2,1,0:T(8,128)(2,1)}, bf16[4,64,1280]{2,1,0:T(8,128)(2,1)S(1)}, u32[]{:S(2)}, u32[]{:S(2)}) collective-permute-start(bf16[4,64,1280]{2,1,0:T(8,128)(2,1)} %collective-permute-done.9), channel_id=1, source_target_pairs={{0,1},{1,0},{2,3},{3,2},{4,5},{5,4},{6,7},{7,6},{8,9},{9,8},{10,11... | collective-permute-start | bytes 1966088 | tf_op jit(solution)/shard_map/ppermute | solution.py:503
  72.1 29.5 %collective-permute-start.18 = (bf16[128,2048]{1,0:T(8,128)(2,1)S(1)}, bf16[128,2048]{1,0:T(8,128)(2,1)S(1)}, u32[]{:S(2)}, u32[]{:S(2)}) collective-permute-start(bf16[128,2048]{1,0:T(8,128)(2,1)S(1)} %copy-done.109), channel_id=1, source_target_pairs={{0,1},{1,0},{2,3},{3,2},{4,5},{5,4},{6,7},{7,6},{8,9},{9,8},{10,11... | collective-permute-start | bytes 1572872 | tf_op jit(solution)/shard_map/ppermute | solution.py:503
  73.0 28.6 %collective-permute-start.17 = (bf16[4,2,2,20,128]{4,3,2,1,0:T(8,128)(2,1)S(1)}, bf16[4,2,2,20,128]{4,3,2,1,0:T(8,128)(2,1)S(1)}, u32[]{:S(2)}, u32[]{:S(2)}) collective-permute-start(bf16[4,2,2,20,128]{4,3,2,1,0:T(8,128)(2,1)S(1)} %get-tuple-element.539), channel_id=1, source_target_pairs={{0,1},{1,0},{2,3},{3,2},{4,5},{5,4},{6,7},{7,6},{8,9},{9,8},{10,11... | collective-permute-start | bytes 245768 | tf_op jit(solution)/shard_map/ppermute | solution.py:503
  153.9 25.4 %collective-permute-start.27 = (bf16[2,128,2048]{2,1,0:T(8,128)(2,1)S(1)}, bf16[2,128,2048]{2,1,0:T(8,128)(2,1)}, u32[]{:S(2)}, u32[]{:S(2)}) collective-permute-start(bf16[2,128,2048]{2,1,0:T(8,128)(2,1)S(1)} %pad_maximum_fusion.5), channel_id=1, source_target_pairs={{0,4},{4,0},{1,5},{5,1},{2,6},{6,2},{3,7},{7,3},{8,12},{12,8},{9,1... | collective-permute-start | bytes 3145736 | tf_op jit(solution)/shard_map/ppermute | solution.py:503
  188.4 41.4 %collective-permute-start.30 = (bf16[2,128,2048]{2,1,0:T(8,128)(2,1)}, bf16[2,128,2048]{2,1,0:T(8,128)(2,1)}, u32[]{:S(2)}, u32[]{:S(2)}) collective-permute-start(bf16[2,128,2048]{2,1,0:T(8,128)(2,1)} %pad_maximum_fusion.6), channel_id=1, source_target_pairs={{0,2},{2,0},{1,3},{3,1},{4,6},{6,4},{5,7},{7,5},{8,10},{10,8},{9,1... | collective-permute-start | bytes 3145736 | tf_op jit(solution)/shard_map/ppermute | solution.py:503
  188.5 41.4 %collective-permute-start.31 = (bf16[2,128,2048]{2,1,0:T(8,128)(2,1)}, bf16[2,128,2048]{2,1,0:T(8,128)(2,1)}, u32[]{:S(2)}, u32[]{:S(2)}) collective-permute-start(bf16[2,128,2048]{2,1,0:T(8,128)(2,1)} %pad_maximum_fusion.7), channel_id=1, source_target_pairs={{0,1},{1,0},{2,3},{3,2},{4,5},{5,4},{6,7},{7,6},{8,9},{9,8},{10,11... | collective-permute-start | bytes 3145736 | tf_op jit(solution)/shard_map/ppermute | solution.py:503
  190.5 39.3 %collective-permute-start.29 = (bf16[4,3,64,256]{3,2,1,0:T(8,128)(2,1)S(1)}, bf16[4,3,64,256]{3,2,1,0:T(8,128)(2,1)}, u32[]{:S(2)}, u32[]{:S(2)}) collective-permute-start(bf16[4,3,64,256]{3,2,1,0:T(8,128)(2,1)S(1)} %pad_maximum_fusion.11), channel_id=1, source_target_pairs={{0,16},{8,24},{16,0},{24,8},{1,17},{9,25},{17,1},{25,9},{2,18},{10... | collective-permute-start | bytes 1179656 | tf_op jit(solution)/shard_map/ppermute | solution.py:499
  231.3 25.1 %collective-permute-start.32 = (bf16[2,128,2048]{2,1,0:T(8,128)(2,1)}, bf16[2,128,2048]{2,1,0:T(8,128)(2,1)S(1)}, u32[]{:S(2)}, u32[]{:S(2)}) collective-permute-start(bf16[2,128,2048]{2,1,0:T(8,128)(2,1)} %collective-permute-done.30), channel_id=1, source_target_pairs={{0,1},{1,0},{2,3},{3,2},{4,5},{5,4},{6,7},{7,6},{8,9},{9,8},{10,11... | collective-permute-start | bytes 3145736 | tf_op jit(solution)/shard_map/ppermute | solution.py:503
  292.8 47.5 %collective-permute-start.39 = (bf16[1024,768]{1,0:T(8,128)(2,1)}, bf16[1024,768]{1,0:T(8,128)(2,1)}, u32[]{:S(2)}, u32[]{:S(2)}) collective-permute-start(bf16[1024,768]{1,0:T(8,128)(2,1)} %bitcast.89), channel_id=1, source_target_pairs={{0,1},{1,0},{2,3},{3,2},{4,5},{5,4},{6,7},{7,6},{8,9},{9,8},{10,11... | collective-permute-start | bytes 4718600 | tf_op jit(solution)/shard_map/ppermute | solution.py:503
  303.2 37.1 %collective-permute-start.36 = (bf16[192,2048]{1,0:T(8,128)(2,1)}, bf16[192,2048]{1,0:T(8,128)(2,1)}, u32[]{:S(2)}, u32[]{:S(2)}) collective-permute-start(bf16[192,2048]{1,0:T(8,128)(2,1)} %multiply_convert_fusion.refs_1_), channel_id=1, source_target_pairs={{0,16},{8,24},{16,0},{24,8},{1,17},{9,25},{17,1},{25,9},{2,18},{10... | collective-permute-start | bytes 2359304 | tf_op jit(solution)/shard_map/ppermute | solution.py:499
  305.7 34.6 %collective-permute-start.37 = (bf16[192,2048]{1,0:T(8,128)(2,1)}, bf16[192,2048]{1,0:T(8,128)(2,1)}, u32[]{:S(2)}, u32[]{:S(2)}) collective-permute-start(bf16[192,2048]{1,0:T(8,128)(2,1)} %multiply_convert_fusion.refs_1_), channel_id=1, source_target_pairs={{0,4},{4,0},{1,5},{5,1},{2,6},{6,2},{3,7},{7,3},{8,12},{12,8},{9,1... | collective-permute-start | bytes 2359304 | tf_op jit(solution)/shard_map/ppermute | solution.py:503
  306.3 34.0 %collective-permute-start.38 = (bf16[192,2048]{1,0:T(8,128)(2,1)}, bf16[192,2048]{1,0:T(8,128)(2,1)}, u32[]{:S(2)}, u32[]{:S(2)}) collective-permute-start(bf16[192,2048]{1,0:T(8,128)(2,1)} %multiply_convert_fusion.refs_1_), channel_id=1, source_target_pairs={{0,2},{2,0},{1,3},{3,1},{4,6},{6,4},{5,7},{7,5},{8,10},{10,8},{9,1... | collective-permute-start | bytes 2359304 | tf_op jit(solution)/shard_map/ppermute | solution.py:503
  361.7 26.2 %collective-permute-start.44 = (bf16[192,2048]{1,0:T(8,128)(2,1)}, bf16[192,2048]{1,0:T(8,128)(2,1)}, u32[]{:S(2)}, u32[]{:S(2)}) collective-permute-start(bf16[192,2048]{1,0:T(8,128)(2,1)} %multiply_convert_fusion.refs_1_), channel_id=1, source_target_pairs={{0,24},{8,0},{16,8},{24,16},{1,25},{9,1},{17,9},{25,17},{2,26},{10... | collective-permute-start | bytes 2359304 | tf_op jit(solution)/shard_map/ppermute | solution.py:499
  363.5 24.4 %collective-permute-start.45 = (bf16[192,2048]{1,0:T(8,128)(2,1)}, bf16[192,2048]{1,0:T(8,128)(2,1)}, u32[]{:S(2)}, u32[]{:S(2)}) collective-permute-start(bf16[192,2048]{1,0:T(8,128)(2,1)} %collective-permute-done.40.refs_1_), channel_id=1, source_target_pairs={{0,4},{4,0},{1,5},{5,1},{2,6},{6,2},{3,7},{7,3},{8,12},{12,8},{9,1... | collective-permute-start | bytes 2359304 | tf_op jit(solution)/shard_map/ppermute | solution.py:503
  364.1 23.9 %collective-permute-start.46 = (bf16[192,2048]{1,0:T(8,128)(2,1)}, bf16[192,2048]{1,0:T(8,128)(2,1)}, u32[]{:S(2)}, u32[]{:S(2)}) collective-permute-start(bf16[192,2048]{1,0:T(8,128)(2,1)} %collective-permute-done.41.refs_3_), channel_id=1, source_target_pairs={{0,2},{2,0},{1,3},{3,1},{4,6},{6,4},{5,7},{7,5},{8,10},{10,8},{9,1... | collective-permute-start | bytes 2359304 | tf_op jit(solution)/shard_map/ppermute | solution.py:503
  364.1 23.9 %collective-permute-start.47 = (bf16[192,2048]{1,0:T(8,128)(2,1)}, bf16[192,2048]{1,0:T(8,128)(2,1)}, u32[]{:S(2)}, u32[]{:S(2)}) collective-permute-start(bf16[192,2048]{1,0:T(8,128)(2,1)} %collective-permute-done.40.refs_1_), channel_id=1, source_target_pairs={{0,2},{2,0},{1,3},{3,1},{4,6},{6,4},{5,7},{7,5},{8,10},{10,8},{9,1... | collective-permute-start | bytes 2359304 | tf_op jit(solution)/shard_map/ppermute | solution.py:503
  388.0 26.3 %collective-permute-start.51 = (bf16[2,192,2176]{2,1,0:T(8,128)(2,1)}, bf16[2,192,2176]{2,1,0:T(8,128)(2,1)}, u32[]{:S(2)}, u32[]{:S(2)}) collective-permute-start(bf16[2,192,2176]{2,1,0:T(8,128)(2,1)} %get-tuple-element.655), channel_id=1, source_target_pairs={{0,2},{2,0},{1,3},{3,1},{4,6},{6,4},{5,7},{7,5},{8,10},{10,8},{9,1... | collective-permute-start | bytes 5013512 | tf_op jit(solution)/shard_map/ppermute | solution.py:503
  388.0 26.2 %collective-permute-start.52 = (bf16[2,192,2048]{2,1,0:T(8,128)(2,1)}, bf16[2,192,2048]{2,1,0:T(8,128)(2,1)}, u32[]{:S(2)}, u32[]{:S(2)}) collective-permute-start(bf16[2,192,2048]{2,1,0:T(8,128)(2,1)} %get-tuple-element.656), channel_id=1, source_target_pairs={{0,2},{2,0},{1,3},{3,1},{4,6},{6,4},{5,7},{7,5},{8,10},{10,8},{9,1... | collective-permute-start | bytes 4718600 | tf_op jit(solution)/shard_map/ppermute | solution.py:503
  389.1 25.1 %collective-permute-start.48 = (bf16[192,2048]{1,0:T(8,128)(2,1)}, bf16[192,2048]{1,0:T(8,128)(2,1)S(1)}, u32[]{:S(2)}, u32[]{:S(2)}) collective-permute-start(bf16[192,2048]{1,0:T(8,128)(2,1)} %collective-permute-done.44.refs_1_), channel_id=1, source_target_pairs={{0,4},{4,0},{1,5},{5,1},{2,6},{6,2},{3,7},{7,3},{8,12},{12,8},{9,1... | collective-permute-start | bytes 2359304 | tf_op jit(solution)/shard_map/ppermute | solution.py:503
  416.8 25.6 %collective-permute-start.54 = (bf16[2,192,2176]{2,1,0:T(8,128)(2,1)}, bf16[2,192,2176]{2,1,0:T(8,128)(2,1)}, u32[]{:S(2)}, u32[]{:S(2)}) collective-permute-start(bf16[2,192,2176]{2,1,0:T(8,128)(2,1)} %get-tuple-element.691), channel_id=1, source_target_pairs={{0,2},{2,0},{1,3},{3,1},{4,6},{6,4},{5,7},{7,5},{8,10},{10,8},{9,1... | collective-permute-start | bytes 5013512 | tf_op jit(solution)/shard_map/ppermute | solution.py:503
  416.8 25.6 %collective-permute-start.55 = (bf16[2,192,2048]{2,1,0:T(8,128)(2,1)}, bf16[2,192,2048]{2,1,0:T(8,128)(2,1)}, u32[]{:S(2)}, u32[]{:S(2)}) collective-permute-start(bf16[2,192,2048]{2,1,0:T(8,128)(2,1)} %get-tuple-element.692), channel_id=1, source_target_pairs={{0,2},{2,0},{1,3},{3,1},{4,6},{6,4},{5,7},{7,5},{8,10},{10,8},{9,1... | collective-permute-start | bytes 4718600 | tf_op jit(solution)/shard_map/ppermute | solution.py:503
  418.6 23.7 %collective-permute-start.56 = (bf16[192,2176]{1,0:T(8,128)(2,1)}, bf16[192,2176]{1,0:T(8,128)(2,1)S(1)}, u32[]{:S(2)}, u32[]{:S(2)}) collective-permute-start(bf16[192,2176]{1,0:T(8,128)(2,1)} %fusion.39), channel_id=1, source_target_pairs={{0,4},{4,0},{1,5},{5,1},{2,6},{6,2},{3,7},{7,3},{8,12},{12,8},{9,1... | collective-permute-start | bytes 2506760 | tf_op jit(solution)/shard_map/ppermute | solution.py:503
  444.9 29.7 %collective-permute-start.57 = (bf16[2,192,2176]{2,1,0:T(8,128)(2,1)}, bf16[2,192,2176]{2,1,0:T(8,128)(2,1)}, u32[]{:S(2)}, u32[]{:S(2)}) collective-permute-start(bf16[2,192,2176]{2,1,0:T(8,128)(2,1)} %get-tuple-element.726), channel_id=1, source_target_pairs={{0,2},{2,0},{1,3},{3,1},{4,6},{6,4},{5,7},{7,5},{8,10},{10,8},{9,1... | collective-permute-start | bytes 5013512 | tf_op jit(solution)/shard_map/ppermute | solution.py:503
  445.4 29.1 %collective-permute-start.58 = (bf16[2,192,2048]{2,1,0:T(8,128)(2,1)}, bf16[2,192,2048]{2,1,0:T(8,128)(2,1)}, u32[]{:S(2)}, u32[]{:S(2)}) collective-permute-start(bf16[2,192,2048]{2,1,0:T(8,128)(2,1)} %get-tuple-element.727), channel_id=1, source_target_pairs={{0,2},{2,0},{1,3},{3,1},{4,6},{6,4},{5,7},{7,5},{8,10},{10,8},{9,1... | collective-permute-start | bytes 4718600 | tf_op jit(solution)/shard_map/ppermute | solution.py:503
  447.2 27.4 %collective-permute-start.59 = (bf16[192,2176]{1,0:T(8,128)(2,1)}, bf16[192,2176]{1,0:T(8,128)(2,1)S(1)}, u32[]{:S(2)}, u32[]{:S(2)}) collective-permute-start(bf16[192,2176]{1,0:T(8,128)(2,1)} %fusion.40), channel_id=1, source_target_pairs={{0,4},{4,0},{1,5},{5,1},{2,6},{6,2},{3,7},{7,3},{8,12},{12,8},{9,1... | collective-permute-start | bytes 2506760 | tf_op jit(solution)/shard_map/ppermute | solution.py:503
  632.3 40.1 %collective-permute-start.80 = (bf16[3,128,2048]{2,1,0:T(8,128)(2,1)}, bf16[3,128,2048]{2,1,0:T(8,128)(2,1)}, u32[]{:S(2)}, u32[]{:S(2)}) collective-permute-start(bf16[3,128,2048]{2,1,0:T(8,128)(2,1)} %dynamic-slice_bitcast_fusion), channel_id=1, source_target_pairs={{0,1},{1,0},{2,3},{3,2},{4,5},{5,4},{6,7},{7,6},{8,9},{9,8},{10,11... | collective-permute-start | bytes 4718600 | tf_op jit(solution)/shard_map/ppermute | solution.py:503
  633.7 38.7 %collective-permute-start.82 = (bf16[192,2048]{1,0:T(8,128)(2,1)}, bf16[192,2048]{1,0:T(8,128)(2,1)S(1)}, u32[]{:S(2)}, u32[]{:S(2)}) collective-permute-start(bf16[192,2048]{1,0:T(8,128)(2,1)} %fusion.30), channel_id=1, source_target_pairs={{0,24},{8,0},{16,8},{24,16},{1,25},{9,1},{17,9},{25,17},{2,26},{10... | collective-permute-start | bytes 2359304 | tf_op jit(solution)/shard_map/ppermute | solution.py:499
  638.8 33.6 %collective-permute-start.83 = (bf16[96,2048]{1,0:T(8,128)(2,1)S(1)}, bf16[96,2048]{1,0:T(8,128)(2,1)S(1)}, u32[]{:S(2)}, u32[]{:S(2)}) collective-permute-start(bf16[96,2048]{1,0:T(8,128)(2,1)S(1)} %copy-done.124), channel_id=1, source_target_pairs={{0,16},{8,24},{16,0},{24,8},{1,17},{9,25},{17,1},{25,9},{2,18},{10... | collective-permute-start | bytes 1179656 | tf_op jit(solution)/shard_map/ppermute | solution.py:499
  638.9 33.5 %collective-permute-start.81 = (f32[17,2048]{1,0:T(8,128)S(1)}, f32[17,2048]{1,0:T(8,128)S(1)}, u32[]{:S(2)}, u32[]{:S(2)}) collective-permute-start(f32[17,2048]{1,0:T(8,128)S(1)} %pad_maximum_fusion.20), channel_id=1, source_target_pairs={{0,1},{1,0},{2,3},{3,2},{4,5},{5,4},{6,7},{7,6},{8,9},{9,8},{10,11... | collective-permute-start | bytes 417800 | tf_op jit(solution)/shard_map/ppermute | solution.py:503
  683.3 37.2 %collective-permute-start.89 = (bf16[2,128,2048]{2,1,0:T(8,128)(2,1)S(1)}, bf16[2,128,2048]{2,1,0:T(8,128)(2,1)S(1)}, u32[]{:S(2)}, u32[]{:S(2)}) collective-permute-start(bf16[2,128,2048]{2,1,0:T(8,128)(2,1)S(1)} %add_convert_fusion.1), channel_id=1, source_target_pairs={{0,4},{4,0},{1,5},{5,1},{2,6},{6,2},{3,7},{7,3},{8,12},{12,8},{9,1... | collective-permute-start | bytes 3145736 | tf_op jit(solution)/shard_map/ppermute | solution.py:503
  684.0 36.5 %collective-permute-start.87 = (bf16[4,64,1024]{2,1,0:T(8,128)(2,1)S(1)}, bf16[4,64,1024]{2,1,0:T(8,128)(2,1)S(1)}, u32[]{:S(2)}, u32[]{:S(2)}) collective-permute-start(bf16[4,64,1024]{2,1,0:T(8,128)(2,1)S(1)} %get-tuple-element.854), channel_id=1, source_target_pairs={{0,1},{1,0},{2,3},{3,2},{4,5},{5,4},{6,7},{7,6},{8,9},{9,8},{10,11... | collective-permute-start | bytes 1572872 | tf_op jit(solution)/shard_map/ppermute | solution.py:503
  685.4 35.2 %collective-permute-start.88 = (bf16[1,128,2048]{2,1,0:T(8,128)(2,1)S(1)}, bf16[1,128,2048]{2,1,0:T(8,128)(2,1)S(1)}, u32[]{:S(2)}, u32[]{:S(2)}) collective-permute-start(bf16[1,128,2048]{2,1,0:T(8,128)(2,1)S(1)} %copy-done.107), channel_id=1, source_target_pairs={{0,1},{1,0},{2,3},{3,2},{4,5},{5,4},{6,7},{7,6},{8,9},{9,8},{10,11... | collective-permute-start | bytes 1572872 | tf_op jit(solution)/shard_map/ppermute | solution.py:503
  688.7 31.0 %collective-permute-start.85 = (bf16[4,3,64,256]{3,2,1,0:T(8,128)(2,1)S(1)}, bf16[4,3,64,256]{3,2,1,0:T(8,128)(2,1)S(1)}, u32[]{:S(2)}, u32[]{:S(2)}) collective-permute-start(bf16[4,3,64,256]{3,2,1,0:T(8,128)(2,1)S(1)} %get-tuple-element.852), channel_id=1, source_target_pairs={{0,16},{8,24},{16,0},{24,8},{1,17},{9,25},{17,1},{25,9},{2,18},{10... | collective-permute-start | bytes 1179656 | tf_op jit(solution)/shard_map/ppermute | solution.py:499
  737.5 36.5 %collective-permute-start.92 = (bf16[2,4,64,1024]{3,2,1,0:T(8,128)(2,1)}, bf16[2,4,64,1024]{3,2,1,0:T(8,128)(2,1)S(1)}, u32[]{:S(2)}, u32[]{:S(2)}) collective-permute-start(bf16[2,4,64,1024]{3,2,1,0:T(8,128)(2,1)} %pad_maximum_fusion.8), channel_id=1, source_target_pairs={{0,1},{1,0},{2,3},{3,2},{4,5},{5,4},{6,7},{7,6},{8,9},{9,8},{10,11... | collective-permute-start | bytes 3145736 | tf_op jit(solution)/shard_map/ppermute | solution.py:503
  738.9 35.1 %collective-permute-start.93 = (bf16[2,128,2048]{2,1,0:T(8,128)(2,1)}, bf16[2,128,2048]{2,1,0:T(8,128)(2,1)S(1)}, u32[]{:S(2)}, u32[]{:S(2)}) collective-permute-start(bf16[2,128,2048]{2,1,0:T(8,128)(2,1)} %pad_maximum_fusion.9), channel_id=1, source_target_pairs={{0,2},{2,0},{1,3},{3,1},{4,6},{6,4},{5,7},{7,5},{8,10},{10,8},{9,1... | collective-permute-start | bytes 3145736 | tf_op jit(solution)/shard_map/ppermute | solution.py:503
  738.9 35.1 %collective-permute-start.90 = (bf16[4,64,1024]{2,1,0:T(8,128)(2,1)}, bf16[4,64,1024]{2,1,0:T(8,128)(2,1)S(1)}, u32[]{:S(2)}, u32[]{:S(2)}) collective-permute-start(bf16[4,64,1024]{2,1,0:T(8,128)(2,1)} %fusion.38), channel_id=1, source_target_pairs={{0,16},{8,24},{16,0},{24,8},{1,17},{9,25},{17,1},{25,9},{2,18},{10... | collective-permute-start | bytes 1572872 | tf_op jit(solution)/shard_map/ppermute | solution.py:499
  741.0 23.8 %collective-permute-start.91 = (bf16[96,2048]{1,0:T(8,128)(2,1)}, bf16[96,2048]{1,0:T(8,128)(2,1)S(1)}, u32[]{:S(2)}, u32[]{:S(2)}) collective-permute-start(bf16[96,2048]{1,0:T(8,128)(2,1)} %get-tuple-element.875), channel_id=1, source_target_pairs={{0,8},{8,16},{16,24},{24,0},{1,9},{9,17},{17,25},{25,1},{2,10},{10... | collective-permute-start | bytes 1179656 | tf_op jit(solution)/shard_map/ppermute | solution.py:499
  776.9 28.4 %collective-permute-start.96 = (bf16[4,64,1024]{2,1,0:T(8,128)(2,1)S(1)}, bf16[4,64,1024]{2,1,0:T(8,128)(2,1)S(1)}, u32[]{:S(2)}, u32[]{:S(2)}) collective-permute-start(bf16[4,64,1024]{2,1,0:T(8,128)(2,1)S(1)} %get-tuple-element.894), channel_id=1, source_target_pairs={{0,8},{8,16},{16,24},{24,0},{1,9},{9,17},{17,25},{25,1},{2,10},{10... | collective-permute-start | bytes 1572872 | tf_op jit(solution)/shard_map/ppermute | solution.py:499
  777.0 28.3 %collective-permute-start.97 = (bf16[4,64,1024]{2,1,0:T(8,128)(2,1)S(1)}, bf16[4,64,1024]{2,1,0:T(8,128)(2,1)S(1)}, u32[]{:S(2)}, u32[]{:S(2)}) collective-permute-start(bf16[4,64,1024]{2,1,0:T(8,128)(2,1)S(1)} %get-tuple-element.895), channel_id=1, source_target_pairs={{0,24},{8,0},{16,8},{24,16},{1,25},{9,1},{17,9},{25,17},{2,26},{10... | collective-permute-start | bytes 1572872 | tf_op jit(solution)/shard_map/ppermute | solution.py:499
  780.8 24.5 %collective-permute-start.98 = (bf16[4,64,1024]{2,1,0:T(8,128)(2,1)S(1)}, bf16[4,64,1024]{2,1,0:T(8,128)(2,1)S(1)}, u32[]{:S(2)}, u32[]{:S(2)}) collective-permute-start(bf16[4,64,1024]{2,1,0:T(8,128)(2,1)S(1)} %copy-done.116), channel_id=1, source_target_pairs={{0,1},{1,0},{2,3},{3,2},{4,5},{5,4},{6,7},{7,6},{8,9},{9,8},{10,11... | collective-permute-start | bytes 1572872 | tf_op jit(solution)/shard_map/ppermute | solution.py:503
  781.5 23.8 %collective-permute-start.99 = (bf16[4,4,64,256]{3,2,1,0:T(8,128)(2,1)S(1)}, bf16[4,4,64,256]{3,2,1,0:T(8,128)(2,1)S(1)}, u32[]{:S(2)}, u32[]{:S(2)}) collective-permute-start(bf16[4,4,64,256]{3,2,1,0:T(8,128)(2,1)S(1)} %get-tuple-element.897), channel_id=1, source_target_pairs={{0,1},{1,0},{2,3},{3,2},{4,5},{5,4},{6,7},{7,6},{8,9},{9,8},{10,11... | collective-permute-start | bytes 1572872 | tf_op jit(solution)/shard_map/ppermute | solution.py:503
  809.2 43.2 %collective-permute-start.104 = (bf16[192,2048]{1,0:T(8,128)(2,1)}, bf16[192,2048]{1,0:T(8,128)(2,1)}, u32[]{:S(2)}, u32[]{:S(2)}) collective-permute-start(bf16[192,2048]{1,0:T(8,128)(2,1)} %fusion.46), channel_id=1, source_target_pairs={{0,4},{4,0},{1,5},{5,1},{2,6},{6,2},{3,7},{7,3},{8,12},{12,8},{9,1... | collective-permute-start | bytes 2359304 | tf_op jit(solution)/shard_map/ppermute | solution.py:503
  809.9 42.5 %collective-permute-start.101 = (bf16[128,2048]{1,0:T(8,128)(2,1)}, bf16[128,2048]{1,0:T(8,128)(2,1)S(1)}, u32[]{:S(2)}, u32[]{:S(2)}) collective-permute-start(bf16[128,2048]{1,0:T(8,128)(2,1)} %get-tuple-element.917), channel_id=1, source_target_pairs={{0,8},{8,16},{16,24},{24,0},{1,9},{9,17},{17,25},{25,1},{2,10},{10... | collective-permute-start | bytes 1572872 | tf_op jit(solution)/shard_map/ppermute | solution.py:499
  810.2 30.5 %collective-permute-start.107 = (bf16[4,64,256]{2,1,0:T(8,128)(2,1)S(1)}, bf16[4,64,256]{2,1,0:T(8,128)(2,1)S(1)}, u32[]{:S(2)}, u32[]{:S(2)}) collective-permute-start(bf16[4,64,256]{2,1,0:T(8,128)(2,1)S(1)} %get-tuple-element.923), channel_id=1, source_target_pairs={{0,16},{8,24},{16,0},{24,8},{1,17},{9,25},{17,1},{25,9},{2,18},{10... | collective-permute-start | bytes 393224 | tf_op jit(solution)/shard_map/ppermute | solution.py:499
  814.3 38.1 %collective-permute-start.105 = (bf16[96,2048]{1,0:T(8,128)(2,1)}, bf16[96,2048]{1,0:T(8,128)(2,1)}, u32[]{:S(2)}, u32[]{:S(2)}) collective-permute-start(bf16[96,2048]{1,0:T(8,128)(2,1)} %get-tuple-element.921), channel_id=1, source_target_pairs={{0,8},{8,16},{16,24},{24,0},{1,9},{9,17},{17,25},{25,1},{2,10},{10... | collective-permute-start | bytes 1179656 | tf_op jit(solution)/shard_map/ppermute | solution.py:499
  (243 other events, 3035.2 us)
Sparse Core Ops, SparseCore 0:
  179.4 120.5 all-gather.1

commit v3 on v2

--- a/solution.py
+++ b/solution.py
@@ -523,16 +523,6 @@
         moved, done, join, mark = lax.optimization_barrier((moved, done, tuple(join), mark))
         self.mark = jax.tree.leaves((moved, done, join))[0]
         return moved, done, join
-
-    def start(self, block, axis):
-        return swap(after(block, self.mark), axis)
-
-
-def scatter_members(parts):
-    low, wide = jnp.bfloat16, jnp.float32
-    near = swap(parts[1].astype(low), "c")
-    far = swap((parts[0, 1] + near[1].astype(wide)).astype(low), "y")
-    return parts[0, 0] + near[0].astype(wide) + far.astype(wide)
 
 
 def pick(stack, index):
@@ -820,8 +810,8 @@
 
 
 def expert_kernel(*refs):
-    scalars_ref, x_refs = refs[0], refs[1:5]
-    c_ref, rank_ref, chosen_ref, router_ref, gate_ref, up_ref, down_ref = refs[5:12]
+    scalars_ref, x_refs, c_refs = refs[0], refs[1:5], refs[5:9]
+    rank_ref, chosen_ref, router_ref, gate_ref, up_ref, down_ref = refs[9:15]
     rows_ref, hidden_ref, dresults_ref, dgate_ref, dup_ref = refs[-9:-4]
     sent_refs, back_refs = refs[-4:-2], refs[-2:]
     low, wide = jnp.bfloat16, jnp.float32
@@ -832,7 +822,7 @@
     experts_all = router_ref.shape[0]
     across = (((1,), (1,)), ((), ()))
     down = (((0,), (0,)), ((), ()))
-    own_expert = scalars_ref[3]
+    own_expert = scalars_ref[0]
     places, picked, upstream, gates = [], [], [], []
     for block in range(blocks):
         rows = jnp.where(opening, x_refs[block][...], x_refs[2 + block][...])
@@ -849,7 +839,7 @@
         place = place.astype(low)
         places.append(place)
         picked.append(jnp.dot(place, rows, preferred_element_type=wide).astype(low))
-        cotangent = c_ref[0, block ^ scalars_ref[2]]
+        cotangent = jnp.where(opening, c_refs[block][...], c_refs[2 + block][...])
         upstream.append(jnp.dot(place, cotangent, preferred_element_type=wide))
     rows = jnp.concatenate(picked, 0)
     upstream = jnp.concatenate(upstream, 0)
@@ -893,9 +883,9 @@
         dup_ref[0, block] = dup_low[part]
 
 
-def experts(scalars, x_blocks, cotangents, ranks, chosen, router, gate, up, down, slots, earlier):
+def experts(scalars, x_blocks, c_blocks, ranks, chosen, router, gate, up, down, slots, earlier):
     tokens, model = x_blocks[0].shape
-    nz, members = cotangents.shape[:2]
+    nz, members = ranks.shape[:2]
     hidden = gate.shape[1]
     low = jnp.bfloat16
     pair = members // 2
@@ -903,13 +893,10 @@
     whole = lambda array: pl.BlockSpec(
         array.shape, lambda a, s: (0, 0), pipeline_mode=pl.Buffered(1)
     )
-    by_plane = pl.BlockSpec(
-        (1, pair, tokens, model), lambda a, s: (s[0], a ^ s[1], 0, 0)
-    )
-    turn = lambda *tail: pl.BlockSpec((1, pair) + tail, lambda a, s: (s[4], a, 0, 0))
+    turn = lambda *tail: pl.BlockSpec((1, pair) + tail, lambda a, s: (s[1], a, 0, 0))
     in_specs = [
         *[whole(block) for block in x_blocks],
-        by_plane,
+        *[whole(block) for block in c_blocks],
         turn(1, tokens),
         turn(experts_all, tokens),
         whole(router),
@@ -928,7 +915,7 @@
     aliases = {}
     if earlier:
         in_specs = in_specs + [pl.BlockSpec(memory_space=pl.ANY)] * len(earlier)
-        aliases = {12 + i: i for i in range(len(earlier))}
+        aliases = {15 + i: i for i in range(len(earlier))}
     return pl.pallas_call(
         expert_kernel,
         grid_spec=pltpu.PrefetchScalarGridSpec(
@@ -942,7 +929,7 @@
             bytes_accessed=40 * 2**20,
             transcendentals=2 * members * slots * hidden,
         ),
-    )(scalars, *x_blocks, cotangents, ranks, chosen, router, gate, up, down, *earlier)
+    )(scalars, *x_blocks, *c_blocks, ranks, chosen, router, gate, up, down, *earlier)
 
 
 def dot32(subscripts, left, right):
@@ -994,6 +981,49 @@
     query_width = groups * HEAD_SIZE
     third = w_down.shape[1] // 3
 
+    def make_tables(zi, token_members):
+        own_pos = jax.vmap(lambda device: shard_positions(device, context_count, block_len))(
+            zi * MEMBERS + token_members
+        )
+        cosine, sine_tab = rotary(own_pos.reshape(-1), HEAD_SIZE)
+        row_cosine = cosine.reshape(MEMBERS, 1, paired, HEAD_SIZE)
+        row_sine = sine_tab.reshape(MEMBERS, 1, paired, HEAD_SIZE)
+
+        def halves(table):
+            table = table.reshape(MEMBERS, 2, block_len, HEAD_SIZE).transpose(1, 0, 2, 3)
+            return table.reshape(2, MEMBERS * block_len, HEAD_SIZE)
+
+        half = HEAD_SIZE // 2
+        signs = jnp.where(jnp.arange(HEAD_SIZE) < half, -1.0, 1.0)
+        kernel_cosine, kernel_sine = halves(row_cosine), halves(row_sine * signs)
+        half_pos = own_pos.reshape(MEMBERS, 2, block_len).transpose(1, 0, 2).reshape(2, -1)
+        mask = (half_pos[:, :, None] <= half_pos[:, None, :]).astype(wide)
+        mask = jnp.concatenate([mask, mask], 2)
+        return row_cosine, row_sine, kernel_cosine, kernel_sine, mask
+
+    def make_slots(packed):
+        width_small = piece * experts_all
+        flat = packed.reshape(nz * 8, -1)
+        device = jnp.arange(nz * 8, dtype=jnp.int32)
+        source = ((zi - device // 8) % nz) * 8 + ((device & 1) ^ xi) * 4
+        source = source + (((device >> 1) & 1) ^ ci) * 2 + (((device >> 2) & 1) ^ yi)
+        router = flat[:, :width_small][source].reshape(nz * 8, experts_all, piece)
+        router = router.transpose(1, 0, 2).reshape(experts_all, model)
+        ids_all = packed.reshape(nz, 2, 2, 2, -1)[:, 0, :, :, width_small:].transpose(0, 2, 1, 3)
+        ids_all = ids_all.reshape(nz, MEMBERS, TOP, rows).astype(jnp.int32)
+        named = jnp.any(ids_all == own_expert, 2)
+        before = (
+            jnp.arange(rows, dtype=jnp.int32)[:, None] <= jnp.arange(rows, dtype=jnp.int32)[None, :]
+        )
+        ranks = dot32("kjs,st->kjt", named.astype(low), before.astype(low)).astype(jnp.int32) - 1
+        ranks = jnp.where(named, ranks, -1)[:, :, None, :]
+        expert_column = jnp.arange(experts_all, dtype=jnp.int32)[:, None]
+        chosen_all = jnp.any(ids_all[:, :, :, None, :] == expert_column, 2).astype(wide)
+        return router, ranks, chosen_all
+
+    cap_rows = rows * TOP * 5 // (4 * experts_all)
+    slots = -(-cap_rows // 16) * 16
+
     def prepare(w_query, key_weight, value_weight, w_router, expert_ids):
         columns = jnp.concatenate(
             [w.reshape(piece, KEY_VALUE_HEADS, -1) for w in (w_query, key_weight, value_weight)],
@@ -1010,9 +1040,8 @@
     )
     width = part0.shape[-1]
     inputs = tokens.astype(wide)
-    (far, plane3, down0, *small), (normed_attn, inverse_attn), _ = step(
-        [(parts_far, "y"), (w_output, "z", 3), (w_down[0, :third], "x")]
-        + [(packed, "z", k) for k in range(1, nz)],
+    (far, plane3, *small), (normed_attn, inverse_attn), _ = step(
+        [(parts_far, "y"), (w_output, "z", 3)] + [(packed, "z", k) for k in range(1, nz)],
         lambda tokens: rms_apply(tokens.astype(wide), attention_gain),
         (tokens,),
     )
@@ -1035,24 +1064,32 @@
     held.append(moved)
     over_x.append(cross)
     packed = jnp.stack([packed, packed_near], 1)
-    (moved, cross, other_near, packed_cross, down1), _, _ = step(
+    (moved, cross, other_near, packed_cross, down1), tables, _ = step(
         [
             (ordered, "z", 2),
             (held[1], "x"),
             (other, "c"),
             (packed, "x"),
             (w_down[0, third : 2 * third], "x"),
-        ]
-    )
+        ],
+        make_tables,
+        (zi, token_members),
+    )
+    row_cosine, row_sine, kernel_cosine, kernel_sine, mask = tables
     held.append(moved)
     over_x.append(cross)
     normed_all = jnp.concatenate([normed_low, other, near, other_near])
     packed = jnp.stack([packed, packed_cross], 1)
-    (moved, cross), _, _ = step([(ordered, "z", 3), (held[2], "x")])
+    (moved, cross, c_near0), (router, ranks, chosen_all), _ = step(
+        [(ordered, "z", 3), (held[2], "x"), (cotangent, "c")], make_slots, (packed,)
+    )
     held.append(moved)
     over_x.append(cross)
-    middle = head_rows // 2
-    (cross, plane2_low), _, _ = step([(held[3], "x"), (w_output[:middle], "z", 2)])
+    (cross, plane2, c_far0, down0), (planes,), _ = step(
+        [(held[3], "x"), (w_output, "z", 2), (cotangent, "y"), (w_down[0, :third], "x")],
+        lambda own, one, three: (jnp.stack([own, one, one, three]),),
+        (w_output, plane1, plane3),
+    )
     over_x.append(cross)
 
     def assemble(start, stop):
@@ -1069,44 +1106,6 @@
     query_weight = assemble(0, query_width)
     key_value_weight = assemble(query_width, width)
 
-    own_pos = jax.vmap(lambda device: shard_positions(device, context_count, block_len))(
-        zi * MEMBERS + token_members
-    )
-    cosine, sine_tab = rotary(own_pos.reshape(-1), HEAD_SIZE)
-    row_cosine = cosine.reshape(MEMBERS, 1, paired, HEAD_SIZE)
-    row_sine = sine_tab.reshape(MEMBERS, 1, paired, HEAD_SIZE)
-
-    def halves(table):
-        table = table.reshape(MEMBERS, 2, block_len, HEAD_SIZE).transpose(1, 0, 2, 3)
-        return table.reshape(2, MEMBERS * block_len, HEAD_SIZE)
-
-    half = HEAD_SIZE // 2
-    signs = jnp.where(jnp.arange(HEAD_SIZE) < half, -1.0, 1.0)
-    kernel_cosine, kernel_sine = halves(row_cosine), halves(row_sine * signs)
-    half_pos = own_pos.reshape(MEMBERS, 2, block_len).transpose(1, 0, 2).reshape(2, -1)
-    mask = (half_pos[:, :, None] <= half_pos[:, None, :]).astype(wide)
-    mask = jnp.concatenate([mask, mask], 2)
-
-    width_small = piece * experts_all
-    flat = packed.reshape(nz * 8, -1)
-    device = jnp.arange(nz * 8, dtype=jnp.int32)
-    source = ((zi - device // 8) % nz) * 8 + ((device & 1) ^ xi) * 4
-    source = source + (((device >> 1) & 1) ^ ci) * 2 + (((device >> 2) & 1) ^ yi)
-    router = flat[:, :width_small][source].reshape(nz * 8, experts_all, piece)
-    router = router.transpose(1, 0, 2).reshape(experts_all, model)
-    ids_all = packed.reshape(nz, 2, 2, 2, -1)[:, 0, :, :, width_small:].transpose(0, 2, 1, 3)
-    ids_all = ids_all.reshape(nz, MEMBERS, TOP, rows).astype(jnp.int32)
-    named = jnp.any(ids_all == own_expert, 2)
-    before = (
-        jnp.arange(rows, dtype=jnp.int32)[:, None] <= jnp.arange(rows, dtype=jnp.int32)[None, :]
-    )
-    ranks = dot32("kjs,st->kjt", named.astype(low), before.astype(low)).astype(jnp.int32) - 1
-    ranks = jnp.where(named, ranks, -1)[:, :, None, :]
-    expert_column = jnp.arange(experts_all, dtype=jnp.int32)[:, None]
-    chosen_all = jnp.any(ids_all[:, :, :, None, :] == expert_column, 2).astype(wide)
-    cap_rows = rows * TOP * 5 // (4 * experts_all)
-    slots = -(-cap_rows // 16) * 16
-
     def project_keys(normed_all, key_value_weight):
         raw = jnp.dot(normed_all, key_value_weight, preferred_element_type=wide)
         raw = raw.reshape(MEMBERS, LOCAL_SEQUENCES, paired, 2 * HEAD_SIZE)
@@ -1116,55 +1115,74 @@
         value_low = raw[..., HEAD_SIZE:].astype(low)
         return key_proj, key_inverse, jnp.concatenate([key_low, value_low], -1)
 
-    gate_cut = w_gate.shape[1] * 5 // 8
-    (plane2_high, down2), (key_proj, key_inverse, key_value), _ = step(
-        [(w_output[middle:], "z", 2), (w_down[0, 2 * third :], "x")],
+    planes = lax.dynamic_update_index_in_dim(planes, plane2, 2, 0)
+    wanted = [pick(planes, lax.rem(zi + nz - crossed[r], jnp.int32(nz))) for r in range(MEMBERS)]
+    cut = rows // 2
+    gate_cut = w_gate.shape[1] * 5 // 16
+    gate_next = w_gate.shape[1] * 9 // 16
+    moved, (key_proj, key_inverse, key_value), _ = step(
+        [
+            (jnp.stack(wanted[2:]), "y"),
+            (cotangent, "z", 1),
+            (w_down[0, 2 * third :], "x"),
+            (w_gate[0, :gate_cut], "x"),
+            (c_far0, "c"),
+        ],
         project_keys,
         (normed_all, key_value_weight),
     )
-    planes = jnp.stack([w_output, plane1, jnp.concatenate([plane2_low, plane2_high]), plane3])
-    wanted = [pick(planes, lax.rem(zi + nz - crossed[r], jnp.int32(nz))) for r in range(MEMBERS)]
-    (key_value1, key_value3, far, gate0), queries, _ = step(
-        [
-            (key_value, "z", 1),
-            (key_value, "z", 3),
-            (jnp.stack(wanted[2:]), "y"),
-            (w_gate[0, :gate_cut], "x"),
-        ],
-        lambda normed_all, query_weight: jnp.dot(
-            normed_all, query_weight, preferred_element_type=wide
-        ),
-        (normed_all, query_weight),
-    )
+    far, c1, down2, gate0, c_far_near0 = moved
+    mine = jnp.stack([wanted[0], far[0]])
+
+    def project_queries(normed_all, query_weight, pair):
+        near = swap(pair, "c")
+        return (
+            near,
+            swap(near[0], "x"),
+            jnp.dot(normed_all, query_weight, preferred_element_type=wide),
+        )
+
+    moved, (near, cross_first, queries), _ = step(
+        [(key_value, "z", k) for k in range(1, nz)] + [(mine, "x")],
+        project_queries,
+        (normed_all, query_weight, jnp.stack([wanted[1], far[1]])),
+    )
+    key_value = jnp.stack((key_value,) + moved[: nz - 1])
+    cross_mine = moved[nz - 1]
     queries = queries.reshape(MEMBERS, LOCAL_SEQUENCES, paired, query_width)
-    cotangents = lax.all_gather(
-        after(cotangent, step.mark), ("z", "y", "c"), axis=0, tiled=True
-    ).reshape(nz, MEMBERS, rows, model)
-    mine = jnp.stack([wanted[0], far[0]])
-    (key_value2, near, cross_mine), _, _ = step(
-        [(key_value, "z", 2), (jnp.stack([wanted[1], far[1]]), "c"), (mine, "x")]
-    )
-    key_value = jnp.stack([key_value, key_value1, key_value2, key_value3])
 
     places = jnp.stack([member, zi]).astype(jnp.int32)
     gain_row = query_gain[None]
-    (cross_near,), attended, _ = step(
-        [(near, "x")],
+    (cross_last, c2_low, c_far1, gate1), attended, _ = step(
+        [
+            (near[1], "x"),
+            (cotangent[:cut], "z", 2),
+            (c1, "y"),
+            (w_gate[0, gate_cut:gate_next], "x"),
+        ],
         attend,
         (places, queries, key_value, kernel_cosine, kernel_sine, gain_row, mask),
     )
     attended = attended.reshape(MEMBERS * rows, query_width)
     own_heads = jnp.stack([mine[0], near[0], mine[1], near[1]])
-    other_heads = jnp.stack([cross_mine[0], cross_near[0], cross_mine[1], cross_near[1]])
+    other_heads = jnp.stack([cross_mine[0], cross_first, cross_mine[1], cross_last])
     output_weight = jnp.where(
         xi == 0, jnp.stack([own_heads, other_heads], 1), jnp.stack([other_heads, own_heads], 1)
     ).reshape(query_width, model)
 
     mixed_part = jnp.dot(attended, output_weight, preferred_element_type=wide)
     mixed_part = mixed_part.reshape(2, 2, rows, model)
-    (near,), _, _ = step([(mixed_part[1].astype(low), "c")])
+    (near, c_near1), _, _ = step([(mixed_part[1].astype(low), "c"), (c1, "c")])
     summed_far = (mixed_part[0, 1] + near[1].astype(wide)).astype(low)
-    (other, gate1), _, _ = step([(summed_far, "y"), (w_gate[0, gate_cut:], "x")])
+    (other, gate2, c2_high, c_far_near1), _, _ = step(
+        [
+            (summed_far, "y"),
+            (w_gate[0, gate_next:], "x"),
+            (cotangent[cut:], "z", 2),
+            (c_far1, "c"),
+        ]
+    )
+    c2 = jnp.concatenate([c2_low, c2_high])
     mixed_attn = inputs + (mixed_part[0, 0] + near[0].astype(wide) + other.astype(wide))
     normed_ffn, inverse_ffn = rms_apply(mixed_attn, ffn_gain)
     ffn_low = normed_ffn.astype(low)
@@ -1186,174 +1204,194 @@
             start += other.shape[0]
         return full.reshape(2 * own.shape[0], own.shape[1])
 
-    def run_experts(k, x_blocks, kept, weights):
-        scalars = jnp.stack([from_z[k], yi, ci, own_expert, jnp.int32(k)]).astype(jnp.int32)
+    def run_experts(k, x_blocks, c_blocks, kept, weights):
+        scalars = jnp.stack([own_expert, jnp.int32(k)]).astype(jnp.int32)
         out = experts(
-            scalars, x_blocks, cotangents, ranks, chosen_all, router, *weights, slots, kept
+            scalars, x_blocks, c_blocks, ranks, chosen_all, router, *weights, slots, kept
         )
         return tuple(out[:-4]), out[-4:-2], out[-2:]
 
     def added(pair, back, a):
         return pair[0][a].astype(wide) + back[a].astype(wide)
 
-    def assemble_experts(*pieces):
-        gates_part, ups_part, downs_part = pieces
-        return (
-            whole(w_gate[0], gates_part),
-            whole(w_up[0], ups_part),
-            whole(w_down[0], downs_part),
-        )
-
-    (x2, y0, n0, up_other), _, _ = step(
-        [(ffn_low, "z", 2), (ffn_low, "y"), (ffn_low, "c"), (w_up[0], "x")]
-    )
-    (x1, y2, ny0, n2), weights, _ = step(
-        [(ffn_low, "z", 1), (x2, "y"), (y0, "c"), (x2, "c")],
-        assemble_experts,
-        ([gate0, gate1], [up_other], [down0, down1, down2]),
-    )
-    (x3, y1, ny2, n1), (kept, mixed0, rows0), _ = step(
-        [(ffn_low, "z", 3), (x1, "y"), (y2, "c"), (x1, "c")],
-        functools.partial(run_experts, 0),
-        ([ffn_low, n0, y0, ny0], (), weights),
-    )
-    (y3, ny1, n3, back0, mixed_back0), (kept, mixed2, rows2), _ = step(
-        [(x3, "y"), (y1, "c"), (x3, "c"), (rows0[1], "c"), (mixed0[1], "c")],
+    def both_rows(block):
+        far = swap(block, "y")
+        return far, swap(far, "c")
+
+    (x2, up_other, c_far2, y0, c_near2), (gate_all, down_all), _ = step(
+        [
+            (ffn_low, "z", 2),
+            (w_up[0], "x"),
+            (c2, "y"),
+            (ffn_low, "y"),
+            (c2, "c"),
+        ],
+        lambda owns, others: [whole(own, other) for own, other in zip(owns, others)],
+        ([w_gate[0], w_down[0]], [[gate0, gate1, gate2], [down0, down1, down2]]),
+    )
+    (x1, c3_low, y2, n2, c_far_near2), up_all, _ = step(
+        [
+            (ffn_low, "z", 1),
+            (cotangent[:cut], "z", 3),
+            (x2, "y"),
+            (x2, "c"),
+            (c_far2, "c"),
+        ],
+        lambda own, other: whole(own, [other]),
+        (w_up[0], up_other),
+    )
+    weights = [gate_all, up_all, down_all]
+    (ny2, n0, ny0), _, _ = step([(y2, "c"), (ffn_low, "c"), (y0, "c")])
+    (x3, c3_high, y1, c_far3_low, n1), (kept, mixed2, rows2), _ = step(
+        [
+            (ffn_low, "z", 3),
+            (cotangent[cut:], "z", 3),
+            (x1, "y"),
+            (c3_low, "y"),
+            (x1, "c"),
+        ],
         functools.partial(run_experts, 2),
-        ([x2, n2, y2, ny2], kept, weights),
-    )
-    (ny3, back2, mixed_back2, far0), (kept, mixed1, rows1), _ = step(
-        [
-            (y3, "c"),
-            (rows2[1], "c"),
-            (mixed2[1], "c"),
-            (added(rows0, back0, 1).astype(low), "y"),
+        ([x2, n2, y2, ny2], [c2, c_near2, c_far2, c_far_near2], (), weights),
+    )
+    (ny1,), c3, _ = step(
+        [(y1, "c")], lambda *halves: jnp.concatenate(halves), (c3_low, c3_high)
+    )
+    (y3, c_far3_high, n3, c_near3, back2), (kept, mixed1, rows1), _ = step(
+        [(x3, "y"), (c3_high, "y"), (x3, "c"), (c3, "c"), (rows2[1], "c")],
+        functools.partial(run_experts, 1),
+        ([x1, n1, y1, ny1], [c1, c_near1, c_far1, c_far_near1], kept, weights),
+    )
+    c_far3 = jnp.concatenate([c_far3_low, c_far3_high])
+    (ny3, c_far_near3, mixed_back2), row_send2, _ = step(
+        [(y3, "c"), (c_far3, "c"), (mixed2[1], "c")],
+        lambda pair, back: added(pair, back, 1).astype(low),
+        (rows2, back2),
+    )
+    (far2, mixed_far2, back1, mixed_back1), (kept, mixed3, rows3), _ = step(
+        [
+            (row_send2, "y"),
+            (added(mixed2, mixed_back2, 1).astype(low), "y"),
+            (rows1[1], "c"),
+            (mixed1[1], "c"),
         ],
-        functools.partial(run_experts, 1),
-        ([x1, n1, y1, ny1], kept, weights),
-    )
-    (back1, mixed_back1, far2), (kept, mixed3, rows3), _ = step(
-        [(rows1[1], "c"), (mixed1[1], "c"), (added(rows2, back2, 1).astype(low), "y")],
         functools.partial(run_experts, 3),
-        ([x3, n3, y3, ny3], kept, weights),
-    )
-    expert_rows, hidden_low, dresults, dgate_low, dup_low = (
-        block.reshape(context_count * slots, -1) for block in kept
-    )
-
-    def halved(grad, cuts):
-        size = grad.shape[0] // 2
-        own = lax.dynamic_slice_in_dim(grad, xi * size, size, 0)
-        other = lax.dynamic_slice_in_dim(grad, (1 - xi) * size, size, 0).astype(low)
-        cut = size // cuts
-        return own, [other[i * cut : (i + 1) * cut] for i in range(cuts)]
-
-    def joined(own, moved):
-        return (own + jnp.concatenate(moved, 0).astype(wide))[None]
-
+        ([x3, n3, y3, ny3], [c3, c_near3, c_far3, c_far_near3], kept, weights),
+    )
     total2 = (added(rows2, back2, 0) + far2.astype(wide)).astype(low)
-    cut = rows // 2
-    (z2_low, far1, back3, mixed_back3), down_grad, _ = step(
-        [
-            (total2[:cut], "z", -2),
+    (z2, far1, mixed_far1, back3, mixed_back3), (kept, mixed0, rows0), _ = step(
+        [
+            (total2, "z", -2),
             (added(rows1, back1, 1).astype(low), "y"),
+            (added(mixed1, mixed_back1, 1).astype(low), "y"),
             (rows3[1], "c"),
             (mixed3[1], "c"),
         ],
-        functools.partial(dot32, "sf,sd->fd"),
-        (hidden_low, dresults),
-    )
-    down_grad, down_sends = halved(down_grad, 2)
-    (z2_high, far3, down0), gate_grad, _ = step(
-        [
-            (total2[cut:], "z", -2),
+        functools.partial(run_experts, 0),
+        (
+            [ffn_low, n0, y0, ny0],
+            [cotangent, c_near0, c_far0, c_far_near0],
+            kept,
+            weights,
+        ),
+    )
+    expert_rows, hidden_low, dresults, dgate_low, dup_low = (
+        block.reshape(context_count * slots, -1) for block in kept
+    )
+
+    def halved(grad):
+        size = grad.shape[0] // 2
+        own = lax.dynamic_slice_in_dim(grad, xi * size, size, 0)
+        return own, lax.dynamic_slice_in_dim(grad, (1 - xi) * size, size, 0).astype(low)
+
+    def joined(own, moved):
+        return (own + jnp.concatenate(moved, 0).astype(wide))[None]
+
+    total1 = (added(rows1, back1, 0) + far1.astype(wide)).astype(low)
+
+    def total(pair, back, far):
+        return (added(pair, back, 0) + far.astype(wide)).astype(low)
+
+    (z1, far3, back0, mixed_back0), ((down_grad, down_send), mixed_send1), _ = step(
+        [
+            (total1, "z", -1),
             (added(rows3, back3, 1).astype(low), "y"),
-            (down_sends[0], "x"),
+            (rows0[1], "c"),
+            (mixed0[1], "c"),
         ],
-        functools.partial(dot32, "sd,sf->df"),
-        (expert_rows, dgate_low),
-    )
-    total1 = (added(rows1, back1, 0) + far1.astype(wide)).astype(low)
+        lambda rows, grad, *given: (halved(dot32("sf,sd->fd", rows, grad)), total(*given)),
+        (hidden_low, dresults, mixed1, mixed_back1, mixed_far1),
+    )
     total3 = (added(rows3, back3, 0) + far3.astype(wide)).astype(low)
-    (z1, down1, mixed_far2), up_grad, _ = step(
-        [
-            (total1, "z", -1),
-            (down_sends[1], "x"),
-            (added(mixed2, mixed_back2, 1).astype(low), "y"),
+    down_cut = down_send.shape[0] * 5 // 8
+    (z3, far0, down0), ((gate_grad, gate_send), mixed_send2), _ = step(
+        [
+            (total3, "z", -3),
+            (added(rows0, back0, 1).astype(low), "y"),
+            (down_send[:down_cut], "x"),
         ],
-        functools.partial(dot32, "sd,sf->df"),
-        (expert_rows, dup_low),
-    )
-    gate_grad, gate_sends = halved(gate_grad, 2)
-    (z3, gate0, mixed_far1), (down_grad, mixed_send2), _ = step(
-        [
-            (total3, "z", -3),
-            (gate_sends[0], "x"),
-            (added(mixed1, mixed_back1, 1).astype(low), "y"),
-        ],
-        lambda own, moved, pair, back, far: (
-            joined(own, moved),
-            (added(pair, back, 0) + far.astype(wide)).astype(low),
-        ),
-        (down_grad, [down0, down1], mixed2, mixed_back2, mixed_far2),
-    )
-    returned = added(rows0, back0, 0) + far0.astype(wide) + z1.astype(wide) + z3.astype(wide)
-    returned = returned + jnp.concatenate([z2_low, z2_high], 0).astype(wide)
+        lambda rows, grad, *given: (halved(dot32("sd,sf->df", rows, grad)), total(*given)),
+        (expert_rows, dgate_low, mixed2, mixed_back2, mixed_far2),
+    )
+    returned = added(rows0, back0, 0) + far0.astype(wide) + z1.astype(wide)
+    returned = returned + z2.astype(wide) + z3.astype(wide)
     dffn_routed = returned[:, :model]
     dgates = returned[:, model : model + experts_all]
     dgates = dgates + returned[:, model + experts_all : model + 2 * experts_all]
     dlogits = gates * (dgates - jnp.sum(gates * dgates, 1, keepdims=True))
     dlogits_low = dlogits.astype(low)
-    router_grad = dot32("te,td->ed", dlogits_low, ffn_low)
+    router_rows = dot32("td,te->de", ffn_low, dlogits_low).astype(low)
+    router_rows = router_rows.reshape(nz, MEMBERS, 2, -1, 2 * HEAD_SIZE)
+    extra_rows = router_rows.shape[3]
+    router_rows = jnp.pad(router_rows, ((0, 0),) * 3 + ((0, -extra_rows % 16), (0, 0)))
 
     upstream = cotangent.astype(wide)
     dffn_rows = dffn_routed + dot32("te,ed->td", dlogits_low, router)
     dmixed_norm, ffn_gain_part = rms_back(mixed_attn, inverse_ffn, ffn_gain, dffn_rows)
     dmixed_attn = upstream + dmixed_norm
     dattn_low = dmixed_attn.astype(low)
-    (other, near, gate1, mixed_z2_low), (mixed_send1, up_grad, up_sends), _ = step(
+    gate_cut = gate_send.shape[0] * 5 // 8
+    moved, (up_grad, up_send), _ = step(
         [
             (dattn_low, "y"),
             (dattn_low, "c"),
-            (gate_sends[1], "x"),
-            (mixed_send2[:cut], "z", -2),
+            (gate_send[:gate_cut], "x"),
+            (mixed_send1, "z", -1),
         ],
-        lambda pair, back, far, grad: (
-            (added(pair, back, 0) + far.astype(wide)).astype(low),
-            *halved(grad, 2),
-        ),
-        (mixed1, mixed_back1, mixed_far1, up_grad),
-    )
+        lambda rows, grad: halved(dot32("sd,sf->df", rows, grad)),
+        (expert_rows, dup_low),
+    )
+    other, near, gate0, mixed_z1 = moved
     (other_near,), _, _ = step([(other, "c")])
     dattn_all = jnp.concatenate([dattn_low, other, near, other_near])
 
-    def through_output(dattn_all, output_weight, attended):
+    output_part = dot32("tc,td->cd", attended, dattn_all).astype(low)
+    output_part = output_part.reshape(MEMBERS, 2, head_rows, model)
+    output_own = lax.dynamic_index_in_dim(output_part, xi, 1, keepdims=False)
+    output_other = lax.dynamic_index_in_dim(output_part, 1 - xi, 1, keepdims=False)
+
+    def planes_of(part):
+        own = lax.dynamic_index_in_dim(part, xi, 2, keepdims=False)
+        other = lax.dynamic_index_in_dim(part, 1 - xi, 2, keepdims=False)
+        return [(pick(own, around(k)), pick(other, around(k))) for k in range(nz)]
+
+    def attention_back(dattn_all, output_weight, *given):
         attended_grad = dot32("td,cd->tc", dattn_all, output_weight).astype(low)
-        output_part = dot32("tc,td->cd", attended, dattn_all).astype(low)
-        output_part = output_part.reshape(MEMBERS, 2, head_rows, model)
-        own = lax.dynamic_index_in_dim(output_part, xi, 1, keepdims=False)
-        other = lax.dynamic_index_in_dim(output_part, 1 - xi, 1, keepdims=False)
-        return attended_grad, own[:2], own[2:], other[:1], other[1:]
-
-    (mixed_far3, up0), (attended_grad, own_near, own_far, cross_first, cross_rest), _ = step(
-        [(added(mixed3, mixed_back3, 1).astype(low), "y"), (up_sends[0], "x")],
-        through_output,
-        (dattn_all, output_weight, attended),
-    )
-    attended_grad = attended_grad.reshape(MEMBERS, LOCAL_SEQUENCES, paired, query_width)
-    early = jnp.concatenate([router_grad, ffn_gain_part[None]], 0)
-    moved, (dquery_low, dkey_value, query_gain_part), _ = step(
-        [
-            (cross_rest, "x"),
-            (early, "x"),
-            (mixed_send1, "z", -1),
-            (mixed_send2[cut:], "z", -2),
+        attended_grad = attended_grad.reshape(MEMBERS, LOCAL_SEQUENCES, paired, query_width)
+        return attend_back(*given[:2], attended_grad, *given[2:])
+
+    moved, attention_grads, _ = step(
+        [
+            (output_other[1:], "x"),
+            (mixed_send2, "z", -2),
+            (added(mixed3, mixed_back3, 1).astype(low), "y"),
+            (added(mixed0, mixed_back0, 1).astype(low), "y"),
         ],
-        attend_back,
+        attention_back,
         (
+            dattn_all,
+            output_weight,
             places,
             queries,
-            attended_grad,
             key_value,
             kernel_cosine,
             kernel_sine,
@@ -1361,42 +1399,35 @@
             mask,
         ),
     )
-    cross, early_x, mixed_z1, mixed_z2_high = moved
-    early = early + early_x
-    output_far = (own_far.astype(wide) + cross[1:].astype(wide)).astype(low)
+    cross_rest, mixed_z2, mixed_far3, mixed_far0 = moved
+    dquery_low, dkey_value, query_gain_part = attention_grads
     query_gain_part = query_gain_part[0]
     dquery_low = dquery_low.reshape(MEMBERS * rows, query_width)
-
-    def planes_of(part):
-        own = lax.dynamic_index_in_dim(part, xi, 2, keepdims=False)
-        other = lax.dynamic_index_in_dim(part, 1 - xi, 2, keepdims=False)
-        return [(pick(own, around(k)), pick(other, around(k))) for k in range(nz)]
-
     query_part = dot32("td,tc->dc", normed_all, dquery_low).astype(low)
     query_planes = planes_of(query_part.reshape(nz, MEMBERS, 2, piece, query_width))
-    near_rest = cross[:1]
-    moved, (dnormed, mixed_send3, gate_grad), _ = step(
+    output_far = (output_own[2:].astype(wide) + cross_rest[1:].astype(wide)).astype(low)
+
+    def query_back(grad, weight, third):
+        return dot32("tc,dc->td", grad, weight), total(*third)
+
+    query_plane = query_planes[2][1].reshape(-1, query_width)
+    first_head = [output_other[0][:, a : a + query_width] for a in range(0, model, query_width)]
+    moved, (dnormed, mixed_send3), _ = step(
         [(dkey_value[k].astype(low), "z", -k) for k in range(1, nz)]
-        + [(query_planes[2][1], "x"), (cross_first, "x"), (output_far, "y")],
-        lambda grad, weight, pair, back, far, own, moved: (
-            dot32("tc,dc->td", grad, weight),
-            (added(pair, back, 0) + far.astype(wide)).astype(low),
-            joined(own, moved),
-        ),
-        (
-            dquery_low,
-            query_weight,
-            mixed3,
-            mixed_back3,
-            mixed_far3,
-            gate_grad,
-            [gate0, gate1],
-        ),
-    )
-    cross, near_first, output_far = moved[nz - 1 :]
-    output_cross = jnp.concatenate([near_first, near_rest])
+        + [(jnp.concatenate([query_plane] + first_head), "x"), (output_far, "y")],
+        query_back,
+        (dquery_low, query_weight, [mixed3, mixed_back3, mixed_far3]),
+    )
+    *key_moves, cross, output_far = moved
+    plane_rows = query_plane.shape[0]
+    cross_first = [
+        cross[a : a + head_rows] for a in range(plane_rows, cross.shape[0], head_rows)
+    ]
+    cross_first = jnp.concatenate(cross_first, 1)
+    cross = cross[:plane_rows].reshape(query_planes[2][0].shape)
     query_sum2 = (query_planes[2][0].astype(wide) + cross.astype(wide)).astype(low)
-    output_near = (own_near.astype(wide) + output_cross.astype(wide)).astype(low)
+    near_first = (output_own[0].astype(wide) + cross_first.astype(wide)).astype(low)
+    near_last = (output_own[1].astype(wide) + cross_rest[0].astype(wide)).astype(low)
 
     def project_keys_back(dnormed, dkey_value_own, moved, key_value_weight):
         dkey_value_own = dkey_value_own + sum(block.astype(wide) for block in moved)
@@ -1407,49 +1438,44 @@
         dkey_value_low = jnp.concatenate([dkey_proj, dvalue], -1).astype(low)
         dkey_value_low = dkey_value_low.reshape(MEMBERS * rows, 2 * HEAD_SIZE)
         dnormed = dnormed + dot32("tc,dc->td", dkey_value_low, key_value_weight)
-        dnormed = scatter_members(dnormed.reshape(2, 2, rows, model))
+        dnormed = dnormed.reshape(2, 2, rows, model)
         key_part = dot32("td,tc->dc", normed_all, dkey_value_low).astype(low)
         key_part = key_part.reshape(nz, MEMBERS, 2, piece, 2 * HEAD_SIZE)
+        key_part = jnp.concatenate([key_part, router_rows], 3)
         key_own = lax.dynamic_index_in_dim(key_part, xi, 2, keepdims=False)
         key_other = lax.dynamic_index_in_dim(key_part, 1 - xi, 2, keepdims=False)
-        return dnormed, key_own, key_other, key_gain_part
-
-    moved_z, (dnormed, key_own, key_other, key_gain_part), _ = step(
+        return dnormed[0], dnormed[1].astype(low), key_own, key_other, key_gain_part
+
+    moved, (dnormed_own, dnormed_send, key_own, key_other, key_gain_part), _ = step(
         [
             (query_sum2, "z", 2),
-            (mixed_send3[:cut], "z", -3),
             (jnp.stack([query_planes[1][1], query_planes[3][1]]), "x"),
-            (jnp.stack([output_near[1], output_far[1]]), "c"),
+            (jnp.stack([near_last, output_far[1]]), "c"),
         ],
         project_keys_back,
-        (dnormed, dkey_value[0], moved[: nz - 1], key_value_weight),
-    )
-    query_z2, mixed_z3_low, cross, output_back = moved_z
+        (dnormed, dkey_value[0], key_moves, key_value_weight),
+    )
+    query_z2, cross, output_back = moved
     query_sum1 = (query_planes[1][0].astype(wide) + cross[0].astype(wide)).astype(low)
     query_sum3 = (query_planes[3][0].astype(wide) + cross[1].astype(wide)).astype(low)
-    dinput_norm, attention_gain_part = rms_back(inputs, inverse_attn, attention_gain, dnormed)
-    late = jnp.concatenate([attention_gain_part, query_gain_part, key_gain_part])
-    small = jnp.concatenate([early.reshape(-1, 128), late.reshape(-1, 128)], 0)
-    output_blocks = [output_near[0], output_back[0], output_far[0], output_back[1]]
-
-    def order_output(blocks, dmixed_attn, dinput_norm):
+
+    def order_output(blocks):
         blocks = uncrossed(blocks)
-        sends = [pick(blocks, around(k)) for k in range(nz)]
-        return sends, (dmixed_attn + dinput_norm).astype(low)
-
-    (query_z1, query_z3, cross, key_cross, late_x), (output_sends, d_tokens), _ = step(
+        return [pick(blocks, around(k)) for k in range(nz)]
+
+    moved, output_sends, _ = step(
         [
             (query_sum1, "z", 1),
             (query_sum3, "z", 3),
             (query_planes[0][1], "x"),
             (key_other, "x"),
-            (late.reshape(-1, 128), "x"),
+            (dnormed_send, "c"),
         ],
         order_output,
-        (output_blocks, dmixed_attn, dinput_norm),
-    )
-    early_rows = early.size // 128
-    small = jnp.concatenate([small[:early_rows], small[early_rows:] + late_x], 0)
+        ([near_first, output_back[0], output_far[0], output_back[1]],),
+    )
+    query_z1, query_z3, cross, key_cross, near = moved
+    dnormed_far = (dnormed_own[1] + near[1].astype(wide)).astype(low)
     key_sum = (key_own.astype(wide) + key_cross.astype(wide)).astype(low)
 
     def total_queries(own, cross, *moved):
@@ -1458,102 +1484,108 @@
         parts = [pick(total, crossed[r]) for r in range(MEMBERS)]
         return parts[0], parts[1], jnp.stack(parts[2:])
 
-    query_parts = total_queries(query_planes[0][0], cross, query_z1, query_z2, query_z3)
-    (output_z1, query_far, small_y, mixed_far0, mixed_z3_high, *key_moves), _, _ = step(
+    (output_z1, output_z3, other, gate1, down1), query_parts, _ = step(
         [
             (output_sends[1], "z", 1),
-            (query_parts[2], "y"),
-            (small, "y"),
-            (added(mixed0, mixed_back0, 1).astype(low), "y"),
-            (mixed_send3[cut:], "z", -3),
-        ]
-        + [(pick(key_sum, around(k)), "z", k) for k in range(1, nz)],
-    )
-    small = small + small_y
+            (output_sends[3], "z", 3),
+            (dnormed_far, "y"),
+            (gate_send[gate_cut:], "x"),
+            (down_send[down_cut:], "x"),
+        ],
+        total_queries,
+        (query_planes[0][0], cross, query_z1, query_z2, query_z3),
+    )
+    dnormed = dnormed_own[0] + near[0].astype(wide) + other.astype(wide)
+    dinput_norm, attention_gain_part = rms_back(inputs, inverse_attn, attention_gain, dnormed)
+    small = [attention_gain_part, ffn_gain_part, query_gain_part, key_gain_part]
+    small = jnp.concatenate(small).reshape(-1, 128)
+    (*key_moves, small_x, query_far), d_tokens, _ = step(
+        [(pick(key_sum, around(k)), "z", k) for k in range(1, nz)]
+        + [(small, "x"), (query_parts[2], "y")],
+        lambda a, b: (a + b).astype(low),
+        (dmixed_attn, dinput_norm),
+    )
+    small = small + small_x
     key_total = pick(key_sum, zi).astype(wide)
     key_total = (key_total + sum(m.astype(wide) for m in key_moves)).astype(low)
     key_parts = [pick(key_total, crossed[r]) for r in range(MEMBERS)]
 
-    def member_columns(part0, near, far):
-        grads = uncrossed([part0, near[0], far[0], near[1]])
-        return grads.astype(wide).transpose(1, 0, 2)
-
-    (output_z2, up1, key_far, query_near, small_c), (mixed,), _ = step(
+    def member_columns(parts):
+        return uncrossed(parts).astype(wide).transpose(1, 0, 2)
+
+    up_cut = up_send.shape[0] * 11 // 16
+    (output_z2, up0, key_far, small_y, query_near), (down_grad, gate_grad), _ = step(
         [
             (output_sends[2], "z", 2),
-            (up_sends[1], "x"),
+            (up_send[:up_cut], "x"),
             (jnp.stack(key_parts[2:]), "y"),
+            (small, "y"),
             (jnp.stack([query_parts[1], query_far[1]]), "c"),
+        ],
+        lambda down, downs, gate, gates: (joined(down, downs), joined(gate, gates)),
+        (down_grad, [down0, down1], gate_grad, [gate0, gate1]),
+    )
+    small = small + small_y
+    query_blocks = [query_parts[0], query_near[0], query_far[0], query_near[1]]
+    (mixed_z3, up1, key_near, small_c), (query_grad, output_grad), _ = step(
+        [
+            (mixed_send3, "z", -3),
+            (up_send[up_cut:], "x"),
+            (jnp.stack([key_parts[1], key_far[1]]), "c"),
             (small, "c"),
         ],
-        lambda base, pair, back, far, z1, *halves: (
-            (
-                base
-                + added(pair, back, 0)
-                + far.astype(wide)
-                + z1.astype(wide)
-                + jnp.concatenate(halves[:2], 0).astype(wide)
-                + jnp.concatenate(halves[2:], 0).astype(wide)
-            ).astype(low),
+        lambda blocks, own, *parts: (
+            member_columns(blocks).reshape(piece, -1),
+            own.astype(wide) + sum(part.astype(wide) for part in parts),
         ),
+        (query_blocks, output_sends[0], output_z1, output_z2, output_z3),
+    )
+    small = small + small_c
+    key_blocks = [key_parts[0], key_near[0], key_far[0], key_near[1]]
+
+    def finish(up, ups, key_blocks, base, pair, back, far, z1, z2, z3):
+        router = sum(block[piece : piece + extra_rows].astype(wide) for block in key_blocks)
+        mixed = base + added(pair, back, 0) + far.astype(wide) + z1.astype(wide)
+        mixed = mixed + z2.astype(wide) + z3.astype(wide)
+        return (
+            joined(up, ups),
+            member_columns([block[:piece] for block in key_blocks]),
+            router.reshape(piece, experts_all),
+            mixed.astype(low),
+        )
+
+    small_z, results, _ = step(
+        [(small, "z", k) for k in range(1, nz)],
+        finish,
         (
+            up_grad,
+            [up0, up1],
+            key_blocks,
             mixed_attn,
             mixed0,
             mixed_back0,
             mixed_far0,
             mixed_z1,
-            mixed_z2_low,
-            mixed_z2_high,
-            mixed_z3_low,
-            mixed_z3_high,
+            mixed_z2,
+            mixed_z3,
         ),
     )
-    small = small + small_c
-
-    def finish(own, moved, output_own, z1, z2, parts, near, far):
-        output = output_own.astype(wide) + z1.astype(wide) + z2.astype(wide)
-        return joined(own, moved), output, member_columns(parts, near, far)
-
-    (output_z3, key_near, *small_z), (up_grad, output_grad, query_grad), _ = step(
-        [
-            (output_sends[3], "z", 3),
-            (jnp.stack([key_parts[1], key_far[1]]), "c"),
-        ]
-        + [(small, "z", k) for k in range(1, nz)],
-        finish,
-        (
-            up_grad,
-            [up0, up1],
-            output_sends[0],
-            output_z1,
-            output_z2,
-            query_parts[0],
-            query_near,
-            query_far,
-        ),
-    )
-    query_grad = query_grad.reshape(piece, -1)
-    output_grad = output_grad + output_z3.astype(wide)
-    small = small + sum(small_z)
-    early = small[:early_rows].reshape(early.shape)
-    gains = small[early_rows:].reshape(-1)
-    key_grads = member_columns(key_parts[0], key_near, key_far)
+    up_grad, key_grads, router_grad, mixed = results
+    gains = (small + sum(small_z)).reshape(-1)
     key_grad = key_grads[..., :HEAD_SIZE].reshape(piece, -1)
     value_grad = key_grads[..., HEAD_SIZE:].reshape(piece, -1)
-    device = own_expert * 2 + xi
-    router_own = lax.dynamic_slice_in_dim(early[:experts_all], device * piece, piece, 1).T
     return (
         mixed,
         d_tokens,
         gains[:model],
-        early[experts_all],
-        gains[model : model + HEAD_SIZE],
-        gains[model + HEAD_SIZE :],
+        gains[model : 2 * model],
+        gains[2 * model : 2 * model + HEAD_SIZE],
+        gains[2 * model + HEAD_SIZE :],
         query_grad,
         key_grad,
         value_grad,
         output_grad,
-        router_own,
+        router_grad,
         gate_grad,
         up_grad,
         down_grad,

time: 928 us -> 866 us (0.933)
  waiting for transfers between devices: 415 us -> 369 us
  other arithmetic: 93.6 us -> 74.3 us
  between operations: 17 us -> 3.77 us
  starting transfers between devices: 119 us -> 131 us
    ppermute x79 -> x92, waiting for transfers between devices: 157 us -> 105 us  [swap(): return lax.ppermute(block, axis, [(0, 1), (1, 0)])]
    unnamed x348 -> x327, local copies, waits for them, and re-layouts: 19.3 us -> 28.8 us
    ppermute x79 -> x92, starting transfers between devices: 56.5 us -> 65.4 us  [swap(): return lax.ppermute(block, axis, [(0, 1), (1, 0)])]
    ppermute x40 -> x41, waiting for transfers between devices: 257 us -> 264 us  [shift(): lax.ppermute(block, axis, [(i, (i + step) % count) for i in range(count)])]
    ppermute x40 -> x41, starting transfers between devices: 62.9 us -> 65.8 us  [shift(): lax.ppermute(block, axis, [(i, (i + step) % count) for i in range(count)])]
  transfers between devices with their start and end apart: 120 -> 133, of which waited for: 50 -> 51; matrix products, arithmetic and copies ran while one was open for 17% -> 16% of each run, Pallas kernels for 14% -> 15%
where the time goes in v3:
time: 866 us; the launch traced here: 857 us
  waiting for transfers between devices  369 us (43%)
  starting transfers between devices  131 us (15%)
  Pallas kernels  128 us (15%)
  local copies, waits for them, and re-layouts  95.9 us (11%)
  other arithmetic  74.3 us (9%)
  matrix products  54.7 us (6%)
    ppermute x41, waiting for transfers between devices, shift(): lax.ppermute(block, axis, [(i, (i + step) % count) for i in range(count)])  264 us
    ppermute x92, waiting for transfers between devices, swap(): return lax.ppermute(block, axis, [(0, 1), (1, 0)])  105 us
    pallas_call x4, Pallas kernels, experts(): pl.pallas_call(expert_kernel, grid_spec=pltpu.PrefetchScalarGridSpec(num_...  94.9 us
    ppermute x41, starting transfers between devices, shift(): lax.ppermute(block, axis, [(i, (i + step) % count) for i in range(count)])  65.8 us
    ppermute x92, starting transfers between devices, swap(): return lax.ppermute(block, axis, [(0, 1), (1, 0)])  65.4 us
    dot_general x13, matrix products, dot32(): jnp.einsum(subscripts, left, right, preferred_element_type=jnp.float32)  45.1 us
    unnamed x327, local copies, waits for them, and re-layouts  28.8 us
    pallas_call x1, Pallas kernels, attend_back(): pl.pallas_call(attend_back_kernel, grid_spec=pltpu.PrefetchScalarGridSpec...  20.8 us
  transfers between devices with their start and end apart: 133, of which 51 were waited for; matrix products, arithmetic and copies ran while one was open for 16% of the time, Pallas kernels for 15%

profile of v3, /device:TPU:0, one launch (start us, length us, event | category | flops | bytes accessed | tf_op | source)
XLA Modules:
  0.0 856.6 jit_solution(8893497841095857949)
XLA Ops:
  8.6 9.3 %collective-permute-done = bf16[128,2048]{1,0:T(8,128)(2,1)S(1)} collective-permute-done((bf16[128,2048]{1,0:T(8,128)(2,1)}, bf16[128,2048]{1,0:T(8,128)(2,1)S(1)}, u32[]{:S(2)}, u32[]{:S(2)}) %collective-permute-start) | collective-permute-done | bytes 524320 | tf_op jit(solution)/shard_map/ppermute | solution.py:499
  25.6 6.0 collective-permute-done.3
  46.6 12.2 %collective-permute-done.8 = bf16[4,64,1280]{2,1,0:T(8,128)(2,1)S(1)} collective-permute-done((bf16[4,64,1280]{2,1,0:T(8,128)(2,1)S(1)}, bf16[4,64,1280]{2,1,0:T(8,128)(2,1)S(1)}, u32[]{:S(2)}, u32[]{:S(2)}) %collective-permute-start.8) | collective-permute-done | bytes 655392 | tf_op jit(solution)/shard_map/ppermute | solution.py:499
  74.3 20.2 %collective-permute-done.16 = bf16[4,2,2,20,128]{4,3,2,1,0:T(8,128)(2,1)S(1)} collective-permute-done((bf16[4,2,2,20,128]{4,3,2,1,0:T(8,128)(2,1)}, bf16[4,2,2,20,128]{4,3,2,1,0:T(8,128)(2,1)S(1)}, u32[]{:S(2)}, u32[]{:S(2)}) %collective-permute-start.16) | collective-permute-done | bytes 81952 | tf_op jit(solution)/shard_map/ppermute | solution.py:503
  128.4 17.9 %collective-permute-done.22 = bf16[128,2048]{1,0:T(8,128)(2,1)S(1)} collective-permute-done((bf16[128,2048]{1,0:T(8,128)(2,1)S(1)}, bf16[128,2048]{1,0:T(8,128)(2,1)S(1)}, u32[]{:S(2)}, u32[]{:S(2)}) %collective-permute-start.22) | collective-permute-done | bytes 524320 | tf_op jit(solution)/shard_map/ppermute | solution.py:499
  158.5 19.8 %collective-permute-done.28 = bf16[320,768]{1,0:T(8,128)(2,1)S(1)} collective-permute-done((bf16[320,768]{1,0:T(8,128)(2,1)S(1)}, bf16[320,768]{1,0:T(8,128)(2,1)S(1)}, u32[]{:S(2)}, u32[]{:S(2)}) %collective-permute-start.28) | collective-permute-done | bytes 491552 | tf_op jit(solution)/shard_map/ppermute | solution.py:503
  186.0 3.5 collective-permute-start.31
  192.7 5.2 fusion.87
  199.5 16.1 %collective-permute-done.31 = bf16[4,3,64,256]{3,2,1,0:T(8,128)(2,1)S(1)} collective-permute-done((bf16[4,3,64,256]{3,2,1,0:T(8,128)(2,1)}, bf16[4,3,64,256]{3,2,1,0:T(8,128)(2,1)S(1)}, u32[]{:S(2)}, u32[]{:S(2)}) %collective-permute-start.31) | collective-permute-done | bytes 393248 | tf_op jit(solution)/shard_map/ppermute | solution.py:499
  215.6 5.3 collective-permute-done.35
  230.2 12.2 %shard_map.263 = bf16[4,3,64,1024]{3,2,1,0:T(8,128)(2,1)S(1)} custom-call(s32[2]{0:T(128)S(1)} %pad_add_fusion.places_ref, f32[4,3,64,1024]{3,2,1,0:T(8,128)S(1)} %bitcast.550, bf16[4,4,3,64,256]{4,3,2,1,0:T(8,128)(2,1)S(1)} %pad_maximum_fusion.4.k_ref.v_ref, bf16[4,4,3,64,256]{4,3,2,1,0:T(8,128)(2,1)S(1)} %pad_maximum_fusion.4.k_ref.v_ref, ...), custom_call_target="tpu_custom_call" | custom-call | flops 3221225472 | bytes 8388608 | tf_op jit(solution)/shard_map/pallas_call | solution.py:768
  242.4 3.3 collective-permute-done.37
  247.2 3.4 fusion.88
  252.1 3.4 collective-permute-done.41.refs_6_
  261.6 18.1 %collective-permute-done.44 = bf16[96,2048]{1,0:T(8,128)(2,1)S(1)} collective-permute-done((bf16[96,2048]{1,0:T(8,128)(2,1)}, bf16[96,2048]{1,0:T(8,128)(2,1)S(1)}, u32[]{:S(2)}, u32[]{:S(2)}) %collective-permute-start.44) | collective-permute-done | bytes 393248 | tf_op jit(solution)/shard_map/ppermute | solution.py:499
  290.0 30.7 %collective-permute-done.46.refs_1_ = bf16[192,2048]{1,0:T(8,128)(2,1)S(1)} collective-permute-done((bf16[192,2048]{1,0:T(8,128)(2,1)S(1)}, bf16[192,2048]{1,0:T(8,128)(2,1)S(1)}, u32[]{:S(2)}, u32[]{:S(2)}) %collective-permute-start.46) | collective-permute-done | bytes 786464 | tf_op jit(solution)/shard_map/ppermute | solution.py:499
  332.0 18.5 %collective-permute-done.52 = bf16[96,2048]{1,0:T(8,128)(2,1)} collective-permute-done((bf16[96,2048]{1,0:T(8,128)(2,1)S(1)}, bf16[96,2048]{1,0:T(8,128)(2,1)}, u32[]{:S(2)}, u32[]{:S(2)}) %collective-permute-start.52) | collective-permute-done | bytes 393248 | tf_op jit(solution)/shard_map/ppermute | solution.py:499
  361.0 23.5 %shard_map.264 = (bf16[4,4,128,2048]{3,2,1,0:T(8,128)(2,1)}, bf16[4,4,128,768]{3,2,1,0:T(8,128)(2,1)}, bf16[4,4,128,2048]{3,2,1,0:T(8,128)(2,1)}, bf16[4,4,128,7...) custom-call(s32[2]{0:T(128)} %get-tuple-element.1305.refs_0_, ...), custom_call_target="tpu_custom_call" | custom-call | flops 9663676416 | bytes 41943040 | tf_op jit(solution)/shard_map/pallas_call | solution.py:919
  391.0 23.6 %shard_map.265 = (bf16[4,4,128,2048]{3,2,1,0:T(8,128)(2,1)}, bf16[4,4,128,768]{3,2,1,0:T(8,128)(2,1)}, bf16[4,4,128,2048]{3,2,1,0:T(8,128)(2,1)}, bf16[4,4,128,7...) custom-call(s32[2]{0:T(128)} %get-tuple-element.1306.refs_0_, ...), custom_call_target="tpu_custom_call", output_to_operand_aliasing={{0}: (15, {}), {1}: (16, {}), {2}: (17, {}), {3}: (18, {}),... | custom-call | flops 9663676416 | bytes 41943040 | tf_op jit(solution)/shard_map/pallas_call | solution.py:919
  419.0 3.7 collective-permute-done.70.refs_4_
  427.4 24.1 %shard_map.266 = (bf16[4,4,128,2048]{3,2,1,0:T(8,128)(2,1)}, bf16[4,4,128,768]{3,2,1,0:T(8,128)(2,1)}, bf16[4,4,128,2048]{3,2,1,0:T(8,128)(2,1)}, bf16[4,4,128,7...) custom-call(s32[2]{0:T(128)} %get-tuple-element.1307.refs_0_, ...), custom_call_target="tpu_custom_call", output_to_operand_aliasing={{0}: (15, {}), {1}: (16, {}), {2}: (17, {}), {3}: (18, {}),... | custom-call | flops 9663676416 | bytes 41943040 | tf_op jit(solution)/shard_map/pallas_call | solution.py:919
  451.5 11.5 %collective-permute-done.74 = bf16[192,2048]{1,0:T(8,128)(2,1)} collective-permute-done((bf16[192,2048]{1,0:T(8,128)(2,1)}, bf16[192,2048]{1,0:T(8,128)(2,1)}, u32[]{:S(2)}, u32[]{:S(2)}) %collective-permute-start.74) | collective-permute-done | bytes 786464 | tf_op jit(solution)/shard_map/ppermute | solution.py:503
  473.9 23.7 %shard_map.267 = (bf16[4,4,128,2048]{3,2,1,0:T(8,128)(2,1)}, bf16[4,4,128,768]{3,2,1,0:T(8,128)(2,1)}, bf16[4,4,128,2048]{3,2,1,0:T(8,128)(2,1)}, bf16[4,4,128,7...) custom-call(s32[2]{0:T(128)} %get-tuple-element.1308.refs_0_, ...), custom_call_target="tpu_custom_call", output_to_operand_aliasing={{0}: (15, {}), {1}: (16, {}), {2}: (17, {}), {3}: (18, {}),... | custom-call | flops 9663676416 | bytes 41943040 | tf_op jit(solution)/shard_map/pallas_call | solution.py:919
  497.6 11.9 %collective-permute-done.79 = bf16[192,2048]{1,0:T(8,128)(2,1)} collective-permute-done((bf16[192,2048]{1,0:T(8,128)(2,1)}, bf16[192,2048]{1,0:T(8,128)(2,1)}, u32[]{:S(2)}, u32[]{:S(2)}) %collective-permute-start.79) | collective-permute-done | bytes 786464 | tf_op jit(solution)/shard_map/ppermute | solution.py:503
  517.6 9.3 %fusion.89 = f32[768,2048]{1,0:T(8,128)S(1)} fusion(bf16[2048,768]{1,0:T(8,128)(2,1)S(1)} %bitcast.570, bf16[2048,2048]{1,0:T(8,128)(2,1)} %bitcast.561), kind=kOutput, calls=%fused_computation.384 | convolution fusion | flops 6442450944 | bytes 17825792 | tf_op jit(solution)/shard_map/sf,sd->fd/dot_general | solution.py:936
  542.0 7.4 fusion.90
  555.5 5.7 collective-permute-done.86
  571.7 7.4 fusion.91
  584.9 4.3 collective-permute-done.92
  597.2 4.9 convolution_convert_fusion.1
  606.9 3.5 convolution_convert_fusion.4
  610.5 20.8 %shard_map.268 = (bf16[4,3,64,1024]{3,2,1,0:T(8,128)(2,1)S(1)}, f32[4,4,3,64,256]{4,3,2,1,0:T(8,128)S(1)}, f32[8,128]{1,0:T(8,128)S(1)}) custom-call(s32[2]{0:T(128)S(1)} %pad_add_fusion.places_ref, f32[4,3,64,1024]{3,2,1,0:T(8,128)S(1)} %bitcast.551, bf16[4,3,64,1024]{3,2,1,0:T(8,128)(2,1)S(1)} %bitcast.556, ...), custom_call_target="tpu_custom_call" | custom-call | flops 8053063680 | bytes 16777216 | tf_op jit(solution)/shard_map/pallas_call | solution.py:788
  631.3 9.4 %collective-permute-done.95 = bf16[192,2048]{1,0:T(8,128)(2,1)S(1)} collective-permute-done((bf16[192,2048]{1,0:T(8,128)(2,1)}, bf16[192,2048]{1,0:T(8,128)(2,1)S(1)}, u32[]{:S(2)}, u32[]{:S(2)}) %collective-permute-start.95) | collective-permute-done | bytes 786464 | tf_op jit(solution)/shard_map/ppermute | solution.py:499
  643.2 3.7 convolution_convert_fusion
  655.4 5.5 fusion.92
  665.1 6.9 collective-permute-done.98
  672.0 15.0 %collective-permute-done.99 = bf16[4,3,64,256]{3,2,1,0:T(8,128)(2,1)S(1)} collective-permute-done((bf16[4,3,64,256]{3,2,1,0:T(8,128)(2,1)S(1)}, bf16[4,3,64,256]{3,2,1,0:T(8,128)(2,1)S(1)}, u32[]{:S(2)}, u32[]{:S(2)}) %collective-permute-start.99) | collective-permute-done | bytes 393248 | tf_op jit(solution)/shard_map/ppermute | solution.py:499
  699.0 17.5 %collective-permute-done.103 = bf16[4,64,1024]{2,1,0:T(8,128)(2,1)S(1)} collective-permute-done((bf16[4,64,1024]{2,1,0:T(8,128)(2,1)S(1)}, bf16[4,64,1024]{2,1,0:T(8,128)(2,1)S(1)}, u32[]{:S(2)}, u32[]{:S(2)}) %collective-permute-start.103) | collective-permute-done | bytes 524320 | tf_op jit(solution)/shard_map/ppermute | solution.py:499
  723.4 3.8 collective-permute-start.107
  728.9 11.0 %collective-permute-done.106 = bf16[4,64,1024]{2,1,0:T(8,128)(2,1)S(1)} collective-permute-done((bf16[4,64,1024]{2,1,0:T(8,128)(2,1)S(1)}, bf16[4,64,1024]{2,1,0:T(8,128)(2,1)S(1)}, u32[]{:S(2)}, u32[]{:S(2)}) %collective-permute-start.106) | collective-permute-done | bytes 524320 | tf_op jit(solution)/shard_map/ppermute | solution.py:499
  740.0 8.7 %collective-permute-done.107 = bf16[4,64,1024]{2,1,0:T(8,128)(2,1)S(1)} collective-permute-done((bf16[4,64,1024]{2,1,0:T(8,128)(2,1)S(1)}, bf16[4,64,1024]{2,1,0:T(8,128)(2,1)S(1)}, u32[]{:S(2)}, u32[]{:S(2)}) %collective-permute-start.107) | collective-permute-done | bytes 524320 | tf_op jit(solution)/shard_map/ppermute | solution.py:499
  755.5 3.8 collective-permute-start.112
  760.1 12.0 %collective-permute-done.111 = bf16[128,2048]{1,0:T(8,128)(2,1)S(1)} collective-permute-done((bf16[128,2048]{1,0:T(8,128)(2,1)S(1)}, bf16[128,2048]{1,0:T(8,128)(2,1)S(1)}, u32[]{:S(2)}, u32[]{:S(2)}) %collective-permute-start.111) | collective-permute-done | bytes 524320 | tf_op jit(solution)/shard_map/ppermute | solution.py:499
  772.1 7.2 collective-permute-done.112
  794.2 4.3 collective-permute-done.117
  808.2 15.8 %collective-permute-done.121 = bf16[128,2048]{1,0:T(8,128)(2,1)S(1)} collective-permute-done((bf16[128,2048]{1,0:T(8,128)(2,1)S(1)}, bf16[128,2048]{1,0:T(8,128)(2,1)S(1)}, u32[]{:S(2)}, u32[]{:S(2)}) %collective-permute-start.121) | collective-permute-done | bytes 524320 | tf_op jit(solution)/shard_map/ppermute | solution.py:499
  830.8 7.0 collective-permute-done.127
  837.8 7.3 collective-permute-done.126
  (810 shorter events, 323.7 us)
Async XLA Ops:
  62.0 32.5 %collective-permute-start.15 = (bf16[192,2048]{1,0:T(8,128)(2,1)}, bf16[192,2048]{1,0:T(8,128)(2,1)S(1)}, u32[]{:S(2)}, u32[]{:S(2)}) collective-permute-start(bf16[192,2048]{1,0:T(8,128)(2,1)} %copy-done.85), channel_id=1, source_target_pairs={{0,2},{2,0},{1,3},{3,1},{4,6},{6,4},{5,7},{7,5},{8,10},{10,8},{9,1... | collective-permute-start | bytes 2359304 | tf_op jit(solution)/shard_map/ppermute | solution.py:503
  62.1 32.4 %collective-permute-start.13 = (bf16[4,64,1280]{2,1,0:T(8,128)(2,1)}, bf16[4,64,1280]{2,1,0:T(8,128)(2,1)S(1)}, u32[]{:S(2)}, u32[]{:S(2)}) collective-permute-start(bf16[4,64,1280]{2,1,0:T(8,128)(2,1)} %copy-done.45), channel_id=1, source_target_pairs={{0,16},{8,24},{16,0},{24,8},{1,17},{9,25},{17,1},{25,9},{2,18},{10... | collective-permute-start | bytes 1966088 | tf_op jit(solution)/shard_map/ppermute | solution.py:499
  64.2 30.4 %collective-permute-start.14 = (bf16[4,64,1280]{2,1,0:T(8,128)(2,1)}, bf16[4,64,1280]{2,1,0:T(8,128)(2,1)S(1)}, u32[]{:S(2)}, u32[]{:S(2)}) collective-permute-start(bf16[4,64,1280]{2,1,0:T(8,128)(2,1)} %copy-done.108), channel_id=1, source_target_pairs={{0,1},{1,0},{2,3},{3,2},{4,5},{5,4},{6,7},{7,6},{8,9},{9,8},{10,11... | collective-permute-start | bytes 1966088 | tf_op jit(solution)/shard_map/ppermute | solution.py:503
  65.6 28.9 %collective-permute-start.17 = (bf16[128,2048]{1,0:T(8,128)(2,1)}, bf16[128,2048]{1,0:T(8,128)(2,1)S(1)}, u32[]{:S(2)}, u32[]{:S(2)}) collective-permute-start(bf16[128,2048]{1,0:T(8,128)(2,1)} %get-tuple-element.618), channel_id=1, source_target_pairs={{0,1},{1,0},{2,3},{3,2},{4,5},{5,4},{6,7},{7,6},{8,9},{9,8},{10,11... | collective-permute-start | bytes 1572872 | tf_op jit(solution)/shard_map/ppermute | solution.py:503
  119.0 28.5 %collective-permute-start.23 = (bf16[192,2048]{1,0:T(8,128)(2,1)S(1)}, bf16[192,2048]{1,0:T(8,128)(2,1)S(1)}, u32[]{:S(2)}, u32[]{:S(2)}) collective-permute-start(bf16[192,2048]{1,0:T(8,128)(2,1)S(1)} %copy-done.21), channel_id=1, source_target_pairs={{0,4},{4,0},{1,5},{5,1},{2,6},{6,2},{3,7},{7,3},{8,12},{12,8},{9,1... | collective-permute-start | bytes 2359304 | tf_op jit(solution)/shard_map/ppermute | solution.py:503
  120.2 27.2 %collective-permute-start.21 = (bf16[4,64,1280]{2,1,0:T(8,128)(2,1)}, bf16[4,64,1280]{2,1,0:T(8,128)(2,1)S(1)}, u32[]{:S(2)}, u32[]{:S(2)}) collective-permute-start(bf16[4,64,1280]{2,1,0:T(8,128)(2,1)} %collective-permute-done.18), channel_id=1, source_target_pairs={{0,1},{1,0},{2,3},{3,2},{4,5},{5,4},{6,7},{7,6},{8,9},{9,8},{10,11... | collective-permute-start | bytes 1966088 | tf_op jit(solution)/shard_map/ppermute | solution.py:503
  152.0 26.4 %collective-permute-start.25 = (bf16[2,128,2048]{2,1,0:T(8,128)(2,1)S(1)}, bf16[2,128,2048]{2,1,0:T(8,128)(2,1)S(1)}, u32[]{:S(2)}, u32[]{:S(2)}) collective-permute-start(bf16[2,128,2048]{2,1,0:T(8,128)(2,1)S(1)} %pad_maximum_fusion.5), channel_id=1, source_target_pairs={{0,4},{4,0},{1,5},{5,1},{2,6},{6,2},{3,7},{7,3},{8,12},{12,8},{9,1... | collective-permute-start | bytes 3145736 | tf_op jit(solution)/shard_map/ppermute | solution.py:503
  183.9 31.7 %collective-permute-start.33 = (bf16[2,128,2048]{2,1,0:T(8,128)(2,1)}, bf16[2,128,2048]{2,1,0:T(8,128)(2,1)S(1)}, u32[]{:S(2)}, u32[]{:S(2)}) collective-permute-start(bf16[2,128,2048]{2,1,0:T(8,128)(2,1)} %pad_maximum_fusion.6), channel_id=1, source_target_pairs={{0,1},{1,0},{2,3},{3,2},{4,5},{5,4},{6,7},{7,6},{8,9},{9,8},{10,11... | collective-permute-start | bytes 3145736 | tf_op jit(solution)/shard_map/ppermute | solution.py:503
  186.0 29.6 %collective-permute-start.31 = (bf16[4,3,64,256]{3,2,1,0:T(8,128)(2,1)}, bf16[4,3,64,256]{3,2,1,0:T(8,128)(2,1)S(1)}, u32[]{:S(2)}, u32[]{:S(2)}) collective-permute-start(bf16[4,3,64,256]{3,2,1,0:T(8,128)(2,1)} %pad_maximum_fusion.13), channel_id=1, source_target_pairs={{0,16},{8,24},{16,0},{24,8},{1,17},{9,25},{17,1},{25,9},{2,18},{10... | collective-permute-start | bytes 1179656 | tf_op jit(solution)/shard_map/ppermute | solution.py:499
  189.5 26.1 %collective-permute-start.32 = (bf16[4,3,64,256]{3,2,1,0:T(8,128)(2,1)}, bf16[4,3,64,256]{3,2,1,0:T(8,128)(2,1)S(1)}, u32[]{:S(2)}, u32[]{:S(2)}) collective-permute-start(bf16[4,3,64,256]{3,2,1,0:T(8,128)(2,1)} %pad_maximum_fusion.13), channel_id=1, source_target_pairs={{0,24},{8,0},{16,8},{24,16},{1,25},{9,1},{17,9},{25,17},{2,26},{10... | collective-permute-start | bytes 1179656 | tf_op jit(solution)/shard_map/ppermute | solution.py:499
  192.1 28.8 %collective-permute-start.35 = (bf16[128,2048]{1,0:T(8,128)(2,1)S(1)}, bf16[128,2048]{1,0:T(8,128)(2,1)S(1)}, u32[]{:S(2)}, u32[]{:S(2)}) collective-permute-start(bf16[128,2048]{1,0:T(8,128)(2,1)S(1)} %slice_bitcast_fusion.5), channel_id=1, source_target_pairs={{0,1},{1,0},{2,3},{3,2},{4,5},{5,4},{6,7},{7,6},{8,9},{9,8},{10,11... | collective-permute-start | bytes 1572872 | tf_op jit(solution)/shard_map/ppermute | solution.py:503
  283.2 37.6 %collective-permute-start.47 = (bf16[1024,768]{1,0:T(8,128)(2,1)S(1)}, bf16[1024,768]{1,0:T(8,128)(2,1)S(1)}, u32[]{:S(2)}, u32[]{:S(2)}) collective-permute-start(bf16[1024,768]{1,0:T(8,128)(2,1)S(1)} %bitcast.597), channel_id=1, source_target_pairs={{0,1},{1,0},{2,3},{3,2},{4,5},{5,4},{6,7},{7,6},{8,9},{9,8},{10,11... | collective-permute-start | bytes 4718600 | tf_op jit(solution)/shard_map/ppermute | solution.py:503
  284.1 36.6 %collective-permute-start.46 = (bf16[192,2048]{1,0:T(8,128)(2,1)S(1)}, bf16[192,2048]{1,0:T(8,128)(2,1)S(1)}, u32[]{:S(2)}, u32[]{:S(2)}) collective-permute-start(bf16[192,2048]{1,0:T(8,128)(2,1)S(1)} %multiply_convert_fusion.refs_1_), channel_id=1, source_target_pairs={{0,16},{8,24},{16,0},{24,8},{1,17},{9,25},{17,1},{25,9},{2,18},{10... | collective-permute-start | bytes 2359304 | tf_op jit(solution)/shard_map/ppermute | solution.py:499
  284.1 36.6 %collective-permute-start.48 = (bf16[192,2048]{1,0:T(8,128)(2,1)S(1)}, bf16[192,2048]{1,0:T(8,128)(2,1)S(1)}, u32[]{:S(2)}, u32[]{:S(2)}) collective-permute-start(bf16[192,2048]{1,0:T(8,128)(2,1)S(1)} %constant_dynamic-update-slice_fusion.3.refs_5_), channel_id=1, source_target_pairs={{0,4},{4,0},{1,5},{5,1},{2,6},{6,2},{3,7},{7,3},{8,12},{12,8},{9,1... | collective-permute-start | bytes 2359304 | tf_op jit(solution)/shard_map/ppermute | solution.py:503
  285.3 35.4 %collective-permute-start.49 = (bf16[192,2048]{1,0:T(8,128)(2,1)S(1)}, bf16[192,2048]{1,0:T(8,128)(2,1)S(1)}, u32[]{:S(2)}, u32[]{:S(2)}) collective-permute-start(bf16[192,2048]{1,0:T(8,128)(2,1)S(1)} %multiply_convert_fusion.refs_1_), channel_id=1, source_target_pairs={{0,4},{4,0},{1,5},{5,1},{2,6},{6,2},{3,7},{7,3},{8,12},{12,8},{9,1... | collective-permute-start | bytes 2359304 | tf_op jit(solution)/shard_map/ppermute | solution.py:503
  286.1 34.6 %collective-permute-start.50 = (bf16[192,2048]{1,0:T(8,128)(2,1)S(1)}, bf16[192,2048]{1,0:T(8,128)(2,1)S(1)}, u32[]{:S(2)}, u32[]{:S(2)}) collective-permute-start(bf16[192,2048]{1,0:T(8,128)(2,1)S(1)} %constant_dynamic-update-slice_fusion.3.refs_5_), channel_id=1, source_target_pairs={{0,2},{2,0},{1,3},{3,1},{4,6},{6,4},{5,7},{7,5},{8,10},{10,8},{9,1... | collective-permute-start | bytes 2359304 | tf_op jit(solution)/shard_map/ppermute | solution.py:503
  321.9 28.6 %collective-permute-start.51 = (bf16[192,2048]{1,0:T(8,128)(2,1)S(1)}, bf16[192,2048]{1,0:T(8,128)(2,1)S(1)}, u32[]{:S(2)}, u32[]{:S(2)}) collective-permute-start(bf16[192,2048]{1,0:T(8,128)(2,1)S(1)} %multiply_convert_fusion.refs_1_), channel_id=1, source_target_pairs={{0,8},{8,16},{16,24},{24,0},{1,9},{9,17},{17,25},{25,1},{2,10},{10... | collective-permute-start | bytes 2359304 | tf_op jit(solution)/shard_map/ppermute | solution.py:499
  355.1 30.7 %collective-permute-start.59 = (bf16[192,2048]{1,0:T(8,128)(2,1)S(1)}, bf16[192,2048]{1,0:T(8,128)(2,1)S(1)}, u32[]{:S(2)}, u32[]{:S(2)}) collective-permute-start(bf16[192,2048]{1,0:T(8,128)(2,1)S(1)} %multiply_convert_fusion.refs_1_), channel_id=1, source_target_pairs={{0,24},{8,0},{16,8},{24,16},{1,25},{9,1},{17,9},{25,17},{2,26},{10... | collective-permute-start | bytes 2359304 | tf_op jit(solution)/shard_map/ppermute | solution.py:499
  358.1 27.7 %collective-permute-start.61 = (bf16[192,2048]{1,0:T(8,128)(2,1)S(1)}, bf16[192,2048]{1,0:T(8,128)(2,1)S(1)}, u32[]{:S(2)}, u32[]{:S(2)}) collective-permute-start(bf16[192,2048]{1,0:T(8,128)(2,1)S(1)} %collective-permute-done.51.refs_1_), channel_id=1, source_target_pairs={{0,4},{4,0},{1,5},{5,1},{2,6},{6,2},{3,7},{7,3},{8,12},{12,8},{9,1... | collective-permute-start | bytes 2359304 | tf_op jit(solution)/shard_map/ppermute | solution.py:503
  359.3 26.5 %collective-permute-start.63 = (bf16[192,2048]{1,0:T(8,128)(2,1)S(1)}, bf16[192,2048]{1,0:T(8,128)(2,1)}, u32[]{:S(2)}, u32[]{:S(2)}) collective-permute-start(bf16[192,2048]{1,0:T(8,128)(2,1)S(1)} %collective-permute-done.51.refs_1_), channel_id=1, source_target_pairs={{0,2},{2,0},{1,3},{3,1},{4,6},{6,4},{5,7},{7,5},{8,10},{10,8},{9,1... | collective-permute-start | bytes 2359304 | tf_op jit(solution)/shard_map/ppermute | solution.py:503
  388.2 28.5 %collective-permute-start.69 = (bf16[2,192,2176]{2,1,0:T(8,128)(2,1)}, bf16[2,192,2176]{2,1,0:T(8,128)(2,1)}, u32[]{:S(2)}, u32[]{:S(2)}) collective-permute-start(bf16[2,192,2176]{2,1,0:T(8,128)(2,1)} %get-tuple-element.790), channel_id=1, source_target_pairs={{0,2},{2,0},{1,3},{3,1},{4,6},{6,4},{5,7},{7,5},{8,10},{10,8},{9,1... | collective-permute-start | bytes 5013512 | tf_op jit(solution)/shard_map/ppermute | solution.py:503
  388.4 28.3 %collective-permute-start.65 = (bf16[192,2048]{1,0:T(8,128)(2,1)S(1)}, bf16[192,2048]{1,0:T(8,128)(2,1)}, u32[]{:S(2)}, u32[]{:S(2)}) collective-permute-start(bf16[192,2048]{1,0:T(8,128)(2,1)S(1)} %collective-permute-done.59.refs_1_), channel_id=1, source_target_pairs={{0,4},{4,0},{1,5},{5,1},{2,6},{6,2},{3,7},{7,3},{8,12},{12,8},{9,1... | collective-permute-start | bytes 2359304 | tf_op jit(solution)/shard_map/ppermute | solution.py:503
  389.7 27.0 %collective-permute-start.67 = (bf16[192,2048]{1,0:T(8,128)(2,1)S(1)}, bf16[192,2048]{1,0:T(8,128)(2,1)}, u32[]{:S(2)}, u32[]{:S(2)}) collective-permute-start(bf16[192,2048]{1,0:T(8,128)(2,1)S(1)} %collective-permute-done.59.refs_1_), channel_id=1, source_target_pairs={{0,2},{2,0},{1,3},{3,1},{4,6},{6,4},{5,7},{7,5},{8,10},{10,8},{9,1... | collective-permute-start | bytes 2359304 | tf_op jit(solution)/shard_map/ppermute | solution.py:503
  389.8 26.9 %collective-permute-start.68 = (bf16[192,2048]{1,0:T(8,128)(2,1)S(1)}, bf16[192,2048]{1,0:T(8,128)(2,1)}, u32[]{:S(2)}, u32[]{:S(2)}) collective-permute-start(bf16[192,2048]{1,0:T(8,128)(2,1)S(1)} %pad_maximum_fusion.11.refs_5_), channel_id=1, source_target_pairs={{0,2},{2,0},{1,3},{3,1},{4,6},{6,4},{5,7},{7,5},{8,10},{10,8},{9,1... | collective-permute-start | bytes 2359304 | tf_op jit(solution)/shard_map/ppermute | solution.py:503
  390.2 26.5 %collective-permute-start.66 = (bf16[96,2048]{1,0:T(8,128)(2,1)}, bf16[96,2048]{1,0:T(8,128)(2,1)S(1)}, u32[]{:S(2)}, u32[]{:S(2)}) collective-permute-start(bf16[96,2048]{1,0:T(8,128)(2,1)} %collective-permute-done.60), channel_id=1, source_target_pairs={{0,4},{4,0},{1,5},{5,1},{2,6},{6,2},{3,7},{7,3},{8,12},{12,8},{9,1... | collective-permute-start | bytes 1179656 | tf_op jit(solution)/shard_map/ppermute | solution.py:503
  424.2 38.8 %collective-permute-start.75 = (bf16[2,192,2176]{2,1,0:T(8,128)(2,1)}, bf16[2,192,2176]{2,1,0:T(8,128)(2,1)}, u32[]{:S(2)}, u32[]{:S(2)}) collective-permute-start(bf16[2,192,2176]{2,1,0:T(8,128)(2,1)} %get-tuple-element.842), channel_id=1, source_target_pairs={{0,2},{2,0},{1,3},{3,1},{4,6},{6,4},{5,7},{7,5},{8,10},{10,8},{9,1... | collective-permute-start | bytes 5013512 | tf_op jit(solution)/shard_map/ppermute | solution.py:503
  424.4 38.6 %collective-permute-start.76 = (bf16[2,192,2048]{2,1,0:T(8,128)(2,1)}, bf16[2,192,2048]{2,1,0:T(8,128)(2,1)}, u32[]{:S(2)}, u32[]{:S(2)}) collective-permute-start(bf16[2,192,2048]{2,1,0:T(8,128)(2,1)} %get-tuple-element.843), channel_id=1, source_target_pairs={{0,2},{2,0},{1,3},{3,1},{4,6},{6,4},{5,7},{7,5},{8,10},{10,8},{9,1... | collective-permute-start | bytes 4718600 | tf_op jit(solution)/shard_map/ppermute | solution.py:503
  425.4 37.6 %collective-permute-start.73 = (bf16[192,2176]{1,0:T(8,128)(2,1)S(1)}, bf16[192,2176]{1,0:T(8,128)(2,1)}, u32[]{:S(2)}, u32[]{:S(2)}) collective-permute-start(bf16[192,2176]{1,0:T(8,128)(2,1)S(1)} %fusion.38), channel_id=1, source_target_pairs={{0,4},{4,0},{1,5},{5,1},{2,6},{6,2},{3,7},{7,3},{8,12},{12,8},{9,1... | collective-permute-start | bytes 2506760 | tf_op jit(solution)/shard_map/ppermute | solution.py:503
  426.6 36.3 %collective-permute-start.74 = (bf16[192,2048]{1,0:T(8,128)(2,1)}, bf16[192,2048]{1,0:T(8,128)(2,1)}, u32[]{:S(2)}, u32[]{:S(2)}) collective-permute-start(bf16[192,2048]{1,0:T(8,128)(2,1)} %fusion.42), channel_id=1, source_target_pairs={{0,4},{4,0},{1,5},{5,1},{2,6},{6,2},{3,7},{7,3},{8,12},{12,8},{9,1... | collective-permute-start | bytes 2359304 | tf_op jit(solution)/shard_map/ppermute | solution.py:503
  470.4 40.5 %collective-permute-start.80 = (bf16[2,192,2176]{2,1,0:T(8,128)(2,1)}, bf16[2,192,2176]{2,1,0:T(8,128)(2,1)}, u32[]{:S(2)}, u32[]{:S(2)}) collective-permute-start(bf16[2,192,2176]{2,1,0:T(8,128)(2,1)} %get-tuple-element.888), channel_id=1, source_target_pairs={{0,2},{2,0},{1,3},{3,1},{4,6},{6,4},{5,7},{7,5},{8,10},{10,8},{9,1... | collective-permute-start | bytes 5013512 | tf_op jit(solution)/shard_map/ppermute | solution.py:503
  470.4 40.5 %collective-permute-start.81 = (bf16[2,192,2048]{2,1,0:T(8,128)(2,1)}, bf16[2,192,2048]{2,1,0:T(8,128)(2,1)}, u32[]{:S(2)}, u32[]{:S(2)}) collective-permute-start(bf16[2,192,2048]{2,1,0:T(8,128)(2,1)} %get-tuple-element.889), channel_id=1, source_target_pairs={{0,2},{2,0},{1,3},{3,1},{4,6},{6,4},{5,7},{7,5},{8,10},{10,8},{9,1... | collective-permute-start | bytes 4718600 | tf_op jit(solution)/shard_map/ppermute | solution.py:503
  471.7 39.1 %collective-permute-start.77 = (bf16[192,2176]{1,0:T(8,128)(2,1)}, bf16[192,2176]{1,0:T(8,128)(2,1)S(1)}, u32[]{:S(2)}, u32[]{:S(2)}) collective-permute-start(bf16[192,2176]{1,0:T(8,128)(2,1)} %fusion.11), channel_id=1, source_target_pairs={{0,16},{8,24},{16,0},{24,8},{1,17},{9,25},{17,1},{25,9},{2,18},{10... | collective-permute-start | bytes 2506760 | tf_op jit(solution)/shard_map/ppermute | solution.py:499
  471.8 39.1 %collective-permute-start.78 = (bf16[192,2176]{1,0:T(8,128)(2,1)}, bf16[192,2176]{1,0:T(8,128)(2,1)}, u32[]{:S(2)}, u32[]{:S(2)}) collective-permute-start(bf16[192,2176]{1,0:T(8,128)(2,1)} %fusion.39), channel_id=1, source_target_pairs={{0,4},{4,0},{1,5},{5,1},{2,6},{6,2},{3,7},{7,3},{8,12},{12,8},{9,1... | collective-permute-start | bytes 2506760 | tf_op jit(solution)/shard_map/ppermute | solution.py:503
  473.1 36.4 %collective-permute-start.79 = (bf16[192,2048]{1,0:T(8,128)(2,1)}, bf16[192,2048]{1,0:T(8,128)(2,1)}, u32[]{:S(2)}, u32[]{:S(2)}) collective-permute-start(bf16[192,2048]{1,0:T(8,128)(2,1)} %fusion.43), channel_id=1, source_target_pairs={{0,4},{4,0},{1,5},{5,1},{2,6},{6,2},{3,7},{7,3},{8,12},{12,8},{9,1... | collective-permute-start | bytes 2359304 | tf_op jit(solution)/shard_map/ppermute | solution.py:503
  602.6 38.2 %collective-permute-start.94 = (bf16[3,128,2048]{2,1,0:T(8,128)(2,1)S(1)}, bf16[3,128,2048]{2,1,0:T(8,128)(2,1)S(1)}, u32[]{:S(2)}, u32[]{:S(2)}) collective-permute-start(bf16[3,128,2048]{2,1,0:T(8,128)(2,1)S(1)} %dynamic-slice_bitcast_fusion.1), channel_id=1, source_target_pairs={{0,1},{1,0},{2,3},{3,2},{4,5},{5,4},{6,7},{7,6},{8,9},{9,8},{10,11... | collective-permute-start | bytes 4718600 | tf_op jit(solution)/shard_map/ppermute | solution.py:503
  603.7 37.1 %collective-permute-start.95 = (bf16[192,2048]{1,0:T(8,128)(2,1)}, bf16[192,2048]{1,0:T(8,128)(2,1)S(1)}, u32[]{:S(2)}, u32[]{:S(2)}) collective-permute-start(bf16[192,2048]{1,0:T(8,128)(2,1)} %fusion.28), channel_id=1, source_target_pairs={{0,16},{8,24},{16,0},{24,8},{1,17},{9,25},{17,1},{25,9},{2,18},{10... | collective-permute-start | bytes 2359304 | tf_op jit(solution)/shard_map/ppermute | solution.py:499
  604.9 35.8 %collective-permute-start.96 = (bf16[192,2048]{1,0:T(8,128)(2,1)}, bf16[192,2048]{1,0:T(8,128)(2,1)}, u32[]{:S(2)}, u32[]{:S(2)}) collective-permute-start(bf16[192,2048]{1,0:T(8,128)(2,1)} %fusion.44), channel_id=1, source_target_pairs={{0,4},{4,0},{1,5},{5,1},{2,6},{6,2},{3,7},{7,3},{8,12},{12,8},{9,1... | collective-permute-start | bytes 2359304 | tf_op jit(solution)/shard_map/ppermute | solution.py:503
  605.7 35.1 %collective-permute-start.97 = (bf16[192,2048]{1,0:T(8,128)(2,1)}, bf16[192,2048]{1,0:T(8,128)(2,1)S(1)}, u32[]{:S(2)}, u32[]{:S(2)}) collective-permute-start(bf16[192,2048]{1,0:T(8,128)(2,1)} %fusion.45), channel_id=1, source_target_pairs={{0,4},{4,0},{1,5},{5,1},{2,6},{6,2},{3,7},{7,3},{8,12},{12,8},{9,1... | collective-permute-start | bytes 2359304 | tf_op jit(solution)/shard_map/ppermute | solution.py:503
  648.9 38.1 %collective-permute-start.101 = (bf16[512,1024]{1,0:T(8,128)(2,1)S(1)}, bf16[512,1024]{1,0:T(8,128)(2,1)S(1)}, u32[]{:S(2)}, u32[]{:S(2)}) collective-permute-start(bf16[512,1024]{1,0:T(8,128)(2,1)S(1)} %pad_maximum_fusion.8), channel_id=1, source_target_pairs={{0,1},{1,0},{2,3},{3,2},{4,5},{5,4},{6,7},{7,6},{8,9},{9,8},{10,11... | collective-permute-start | bytes 3145736 | tf_op jit(solution)/shard_map/ppermute | solution.py:503
  649.9 37.0 %collective-permute-start.102 = (bf16[2,128,2048]{2,1,0:T(8,128)(2,1)S(1)}, bf16[2,128,2048]{2,1,0:T(8,128)(2,1)S(1)}, u32[]{:S(2)}, u32[]{:S(2)}) collective-permute-start(bf16[2,128,2048]{2,1,0:T(8,128)(2,1)S(1)} %fusion.1), channel_id=1, source_target_pairs={{0,4},{4,0},{1,5},{5,1},{2,6},{6,2},{3,7},{7,3},{8,12},{12,8},{9,1... | collective-permute-start | bytes 3145736 | tf_op jit(solution)/shard_map/ppermute | solution.py:503
  654.5 32.5 %collective-permute-start.99 = (bf16[4,3,64,256]{3,2,1,0:T(8,128)(2,1)S(1)}, bf16[4,3,64,256]{3,2,1,0:T(8,128)(2,1)S(1)}, u32[]{:S(2)}, u32[]{:S(2)}) collective-permute-start(bf16[4,3,64,256]{3,2,1,0:T(8,128)(2,1)S(1)} %get-tuple-element.989), channel_id=1, source_target_pairs={{0,16},{8,24},{16,0},{24,8},{1,17},{9,25},{17,1},{25,9},{2,18},{10... | collective-permute-start | bytes 1179656 | tf_op jit(solution)/shard_map/ppermute | solution.py:499
  689.7 26.8 %collective-permute-start.104 = (bf16[2,4,64,1024]{3,2,1,0:T(8,128)(2,1)S(1)}, bf16[2,4,64,1024]{3,2,1,0:T(8,128)(2,1)S(1)}, u32[]{:S(2)}, u32[]{:S(2)}) collective-permute-start(bf16[2,4,64,1024]{3,2,1,0:T(8,128)(2,1)S(1)} %pad_maximum_fusion.9), channel_id=1, source_target_pairs={{0,1},{1,0},{2,3},{3,2},{4,5},{5,4},{6,7},{7,6},{8,9},{9,8},{10,11... | collective-permute-start | bytes 3145736 | tf_op jit(solution)/shard_map/ppermute | solution.py:503
  690.8 25.6 %collective-permute-start.105 = (bf16[2,128,2048]{2,1,0:T(8,128)(2,1)S(1)}, bf16[2,128,2048]{2,1,0:T(8,128)(2,1)S(1)}, u32[]{:S(2)}, u32[]{:S(2)}) collective-permute-start(bf16[2,128,2048]{2,1,0:T(8,128)(2,1)S(1)} %pad_maximum_fusion.10), channel_id=1, source_target_pairs={{0,2},{2,0},{1,3},{3,1},{4,6},{6,4},{5,7},{7,5},{8,10},{10,8},{9,1... | collective-permute-start | bytes 3145736 | tf_op jit(solution)/shard_map/ppermute | solution.py:503
  719.8 31.0 %collective-permute-start.110 = (bf16[2,192,2048]{2,1,0:T(8,128)(2,1)}, bf16[2,192,2048]{2,1,0:T(8,128)(2,1)}, u32[]{:S(2)}, u32[]{:S(2)}) collective-permute-start(bf16[2,192,2048]{2,1,0:T(8,128)(2,1)} %bitcast.164), channel_id=1, source_target_pairs={{0,2},{2,0},{1,3},{3,1},{4,6},{6,4},{5,7},{7,5},{8,10},{10,8},{9,1... | collective-permute-start | bytes 4718600 | tf_op jit(solution)/shard_map/ppermute | solution.py:503
  722.4 28.4 %collective-permute-start.109 = (bf16[4,4,80,256]{3,2,1,0:T(8,128)(2,1)S(1)}, bf16[4,4,80,256]{3,2,1,0:T(8,128)(2,1)S(1)}, u32[]{:S(2)}, u32[]{:S(2)}) collective-permute-start(bf16[4,4,80,256]{3,2,1,0:T(8,128)(2,1)S(1)} %copy-done.112), channel_id=1, source_target_pairs={{0,1},{1,0},{2,3},{3,2},{4,5},{5,4},{6,7},{7,6},{8,9},{9,8},{10,11... | collective-permute-start | bytes 1966088 | tf_op jit(solution)/shard_map/ppermute | solution.py:503
  752.1 28.6 %collective-permute-start.113 = (bf16[192,2048]{1,0:T(8,128)(2,1)S(1)}, bf16[192,2048]{1,0:T(8,128)(2,1)S(1)}, u32[]{:S(2)}, u32[]{:S(2)}) collective-permute-start(bf16[192,2048]{1,0:T(8,128)(2,1)S(1)} %fusion.46), channel_id=1, source_target_pairs={{0,4},{4,0},{1,5},{5,1},{2,6},{6,2},{3,7},{7,3},{8,12},{12,8},{9,1... | collective-permute-start | bytes 2359304 | tf_op jit(solution)/shard_map/ppermute | solution.py:503
  753.4 25.9 %collective-permute-start.114 = (bf16[384,768]{1,0:T(8,128)(2,1)S(1)}, bf16[384,768]{1,0:T(8,128)(2,1)S(1)}, u32[]{:S(2)}, u32[]{:S(2)}) collective-permute-start(bf16[384,768]{1,0:T(8,128)(2,1)S(1)} %slice.573), channel_id=1, source_target_pairs={{0,1},{1,0},{2,3},{3,2},{4,5},{5,4},{6,7},{7,6},{8,9},{9,8},{10,11... | collective-permute-start | bytes 1769480 | tf_op jit(solution)/shard_map/ppermute | solution.py:503
  754.4 26.3 %collective-permute-start.115 = (bf16[144,2048]{1,0:T(8,128)(2,1)S(1)}, bf16[144,2048]{1,0:T(8,128)(2,1)S(1)}, u32[]{:S(2)}, u32[]{:S(2)}) collective-permute-start(bf16[144,2048]{1,0:T(8,128)(2,1)S(1)} %slice.574), channel_id=1, source_target_pairs={{0,1},{1,0},{2,3},{3,2},{4,5},{5,4},{6,7},{7,6},{8,9},{9,8},{10,11... | collective-permute-start | bytes 1769480 | tf_op jit(solution)/shard_map/ppermute | solution.py:503
  (244 other events, 3065.0 us)

commit v4 on v3

--- a/solution.py
+++ b/solution.py
@@ -1040,36 +1040,40 @@
     )
     width = part0.shape[-1]
     inputs = tokens.astype(wide)
-    (far, plane3, *small), (normed_attn, inverse_attn), _ = step(
-        [(parts_far, "y"), (w_output, "z", 3)] + [(packed, "z", k) for k in range(1, nz)],
-        lambda tokens: rms_apply(tokens.astype(wide), attention_gain),
-        (tokens,),
+
+    def first_members(part0, part1, parts_far, tokens):
+        far = swap(parts_far, "y")
+        near = swap(jnp.stack([part1, far[1]]), "c")
+        blocks = [part0, near[0], far[0], near[1]]
+        return uncrossed(blocks), rms_apply(tokens.astype(wide), attention_gain)
+
+    (plane3, *small), (ordered, (normed_attn, inverse_attn)), _ = step(
+        [(w_output, "z", 3)] + [(packed, "z", k) for k in range(1, nz)],
+        first_members,
+        (part0, part1, parts_far, tokens),
     )
     packed = jnp.stack([packed] + small)
     normed_low = normed_attn.astype(low)
-    (near, other), _, _ = step([(jnp.stack([part1, far[1]]), "c"), (packed, "y")])
-    packed = jnp.stack([packed, other], 1)
-    ordered = uncrossed([part0, near[0], far[0], near[1]])
     held = [ordered]
     over_x = []
-    (moved, cross, other, near, packed_near), _, _ = step(
+    (moved, cross, other, near, packed_far), _, _ = step(
         [
             (ordered, "z", 1),
             (ordered, "x"),
             (normed_low, "y"),
             (normed_low, "c"),
-            (packed, "c"),
+            (packed, "y"),
         ]
     )
     held.append(moved)
     over_x.append(cross)
-    packed = jnp.stack([packed, packed_near], 1)
-    (moved, cross, other_near, packed_cross, down1), tables, _ = step(
+    packed = jnp.stack([packed, packed_far], 1)
+    (moved, cross, other_near, packed_near, down1), tables, _ = step(
         [
             (ordered, "z", 2),
             (held[1], "x"),
             (other, "c"),
-            (packed, "x"),
+            (packed, "c"),
             (w_down[0, third : 2 * third], "x"),
         ],
         make_tables,
@@ -1079,16 +1083,26 @@
     held.append(moved)
     over_x.append(cross)
     normed_all = jnp.concatenate([normed_low, other, near, other_near])
+    packed = jnp.stack([packed, packed_near], 1)
+    (moved, cross, c_near0, packed_cross), _, _ = step(
+        [(ordered, "z", 3), (held[2], "x"), (cotangent, "c"), (packed, "x")]
+    )
     packed = jnp.stack([packed, packed_cross], 1)
-    (moved, cross, c_near0), (router, ranks, chosen_all), _ = step(
-        [(ordered, "z", 3), (held[2], "x"), (cotangent, "c")], make_slots, (packed,)
-    )
     held.append(moved)
     over_x.append(cross)
-    (cross, plane2, c_far0, down0), (planes,), _ = step(
+    cut = rows // 2
+    gate_cut = w_gate.shape[1] * 5 // 16
+    gate_next = w_gate.shape[1] * 9 // 16
+
+    def cut_pieces(own, one, three, gate, down, cotangent):
+        gates = (gate[:gate_cut], gate[gate_cut:gate_next], gate[gate_next:])
+        halves = (cotangent[:cut], cotangent[cut:])
+        return jnp.stack([own, one, one, three]), gates, down[2 * third :], halves
+
+    (cross, plane2, c_far0, down0), (planes, gate_pieces, down_piece, c_halves), _ = step(
         [(held[3], "x"), (w_output, "z", 2), (cotangent, "y"), (w_down[0, :third], "x")],
-        lambda own, one, three: (jnp.stack([own, one, one, three]),),
-        (w_output, plane1, plane3),
+        cut_pieces,
+        (w_output, plane1, plane3, w_gate[0], w_down[0], cotangent),
     )
     over_x.append(cross)
 
@@ -1117,15 +1131,12 @@
 
     planes = lax.dynamic_update_index_in_dim(planes, plane2, 2, 0)
     wanted = [pick(planes, lax.rem(zi + nz - crossed[r], jnp.int32(nz))) for r in range(MEMBERS)]
-    cut = rows // 2
-    gate_cut = w_gate.shape[1] * 5 // 16
-    gate_next = w_gate.shape[1] * 9 // 16
     moved, (key_proj, key_inverse, key_value), _ = step(
         [
             (jnp.stack(wanted[2:]), "y"),
             (cotangent, "z", 1),
-            (w_down[0, 2 * third :], "x"),
-            (w_gate[0, :gate_cut], "x"),
+            (down_piece, "x"),
+            (gate_pieces[0], "x"),
             (c_far0, "c"),
         ],
         project_keys,
@@ -1156,9 +1167,9 @@
     (cross_last, c2_low, c_far1, gate1), attended, _ = step(
         [
             (near[1], "x"),
-            (cotangent[:cut], "z", 2),
+            (c_halves[0], "z", 2),
             (c1, "y"),
-            (w_gate[0, gate_cut:gate_next], "x"),
+            (gate_pieces[1], "x"),
         ],
         attend,
         (places, queries, key_value, kernel_cosine, kernel_sine, gain_row, mask),
@@ -1172,28 +1183,21 @@
 
     mixed_part = jnp.dot(attended, output_weight, preferred_element_type=wide)
     mixed_part = mixed_part.reshape(2, 2, rows, model)
-    (near, c_near1), _, _ = step([(mixed_part[1].astype(low), "c"), (c1, "c")])
-    summed_far = (mixed_part[0, 1] + near[1].astype(wide)).astype(low)
-    (other, gate2, c2_high, c_far_near1), _, _ = step(
-        [
-            (summed_far, "y"),
-            (w_gate[0, gate_next:], "x"),
-            (cotangent[cut:], "z", 2),
-            (c_far1, "c"),
-        ]
+
+    def summed_members(own, send):
+        near = swap(send, "c")
+        far = swap((own[1] + near[1].astype(wide)).astype(low), "y")
+        return own[0] + near[0].astype(wide) + far.astype(wide)
+
+    (gate2, c2_high, c_near1), mixed_sum, _ = step(
+        [(gate_pieces[2], "x"), (c_halves[1], "z", 2), (c1, "c")],
+        summed_members,
+        (mixed_part[0], mixed_part[1].astype(low)),
     )
     c2 = jnp.concatenate([c2_low, c2_high])
-    mixed_attn = inputs + (mixed_part[0, 0] + near[0].astype(wide) + other.astype(wide))
+    mixed_attn = inputs + mixed_sum
     normed_ffn, inverse_ffn = rms_apply(mixed_attn, ffn_gain)
     ffn_low = normed_ffn.astype(low)
-
-    logits = dot32("td,ed->te", ffn_low, router)
-    chosen = jnp.any(
-        expert_ids[:, :, None] == jnp.arange(experts_all, dtype=jnp.int32)[None, None, :], 1
-    )
-    highest = jnp.max(jnp.where(chosen, logits, NEGATIVE_LIMIT), 1, keepdims=True)
-    raised = jnp.where(chosen, jnp.exp(jnp.minimum(logits - highest, 0.0)), 0.0)
-    gates = raised / jnp.sum(raised, 1, keepdims=True)
 
     def whole(own, others):
         full = jnp.zeros((2,) + own.shape, low)
@@ -1218,7 +1222,7 @@
         far = swap(block, "y")
         return far, swap(far, "c")
 
-    (x2, up_other, c_far2, y0, c_near2), (gate_all, down_all), _ = step(
+    moved, ((gate_all, down_all), (router, ranks, chosen_all)), _ = step(
         [
             (ffn_low, "z", 2),
             (w_up[0], "x"),
@@ -1226,13 +1230,26 @@
             (ffn_low, "y"),
             (c2, "c"),
         ],
-        lambda owns, others: [whole(own, other) for own, other in zip(owns, others)],
-        ([w_gate[0], w_down[0]], [[gate0, gate1, gate2], [down0, down1, down2]]),
-    )
+        lambda owns, others, packed: (
+            [whole(own, other) for own, other in zip(owns, others)],
+            make_slots(packed),
+        ),
+        ([w_gate[0], w_down[0]], [[gate0, gate1, gate2], [down0, down1, down2]], packed),
+    )
+    x2, up_other, c_far2, y0, c_near2 = moved
+
+    logits = dot32("td,ed->te", ffn_low, router)
+    chosen = jnp.any(
+        expert_ids[:, :, None] == jnp.arange(experts_all, dtype=jnp.int32)[None, None, :], 1
+    )
+    highest = jnp.max(jnp.where(chosen, logits, NEGATIVE_LIMIT), 1, keepdims=True)
+    raised = jnp.where(chosen, jnp.exp(jnp.minimum(logits - highest, 0.0)), 0.0)
+    gates = raised / jnp.sum(raised, 1, keepdims=True)
+
     (x1, c3_low, y2, n2, c_far_near2), up_all, _ = step(
         [
             (ffn_low, "z", 1),
-            (cotangent[:cut], "z", 3),
+            (c_halves[0], "z", 3),
             (x2, "y"),
             (x2, "c"),
             (c_far2, "c"),
@@ -1241,11 +1258,13 @@
         (w_up[0], up_other),
     )
     weights = [gate_all, up_all, down_all]
-    (ny2, n0, ny0), _, _ = step([(y2, "c"), (ffn_low, "c"), (y0, "c")])
+    (ny2, n0, ny0, c_far_near1), _, _ = step(
+        [(y2, "c"), (ffn_low, "c"), (y0, "c"), (c_far1, "c")]
+    )
     (x3, c3_high, y1, c_far3_low, n1), (kept, mixed2, rows2), _ = step(
         [
             (ffn_low, "z", 3),
-            (cotangent[cut:], "z", 3),
+            (c_halves[1], "z", 3),
             (x1, "y"),
             (c3_low, "y"),
             (x1, "c"),
@@ -1253,17 +1272,17 @@
         functools.partial(run_experts, 2),
         ([x2, n2, y2, ny2], [c2, c_near2, c_far2, c_far_near2], (), weights),
     )
-    (ny1,), c3, _ = step(
-        [(y1, "c")], lambda *halves: jnp.concatenate(halves), (c3_low, c3_high)
-    )
-    (y3, c_far3_high, n3, c_near3, back2), (kept, mixed1, rows1), _ = step(
-        [(x3, "y"), (c3_high, "y"), (x3, "c"), (c3, "c"), (rows2[1], "c")],
+    (ny1, n3), c3, _ = step(
+        [(y1, "c"), (x3, "c")], lambda *halves: jnp.concatenate(halves), (c3_low, c3_high)
+    )
+    (y3, c_far3_high, c_near3, back2, mixed_back2), (kept, mixed1, rows1), _ = step(
+        [(x3, "y"), (c3_high, "y"), (c3, "c"), (rows2[1], "c"), (mixed2[1], "c")],
         functools.partial(run_experts, 1),
         ([x1, n1, y1, ny1], [c1, c_near1, c_far1, c_far_near1], kept, weights),
     )
     c_far3 = jnp.concatenate([c_far3_low, c_far3_high])
-    (ny3, c_far_near3, mixed_back2), row_send2, _ = step(
-        [(y3, "c"), (c_far3, "c"), (mixed2[1], "c")],
+    (ny3, c_far_near3), row_send2, _ = step(
+        [(y3, "c"), (c_far3, "c")],
         lambda pair, back: added(pair, back, 1).astype(low),
         (rows2, back2),
     )
@@ -1298,10 +1317,13 @@
         block.reshape(context_count * slots, -1) for block in kept
     )
 
-    def halved(grad):
+    def halved(grad, sixteenths):
         size = grad.shape[0] // 2
+        cut = size * sixteenths // 16
         own = lax.dynamic_slice_in_dim(grad, xi * size, size, 0)
-        return own, lax.dynamic_slice_in_dim(grad, (1 - xi) * size, size, 0).astype(low)
+        first = lax.dynamic_slice_in_dim(grad, (1 - xi) * size, cut, 0)
+        rest = lax.dynamic_slice_in_dim(grad, (1 - xi) * size + cut, size - cut, 0)
+        return own, first.astype(low), rest.astype(low)
 
     def joined(own, moved):
         return (own + jnp.concatenate(moved, 0).astype(wide))[None]
@@ -1311,25 +1333,24 @@
     def total(pair, back, far):
         return (added(pair, back, 0) + far.astype(wide)).astype(low)
 
-    (z1, far3, back0, mixed_back0), ((down_grad, down_send), mixed_send1), _ = step(
+    (z1, far3, back0, mixed_back0), ((down_grad, down_first, down_rest), mixed_send1), _ = step(
         [
             (total1, "z", -1),
             (added(rows3, back3, 1).astype(low), "y"),
             (rows0[1], "c"),
             (mixed0[1], "c"),
         ],
-        lambda rows, grad, *given: (halved(dot32("sf,sd->fd", rows, grad)), total(*given)),
+        lambda rows, grad, *given: (halved(dot32("sf,sd->fd", rows, grad), 10), total(*given)),
         (hidden_low, dresults, mixed1, mixed_back1, mixed_far1),
     )
     total3 = (added(rows3, back3, 0) + far3.astype(wide)).astype(low)
-    down_cut = down_send.shape[0] * 5 // 8
-    (z3, far0, down0), ((gate_grad, gate_send), mixed_send2), _ = step(
+    (z3, far0, down0), ((gate_grad, gate_first, gate_rest), mixed_send2), _ = step(
         [
             (total3, "z", -3),
             (added(rows0, back0, 1).astype(low), "y"),
-            (down_send[:down_cut], "x"),
+            (down_first, "x"),
         ],
-        lambda rows, grad, *given: (halved(dot32("sd,sf->df", rows, grad)), total(*given)),
+        lambda rows, grad, *given: (halved(dot32("sd,sf->df", rows, grad), 10), total(*given)),
         (expert_rows, dgate_low, mixed2, mixed_back2, mixed_far2),
     )
     returned = added(rows0, back0, 0) + far0.astype(wide) + z1.astype(wide)
@@ -1349,20 +1370,23 @@
     dmixed_norm, ffn_gain_part = rms_back(mixed_attn, inverse_ffn, ffn_gain, dffn_rows)
     dmixed_attn = upstream + dmixed_norm
     dattn_low = dmixed_attn.astype(low)
-    gate_cut = gate_send.shape[0] * 5 // 8
-    moved, (up_grad, up_send), _ = step(
+    moved, (up_grad, up_first, up_rest), _ = step(
         [
             (dattn_low, "y"),
             (dattn_low, "c"),
-            (gate_send[:gate_cut], "x"),
+            (gate_first, "x"),
             (mixed_send1, "z", -1),
         ],
-        lambda rows, grad: halved(dot32("sd,sf->df", rows, grad)),
+        lambda rows, grad: halved(dot32("sd,sf->df", rows, grad), 11),
         (expert_rows, dup_low),
     )
     other, near, gate0, mixed_z1 = moved
-    (other_near,), _, _ = step([(other, "c")])
-    dattn_all = jnp.concatenate([dattn_low, other, near, other_near])
+    (other_near,), (dattn_all,), _ = step(
+        [(other, "c")],
+        lambda *blocks: (jnp.concatenate(blocks),),
+        (dattn_low, other, near, dattn_low),
+    )
+    dattn_all = lax.dynamic_update_slice_in_dim(dattn_all, other_near, 3 * rows, 0)
 
     output_part = dot32("tc,td->cd", attended, dattn_all).astype(low)
     output_part = output_part.reshape(MEMBERS, 2, head_rows, model)
@@ -1489,8 +1513,8 @@
             (output_sends[1], "z", 1),
             (output_sends[3], "z", 3),
             (dnormed_far, "y"),
-            (gate_send[gate_cut:], "x"),
-            (down_send[down_cut:], "x"),
+            (gate_rest, "x"),
+            (down_rest, "x"),
         ],
         total_queries,
         (query_planes[0][0], cross, query_z1, query_z2, query_z3),
@@ -1513,11 +1537,10 @@
     def member_columns(parts):
         return uncrossed(parts).astype(wide).transpose(1, 0, 2)
 
-    up_cut = up_send.shape[0] * 11 // 16
     (output_z2, up0, key_far, small_y, query_near), (down_grad, gate_grad), _ = step(
         [
             (output_sends[2], "z", 2),
-            (up_send[:up_cut], "x"),
+            (up_first, "x"),
             (jnp.stack(key_parts[2:]), "y"),
             (small, "y"),
             (jnp.stack([query_parts[1], query_far[1]]), "c"),
@@ -1530,7 +1553,7 @@
     (mixed_z3, up1, key_near, small_c), (query_grad, output_grad), _ = step(
         [
             (mixed_send3, "z", -3),
-            (up_send[up_cut:], "x"),
+            (up_rest, "x"),
             (jnp.stack([key_parts[1], key_far[1]]), "c"),
             (small, "c"),
         ],

time: 866 us -> 852 us (0.984)
    ppermute x41, waiting for transfers between devices: 264 us -> 218 us  [shift(): lax.ppermute(block, axis, [(i, (i + step) % count) for i in range(count)])]
    ppermute x92, waiting for transfers between devices: 105 us -> 144 us  [swap(): return lax.ppermute(block, axis, [(0, 1), (1, 0)])]
    unnamed x327 -> x331, local copies, waits for them, and re-layouts: 28.8 us -> 21.5 us
  transfers between devices with their start and end apart: 133 -> 133, of which waited for: 51 -> 55; matrix products, arithmetic and copies ran while one was open for 16% -> 18% of each run, Pallas kernels for 15% -> 15%
where the time goes in v4:
time: 852 us; the launch traced here: 842 us
  waiting for transfers between devices  362 us (42%)
  Pallas kernels  128 us (15%)
  starting transfers between devices  127 us (15%)
  local copies, waits for them, and re-layouts  93.3 us (11%)
  other arithmetic  73.1 us (9%)
  matrix products  55 us (6%)
    ppermute x41, waiting for transfers between devices, shift(): lax.ppermute(block, axis, [(i, (i + step) % count) for i in range(count)])  218 us
    ppermute x92, waiting for transfers between devices, swap(): return lax.ppermute(block, axis, [(0, 1), (1, 0)])  144 us
    pallas_call x4, Pallas kernels, experts(): pl.pallas_call(expert_kernel, grid_spec=pltpu.PrefetchScalarGridSpec(num_...  94.5 us
    ppermute x92, starting transfers between devices, swap(): return lax.ppermute(block, axis, [(0, 1), (1, 0)])  64.6 us
    ppermute x41, starting transfers between devices, shift(): lax.ppermute(block, axis, [(i, (i + step) % count) for i in range(count)])  62.6 us
    dot_general x13, matrix products, dot32(): jnp.einsum(subscripts, left, right, preferred_element_type=jnp.float32)  44.5 us
    unnamed x331, local copies, waits for them, and re-layouts  21.5 us
    pallas_call x1, Pallas kernels, attend_back(): pl.pallas_call(attend_back_kernel, grid_spec=pltpu.PrefetchScalarGridSpec...  20.8 us
  transfers between devices with their start and end apart: 133, of which 55 were waited for; matrix products, arithmetic and copies ran while one was open for 18% of the time, Pallas kernels for 15%

profile of v4, /device:TPU:0, one launch (start us, length us, event | category | flops | bytes accessed | tf_op | source)
XLA Modules:
  0.0 841.8 jit_solution(3715741935042949068)
XLA Ops:
  9.6 8.4 collective-permute-done
  28.9 3.9 collective-permute-done.2
  41.7 11.7 %collective-permute-done.11 = bf16[4,20,128]{2,1,0:T(8,128)(2,1)S(1)} collective-permute-done((bf16[4,20,128]{2,1,0:T(8,128)(2,1)S(1)}, bf16[4,20,128]{2,1,0:T(8,128)(2,1)S(1)}, u32[]{:S(2)}, u32[]{:S(2)}) %collective-permute-start.11) | collective-permute-done | bytes 20512 | tf_op jit(solution)/shard_map/ppermute | solution.py:503
  68.6 18.9 %collective-permute-done.16 = bf16[128,2048]{1,0:T(8,128)(2,1)S(1)} collective-permute-done((bf16[128,2048]{1,0:T(8,128)(2,1)}, bf16[128,2048]{1,0:T(8,128)(2,1)S(1)}, u32[]{:S(2)}, u32[]{:S(2)}) %collective-permute-start.16) | collective-permute-done | bytes 524320 | tf_op jit(solution)/shard_map/ppermute | solution.py:503
  89.4 3.5 collective-permute-start.17
  97.3 14.6 %collective-permute-done.20 = bf16[4,2,2,20,128]{4,3,2,1,0:T(8,128)(2,1)S(1)} collective-permute-done((bf16[4,2,2,20,128]{4,3,2,1,0:T(8,128)(2,1)S(1)}, bf16[4,2,2,20,128]{4,3,2,1,0:T(8,128)(2,1)S(1)}, u32[]{:S(2)}, u32[]{:S(2)}) %collective-permute-start.20) | collective-permute-done | bytes 81952 | tf_op jit(solution)/shard_map/ppermute | solution.py:503
  121.7 15.0 %collective-permute-done.22 = bf16[128,2048]{1,0:T(8,128)(2,1)S(1)} collective-permute-done((bf16[128,2048]{1,0:T(8,128)(2,1)S(1)}, bf16[128,2048]{1,0:T(8,128)(2,1)S(1)}, u32[]{:S(2)}, u32[]{:S(2)}) %collective-permute-start.22) | collective-permute-done | bytes 524320 | tf_op jit(solution)/shard_map/ppermute | solution.py:499
  148.6 19.8 %collective-permute-done.28 = bf16[320,768]{1,0:T(8,128)(2,1)S(1)} collective-permute-done((bf16[320,768]{1,0:T(8,128)(2,1)S(1)}, bf16[320,768]{1,0:T(8,128)(2,1)S(1)}, u32[]{:S(2)}, u32[]{:S(2)}) %collective-permute-start.28) | collective-permute-done | bytes 491552 | tf_op jit(solution)/shard_map/ppermute | solution.py:503
  172.9 4.4 collective-permute-start.31
  178.1 6.1 fusion.82
  186.9 16.4 %collective-permute-done.31 = bf16[4,3,64,256]{3,2,1,0:T(8,128)(2,1)S(1)} collective-permute-done((bf16[4,3,64,256]{3,2,1,0:T(8,128)(2,1)}, bf16[4,3,64,256]{3,2,1,0:T(8,128)(2,1)S(1)}, u32[]{:S(2)}, u32[]{:S(2)}) %collective-permute-start.31) | collective-permute-done | bytes 393248 | tf_op jit(solution)/shard_map/ppermute | solution.py:499
  203.4 5.0 collective-permute-done.35
  216.1 12.2 %shard_map.263 = bf16[4,3,64,1024]{3,2,1,0:T(8,128)(2,1)S(1)} custom-call(s32[2]{0:T(128)S(1)} %pad_add_fusion.places_ref, f32[4,3,64,1024]{3,2,1,0:T(8,128)S(1)} %bitcast.524, bf16[4,4,3,64,256]{4,3,2,1,0:T(8,128)(2,1)S(1)} %pad_maximum_fusion.4.k_ref.v_ref, bf16[4,4,3,64,256]{4,3,2,1,0:T(8,128)(2,1)S(1)} %pad_maximum_fusion.4.k_ref.v_ref, ...), custom_call_target="tpu_custom_call" | custom-call | flops 3221225472 | bytes 8388608 | tf_op jit(solution)/shard_map/pallas_call | solution.py:768
  233.7 3.4 fusion.83
  250.5 12.8 %collective-permute-done.44 = bf16[192,2048]{1,0:T(8,128)(2,1)} collective-permute-done((bf16[192,2048]{1,0:T(8,128)(2,1)}, bf16[192,2048]{1,0:T(8,128)(2,1)}, u32[]{:S(2)}, u32[]{:S(2)}) %collective-permute-start.44) | collective-permute-done | bytes 786464 | tf_op jit(solution)/shard_map/ppermute | solution.py:503
  294.0 15.8 %collective-permute-done.45.refs_1_ = bf16[192,2048]{1,0:T(8,128)(2,1)} collective-permute-done((bf16[192,2048]{1,0:T(8,128)(2,1)S(1)}, bf16[192,2048]{1,0:T(8,128)(2,1)}, u32[]{:S(2)}, u32[]{:S(2)}) %collective-permute-start.45) | collective-permute-done | bytes 786464 | tf_op jit(solution)/shard_map/ppermute | solution.py:499
  322.4 16.5 %collective-permute-done.51 = bf16[96,2048]{1,0:T(8,128)(2,1)} collective-permute-done((bf16[96,2048]{1,0:T(8,128)(2,1)S(1)}, bf16[96,2048]{1,0:T(8,128)(2,1)}, u32[]{:S(2)}, u32[]{:S(2)}) %collective-permute-start.51) | collective-permute-done | bytes 393248 | tf_op jit(solution)/shard_map/ppermute | solution.py:499
  349.0 23.4 %shard_map.264 = (bf16[4,4,128,2048]{3,2,1,0:T(8,128)(2,1)}, bf16[4,4,128,768]{3,2,1,0:T(8,128)(2,1)}, bf16[4,4,128,2048]{3,2,1,0:T(8,128)(2,1)}, bf16[4,4,128,7...) custom-call(s32[2]{0:T(128)} %get-tuple-element.1338.refs_0_, ...), custom_call_target="tpu_custom_call" | custom-call | flops 9663676416 | bytes 41943040 | tf_op jit(solution)/shard_map/pallas_call | solution.py:919
  381.7 23.6 %shard_map.265 = (bf16[4,4,128,2048]{3,2,1,0:T(8,128)(2,1)}, bf16[4,4,128,768]{3,2,1,0:T(8,128)(2,1)}, bf16[4,4,128,2048]{3,2,1,0:T(8,128)(2,1)}, bf16[4,4,128,7...) custom-call(s32[2]{0:T(128)} %get-tuple-element.1339.refs_0_, ...), custom_call_target="tpu_custom_call", output_to_operand_aliasing={{0}: (15, {}), {1}: (16, {}), {2}: (17, {}), {3}: (18, {}),... | custom-call | flops 9663676416 | bytes 41943040 | tf_op jit(solution)/shard_map/pallas_call | solution.py:919
  418.2 23.6 %shard_map.266 = (bf16[4,4,128,2048]{3,2,1,0:T(8,128)(2,1)}, bf16[4,4,128,768]{3,2,1,0:T(8,128)(2,1)}, bf16[4,4,128,2048]{3,2,1,0:T(8,128)(2,1)}, bf16[4,4,128,7...) custom-call(s32[2]{0:T(128)} %get-tuple-element.1340.refs_0_, ...), custom_call_target="tpu_custom_call", output_to_operand_aliasing={{0}: (15, {}), {1}: (16, {}), {2}: (17, {}), {3}: (18, {}),... | custom-call | flops 9663676416 | bytes 41943040 | tf_op jit(solution)/shard_map/pallas_call | solution.py:919
  441.8 12.5 %collective-permute-done.74 = bf16[192,2048]{1,0:T(8,128)(2,1)} collective-permute-done((bf16[192,2048]{1,0:T(8,128)(2,1)}, bf16[192,2048]{1,0:T(8,128)(2,1)}, u32[]{:S(2)}, u32[]{:S(2)}) %collective-permute-start.74) | collective-permute-done | bytes 786464 | tf_op jit(solution)/shard_map/ppermute | solution.py:503
  465.3 23.9 %shard_map.267 = (bf16[4,4,128,2048]{3,2,1,0:T(8,128)(2,1)}, bf16[4,4,128,768]{3,2,1,0:T(8,128)(2,1)}, bf16[4,4,128,2048]{3,2,1,0:T(8,128)(2,1)}, bf16[4,4,128,7...) custom-call(s32[2]{0:T(128)} %get-tuple-element.1341.refs_0_, ...), custom_call_target="tpu_custom_call", output_to_operand_aliasing={{0}: (15, {}), {1}: (16, {}), {2}: (17, {}), {3}: (18, {}),... | custom-call | flops 9663676416 | bytes 41943040 | tf_op jit(solution)/shard_map/pallas_call | solution.py:919
  489.2 11.6 %collective-permute-done.79 = bf16[192,2048]{1,0:T(8,128)(2,1)S(1)} collective-permute-done((bf16[192,2048]{1,0:T(8,128)(2,1)}, bf16[192,2048]{1,0:T(8,128)(2,1)S(1)}, u32[]{:S(2)}, u32[]{:S(2)}) %collective-permute-start.79) | collective-permute-done | bytes 786464 | tf_op jit(solution)/shard_map/ppermute | solution.py:503
  508.4 9.3 %fusion.84 = f32[768,2048]{1,0:T(8,128)S(1)} fusion(bf16[2048,768]{1,0:T(8,128)(2,1)S(1)} %bitcast.536, bf16[2048,2048]{1,0:T(8,128)(2,1)} %bitcast.535), kind=kOutput, calls=%fused_computation.380 | convolution fusion | flops 6442450944 | bytes 17825792 | tf_op jit(solution)/shard_map/sf,sd->fd/dot_general | solution.py:936
  533.0 7.3 fusion.85
  545.9 7.0 collective-permute-done.86
  561.6 7.3 fusion.86
  575.8 4.1 collective-permute-done.92
  586.1 3.8 convolution_convert_fusion.1
  594.0 3.4 convolution_convert_fusion.4
  597.5 20.8 %shard_map.268 = (bf16[4,3,64,1024]{3,2,1,0:T(8,128)(2,1)S(1)}, f32[4,4,3,64,256]{4,3,2,1,0:T(8,128)S(1)}, f32[8,128]{1,0:T(8,128)S(1)}) custom-call(s32[2]{0:T(128)S(1)} %pad_add_fusion.places_ref, f32[4,3,64,1024]{3,2,1,0:T(8,128)S(1)} %bitcast.525, bf16[4,3,64,1024]{3,2,1,0:T(8,128)(2,1)S(1)} %bitcast.530, ...), custom_call_target="tpu_custom_call" | custom-call | flops 8053063680 | bytes 16777216 | tf_op jit(solution)/shard_map/pallas_call | solution.py:788
  618.3 10.3 %collective-permute-done.95 = bf16[192,2048]{1,0:T(8,128)(2,1)S(1)} collective-permute-done((bf16[192,2048]{1,0:T(8,128)(2,1)}, bf16[192,2048]{1,0:T(8,128)(2,1)S(1)}, u32[]{:S(2)}, u32[]{:S(2)}) %collective-permute-start.95) | collective-permute-done | bytes 786464 | tf_op jit(solution)/shard_map/ppermute | solution.py:499
  631.1 3.7 convolution_convert_fusion
  643.6 5.4 fusion.87
  653.2 7.0 collective-permute-done.98
  660.2 15.3 %collective-permute-done.99 = bf16[4,3,64,256]{3,2,1,0:T(8,128)(2,1)S(1)} collective-permute-done((bf16[4,3,64,256]{3,2,1,0:T(8,128)(2,1)S(1)}, bf16[4,3,64,256]{3,2,1,0:T(8,128)(2,1)S(1)}, u32[]{:S(2)}, u32[]{:S(2)}) %collective-permute-start.99) | collective-permute-done | bytes 393248 | tf_op jit(solution)/shard_map/ppermute | solution.py:499
  687.9 16.8 %collective-permute-done.103 = bf16[4,64,1024]{2,1,0:T(8,128)(2,1)S(1)} collective-permute-done((bf16[4,64,1024]{2,1,0:T(8,128)(2,1)S(1)}, bf16[4,64,1024]{2,1,0:T(8,128)(2,1)S(1)}, u32[]{:S(2)}, u32[]{:S(2)}) %collective-permute-start.103) | collective-permute-done | bytes 524320 | tf_op jit(solution)/shard_map/ppermute | solution.py:499
  707.7 3.8 collective-permute-start.107
  713.0 11.6 %collective-permute-done.106 = bf16[4,64,1024]{2,1,0:T(8,128)(2,1)S(1)} collective-permute-done((bf16[4,64,1024]{2,1,0:T(8,128)(2,1)}, bf16[4,64,1024]{2,1,0:T(8,128)(2,1)S(1)}, u32[]{:S(2)}, u32[]{:S(2)}) %collective-permute-start.106) | collective-permute-done | bytes 524320 | tf_op jit(solution)/shard_map/ppermute | solution.py:499
  724.5 8.6 %collective-permute-done.107 = bf16[4,64,1024]{2,1,0:T(8,128)(2,1)S(1)} collective-permute-done((bf16[4,64,1024]{2,1,0:T(8,128)(2,1)}, bf16[4,64,1024]{2,1,0:T(8,128)(2,1)S(1)}, u32[]{:S(2)}, u32[]{:S(2)}) %collective-permute-start.107) | collective-permute-done | bytes 524320 | tf_op jit(solution)/shard_map/ppermute | solution.py:499
  738.9 3.8 collective-permute-start.112
  743.6 12.0 %collective-permute-done.111 = bf16[128,2048]{1,0:T(8,128)(2,1)S(1)} collective-permute-done((bf16[128,2048]{1,0:T(8,128)(2,1)S(1)}, bf16[128,2048]{1,0:T(8,128)(2,1)S(1)}, u32[]{:S(2)}, u32[]{:S(2)}) %collective-permute-start.111) | collective-permute-done | bytes 524320 | tf_op jit(solution)/shard_map/ppermute | solution.py:499
  755.6 7.2 collective-permute-done.112
  778.4 4.2 collective-permute-done.117
  792.6 16.7 %collective-permute-done.121 = bf16[128,2048]{1,0:T(8,128)(2,1)S(1)} collective-permute-done((bf16[128,2048]{1,0:T(8,128)(2,1)S(1)}, bf16[128,2048]{1,0:T(8,128)(2,1)S(1)}, u32[]{:S(2)}, u32[]{:S(2)}) %collective-permute-start.121) | collective-permute-done | bytes 524320 | tf_op jit(solution)/shard_map/ppermute | solution.py:499
  809.4 3.4 collective-permute-start.126
  816.1 8.7 %collective-permute-done.127 = bf16[320,768]{1,0:T(8,128)(2,1)S(1)} collective-permute-done((bf16[320,768]{1,0:T(8,128)(2,1)S(1)}, bf16[320,768]{1,0:T(8,128)(2,1)S(1)}, u32[]{:S(2)}, u32[]{:S(2)}) %collective-permute-start.127) | collective-permute-done | bytes 491552 | tf_op jit(solution)/shard_map/ppermute | solution.py:503
  824.8 5.5 collective-permute-done.126
  (815 shorter events, 323.8 us)
Async XLA Ops:
  56.6 32.2 %collective-permute-start.14 = (bf16[192,2048]{1,0:T(8,128)(2,1)}, bf16[192,2048]{1,0:T(8,128)(2,1)S(1)}, u32[]{:S(2)}, u32[]{:S(2)}) collective-permute-start(bf16[192,2048]{1,0:T(8,128)(2,1)} %copy-done.83), channel_id=1, source_target_pairs={{0,2},{2,0},{1,3},{3,1},{4,6},{6,4},{5,7},{7,5},{8,10},{10,8},{9,1... | collective-permute-start | bytes 2359304 | tf_op jit(solution)/shard_map/ppermute | solution.py:503
  56.6 32.1 %collective-permute-start.12 = (bf16[4,64,1280]{2,1,0:T(8,128)(2,1)S(1)}, bf16[4,64,1280]{2,1,0:T(8,128)(2,1)S(1)}, u32[]{:S(2)}, u32[]{:S(2)}) collective-permute-start(bf16[4,64,1280]{2,1,0:T(8,128)(2,1)S(1)} %pad_maximum_fusion.12), channel_id=1, source_target_pairs={{0,16},{8,24},{16,0},{24,8},{1,17},{9,25},{17,1},{25,9},{2,18},{10... | collective-permute-start | bytes 1966088 | tf_op jit(solution)/shard_map/ppermute | solution.py:499
  59.2 29.5 %collective-permute-start.13 = (bf16[4,64,1280]{2,1,0:T(8,128)(2,1)}, bf16[4,64,1280]{2,1,0:T(8,128)(2,1)S(1)}, u32[]{:S(2)}, u32[]{:S(2)}) collective-permute-start(bf16[4,64,1280]{2,1,0:T(8,128)(2,1)} %copy-done.106), channel_id=1, source_target_pairs={{0,1},{1,0},{2,3},{3,2},{4,5},{5,4},{6,7},{7,6},{8,9},{9,8},{10,11... | collective-permute-start | bytes 1966088 | tf_op jit(solution)/shard_map/ppermute | solution.py:503
  60.7 26.8 %collective-permute-start.16 = (bf16[128,2048]{1,0:T(8,128)(2,1)}, bf16[128,2048]{1,0:T(8,128)(2,1)S(1)}, u32[]{:S(2)}, u32[]{:S(2)}) collective-permute-start(bf16[128,2048]{1,0:T(8,128)(2,1)} %get-tuple-element.634), channel_id=1, source_target_pairs={{0,1},{1,0},{2,3},{3,2},{4,5},{5,4},{6,7},{7,6},{8,9},{9,8},{10,11... | collective-permute-start | bytes 1572872 | tf_op jit(solution)/shard_map/ppermute | solution.py:503
  111.8 27.5 %collective-permute-start.23 = (bf16[192,2048]{1,0:T(8,128)(2,1)S(1)}, bf16[192,2048]{1,0:T(8,128)(2,1)S(1)}, u32[]{:S(2)}, u32[]{:S(2)}) collective-permute-start(bf16[192,2048]{1,0:T(8,128)(2,1)S(1)} %copy-done.20), channel_id=1, source_target_pairs={{0,4},{4,0},{1,5},{5,1},{2,6},{6,2},{3,7},{7,3},{8,12},{12,8},{9,1... | collective-permute-start | bytes 2359304 | tf_op jit(solution)/shard_map/ppermute | solution.py:503
  112.4 26.9 %collective-permute-start.21 = (bf16[4,64,1280]{2,1,0:T(8,128)(2,1)S(1)}, bf16[4,64,1280]{2,1,0:T(8,128)(2,1)S(1)}, u32[]{:S(2)}, u32[]{:S(2)}) collective-permute-start(bf16[4,64,1280]{2,1,0:T(8,128)(2,1)S(1)} %collective-permute-done.17), channel_id=1, source_target_pairs={{0,1},{1,0},{2,3},{3,2},{4,5},{5,4},{6,7},{7,6},{8,9},{9,8},{10,11... | collective-permute-start | bytes 1966088 | tf_op jit(solution)/shard_map/ppermute | solution.py:503
  142.1 26.4 %collective-permute-start.25 = (bf16[2,128,2048]{2,1,0:T(8,128)(2,1)S(1)}, bf16[2,128,2048]{2,1,0:T(8,128)(2,1)S(1)}, u32[]{:S(2)}, u32[]{:S(2)}) collective-permute-start(bf16[2,128,2048]{2,1,0:T(8,128)(2,1)S(1)} %pad_maximum_fusion.5), channel_id=1, source_target_pairs={{0,4},{4,0},{1,5},{5,1},{2,6},{6,2},{3,7},{7,3},{8,12},{12,8},{9,1... | collective-permute-start | bytes 3145736 | tf_op jit(solution)/shard_map/ppermute | solution.py:503
  171.4 32.0 %collective-permute-start.33 = (bf16[2,128,2048]{2,1,0:T(8,128)(2,1)}, bf16[2,128,2048]{2,1,0:T(8,128)(2,1)S(1)}, u32[]{:S(2)}, u32[]{:S(2)}) collective-permute-start(bf16[2,128,2048]{2,1,0:T(8,128)(2,1)} %pad_maximum_fusion.6), channel_id=1, source_target_pairs={{0,1},{1,0},{2,3},{3,2},{4,5},{5,4},{6,7},{7,6},{8,9},{9,8},{10,11... | collective-permute-start | bytes 3145736 | tf_op jit(solution)/shard_map/ppermute | solution.py:503
  172.9 30.5 %collective-permute-start.31 = (bf16[4,3,64,256]{3,2,1,0:T(8,128)(2,1)}, bf16[4,3,64,256]{3,2,1,0:T(8,128)(2,1)S(1)}, u32[]{:S(2)}, u32[]{:S(2)}) collective-permute-start(bf16[4,3,64,256]{3,2,1,0:T(8,128)(2,1)} %pad_maximum_fusion.13), channel_id=1, source_target_pairs={{0,16},{8,24},{16,0},{24,8},{1,17},{9,25},{17,1},{25,9},{2,18},{10... | collective-permute-start | bytes 1179656 | tf_op jit(solution)/shard_map/ppermute | solution.py:499
  177.3 26.1 %collective-permute-start.32 = (bf16[4,3,64,256]{3,2,1,0:T(8,128)(2,1)}, bf16[4,3,64,256]{3,2,1,0:T(8,128)(2,1)S(1)}, u32[]{:S(2)}, u32[]{:S(2)}) collective-permute-start(bf16[4,3,64,256]{3,2,1,0:T(8,128)(2,1)} %pad_maximum_fusion.13), channel_id=1, source_target_pairs={{0,24},{8,0},{16,8},{24,16},{1,25},{9,1},{17,9},{25,17},{2,26},{10... | collective-permute-start | bytes 1179656 | tf_op jit(solution)/shard_map/ppermute | solution.py:499
  177.5 30.9 %collective-permute-start.35 = (bf16[128,2048]{1,0:T(8,128)(2,1)S(1)}, bf16[128,2048]{1,0:T(8,128)(2,1)S(1)}, u32[]{:S(2)}, u32[]{:S(2)}) collective-permute-start(bf16[128,2048]{1,0:T(8,128)(2,1)S(1)} %slice_bitcast_fusion.2), channel_id=1, source_target_pairs={{0,1},{1,0},{2,3},{3,2},{4,5},{5,4},{6,7},{7,6},{8,9},{9,8},{10,11... | collective-permute-start | bytes 1572872 | tf_op jit(solution)/shard_map/ppermute | solution.py:503
  271.5 38.3 %collective-permute-start.46 = (bf16[1024,768]{1,0:T(8,128)(2,1)}, bf16[1024,768]{1,0:T(8,128)(2,1)}, u32[]{:S(2)}, u32[]{:S(2)}) collective-permute-start(bf16[1024,768]{1,0:T(8,128)(2,1)} %bitcast.93), channel_id=1, source_target_pairs={{0,1},{1,0},{2,3},{3,2},{4,5},{5,4},{6,7},{7,6},{8,9},{9,8},{10,11... | collective-permute-start | bytes 4718600 | tf_op jit(solution)/shard_map/ppermute | solution.py:503
  273.1 36.7 %collective-permute-start.45 = (bf16[192,2048]{1,0:T(8,128)(2,1)S(1)}, bf16[192,2048]{1,0:T(8,128)(2,1)}, u32[]{:S(2)}, u32[]{:S(2)}) collective-permute-start(bf16[192,2048]{1,0:T(8,128)(2,1)S(1)} %multiply_convert_fusion.refs_1_), channel_id=1, source_target_pairs={{0,16},{8,24},{16,0},{24,8},{1,17},{9,25},{17,1},{25,9},{2,18},{10... | collective-permute-start | bytes 2359304 | tf_op jit(solution)/shard_map/ppermute | solution.py:499
  273.1 36.7 %collective-permute-start.47 = (bf16[192,2048]{1,0:T(8,128)(2,1)}, bf16[192,2048]{1,0:T(8,128)(2,1)}, u32[]{:S(2)}, u32[]{:S(2)}) collective-permute-start(bf16[192,2048]{1,0:T(8,128)(2,1)} %copy-done.132), channel_id=1, source_target_pairs={{0,4},{4,0},{1,5},{5,1},{2,6},{6,2},{3,7},{7,3},{8,12},{12,8},{9,1... | collective-permute-start | bytes 2359304 | tf_op jit(solution)/shard_map/ppermute | solution.py:503
  273.9 35.9 %collective-permute-start.48 = (bf16[192,2048]{1,0:T(8,128)(2,1)S(1)}, bf16[192,2048]{1,0:T(8,128)(2,1)}, u32[]{:S(2)}, u32[]{:S(2)}) collective-permute-start(bf16[192,2048]{1,0:T(8,128)(2,1)S(1)} %multiply_convert_fusion.refs_1_), channel_id=1, source_target_pairs={{0,4},{4,0},{1,5},{5,1},{2,6},{6,2},{3,7},{7,3},{8,12},{12,8},{9,1... | collective-permute-start | bytes 2359304 | tf_op jit(solution)/shard_map/ppermute | solution.py:503
  275.2 34.6 %collective-permute-start.49 = (bf16[192,2048]{1,0:T(8,128)(2,1)}, bf16[192,2048]{1,0:T(8,128)(2,1)}, u32[]{:S(2)}, u32[]{:S(2)}) collective-permute-start(bf16[192,2048]{1,0:T(8,128)(2,1)} %copy-done.132), channel_id=1, source_target_pairs={{0,2},{2,0},{1,3},{3,1},{4,6},{6,4},{5,7},{7,5},{8,10},{10,8},{9,1... | collective-permute-start | bytes 2359304 | tf_op jit(solution)/shard_map/ppermute | solution.py:503
  309.8 29.1 %collective-permute-start.50 = (bf16[192,2048]{1,0:T(8,128)(2,1)S(1)}, bf16[192,2048]{1,0:T(8,128)(2,1)S(1)}, u32[]{:S(2)}, u32[]{:S(2)}) collective-permute-start(bf16[192,2048]{1,0:T(8,128)(2,1)S(1)} %multiply_convert_fusion.refs_1_), channel_id=1, source_target_pairs={{0,8},{8,16},{16,24},{24,0},{1,9},{9,17},{17,25},{25,1},{2,10},{10... | collective-permute-start | bytes 2359304 | tf_op jit(solution)/shard_map/ppermute | solution.py:499
  312.8 26.1 %collective-permute-start.52 = (bf16[192,2048]{1,0:T(8,128)(2,1)}, bf16[192,2048]{1,0:T(8,128)(2,1)S(1)}, u32[]{:S(2)}, u32[]{:S(2)}) collective-permute-start(bf16[192,2048]{1,0:T(8,128)(2,1)} %collective-permute-done.45.refs_1_), channel_id=1, source_target_pairs={{0,4},{4,0},{1,5},{5,1},{2,6},{6,2},{3,7},{7,3},{8,12},{12,8},{9,1... | collective-permute-start | bytes 2359304 | tf_op jit(solution)/shard_map/ppermute | solution.py:503
  344.7 29.9 %collective-permute-start.59 = (bf16[192,2048]{1,0:T(8,128)(2,1)S(1)}, bf16[192,2048]{1,0:T(8,128)(2,1)S(1)}, u32[]{:S(2)}, u32[]{:S(2)}) collective-permute-start(bf16[192,2048]{1,0:T(8,128)(2,1)S(1)} %multiply_convert_fusion.refs_1_), channel_id=1, source_target_pairs={{0,24},{8,0},{16,8},{24,16},{1,25},{9,1},{17,9},{25,17},{2,26},{10... | collective-permute-start | bytes 2359304 | tf_op jit(solution)/shard_map/ppermute | solution.py:499
  346.8 27.8 %collective-permute-start.61 = (bf16[192,2048]{1,0:T(8,128)(2,1)S(1)}, bf16[192,2048]{1,0:T(8,128)(2,1)S(1)}, u32[]{:S(2)}, u32[]{:S(2)}) collective-permute-start(bf16[192,2048]{1,0:T(8,128)(2,1)S(1)} %collective-permute-done.50.refs_1_), channel_id=1, source_target_pairs={{0,4},{4,0},{1,5},{5,1},{2,6},{6,2},{3,7},{7,3},{8,12},{12,8},{9,1... | collective-permute-start | bytes 2359304 | tf_op jit(solution)/shard_map/ppermute | solution.py:503
  347.3 27.3 %collective-permute-start.63 = (bf16[192,2048]{1,0:T(8,128)(2,1)S(1)}, bf16[192,2048]{1,0:T(8,128)(2,1)S(1)}, u32[]{:S(2)}, u32[]{:S(2)}) collective-permute-start(bf16[192,2048]{1,0:T(8,128)(2,1)S(1)} %collective-permute-done.50.refs_1_), channel_id=1, source_target_pairs={{0,2},{2,0},{1,3},{3,1},{4,6},{6,4},{5,7},{7,5},{8,10},{10,8},{9,1... | collective-permute-start | bytes 2359304 | tf_op jit(solution)/shard_map/ppermute | solution.py:503
  347.8 26.8 %collective-permute-start.62 = (bf16[96,2048]{1,0:T(8,128)(2,1)}, bf16[96,2048]{1,0:T(8,128)(2,1)}, u32[]{:S(2)}, u32[]{:S(2)}) collective-permute-start(bf16[96,2048]{1,0:T(8,128)(2,1)} %collective-permute-done.51), channel_id=1, source_target_pairs={{0,4},{4,0},{1,5},{5,1},{2,6},{6,2},{3,7},{7,3},{8,12},{12,8},{9,1... | collective-permute-start | bytes 1179656 | tf_op jit(solution)/shard_map/ppermute | solution.py:503
  378.1 30.0 %collective-permute-start.69 = (bf16[2,192,2176]{2,1,0:T(8,128)(2,1)}, bf16[2,192,2176]{2,1,0:T(8,128)(2,1)S(1)}, u32[]{:S(2)}, u32[]{:S(2)}) collective-permute-start(bf16[2,192,2176]{2,1,0:T(8,128)(2,1)} %get-tuple-element.816), channel_id=1, source_target_pairs={{0,2},{2,0},{1,3},{3,1},{4,6},{6,4},{5,7},{7,5},{8,10},{10,8},{9,1... | collective-permute-start | bytes 5013512 | tf_op jit(solution)/shard_map/ppermute | solution.py:503
  378.2 29.8 %collective-permute-start.70 = (bf16[2,192,2048]{2,1,0:T(8,128)(2,1)}, bf16[2,192,2048]{2,1,0:T(8,128)(2,1)}, u32[]{:S(2)}, u32[]{:S(2)}) collective-permute-start(bf16[2,192,2048]{2,1,0:T(8,128)(2,1)} %get-tuple-element.817), channel_id=1, source_target_pairs={{0,2},{2,0},{1,3},{3,1},{4,6},{6,4},{5,7},{7,5},{8,10},{10,8},{9,1... | collective-permute-start | bytes 4718600 | tf_op jit(solution)/shard_map/ppermute | solution.py:503
  379.6 28.4 %collective-permute-start.66 = (bf16[192,2048]{1,0:T(8,128)(2,1)}, bf16[192,2048]{1,0:T(8,128)(2,1)}, u32[]{:S(2)}, u32[]{:S(2)}) collective-permute-start(bf16[192,2048]{1,0:T(8,128)(2,1)} %copy-done.96), channel_id=1, source_target_pairs={{0,4},{4,0},{1,5},{5,1},{2,6},{6,2},{3,7},{7,3},{8,12},{12,8},{9,1... | collective-permute-start | bytes 2359304 | tf_op jit(solution)/shard_map/ppermute | solution.py:503
  380.2 27.8 %collective-permute-start.68 = (bf16[192,2048]{1,0:T(8,128)(2,1)S(1)}, bf16[192,2048]{1,0:T(8,128)(2,1)}, u32[]{:S(2)}, u32[]{:S(2)}) collective-permute-start(bf16[192,2048]{1,0:T(8,128)(2,1)S(1)} %pad_maximum_fusion.11.refs_5_), channel_id=1, source_target_pairs={{0,2},{2,0},{1,3},{3,1},{4,6},{6,4},{5,7},{7,5},{8,10},{10,8},{9,1... | collective-permute-start | bytes 2359304 | tf_op jit(solution)/shard_map/ppermute | solution.py:503
  380.2 27.8 %collective-permute-start.67 = (bf16[96,2048]{1,0:T(8,128)(2,1)}, bf16[96,2048]{1,0:T(8,128)(2,1)}, u32[]{:S(2)}, u32[]{:S(2)}) collective-permute-start(bf16[96,2048]{1,0:T(8,128)(2,1)} %collective-permute-done.60), channel_id=1, source_target_pairs={{0,4},{4,0},{1,5},{5,1},{2,6},{6,2},{3,7},{7,3},{8,12},{12,8},{9,1... | collective-permute-start | bytes 1179656 | tf_op jit(solution)/shard_map/ppermute | solution.py:503
  414.6 39.7 %collective-permute-start.75 = (bf16[2,192,2176]{2,1,0:T(8,128)(2,1)}, bf16[2,192,2176]{2,1,0:T(8,128)(2,1)S(1)}, u32[]{:S(2)}, u32[]{:S(2)}) collective-permute-start(bf16[2,192,2176]{2,1,0:T(8,128)(2,1)} %get-tuple-element.867), channel_id=1, source_target_pairs={{0,2},{2,0},{1,3},{3,1},{4,6},{6,4},{5,7},{7,5},{8,10},{10,8},{9,1... | collective-permute-start | bytes 5013512 | tf_op jit(solution)/shard_map/ppermute | solution.py:503
  415.5 38.8 %collective-permute-start.76 = (bf16[2,192,2048]{2,1,0:T(8,128)(2,1)}, bf16[2,192,2048]{2,1,0:T(8,128)(2,1)S(1)}, u32[]{:S(2)}, u32[]{:S(2)}) collective-permute-start(bf16[2,192,2048]{2,1,0:T(8,128)(2,1)} %get-tuple-element.868), channel_id=1, source_target_pairs={{0,2},{2,0},{1,3},{3,1},{4,6},{6,4},{5,7},{7,5},{8,10},{10,8},{9,1... | collective-permute-start | bytes 4718600 | tf_op jit(solution)/shard_map/ppermute | solution.py:503
  416.1 38.1 %collective-permute-start.73 = (bf16[192,2176]{1,0:T(8,128)(2,1)}, bf16[192,2176]{1,0:T(8,128)(2,1)}, u32[]{:S(2)}, u32[]{:S(2)}) collective-permute-start(bf16[192,2176]{1,0:T(8,128)(2,1)} %fusion.34), channel_id=1, source_target_pairs={{0,4},{4,0},{1,5},{5,1},{2,6},{6,2},{3,7},{7,3},{8,12},{12,8},{9,1... | collective-permute-start | bytes 2506760 | tf_op jit(solution)/shard_map/ppermute | solution.py:503
  416.7 37.6 %collective-permute-start.74 = (bf16[192,2048]{1,0:T(8,128)(2,1)}, bf16[192,2048]{1,0:T(8,128)(2,1)}, u32[]{:S(2)}, u32[]{:S(2)}) collective-permute-start(bf16[192,2048]{1,0:T(8,128)(2,1)} %fusion.39), channel_id=1, source_target_pairs={{0,4},{4,0},{1,5},{5,1},{2,6},{6,2},{3,7},{7,3},{8,12},{12,8},{9,1... | collective-permute-start | bytes 2359304 | tf_op jit(solution)/shard_map/ppermute | solution.py:503
  461.8 40.4 %collective-permute-start.80 = (bf16[2,192,2176]{2,1,0:T(8,128)(2,1)}, bf16[2,192,2176]{2,1,0:T(8,128)(2,1)}, u32[]{:S(2)}, u32[]{:S(2)}) collective-permute-start(bf16[2,192,2176]{2,1,0:T(8,128)(2,1)} %get-tuple-element.913), channel_id=1, source_target_pairs={{0,2},{2,0},{1,3},{3,1},{4,6},{6,4},{5,7},{7,5},{8,10},{10,8},{9,1... | collective-permute-start | bytes 5013512 | tf_op jit(solution)/shard_map/ppermute | solution.py:503
  461.8 40.3 %collective-permute-start.81 = (bf16[2,192,2048]{2,1,0:T(8,128)(2,1)}, bf16[2,192,2048]{2,1,0:T(8,128)(2,1)}, u32[]{:S(2)}, u32[]{:S(2)}) collective-permute-start(bf16[2,192,2048]{2,1,0:T(8,128)(2,1)} %get-tuple-element.914), channel_id=1, source_target_pairs={{0,2},{2,0},{1,3},{3,1},{4,6},{6,4},{5,7},{7,5},{8,10},{10,8},{9,1... | collective-permute-start | bytes 4718600 | tf_op jit(solution)/shard_map/ppermute | solution.py:503
  463.1 39.0 %collective-permute-start.77 = (bf16[192,2176]{1,0:T(8,128)(2,1)}, bf16[192,2176]{1,0:T(8,128)(2,1)S(1)}, u32[]{:S(2)}, u32[]{:S(2)}) collective-permute-start(bf16[192,2176]{1,0:T(8,128)(2,1)} %fusion.11), channel_id=1, source_target_pairs={{0,16},{8,24},{16,0},{24,8},{1,17},{9,25},{17,1},{25,9},{2,18},{10... | collective-permute-start | bytes 2506760 | tf_op jit(solution)/shard_map/ppermute | solution.py:499
  463.2 39.0 %collective-permute-start.78 = (bf16[192,2176]{1,0:T(8,128)(2,1)}, bf16[192,2176]{1,0:T(8,128)(2,1)}, u32[]{:S(2)}, u32[]{:S(2)}) collective-permute-start(bf16[192,2176]{1,0:T(8,128)(2,1)} %fusion.35), channel_id=1, source_target_pairs={{0,4},{4,0},{1,5},{5,1},{2,6},{6,2},{3,7},{7,3},{8,12},{12,8},{9,1... | collective-permute-start | bytes 2506760 | tf_op jit(solution)/shard_map/ppermute | solution.py:503
  463.8 37.0 %collective-permute-start.79 = (bf16[192,2048]{1,0:T(8,128)(2,1)}, bf16[192,2048]{1,0:T(8,128)(2,1)S(1)}, u32[]{:S(2)}, u32[]{:S(2)}) collective-permute-start(bf16[192,2048]{1,0:T(8,128)(2,1)} %fusion.40), channel_id=1, source_target_pairs={{0,4},{4,0},{1,5},{5,1},{2,6},{6,2},{3,7},{7,3},{8,12},{12,8},{9,1... | collective-permute-start | bytes 2359304 | tf_op jit(solution)/shard_map/ppermute | solution.py:503
  590.4 38.2 %collective-permute-start.94 = (bf16[3,128,2048]{2,1,0:T(8,128)(2,1)S(1)}, bf16[3,128,2048]{2,1,0:T(8,128)(2,1)S(1)}, u32[]{:S(2)}, u32[]{:S(2)}) collective-permute-start(bf16[3,128,2048]{2,1,0:T(8,128)(2,1)S(1)} %dynamic-slice_bitcast_fusion.1), channel_id=1, source_target_pairs={{0,1},{1,0},{2,3},{3,2},{4,5},{5,4},{6,7},{7,6},{8,9},{9,8},{10,11... | collective-permute-start | bytes 4718600 | tf_op jit(solution)/shard_map/ppermute | solution.py:503
  591.2 37.4 %collective-permute-start.95 = (bf16[192,2048]{1,0:T(8,128)(2,1)}, bf16[192,2048]{1,0:T(8,128)(2,1)S(1)}, u32[]{:S(2)}, u32[]{:S(2)}) collective-permute-start(bf16[192,2048]{1,0:T(8,128)(2,1)} %fusion.24), channel_id=1, source_target_pairs={{0,16},{8,24},{16,0},{24,8},{1,17},{9,25},{17,1},{25,9},{2,18},{10... | collective-permute-start | bytes 2359304 | tf_op jit(solution)/shard_map/ppermute | solution.py:499
  591.9 36.7 %collective-permute-start.96 = (bf16[192,2048]{1,0:T(8,128)(2,1)}, bf16[192,2048]{1,0:T(8,128)(2,1)}, u32[]{:S(2)}, u32[]{:S(2)}) collective-permute-start(bf16[192,2048]{1,0:T(8,128)(2,1)} %fusion.41), channel_id=1, source_target_pairs={{0,4},{4,0},{1,5},{5,1},{2,6},{6,2},{3,7},{7,3},{8,12},{12,8},{9,1... | collective-permute-start | bytes 2359304 | tf_op jit(solution)/shard_map/ppermute | solution.py:503
  593.2 35.4 %collective-permute-start.97 = (bf16[192,2048]{1,0:T(8,128)(2,1)}, bf16[192,2048]{1,0:T(8,128)(2,1)S(1)}, u32[]{:S(2)}, u32[]{:S(2)}) collective-permute-start(bf16[192,2048]{1,0:T(8,128)(2,1)} %fusion.42), channel_id=1, source_target_pairs={{0,4},{4,0},{1,5},{5,1},{2,6},{6,2},{3,7},{7,3},{8,12},{12,8},{9,1... | collective-permute-start | bytes 2359304 | tf_op jit(solution)/shard_map/ppermute | solution.py:503
  636.8 38.8 %collective-permute-start.101 = (bf16[512,1024]{1,0:T(8,128)(2,1)S(1)}, bf16[512,1024]{1,0:T(8,128)(2,1)S(1)}, u32[]{:S(2)}, u32[]{:S(2)}) collective-permute-start(bf16[512,1024]{1,0:T(8,128)(2,1)S(1)} %pad_maximum_fusion.8), channel_id=1, source_target_pairs={{0,1},{1,0},{2,3},{3,2},{4,5},{5,4},{6,7},{7,6},{8,9},{9,8},{10,11... | collective-permute-start | bytes 3145736 | tf_op jit(solution)/shard_map/ppermute | solution.py:503
  638.1 37.5 %collective-permute-start.102 = (bf16[2,128,2048]{2,1,0:T(8,128)(2,1)S(1)}, bf16[2,128,2048]{2,1,0:T(8,128)(2,1)S(1)}, u32[]{:S(2)}, u32[]{:S(2)}) collective-permute-start(bf16[2,128,2048]{2,1,0:T(8,128)(2,1)S(1)} %fusion.1), channel_id=1, source_target_pairs={{0,4},{4,0},{1,5},{5,1},{2,6},{6,2},{3,7},{7,3},{8,12},{12,8},{9,1... | collective-permute-start | bytes 3145736 | tf_op jit(solution)/shard_map/ppermute | solution.py:503
  642.7 32.9 %collective-permute-start.99 = (bf16[4,3,64,256]{3,2,1,0:T(8,128)(2,1)S(1)}, bf16[4,3,64,256]{3,2,1,0:T(8,128)(2,1)S(1)}, u32[]{:S(2)}, u32[]{:S(2)}) collective-permute-start(bf16[4,3,64,256]{3,2,1,0:T(8,128)(2,1)S(1)} %get-tuple-element.1020), channel_id=1, source_target_pairs={{0,16},{8,24},{16,0},{24,8},{1,17},{9,25},{17,1},{25,9},{2,18},{10... | collective-permute-start | bytes 1179656 | tf_op jit(solution)/shard_map/ppermute | solution.py:499
  678.3 26.4 %collective-permute-start.104 = (bf16[2,4,64,1024]{3,2,1,0:T(8,128)(2,1)S(1)}, bf16[2,4,64,1024]{3,2,1,0:T(8,128)(2,1)S(1)}, u32[]{:S(2)}, u32[]{:S(2)}) collective-permute-start(bf16[2,4,64,1024]{3,2,1,0:T(8,128)(2,1)S(1)} %pad_maximum_fusion.9), channel_id=1, source_target_pairs={{0,1},{1,0},{2,3},{3,2},{4,5},{5,4},{6,7},{7,6},{8,9},{9,8},{10,11... | collective-permute-start | bytes 3145736 | tf_op jit(solution)/shard_map/ppermute | solution.py:503
  706.3 28.7 %collective-permute-start.110 = (bf16[2,192,2048]{2,1,0:T(8,128)(2,1)}, bf16[2,192,2048]{2,1,0:T(8,128)(2,1)}, u32[]{:S(2)}, u32[]{:S(2)}) collective-permute-start(bf16[2,192,2048]{2,1,0:T(8,128)(2,1)} %bitcast.158), channel_id=1, source_target_pairs={{0,2},{2,0},{1,3},{3,1},{4,6},{6,4},{5,7},{7,5},{8,10},{10,8},{9,1... | collective-permute-start | bytes 4718600 | tf_op jit(solution)/shard_map/ppermute | solution.py:503
  706.4 28.5 %collective-permute-start.109 = (bf16[4,4,80,256]{3,2,1,0:T(8,128)(2,1)}, bf16[4,4,80,256]{3,2,1,0:T(8,128)(2,1)S(1)}, u32[]{:S(2)}, u32[]{:S(2)}) collective-permute-start(bf16[4,4,80,256]{3,2,1,0:T(8,128)(2,1)} %get-tuple-element.1055), channel_id=1, source_target_pairs={{0,1},{1,0},{2,3},{3,2},{4,5},{5,4},{6,7},{7,6},{8,9},{9,8},{10,11... | collective-permute-start | bytes 1966088 | tf_op jit(solution)/shard_map/ppermute | solution.py:503
  736.3 27.8 %collective-permute-start.113 = (bf16[192,2048]{1,0:T(8,128)(2,1)S(1)}, bf16[192,2048]{1,0:T(8,128)(2,1)S(1)}, u32[]{:S(2)}, u32[]{:S(2)}) collective-permute-start(bf16[192,2048]{1,0:T(8,128)(2,1)S(1)} %fusion.43), channel_id=1, source_target_pairs={{0,4},{4,0},{1,5},{5,1},{2,6},{6,2},{3,7},{7,3},{8,12},{12,8},{9,1... | collective-permute-start | bytes 2359304 | tf_op jit(solution)/shard_map/ppermute | solution.py:503
  782.8 26.4 %collective-permute-start.122 = (bf16[704,768]{1,0:T(8,128)(2,1)S(1)}, bf16[704,768]{1,0:T(8,128)(2,1)S(1)}, u32[]{:S(2)}, u32[]{:S(2)}) collective-permute-start(bf16[704,768]{1,0:T(8,128)(2,1)S(1)} %copy-done.70), channel_id=1, source_target_pairs={{0,1},{1,0},{2,3},{3,2},{4,5},{5,4},{6,7},{7,6},{8,9},{9,8},{10,11... | collective-permute-start | bytes 3244040 | tf_op jit(solution)/shard_map/ppermute | solution.py:503
  (246 other events, 3173.7 us)

commit v5 on v4

--- a/solution.py
+++ b/solution.py
@@ -1275,44 +1275,52 @@
     (ny1, n3), c3, _ = step(
         [(y1, "c"), (x3, "c")], lambda *halves: jnp.concatenate(halves), (c3_low, c3_high)
     )
-    (y3, c_far3_high, c_near3, back2, mixed_back2), (kept, mixed1, rows1), _ = step(
-        [(x3, "y"), (c3_high, "y"), (c3, "c"), (rows2[1], "c"), (mixed2[1], "c")],
-        functools.partial(run_experts, 1),
-        ([x1, n1, y1, ny1], [c1, c_near1, c_far1, c_far_near1], kept, weights),
-    )
+    def core_sums(*pairs):
+        backs = [swap(pair[1], "c") for pair in pairs]
+        return backs, [added(pair, back, 1).astype(low) for pair, back in zip(pairs, backs)]
+
+    def sums_and_experts(pairs, k, *given):
+        return core_sums(*pairs), run_experts(k, *given)
+
+    (y3, c_far3_high, c_near3), (sums, (kept, mixed1, rows1)), _ = step(
+        [(x3, "y"), (c3_high, "y"), (c3, "c")],
+        lambda pairs, *given: sums_and_experts(pairs, 1, *given),
+        (
+            [rows2, mixed2],
+            [x1, n1, y1, ny1],
+            [c1, c_near1, c_far1, c_far_near1],
+            kept,
+            weights,
+        ),
+    )
+    (back2, mixed_back2), (row_send2, mixed_far_send2) = sums
     c_far3 = jnp.concatenate([c_far3_low, c_far3_high])
-    (ny3, c_far_near3), row_send2, _ = step(
-        [(y3, "c"), (c_far3, "c")],
-        lambda pair, back: added(pair, back, 1).astype(low),
-        (rows2, back2),
-    )
-    (far2, mixed_far2, back1, mixed_back1), (kept, mixed3, rows3), _ = step(
-        [
-            (row_send2, "y"),
-            (added(mixed2, mixed_back2, 1).astype(low), "y"),
-            (rows1[1], "c"),
-            (mixed1[1], "c"),
-        ],
-        functools.partial(run_experts, 3),
-        ([x3, n3, y3, ny3], [c3, c_near3, c_far3, c_far_near3], kept, weights),
-    )
+    (ny3, c_far_near3), _, _ = step([(y3, "c"), (c_far3, "c")])
+    (far2, mixed_far2), (sums, (kept, mixed3, rows3)), _ = step(
+        [(row_send2, "y"), (mixed_far_send2, "y")],
+        lambda pairs, *given: sums_and_experts(pairs, 3, *given),
+        (
+            [rows1, mixed1],
+            [x3, n3, y3, ny3],
+            [c3, c_near3, c_far3, c_far_near3],
+            kept,
+            weights,
+        ),
+    )
+    (back1, mixed_back1), (row_send1, mixed_far_send1) = sums
     total2 = (added(rows2, back2, 0) + far2.astype(wide)).astype(low)
-    (z2, far1, mixed_far1, back3, mixed_back3), (kept, mixed0, rows0), _ = step(
-        [
-            (total2, "z", -2),
-            (added(rows1, back1, 1).astype(low), "y"),
-            (added(mixed1, mixed_back1, 1).astype(low), "y"),
-            (rows3[1], "c"),
-            (mixed3[1], "c"),
-        ],
-        functools.partial(run_experts, 0),
+    (z2, far1, mixed_far1), (sums, (kept, mixed0, rows0)), _ = step(
+        [(total2, "z", -2), (row_send1, "y"), (mixed_far_send1, "y")],
+        lambda pairs, *given: sums_and_experts(pairs, 0, *given),
         (
+            [rows3, mixed3],
             [ffn_low, n0, y0, ny0],
             [cotangent, c_near0, c_far0, c_far_near0],
             kept,
             weights,
         ),
     )
+    (back3, mixed_back3), (row_send3, mixed_far_send3) = sums
     expert_rows, hidden_low, dresults, dgate_low, dup_low = (
         block.reshape(context_count * slots, -1) for block in kept
     )
@@ -1333,21 +1341,21 @@
     def total(pair, back, far):
         return (added(pair, back, 0) + far.astype(wide)).astype(low)
 
-    (z1, far3, back0, mixed_back0), ((down_grad, down_first, down_rest), mixed_send1), _ = step(
-        [
-            (total1, "z", -1),
-            (added(rows3, back3, 1).astype(low), "y"),
-            (rows0[1], "c"),
-            (mixed0[1], "c"),
-        ],
-        lambda rows, grad, *given: (halved(dot32("sf,sd->fd", rows, grad), 10), total(*given)),
-        (hidden_low, dresults, mixed1, mixed_back1, mixed_far1),
-    )
+    (z1, far3), (sums, (down_grad, down_first, down_rest), mixed_send1), _ = step(
+        [(total1, "z", -1), (row_send3, "y")],
+        lambda pairs, rows, grad, *given: (
+            core_sums(*pairs),
+            halved(dot32("sf,sd->fd", rows, grad), 10),
+            total(*given),
+        ),
+        ([rows0, mixed0], hidden_low, dresults, mixed1, mixed_back1, mixed_far1),
+    )
+    (back0, mixed_back0), (row_send0, mixed_far_send0) = sums
     total3 = (added(rows3, back3, 0) + far3.astype(wide)).astype(low)
     (z3, far0, down0), ((gate_grad, gate_first, gate_rest), mixed_send2), _ = step(
         [
             (total3, "z", -3),
-            (added(rows0, back0, 1).astype(low), "y"),
+            (row_send0, "y"),
             (down_first, "x"),
         ],
         lambda rows, grad, *given: (halved(dot32("sd,sf->df", rows, grad), 10), total(*given)),
@@ -1398,22 +1406,31 @@
         other = lax.dynamic_index_in_dim(part, 1 - xi, 2, keepdims=False)
         return [(pick(own, around(k)), pick(other, around(k))) for k in range(nz)]
 
-    def attention_back(dattn_all, output_weight, *given):
+    def attention_back(dattn_all, output_weight, normed_all, head, *given):
         attended_grad = dot32("td,cd->tc", dattn_all, output_weight).astype(low)
         attended_grad = attended_grad.reshape(MEMBERS, LOCAL_SEQUENCES, paired, query_width)
-        return attend_back(*given[:2], attended_grad, *given[2:])
+        dquery, dkey_value, gain_part = attend_back(*given[:2], attended_grad, *given[2:])
+        dquery = dquery.reshape(MEMBERS * rows, query_width)
+        part = dot32("td,tc->dc", normed_all, dquery).astype(low)
+        plane = pick(part.reshape(nz, MEMBERS, 2, piece, query_width), around(2))
+        plane = lax.dynamic_index_in_dim(plane, 1 - xi, 1, keepdims=False)
+        plane = [plane.reshape(-1, query_width)]
+        plane += [head[:, a : a + query_width] for a in range(0, model, query_width)]
+        return dquery, dkey_value, gain_part, part, jnp.concatenate(plane)
 
     moved, attention_grads, _ = step(
         [
             (output_other[1:], "x"),
             (mixed_send2, "z", -2),
-            (added(mixed3, mixed_back3, 1).astype(low), "y"),
-            (added(mixed0, mixed_back0, 1).astype(low), "y"),
+            (mixed_far_send3, "y"),
+            (mixed_far_send0, "y"),
         ],
         attention_back,
         (
             dattn_all,
             output_weight,
+            normed_all,
+            output_other[0],
             places,
             queries,
             key_value,
@@ -1424,26 +1441,29 @@
         ),
     )
     cross_rest, mixed_z2, mixed_far3, mixed_far0 = moved
-    dquery_low, dkey_value, query_gain_part = attention_grads
+    dquery_low, dkey_value, query_gain_part, query_part, query_and_head = attention_grads
     query_gain_part = query_gain_part[0]
-    dquery_low = dquery_low.reshape(MEMBERS * rows, query_width)
-    query_part = dot32("td,tc->dc", normed_all, dquery_low).astype(low)
     query_planes = planes_of(query_part.reshape(nz, MEMBERS, 2, piece, query_width))
     output_far = (output_own[2:].astype(wide) + cross_rest[1:].astype(wide)).astype(low)
 
-    def query_back(grad, weight, third):
-        return dot32("tc,dc->td", grad, weight), total(*third)
-
-    query_plane = query_planes[2][1].reshape(-1, query_width)
-    first_head = [output_other[0][:, a : a + query_width] for a in range(0, model, query_width)]
-    moved, (dnormed, mixed_send3), _ = step(
+    def query_back(grad, weight, third, own, other):
+        near = (own.astype(wide) + other.astype(wide)).astype(low)
+        return dot32("tc,dc->td", grad, weight), total(*third), near
+
+    moved, (dnormed, mixed_send3, near_last), _ = step(
         [(dkey_value[k].astype(low), "z", -k) for k in range(1, nz)]
-        + [(jnp.concatenate([query_plane] + first_head), "x"), (output_far, "y")],
+        + [(query_and_head, "x"), (output_far, "y")],
         query_back,
-        (dquery_low, query_weight, [mixed3, mixed_back3, mixed_far3]),
+        (
+            dquery_low,
+            query_weight,
+            [mixed3, mixed_back3, mixed_far3],
+            output_own[1],
+            cross_rest[0],
+        ),
     )
     *key_moves, cross, output_far = moved
-    plane_rows = query_plane.shape[0]
+    plane_rows = MEMBERS * piece
     cross_first = [
         cross[a : a + head_rows] for a in range(plane_rows, cross.shape[0], head_rows)
     ]
@@ -1451,7 +1471,6 @@
     cross = cross[:plane_rows].reshape(query_planes[2][0].shape)
     query_sum2 = (query_planes[2][0].astype(wide) + cross.astype(wide)).astype(low)
     near_first = (output_own[0].astype(wide) + cross_first.astype(wide)).astype(low)
-    near_last = (output_own[1].astype(wide) + cross_rest[0].astype(wide)).astype(low)
 
     def project_keys_back(dnormed, dkey_value_own, moved, key_value_weight):
         dkey_value_own = dkey_value_own + sum(block.astype(wide) for block in moved)

time: 852 us -> 835 us (0.980)
  waiting for transfers between devices: 362 us -> 342 us
    ppermute x92, waiting for transfers between devices: 144 us -> 133 us  [swap(): return lax.ppermute(block, axis, [(0, 1), (1, 0)])]
    unnamed x331 -> x307, local copies, waits for them, and re-layouts: 21.5 us -> 16.5 us
  transfers between devices with their start and end apart: 133 -> 133, of which waited for: 55 -> 57; matrix products, arithmetic and copies ran while one was open for 18% -> 21% of each run, Pallas kernels for 15% -> 15%
where the time goes in v5:
time: 835 us; the launch traced here: 825 us
  waiting for transfers between devices  342 us (41%)
  Pallas kernels  128 us (15%)
  starting transfers between devices  126 us (15%)
  local copies, waits for them, and re-layouts  91.1 us (11%)
  other arithmetic  76.9 us (9%)
  matrix products  57.6 us (7%)
    ppermute x41, waiting for transfers between devices, shift(): lax.ppermute(block, axis, [(i, (i + step) % count) for i in range(count)])  209 us
    ppermute x92, waiting for transfers between devices, swap(): return lax.ppermute(block, axis, [(0, 1), (1, 0)])  133 us
    pallas_call x4, Pallas kernels, experts(): pl.pallas_call(expert_kernel, grid_spec=pltpu.PrefetchScalarGridSpec(num_...  94.5 us
    ppermute x41, starting transfers between devices, shift(): lax.ppermute(block, axis, [(i, (i + step) % count) for i in range(count)])  63.5 us
    ppermute x92, starting transfers between devices, swap(): return lax.ppermute(block, axis, [(0, 1), (1, 0)])  62.5 us
    dot_general x13, matrix products, dot32(): jnp.einsum(subscripts, left, right, preferred_element_type=jnp.float32)  45.7 us
    pallas_call x1, Pallas kernels, attend_back(): pl.pallas_call(attend_back_kernel, grid_spec=pltpu.PrefetchScalarGridSpec...  20.8 us
  transfers between devices with their start and end apart: 133, of which 57 were waited for; matrix products, arithmetic and copies ran while one was open for 21% of the time, Pallas kernels for 15%

profile of v5, /device:TPU:0, one launch (start us, length us, event | category | flops | bytes accessed | tf_op | source)
XLA Modules:
  0.0 824.9 jit_solution(1865357334855897662)
XLA Ops:
  9.4 8.5 %collective-permute-done = bf16[128,2048]{1,0:T(8,128)(2,1)S(1)} collective-permute-done((bf16[128,2048]{1,0:T(8,128)(2,1)}, bf16[128,2048]{1,0:T(8,128)(2,1)S(1)}, u32[]{:S(2)}, u32[]{:S(2)}) %collective-permute-start) | collective-permute-done | bytes 524320 | tf_op jit(solution)/shard_map/ppermute | solution.py:499
  28.8 3.9 collective-permute-done.2
  43.1 10.1 %collective-permute-done.11 = bf16[4,20,128]{2,1,0:T(8,128)(2,1)S(1)} collective-permute-done((bf16[4,20,128]{2,1,0:T(8,128)(2,1)S(1)}, bf16[4,20,128]{2,1,0:T(8,128)(2,1)S(1)}, u32[]{:S(2)}, u32[]{:S(2)}) %collective-permute-start.11) | collective-permute-done | bytes 20512 | tf_op jit(solution)/shard_map/ppermute | solution.py:503
  68.5 18.9 %collective-permute-done.16 = bf16[128,2048]{1,0:T(8,128)(2,1)S(1)} collective-permute-done((bf16[128,2048]{1,0:T(8,128)(2,1)}, bf16[128,2048]{1,0:T(8,128)(2,1)S(1)}, u32[]{:S(2)}, u32[]{:S(2)}) %collective-permute-start.16) | collective-permute-done | bytes 524320 | tf_op jit(solution)/shard_map/ppermute | solution.py:503
  89.3 3.5 collective-permute-start.17
  98.4 13.3 %collective-permute-done.20 = bf16[4,2,2,20,128]{4,3,2,1,0:T(8,128)(2,1)S(1)} collective-permute-done((bf16[4,2,2,20,128]{4,3,2,1,0:T(8,128)(2,1)S(1)}, bf16[4,2,2,20,128]{4,3,2,1,0:T(8,128)(2,1)S(1)}, u32[]{:S(2)}, u32[]{:S(2)}) %collective-permute-start.20) | collective-permute-done | bytes 81952 | tf_op jit(solution)/shard_map/ppermute | solution.py:503
  121.5 15.3 %collective-permute-done.22 = bf16[128,2048]{1,0:T(8,128)(2,1)S(1)} collective-permute-done((bf16[128,2048]{1,0:T(8,128)(2,1)}, bf16[128,2048]{1,0:T(8,128)(2,1)S(1)}, u32[]{:S(2)}, u32[]{:S(2)}) %collective-permute-start.22) | collective-permute-done | bytes 524320 | tf_op jit(solution)/shard_map/ppermute | solution.py:499
  150.1 19.8 %collective-permute-done.28 = bf16[320,768]{1,0:T(8,128)(2,1)S(1)} collective-permute-done((bf16[320,768]{1,0:T(8,128)(2,1)S(1)}, bf16[320,768]{1,0:T(8,128)(2,1)S(1)}, u32[]{:S(2)}, u32[]{:S(2)}) %collective-permute-start.28) | collective-permute-done | bytes 491552 | tf_op jit(solution)/shard_map/ppermute | solution.py:503
  174.6 4.4 collective-permute-start.31
  179.8 6.1 fusion.81
  188.4 16.4 %collective-permute-done.31 = bf16[4,3,64,256]{3,2,1,0:T(8,128)(2,1)S(1)} collective-permute-done((bf16[4,3,64,256]{3,2,1,0:T(8,128)(2,1)S(1)}, bf16[4,3,64,256]{3,2,1,0:T(8,128)(2,1)S(1)}, u32[]{:S(2)}, u32[]{:S(2)}) %collective-permute-start.31) | collective-permute-done | bytes 393248 | tf_op jit(solution)/shard_map/ppermute | solution.py:499
  204.9 5.2 collective-permute-done.35
  217.4 12.2 %shard_map.263 = bf16[4,3,64,1024]{3,2,1,0:T(8,128)(2,1)S(1)} custom-call(s32[2]{0:T(128)S(1)} %pad_add_fusion.places_ref, f32[4,3,64,1024]{3,2,1,0:T(8,128)S(1)} %bitcast.525, bf16[4,4,3,64,256]{4,3,2,1,0:T(8,128)(2,1)S(1)} %pad_maximum_fusion.4.k_ref.v_ref, bf16[4,4,3,64,256]{4,3,2,1,0:T(8,128)(2,1)S(1)} %pad_maximum_fusion.4.k_ref.v_ref, ...), custom_call_target="tpu_custom_call" | custom-call | flops 3221225472 | bytes 8388608 | tf_op jit(solution)/shard_map/pallas_call | solution.py:768
  235.6 3.4 fusion.82
  252.1 13.1 %collective-permute-done.44 = bf16[192,2048]{1,0:T(8,128)(2,1)} collective-permute-done((bf16[192,2048]{1,0:T(8,128)(2,1)}, bf16[192,2048]{1,0:T(8,128)(2,1)}, u32[]{:S(2)}, u32[]{:S(2)}) %collective-permute-start.44) | collective-permute-done | bytes 786464 | tf_op jit(solution)/shard_map/ppermute | solution.py:503
  267.3 3.4 collective-permute-done.41
  295.4 15.9 %collective-permute-done.45.refs_1_ = bf16[192,2048]{1,0:T(8,128)(2,1)} collective-permute-done((bf16[192,2048]{1,0:T(8,128)(2,1)S(1)}, bf16[192,2048]{1,0:T(8,128)(2,1)}, u32[]{:S(2)}, u32[]{:S(2)}) %collective-permute-start.45) | collective-permute-done | bytes 786464 | tf_op jit(solution)/shard_map/ppermute | solution.py:499
  323.9 16.2 %collective-permute-done.51 = bf16[96,2048]{1,0:T(8,128)(2,1)} collective-permute-done((bf16[96,2048]{1,0:T(8,128)(2,1)S(1)}, bf16[96,2048]{1,0:T(8,128)(2,1)}, u32[]{:S(2)}, u32[]{:S(2)}) %collective-permute-start.51) | collective-permute-done | bytes 393248 | tf_op jit(solution)/shard_map/ppermute | solution.py:499
  350.8 23.4 %shard_map.264 = (bf16[4,4,128,2048]{3,2,1,0:T(8,128)(2,1)}, bf16[4,4,128,768]{3,2,1,0:T(8,128)(2,1)}, bf16[4,4,128,2048]{3,2,1,0:T(8,128)(2,1)}, bf16[4,4,128,7...) custom-call(s32[2]{0:T(128)} %get-tuple-element.1379.refs_0_, ...), custom_call_target="tpu_custom_call" | custom-call | flops 9663676416 | bytes 41943040 | tf_op jit(solution)/shard_map/pallas_call | solution.py:919
  383.4 23.6 %shard_map.265 = (bf16[4,4,128,2048]{3,2,1,0:T(8,128)(2,1)}, bf16[4,4,128,768]{3,2,1,0:T(8,128)(2,1)}, bf16[4,4,128,2048]{3,2,1,0:T(8,128)(2,1)}, bf16[4,4,128,7...) custom-call(s32[2]{0:T(128)} %get-tuple-element.1380.refs_0_, ...), custom_call_target="tpu_custom_call", output_to_operand_aliasing={{0}: (15, {}), {1}: (16, {}), {2}: (17, {}), {3}: (18, {}),... | custom-call | flops 9663676416 | bytes 41943040 | tf_op jit(solution)/shard_map/pallas_call | solution.py:919
  418.3 23.6 %shard_map.266 = (bf16[4,4,128,2048]{3,2,1,0:T(8,128)(2,1)}, bf16[4,4,128,768]{3,2,1,0:T(8,128)(2,1)}, bf16[4,4,128,2048]{3,2,1,0:T(8,128)(2,1)}, bf16[4,4,128,7...) custom-call(s32[2]{0:T(128)} %get-tuple-element.1381.refs_0_, ...), custom_call_target="tpu_custom_call", output_to_operand_aliasing={{0}: (15, {}), {1}: (16, {}), {2}: (17, {}), {3}: (18, {}),... | custom-call | flops 9663676416 | bytes 41943040 | tf_op jit(solution)/shard_map/pallas_call | solution.py:919
  446.9 7.0 collective-permute-done.74
  460.4 24.0 %shard_map.267 = (bf16[4,4,128,2048]{3,2,1,0:T(8,128)(2,1)}, bf16[4,4,128,768]{3,2,1,0:T(8,128)(2,1)}, bf16[4,4,128,2048]{3,2,1,0:T(8,128)(2,1)}, bf16[4,4,128,7...) custom-call(s32[2]{0:T(128)} %get-tuple-element.1382.refs_0_, ...), custom_call_target="tpu_custom_call", output_to_operand_aliasing={{0}: (15, {}), {1}: (16, {}), {2}: (17, {}), {3}: (18, {}),... | custom-call | flops 9663676416 | bytes 41943040 | tf_op jit(solution)/shard_map/pallas_call | solution.py:919
  488.6 7.5 collective-permute-done.79
  502.2 9.3 %fusion.83 = f32[768,2048]{1,0:T(8,128)S(1)} fusion(bf16[2048,768]{1,0:T(8,128)(2,1)S(1)} %bitcast.537, bf16[2048,2048]{1,0:T(8,128)(2,1)} %bitcast.536), kind=kOutput, calls=%fused_computation.380 | convolution fusion | flops 6442450944 | bytes 17825792 | tf_op jit(solution)/shard_map/sf,sd->fd/dot_general | solution.py:936
  525.4 7.4 fusion.84
  539.0 6.4 collective-permute-done.86
  554.2 7.4 fusion.85
  577.3 3.8 convolution_convert_fusion.1
  585.9 3.4 convolution_convert_fusion.4
  589.4 20.8 %shard_map.268 = (bf16[4,3,64,1024]{3,2,1,0:T(8,128)(2,1)S(1)}, f32[4,4,3,64,256]{4,3,2,1,0:T(8,128)S(1)}, f32[8,128]{1,0:T(8,128)S(1)}) custom-call(s32[2]{0:T(128)S(1)} %pad_add_fusion.places_ref, f32[4,3,64,1024]{3,2,1,0:T(8,128)S(1)} %bitcast.526, bf16[4,3,64,1024]{3,2,1,0:T(8,128)(2,1)S(1)} %bitcast.531, ...), custom_call_target="tpu_custom_call" | custom-call | flops 8053063680 | bytes 16777216 | tf_op jit(solution)/shard_map/pallas_call | solution.py:788
  610.3 3.7 convolution_convert_fusion
  614.4 6.0 collective-permute-done.95
  623.7 3.5 collective-permute-start.100
  628.7 5.4 fusion.86
  639.6 5.7 collective-permute-done.98
  645.3 15.3 %collective-permute-done.99 = bf16[4,3,64,256]{3,2,1,0:T(8,128)(2,1)S(1)} collective-permute-done((bf16[4,3,64,256]{3,2,1,0:T(8,128)(2,1)S(1)}, bf16[4,3,64,256]{3,2,1,0:T(8,128)(2,1)S(1)}, u32[]{:S(2)}, u32[]{:S(2)}) %collective-permute-start.99) | collective-permute-done | bytes 393248 | tf_op jit(solution)/shard_map/ppermute | solution.py:499
  672.9 17.7 %collective-permute-done.103 = bf16[4,64,1024]{2,1,0:T(8,128)(2,1)S(1)} collective-permute-done((bf16[4,64,1024]{2,1,0:T(8,128)(2,1)S(1)}, bf16[4,64,1024]{2,1,0:T(8,128)(2,1)S(1)}, u32[]{:S(2)}, u32[]{:S(2)}) %collective-permute-start.103) | collective-permute-done | bytes 524320 | tf_op jit(solution)/shard_map/ppermute | solution.py:499
  694.0 3.8 collective-permute-start.107
  700.9 9.9 %collective-permute-done.106 = bf16[4,64,1024]{2,1,0:T(8,128)(2,1)S(1)} collective-permute-done((bf16[4,64,1024]{2,1,0:T(8,128)(2,1)}, bf16[4,64,1024]{2,1,0:T(8,128)(2,1)S(1)}, u32[]{:S(2)}, u32[]{:S(2)}) %collective-permute-start.106) | collective-permute-done | bytes 524320 | tf_op jit(solution)/shard_map/ppermute | solution.py:499
  710.8 8.6 %collective-permute-done.107 = bf16[4,64,1024]{2,1,0:T(8,128)(2,1)S(1)} collective-permute-done((bf16[4,64,1024]{2,1,0:T(8,128)(2,1)}, bf16[4,64,1024]{2,1,0:T(8,128)(2,1)S(1)}, u32[]{:S(2)}, u32[]{:S(2)}) %collective-permute-start.107) | collective-permute-done | bytes 524320 | tf_op jit(solution)/shard_map/ppermute | solution.py:499
  724.5 3.8 collective-permute-start.112
  729.2 12.0 %collective-permute-done.111 = bf16[128,2048]{1,0:T(8,128)(2,1)S(1)} collective-permute-done((bf16[128,2048]{1,0:T(8,128)(2,1)S(1)}, bf16[128,2048]{1,0:T(8,128)(2,1)S(1)}, u32[]{:S(2)}, u32[]{:S(2)}) %collective-permute-start.111) | collective-permute-done | bytes 524320 | tf_op jit(solution)/shard_map/ppermute | solution.py:499
  741.2 7.2 collective-permute-done.112
  761.7 4.3 collective-permute-done.117
  776.7 14.5 %collective-permute-done.121 = bf16[128,2048]{1,0:T(8,128)(2,1)S(1)} collective-permute-done((bf16[128,2048]{1,0:T(8,128)(2,1)S(1)}, bf16[128,2048]{1,0:T(8,128)(2,1)S(1)}, u32[]{:S(2)}, u32[]{:S(2)}) %collective-permute-start.121) | collective-permute-done | bytes 524320 | tf_op jit(solution)/shard_map/ppermute | solution.py:499
  798.2 7.1 collective-permute-done.127
  805.3 7.0 collective-permute-done.126
  (793 shorter events, 328.3 us)
Async XLA Ops:
  56.5 32.2 %collective-permute-start.14 = (bf16[192,2048]{1,0:T(8,128)(2,1)}, bf16[192,2048]{1,0:T(8,128)(2,1)S(1)}, u32[]{:S(2)}, u32[]{:S(2)}) collective-permute-start(bf16[192,2048]{1,0:T(8,128)(2,1)} %copy-done.71), channel_id=1, source_target_pairs={{0,2},{2,0},{1,3},{3,1},{4,6},{6,4},{5,7},{7,5},{8,10},{10,8},{9,1... | collective-permute-start | bytes 2359304 | tf_op jit(solution)/shard_map/ppermute | solution.py:503
  56.5 32.1 %collective-permute-start.12 = (bf16[4,64,1280]{2,1,0:T(8,128)(2,1)S(1)}, bf16[4,64,1280]{2,1,0:T(8,128)(2,1)S(1)}, u32[]{:S(2)}, u32[]{:S(2)}) collective-permute-start(bf16[4,64,1280]{2,1,0:T(8,128)(2,1)S(1)} %pad_maximum_fusion.12), channel_id=1, source_target_pairs={{0,16},{8,24},{16,0},{24,8},{1,17},{9,25},{17,1},{25,9},{2,18},{10... | collective-permute-start | bytes 1966088 | tf_op jit(solution)/shard_map/ppermute | solution.py:499
  59.1 29.5 %collective-permute-start.13 = (bf16[4,64,1280]{2,1,0:T(8,128)(2,1)}, bf16[4,64,1280]{2,1,0:T(8,128)(2,1)S(1)}, u32[]{:S(2)}, u32[]{:S(2)}) collective-permute-start(bf16[4,64,1280]{2,1,0:T(8,128)(2,1)} %copy-done.94), channel_id=1, source_target_pairs={{0,1},{1,0},{2,3},{3,2},{4,5},{5,4},{6,7},{7,6},{8,9},{9,8},{10,11... | collective-permute-start | bytes 1966088 | tf_op jit(solution)/shard_map/ppermute | solution.py:503
  60.6 26.8 %collective-permute-start.16 = (bf16[128,2048]{1,0:T(8,128)(2,1)}, bf16[128,2048]{1,0:T(8,128)(2,1)S(1)}, u32[]{:S(2)}, u32[]{:S(2)}) collective-permute-start(bf16[128,2048]{1,0:T(8,128)(2,1)} %get-tuple-element.653), channel_id=1, source_target_pairs={{0,1},{1,0},{2,3},{3,2},{4,5},{5,4},{6,7},{7,6},{8,9},{9,8},{10,11... | collective-permute-start | bytes 1572872 | tf_op jit(solution)/shard_map/ppermute | solution.py:503
  111.7 27.5 %collective-permute-start.23 = (bf16[192,2048]{1,0:T(8,128)(2,1)S(1)}, bf16[192,2048]{1,0:T(8,128)(2,1)S(1)}, u32[]{:S(2)}, u32[]{:S(2)}) collective-permute-start(bf16[192,2048]{1,0:T(8,128)(2,1)S(1)} %copy-done.20), channel_id=1, source_target_pairs={{0,4},{4,0},{1,5},{5,1},{2,6},{6,2},{3,7},{7,3},{8,12},{12,8},{9,1... | collective-permute-start | bytes 2359304 | tf_op jit(solution)/shard_map/ppermute | solution.py:503
  112.3 26.9 %collective-permute-start.21 = (bf16[4,64,1280]{2,1,0:T(8,128)(2,1)S(1)}, bf16[4,64,1280]{2,1,0:T(8,128)(2,1)S(1)}, u32[]{:S(2)}, u32[]{:S(2)}) collective-permute-start(bf16[4,64,1280]{2,1,0:T(8,128)(2,1)S(1)} %collective-permute-done.17), channel_id=1, source_target_pairs={{0,1},{1,0},{2,3},{3,2},{4,5},{5,4},{6,7},{7,6},{8,9},{9,8},{10,11... | collective-permute-start | bytes 1966088 | tf_op jit(solution)/shard_map/ppermute | solution.py:503
  143.5 26.4 %collective-permute-start.25 = (bf16[2,128,2048]{2,1,0:T(8,128)(2,1)S(1)}, bf16[2,128,2048]{2,1,0:T(8,128)(2,1)S(1)}, u32[]{:S(2)}, u32[]{:S(2)}) collective-permute-start(bf16[2,128,2048]{2,1,0:T(8,128)(2,1)S(1)} %pad_maximum_fusion.5), channel_id=1, source_target_pairs={{0,4},{4,0},{1,5},{5,1},{2,6},{6,2},{3,7},{7,3},{8,12},{12,8},{9,1... | collective-permute-start | bytes 3145736 | tf_op jit(solution)/shard_map/ppermute | solution.py:503
  173.1 31.8 %collective-permute-start.33 = (bf16[2,128,2048]{2,1,0:T(8,128)(2,1)}, bf16[2,128,2048]{2,1,0:T(8,128)(2,1)S(1)}, u32[]{:S(2)}, u32[]{:S(2)}) collective-permute-start(bf16[2,128,2048]{2,1,0:T(8,128)(2,1)} %pad_maximum_fusion.6), channel_id=1, source_target_pairs={{0,1},{1,0},{2,3},{3,2},{4,5},{5,4},{6,7},{7,6},{8,9},{9,8},{10,11... | collective-permute-start | bytes 3145736 | tf_op jit(solution)/shard_map/ppermute | solution.py:503
  174.6 30.3 %collective-permute-start.31 = (bf16[4,3,64,256]{3,2,1,0:T(8,128)(2,1)S(1)}, bf16[4,3,64,256]{3,2,1,0:T(8,128)(2,1)S(1)}, u32[]{:S(2)}, u32[]{:S(2)}) collective-permute-start(bf16[4,3,64,256]{3,2,1,0:T(8,128)(2,1)S(1)} %copy-done.53), channel_id=1, source_target_pairs={{0,16},{8,24},{16,0},{24,8},{1,17},{9,25},{17,1},{25,9},{2,18},{10... | collective-permute-start | bytes 1179656 | tf_op jit(solution)/shard_map/ppermute | solution.py:499
  179.2 30.9 %collective-permute-start.35 = (bf16[128,2048]{1,0:T(8,128)(2,1)S(1)}, bf16[128,2048]{1,0:T(8,128)(2,1)S(1)}, u32[]{:S(2)}, u32[]{:S(2)}) collective-permute-start(bf16[128,2048]{1,0:T(8,128)(2,1)S(1)} %slice_bitcast_fusion.2), channel_id=1, source_target_pairs={{0,1},{1,0},{2,3},{3,2},{4,5},{5,4},{6,7},{7,6},{8,9},{9,8},{10,11... | collective-permute-start | bytes 1572872 | tf_op jit(solution)/shard_map/ppermute | solution.py:503
  273.3 38.0 %collective-permute-start.46 = (bf16[1024,768]{1,0:T(8,128)(2,1)}, bf16[1024,768]{1,0:T(8,128)(2,1)}, u32[]{:S(2)}, u32[]{:S(2)}) collective-permute-start(bf16[1024,768]{1,0:T(8,128)(2,1)} %bitcast.93), channel_id=1, source_target_pairs={{0,1},{1,0},{2,3},{3,2},{4,5},{5,4},{6,7},{7,6},{8,9},{9,8},{10,11... | collective-permute-start | bytes 4718600 | tf_op jit(solution)/shard_map/ppermute | solution.py:503
  274.6 36.7 %collective-permute-start.45 = (bf16[192,2048]{1,0:T(8,128)(2,1)S(1)}, bf16[192,2048]{1,0:T(8,128)(2,1)}, u32[]{:S(2)}, u32[]{:S(2)}) collective-permute-start(bf16[192,2048]{1,0:T(8,128)(2,1)S(1)} %multiply_convert_fusion.refs_1_), channel_id=1, source_target_pairs={{0,16},{8,24},{16,0},{24,8},{1,17},{9,25},{17,1},{25,9},{2,18},{10... | collective-permute-start | bytes 2359304 | tf_op jit(solution)/shard_map/ppermute | solution.py:499
  274.6 36.7 %collective-permute-start.47 = (bf16[192,2048]{1,0:T(8,128)(2,1)}, bf16[192,2048]{1,0:T(8,128)(2,1)}, u32[]{:S(2)}, u32[]{:S(2)}) collective-permute-start(bf16[192,2048]{1,0:T(8,128)(2,1)} %copy-done.122), channel_id=1, source_target_pairs={{0,4},{4,0},{1,5},{5,1},{2,6},{6,2},{3,7},{7,3},{8,12},{12,8},{9,1... | collective-permute-start | bytes 2359304 | tf_op jit(solution)/shard_map/ppermute | solution.py:503
  275.4 35.9 %collective-permute-start.48 = (bf16[192,2048]{1,0:T(8,128)(2,1)S(1)}, bf16[192,2048]{1,0:T(8,128)(2,1)}, u32[]{:S(2)}, u32[]{:S(2)}) collective-permute-start(bf16[192,2048]{1,0:T(8,128)(2,1)S(1)} %multiply_convert_fusion.refs_1_), channel_id=1, source_target_pairs={{0,4},{4,0},{1,5},{5,1},{2,6},{6,2},{3,7},{7,3},{8,12},{12,8},{9,1... | collective-permute-start | bytes 2359304 | tf_op jit(solution)/shard_map/ppermute | solution.py:503
  276.7 34.6 %collective-permute-start.49 = (bf16[192,2048]{1,0:T(8,128)(2,1)}, bf16[192,2048]{1,0:T(8,128)(2,1)}, u32[]{:S(2)}, u32[]{:S(2)}) collective-permute-start(bf16[192,2048]{1,0:T(8,128)(2,1)} %copy-done.122), channel_id=1, source_target_pairs={{0,2},{2,0},{1,3},{3,1},{4,6},{6,4},{5,7},{7,5},{8,10},{10,8},{9,1... | collective-permute-start | bytes 2359304 | tf_op jit(solution)/shard_map/ppermute | solution.py:503
  311.3 28.7 %collective-permute-start.50 = (bf16[192,2048]{1,0:T(8,128)(2,1)S(1)}, bf16[192,2048]{1,0:T(8,128)(2,1)S(1)}, u32[]{:S(2)}, u32[]{:S(2)}) collective-permute-start(bf16[192,2048]{1,0:T(8,128)(2,1)S(1)} %multiply_convert_fusion.refs_1_), channel_id=1, source_target_pairs={{0,8},{8,16},{16,24},{24,0},{1,9},{9,17},{17,25},{25,1},{2,10},{10... | collective-permute-start | bytes 2359304 | tf_op jit(solution)/shard_map/ppermute | solution.py:499
  345.9 30.6 %collective-permute-start.59 = (bf16[192,2048]{1,0:T(8,128)(2,1)S(1)}, bf16[192,2048]{1,0:T(8,128)(2,1)}, u32[]{:S(2)}, u32[]{:S(2)}) collective-permute-start(bf16[192,2048]{1,0:T(8,128)(2,1)S(1)} %multiply_convert_fusion.refs_1_), channel_id=1, source_target_pairs={{0,24},{8,0},{16,8},{24,16},{1,25},{9,1},{17,9},{25,17},{2,26},{10... | collective-permute-start | bytes 2359304 | tf_op jit(solution)/shard_map/ppermute | solution.py:499
  348.7 27.7 %collective-permute-start.61 = (bf16[192,2048]{1,0:T(8,128)(2,1)S(1)}, bf16[192,2048]{1,0:T(8,128)(2,1)S(1)}, u32[]{:S(2)}, u32[]{:S(2)}) collective-permute-start(bf16[192,2048]{1,0:T(8,128)(2,1)S(1)} %collective-permute-done.50.refs_1_), channel_id=1, source_target_pairs={{0,4},{4,0},{1,5},{5,1},{2,6},{6,2},{3,7},{7,3},{8,12},{12,8},{9,1... | collective-permute-start | bytes 2359304 | tf_op jit(solution)/shard_map/ppermute | solution.py:503
  349.2 27.2 %collective-permute-start.63 = (bf16[192,2048]{1,0:T(8,128)(2,1)S(1)}, bf16[192,2048]{1,0:T(8,128)(2,1)}, u32[]{:S(2)}, u32[]{:S(2)}) collective-permute-start(bf16[192,2048]{1,0:T(8,128)(2,1)S(1)} %collective-permute-done.50.refs_1_), channel_id=1, source_target_pairs={{0,2},{2,0},{1,3},{3,1},{4,6},{6,4},{5,7},{7,5},{8,10},{10,8},{9,1... | collective-permute-start | bytes 2359304 | tf_op jit(solution)/shard_map/ppermute | solution.py:503
  349.3 27.1 %collective-permute-start.62 = (bf16[96,2048]{1,0:T(8,128)(2,1)}, bf16[96,2048]{1,0:T(8,128)(2,1)S(1)}, u32[]{:S(2)}, u32[]{:S(2)}) collective-permute-start(bf16[96,2048]{1,0:T(8,128)(2,1)} %collective-permute-done.51), channel_id=1, source_target_pairs={{0,4},{4,0},{1,5},{5,1},{2,6},{6,2},{3,7},{7,3},{8,12},{12,8},{9,1... | collective-permute-start | bytes 1179656 | tf_op jit(solution)/shard_map/ppermute | solution.py:503
  380.1 26.9 %collective-permute-start.70 = (bf16[2,192,2048]{2,1,0:T(8,128)(2,1)}, bf16[2,192,2048]{2,1,0:T(8,128)(2,1)}, u32[]{:S(2)}, u32[]{:S(2)}) collective-permute-start(bf16[2,192,2048]{2,1,0:T(8,128)(2,1)} %get-tuple-element.838), channel_id=1, source_target_pairs={{0,2},{2,0},{1,3},{3,1},{4,6},{6,4},{5,7},{7,5},{8,10},{10,8},{9,1... | collective-permute-start | bytes 4718600 | tf_op jit(solution)/shard_map/ppermute | solution.py:503
  381.0 28.6 %collective-permute-start.69 = (bf16[2,192,2176]{2,1,0:T(8,128)(2,1)}, bf16[2,192,2176]{2,1,0:T(8,128)(2,1)}, u32[]{:S(2)}, u32[]{:S(2)}) collective-permute-start(bf16[2,192,2176]{2,1,0:T(8,128)(2,1)} %get-tuple-element.837), channel_id=1, source_target_pairs={{0,2},{2,0},{1,3},{3,1},{4,6},{6,4},{5,7},{7,5},{8,10},{10,8},{9,1... | collective-permute-start | bytes 5013512 | tf_op jit(solution)/shard_map/ppermute | solution.py:503
  381.2 29.9 %collective-permute-start.66 = (bf16[192,2048]{1,0:T(8,128)(2,1)}, bf16[192,2048]{1,0:T(8,128)(2,1)}, u32[]{:S(2)}, u32[]{:S(2)}) collective-permute-start(bf16[192,2048]{1,0:T(8,128)(2,1)} %collective-permute-done.59.refs_1_), channel_id=1, source_target_pairs={{0,4},{4,0},{1,5},{5,1},{2,6},{6,2},{3,7},{7,3},{8,12},{12,8},{9,1... | collective-permute-start | bytes 2359304 | tf_op jit(solution)/shard_map/ppermute | solution.py:503
  381.8 29.3 %collective-permute-start.68 = (bf16[192,2048]{1,0:T(8,128)(2,1)S(1)}, bf16[192,2048]{1,0:T(8,128)(2,1)}, u32[]{:S(2)}, u32[]{:S(2)}) collective-permute-start(bf16[192,2048]{1,0:T(8,128)(2,1)S(1)} %pad_maximum_fusion.11.refs_5_), channel_id=1, source_target_pairs={{0,2},{2,0},{1,3},{3,1},{4,6},{6,4},{5,7},{7,5},{8,10},{10,8},{9,1... | collective-permute-start | bytes 2359304 | tf_op jit(solution)/shard_map/ppermute | solution.py:503
  381.8 29.2 %collective-permute-start.67 = (bf16[96,2048]{1,0:T(8,128)(2,1)}, bf16[96,2048]{1,0:T(8,128)(2,1)S(1)}, u32[]{:S(2)}, u32[]{:S(2)}) collective-permute-start(bf16[96,2048]{1,0:T(8,128)(2,1)} %collective-permute-done.60), channel_id=1, source_target_pairs={{0,4},{4,0},{1,5},{5,1},{2,6},{6,2},{3,7},{7,3},{8,12},{12,8},{9,1... | collective-permute-start | bytes 1179656 | tf_op jit(solution)/shard_map/ppermute | solution.py:503
  414.6 27.3 %collective-permute-start.76 = (bf16[2,192,2048]{2,1,0:T(8,128)(2,1)}, bf16[2,192,2048]{2,1,0:T(8,128)(2,1)}, u32[]{:S(2)}, u32[]{:S(2)}) collective-permute-start(bf16[2,192,2048]{2,1,0:T(8,128)(2,1)} %get-tuple-element.890), channel_id=1, source_target_pairs={{0,2},{2,0},{1,3},{3,1},{4,6},{6,4},{5,7},{7,5},{8,10},{10,8},{9,1... | collective-permute-start | bytes 4718600 | tf_op jit(solution)/shard_map/ppermute | solution.py:503
  415.5 29.1 %collective-permute-start.75 = (bf16[2,192,2176]{2,1,0:T(8,128)(2,1)}, bf16[2,192,2176]{2,1,0:T(8,128)(2,1)}, u32[]{:S(2)}, u32[]{:S(2)}) collective-permute-start(bf16[2,192,2176]{2,1,0:T(8,128)(2,1)} %get-tuple-element.889), channel_id=1, source_target_pairs={{0,2},{2,0},{1,3},{3,1},{4,6},{6,4},{5,7},{7,5},{8,10},{10,8},{9,1... | collective-permute-start | bytes 5013512 | tf_op jit(solution)/shard_map/ppermute | solution.py:503
  416.2 37.7 %collective-permute-start.73 = (bf16[192,2176]{1,0:T(8,128)(2,1)S(1)}, bf16[192,2176]{1,0:T(8,128)(2,1)}, u32[]{:S(2)}, u32[]{:S(2)}) collective-permute-start(bf16[192,2176]{1,0:T(8,128)(2,1)S(1)} %fusion.33), channel_id=1, source_target_pairs={{0,4},{4,0},{1,5},{5,1},{2,6},{6,2},{3,7},{7,3},{8,12},{12,8},{9,1... | collective-permute-start | bytes 2506760 | tf_op jit(solution)/shard_map/ppermute | solution.py:503
  416.7 37.2 %collective-permute-start.74 = (bf16[192,2048]{1,0:T(8,128)(2,1)}, bf16[192,2048]{1,0:T(8,128)(2,1)S(1)}, u32[]{:S(2)}, u32[]{:S(2)}) collective-permute-start(bf16[192,2048]{1,0:T(8,128)(2,1)} %fusion.38), channel_id=1, source_target_pairs={{0,4},{4,0},{1,5},{5,1},{2,6},{6,2},{3,7},{7,3},{8,12},{12,8},{9,1... | collective-permute-start | bytes 2359304 | tf_op jit(solution)/shard_map/ppermute | solution.py:503
  456.9 27.5 %collective-permute-start.81 = (bf16[2,192,2048]{2,1,0:T(8,128)(2,1)}, bf16[2,192,2048]{2,1,0:T(8,128)(2,1)}, u32[]{:S(2)}, u32[]{:S(2)}) collective-permute-start(bf16[2,192,2048]{2,1,0:T(8,128)(2,1)} %get-tuple-element.938), channel_id=1, source_target_pairs={{0,2},{2,0},{1,3},{3,1},{4,6},{6,4},{5,7},{7,5},{8,10},{10,8},{9,1... | collective-permute-start | bytes 4718600 | tf_op jit(solution)/shard_map/ppermute | solution.py:503
  457.0 30.1 %collective-permute-start.80 = (bf16[2,192,2176]{2,1,0:T(8,128)(2,1)}, bf16[2,192,2176]{2,1,0:T(8,128)(2,1)}, u32[]{:S(2)}, u32[]{:S(2)}) collective-permute-start(bf16[2,192,2176]{2,1,0:T(8,128)(2,1)} %get-tuple-element.937), channel_id=1, source_target_pairs={{0,2},{2,0},{1,3},{3,1},{4,6},{6,4},{5,7},{7,5},{8,10},{10,8},{9,1... | collective-permute-start | bytes 5013512 | tf_op jit(solution)/shard_map/ppermute | solution.py:503
  458.2 39.2 %collective-permute-start.77 = (bf16[192,2176]{1,0:T(8,128)(2,1)}, bf16[192,2176]{1,0:T(8,128)(2,1)S(1)}, u32[]{:S(2)}, u32[]{:S(2)}) collective-permute-start(bf16[192,2176]{1,0:T(8,128)(2,1)} %fusion.11), channel_id=1, source_target_pairs={{0,16},{8,24},{16,0},{24,8},{1,17},{9,25},{17,1},{25,9},{2,18},{10... | collective-permute-start | bytes 2506760 | tf_op jit(solution)/shard_map/ppermute | solution.py:499
  458.3 39.1 %collective-permute-start.78 = (bf16[192,2176]{1,0:T(8,128)(2,1)}, bf16[192,2176]{1,0:T(8,128)(2,1)}, u32[]{:S(2)}, u32[]{:S(2)}) collective-permute-start(bf16[192,2176]{1,0:T(8,128)(2,1)} %fusion.34), channel_id=1, source_target_pairs={{0,4},{4,0},{1,5},{5,1},{2,6},{6,2},{3,7},{7,3},{8,12},{12,8},{9,1... | collective-permute-start | bytes 2506760 | tf_op jit(solution)/shard_map/ppermute | solution.py:503
  458.9 37.2 %collective-permute-start.79 = (bf16[192,2048]{1,0:T(8,128)(2,1)}, bf16[192,2048]{1,0:T(8,128)(2,1)}, u32[]{:S(2)}, u32[]{:S(2)}) collective-permute-start(bf16[192,2048]{1,0:T(8,128)(2,1)} %fusion.39), channel_id=1, source_target_pairs={{0,4},{4,0},{1,5},{5,1},{2,6},{6,2},{3,7},{7,3},{8,12},{12,8},{9,1... | collective-permute-start | bytes 2359304 | tf_op jit(solution)/shard_map/ppermute | solution.py:503
  581.4 39.1 %collective-permute-start.94 = (bf16[3,128,2048]{2,1,0:T(8,128)(2,1)S(1)}, bf16[3,128,2048]{2,1,0:T(8,128)(2,1)S(1)}, u32[]{:S(2)}, u32[]{:S(2)}) collective-permute-start(bf16[3,128,2048]{2,1,0:T(8,128)(2,1)S(1)} %dynamic-slice_bitcast_fusion.1), channel_id=1, source_target_pairs={{0,1},{1,0},{2,3},{3,2},{4,5},{5,4},{6,7},{7,6},{8,9},{9,8},{10,11... | collective-permute-start | bytes 4718600 | tf_op jit(solution)/shard_map/ppermute | solution.py:503
  582.7 37.7 %collective-permute-start.95 = (bf16[192,2048]{1,0:T(8,128)(2,1)}, bf16[192,2048]{1,0:T(8,128)(2,1)}, u32[]{:S(2)}, u32[]{:S(2)}) collective-permute-start(bf16[192,2048]{1,0:T(8,128)(2,1)} %fusion.24), channel_id=1, source_target_pairs={{0,16},{8,24},{16,0},{24,8},{1,17},{9,25},{17,1},{25,9},{2,18},{10... | collective-permute-start | bytes 2359304 | tf_op jit(solution)/shard_map/ppermute | solution.py:499
  583.9 36.5 %collective-permute-start.96 = (bf16[192,2048]{1,0:T(8,128)(2,1)}, bf16[192,2048]{1,0:T(8,128)(2,1)}, u32[]{:S(2)}, u32[]{:S(2)}) collective-permute-start(bf16[192,2048]{1,0:T(8,128)(2,1)} %fusion.40), channel_id=1, source_target_pairs={{0,4},{4,0},{1,5},{5,1},{2,6},{6,2},{3,7},{7,3},{8,12},{12,8},{9,1... | collective-permute-start | bytes 2359304 | tf_op jit(solution)/shard_map/ppermute | solution.py:503
  585.4 35.0 %collective-permute-start.97 = (bf16[192,2048]{1,0:T(8,128)(2,1)}, bf16[192,2048]{1,0:T(8,128)(2,1)}, u32[]{:S(2)}, u32[]{:S(2)}) collective-permute-start(bf16[192,2048]{1,0:T(8,128)(2,1)} %fusion.41), channel_id=1, source_target_pairs={{0,4},{4,0},{1,5},{5,1},{2,6},{6,2},{3,7},{7,3},{8,12},{12,8},{9,1... | collective-permute-start | bytes 2359304 | tf_op jit(solution)/shard_map/ppermute | solution.py:503
  621.3 39.3 %collective-permute-start.101 = (bf16[512,1024]{1,0:T(8,128)(2,1)S(1)}, bf16[512,1024]{1,0:T(8,128)(2,1)S(1)}, u32[]{:S(2)}, u32[]{:S(2)}) collective-permute-start(bf16[512,1024]{1,0:T(8,128)(2,1)S(1)} %pad_maximum_fusion.8), channel_id=1, source_target_pairs={{0,1},{1,0},{2,3},{3,2},{4,5},{5,4},{6,7},{7,6},{8,9},{9,8},{10,11... | collective-permute-start | bytes 3145736 | tf_op jit(solution)/shard_map/ppermute | solution.py:503
  622.2 38.4 %collective-permute-start.102 = (bf16[2,128,2048]{2,1,0:T(8,128)(2,1)S(1)}, bf16[2,128,2048]{2,1,0:T(8,128)(2,1)S(1)}, u32[]{:S(2)}, u32[]{:S(2)}) collective-permute-start(bf16[2,128,2048]{2,1,0:T(8,128)(2,1)S(1)} %fusion.1), channel_id=1, source_target_pairs={{0,4},{4,0},{1,5},{5,1},{2,6},{6,2},{3,7},{7,3},{8,12},{12,8},{9,1... | collective-permute-start | bytes 3145736 | tf_op jit(solution)/shard_map/ppermute | solution.py:503
  627.5 33.1 %collective-permute-start.99 = (bf16[4,3,64,256]{3,2,1,0:T(8,128)(2,1)S(1)}, bf16[4,3,64,256]{3,2,1,0:T(8,128)(2,1)S(1)}, u32[]{:S(2)}, u32[]{:S(2)}) collective-permute-start(bf16[4,3,64,256]{3,2,1,0:T(8,128)(2,1)S(1)} %get-tuple-element.1056), channel_id=1, source_target_pairs={{0,16},{8,24},{16,0},{24,8},{1,17},{9,25},{17,1},{25,9},{2,18},{10... | collective-permute-start | bytes 1179656 | tf_op jit(solution)/shard_map/ppermute | solution.py:499
  663.4 27.2 %collective-permute-start.104 = (bf16[2,4,64,1024]{3,2,1,0:T(8,128)(2,1)S(1)}, bf16[2,4,64,1024]{3,2,1,0:T(8,128)(2,1)S(1)}, u32[]{:S(2)}, u32[]{:S(2)}) collective-permute-start(bf16[2,4,64,1024]{3,2,1,0:T(8,128)(2,1)S(1)} %pad_maximum_fusion.9), channel_id=1, source_target_pairs={{0,1},{1,0},{2,3},{3,2},{4,5},{5,4},{6,7},{7,6},{8,9},{9,8},{10,11... | collective-permute-start | bytes 3145736 | tf_op jit(solution)/shard_map/ppermute | solution.py:503
  664.6 25.9 %collective-permute-start.105 = (bf16[2,128,2048]{2,1,0:T(8,128)(2,1)S(1)}, bf16[2,128,2048]{2,1,0:T(8,128)(2,1)S(1)}, u32[]{:S(2)}, u32[]{:S(2)}) collective-permute-start(bf16[2,128,2048]{2,1,0:T(8,128)(2,1)S(1)} %pad_maximum_fusion.10), channel_id=1, source_target_pairs={{0,2},{2,0},{1,3},{3,1},{4,6},{6,4},{5,7},{7,5},{8,10},{10,8},{9,1... | collective-permute-start | bytes 3145736 | tf_op jit(solution)/shard_map/ppermute | solution.py:503
  664.6 25.9 %collective-permute-start.103 = (bf16[4,64,1024]{2,1,0:T(8,128)(2,1)S(1)}, bf16[4,64,1024]{2,1,0:T(8,128)(2,1)S(1)}, u32[]{:S(2)}, u32[]{:S(2)}) collective-permute-start(bf16[4,64,1024]{2,1,0:T(8,128)(2,1)S(1)} %fusion.32), channel_id=1, source_target_pairs={{0,16},{8,24},{16,0},{24,8},{1,17},{9,25},{17,1},{25,9},{2,18},{10... | collective-permute-start | bytes 1572872 | tf_op jit(solution)/shard_map/ppermute | solution.py:499
  693.1 28.6 %collective-permute-start.110 = (bf16[2,192,2048]{2,1,0:T(8,128)(2,1)}, bf16[2,192,2048]{2,1,0:T(8,128)(2,1)S(1)}, u32[]{:S(2)}, u32[]{:S(2)}) collective-permute-start(bf16[2,192,2048]{2,1,0:T(8,128)(2,1)} %bitcast.161), channel_id=1, source_target_pairs={{0,2},{2,0},{1,3},{3,1},{4,6},{6,4},{5,7},{7,5},{8,10},{10,8},{9,1... | collective-permute-start | bytes 4718600 | tf_op jit(solution)/shard_map/ppermute | solution.py:503
  693.2 28.5 %collective-permute-start.109 = (bf16[4,4,80,256]{3,2,1,0:T(8,128)(2,1)}, bf16[4,4,80,256]{3,2,1,0:T(8,128)(2,1)S(1)}, u32[]{:S(2)}, u32[]{:S(2)}) collective-permute-start(bf16[4,4,80,256]{3,2,1,0:T(8,128)(2,1)} %get-tuple-element.1094), channel_id=1, source_target_pairs={{0,1},{1,0},{2,3},{3,2},{4,5},{5,4},{6,7},{7,6},{8,9},{9,8},{10,11... | collective-permute-start | bytes 1966088 | tf_op jit(solution)/shard_map/ppermute | solution.py:503
  721.9 27.8 %collective-permute-start.113 = (bf16[192,2048]{1,0:T(8,128)(2,1)S(1)}, bf16[192,2048]{1,0:T(8,128)(2,1)S(1)}, u32[]{:S(2)}, u32[]{:S(2)}) collective-permute-start(bf16[192,2048]{1,0:T(8,128)(2,1)S(1)} %fusion.42), channel_id=1, source_target_pairs={{0,4},{4,0},{1,5},{5,1},{2,6},{6,2},{3,7},{7,3},{8,12},{12,8},{9,1... | collective-permute-start | bytes 2359304 | tf_op jit(solution)/shard_map/ppermute | solution.py:503
  723.3 26.4 %collective-permute-start.115 = (bf16[144,2048]{1,0:T(8,128)(2,1)S(1)}, bf16[144,2048]{1,0:T(8,128)(2,1)S(1)}, u32[]{:S(2)}, u32[]{:S(2)}) collective-permute-start(bf16[144,2048]{1,0:T(8,128)(2,1)S(1)} %copy-done.97), channel_id=1, source_target_pairs={{0,1},{1,0},{2,3},{3,2},{4,5},{5,4},{6,7},{7,6},{8,9},{9,8},{10,11... | collective-permute-start | bytes 1769480 | tf_op jit(solution)/shard_map/ppermute | solution.py:503
  (234 other events, 3062.2 us)

commit v6 on v5

--- a/solution.py
+++ b/solution.py
@@ -1056,24 +1056,22 @@
     normed_low = normed_attn.astype(low)
     held = [ordered]
     over_x = []
-    (moved, cross, other, near, packed_far), _, _ = step(
+    (moved, cross, other, near), _, _ = step(
         [
             (ordered, "z", 1),
             (ordered, "x"),
             (normed_low, "y"),
             (normed_low, "c"),
-            (packed, "y"),
         ]
     )
     held.append(moved)
     over_x.append(cross)
-    packed = jnp.stack([packed, packed_far], 1)
-    (moved, cross, other_near, packed_near, down1), tables, _ = step(
+    (moved, cross, other_near, packed_far, down1), tables, _ = step(
         [
             (ordered, "z", 2),
             (held[1], "x"),
             (other, "c"),
-            (packed, "c"),
+            (packed, "y"),
             (w_down[0, third : 2 * third], "x"),
         ],
         make_tables,
@@ -1083,11 +1081,11 @@
     held.append(moved)
     over_x.append(cross)
     normed_all = jnp.concatenate([normed_low, other, near, other_near])
+    packed = jnp.stack([packed, packed_far], 1)
+    (moved, cross, c_near0, packed_near), _, _ = step(
+        [(ordered, "z", 3), (held[2], "x"), (cotangent, "c"), (packed, "c")]
+    )
     packed = jnp.stack([packed, packed_near], 1)
-    (moved, cross, c_near0, packed_cross), _, _ = step(
-        [(ordered, "z", 3), (held[2], "x"), (cotangent, "c"), (packed, "x")]
-    )
-    packed = jnp.stack([packed, packed_cross], 1)
     held.append(moved)
     over_x.append(cross)
     cut = rows // 2
@@ -1099,11 +1097,19 @@
         halves = (cotangent[:cut], cotangent[cut:])
         return jnp.stack([own, one, one, three]), gates, down[2 * third :], halves
 
-    (cross, plane2, c_far0, down0), (planes, gate_pieces, down_piece, c_halves), _ = step(
-        [(held[3], "x"), (w_output, "z", 2), (cotangent, "y"), (w_down[0, :third], "x")],
+    moved, (planes, gate_pieces, down_piece, c_halves), _ = step(
+        [
+            (held[3], "x"),
+            (w_output, "z", 2),
+            (cotangent, "y"),
+            (w_down[0, :third], "x"),
+            (packed, "x"),
+        ],
         cut_pieces,
         (w_output, plane1, plane3, w_gate[0], w_down[0], cotangent),
     )
+    cross, plane2, c_far0, down0, packed_cross = moved
+    packed = jnp.stack([packed, packed_cross], 1)
     over_x.append(cross)
 
     def assemble(start, stop):

time: 835 us -> 835 us (level)
    unnamed x307 -> x315, local copies, waits for them, and re-layouts: 16.5 us -> 20 us
  transfers between devices with their start and end apart: 133 -> 133, of which waited for: 57 -> 58; matrix products, arithmetic and copies ran while one was open for 21% -> 20% of each run, Pallas kernels for 15% -> 15%
where the time goes in v6:
time: 835 us; the launch traced here: 825 us
  waiting for transfers between devices  342 us (41%)
  starting transfers between devices  131 us (16%)
  Pallas kernels  128 us (15%)
  local copies, waits for them, and re-layouts  89.3 us (11%)
  other arithmetic  76.7 us (9%)
  matrix products  55 us (7%)
    ppermute x41, waiting for transfers between devices, shift(): lax.ppermute(block, axis, [(i, (i + step) % count) for i in range(count)])  217 us
    ppermute x92, waiting for transfers between devices, swap(): return lax.ppermute(block, axis, [(0, 1), (1, 0)])  125 us
    pallas_call x4, Pallas kernels, experts(): pl.pallas_call(expert_kernel, grid_spec=pltpu.PrefetchScalarGridSpec(num_...  94.6 us
    ppermute x41, starting transfers between devices, shift(): lax.ppermute(block, axis, [(i, (i + step) % count) for i in range(count)])  67.5 us
    ppermute x92, starting transfers between devices, swap(): return lax.ppermute(block, axis, [(0, 1), (1, 0)])  63.5 us
    dot_general x13, matrix products, dot32(): jnp.einsum(subscripts, left, right, preferred_element_type=jnp.float32)  44.5 us
    pallas_call x1, Pallas kernels, attend_back(): pl.pallas_call(attend_back_kernel, grid_spec=pltpu.PrefetchScalarGridSpec...  20.8 us
    unnamed x315, local copies, waits for them, and re-layouts  20 us
  transfers between devices with their start and end apart: 133, of which 58 were waited for; matrix products, arithmetic and copies ran while one was open for 20% of the time, Pallas kernels for 15%

profile of v6, /device:TPU:0, one launch (start us, length us, event | category | flops | bytes accessed | tf_op | source)
XLA Modules:
  0.0 825.5 jit_solution(692911550998653768)
XLA Ops:
  9.4 8.6 %collective-permute-done = bf16[128,2048]{1,0:T(8,128)(2,1)} collective-permute-done((bf16[128,2048]{1,0:T(8,128)(2,1)}, bf16[128,2048]{1,0:T(8,128)(2,1)}, u32[]{:S(2)}, u32[]{:S(2)}) %collective-permute-start) | collective-permute-done | bytes 524320 | tf_op jit(solution)/shard_map/ppermute | solution.py:499
  28.9 3.7 collective-permute-done.2
  39.9 12.1 %collective-permute-done.7 = bf16[4,64,1280]{2,1,0:T(8,128)(2,1)S(1)} collective-permute-done((bf16[4,64,1280]{2,1,0:T(8,128)(2,1)S(1)}, bf16[4,64,1280]{2,1,0:T(8,128)(2,1)S(1)}, u32[]{:S(2)}, u32[]{:S(2)}) %collective-permute-start.7) | collective-permute-done | bytes 655392 | tf_op jit(solution)/shard_map/ppermute | solution.py:499
  67.2 17.9 %collective-permute-done.15 = bf16[128,2048]{1,0:T(8,128)(2,1)S(1)} collective-permute-done((bf16[128,2048]{1,0:T(8,128)(2,1)}, bf16[128,2048]{1,0:T(8,128)(2,1)S(1)}, u32[]{:S(2)}, u32[]{:S(2)}) %collective-permute-start.15) | collective-permute-done | bytes 524320 | tf_op jit(solution)/shard_map/ppermute | solution.py:503
  94.0 11.1 %collective-permute-done.16 = bf16[4,64,1280]{2,1,0:T(8,128)(2,1)S(1)} collective-permute-done((bf16[4,64,1280]{2,1,0:T(8,128)(2,1)}, bf16[4,64,1280]{2,1,0:T(8,128)(2,1)S(1)}, u32[]{:S(2)}, u32[]{:S(2)}) %collective-permute-start.16) | collective-permute-done | bytes 655392 | tf_op jit(solution)/shard_map/ppermute | solution.py:499
  118.9 19.2 %collective-permute-done.24 = bf16[4,2,2,20,128]{4,3,2,1,0:T(8,128)(2,1)S(1)} collective-permute-done((bf16[4,2,2,20,128]{4,3,2,1,0:T(8,128)(2,1)S(1)}, bf16[4,2,2,20,128]{4,3,2,1,0:T(8,128)(2,1)S(1)}, u32[]{:S(2)}, u32[]{:S(2)}) %collective-permute-start.24) | collective-permute-done | bytes 81952 | tf_op jit(solution)/shard_map/ppermute | solution.py:503
  149.3 19.8 %collective-permute-done.28 = bf16[320,768]{1,0:T(8,128)(2,1)S(1)} collective-permute-done((bf16[320,768]{1,0:T(8,128)(2,1)S(1)}, bf16[320,768]{1,0:T(8,128)(2,1)S(1)}, u32[]{:S(2)}, u32[]{:S(2)}) %collective-permute-start.28) | collective-permute-done | bytes 491552 | tf_op jit(solution)/shard_map/ppermute | solution.py:503
  174.0 4.0 collective-permute-start.31
  180.5 6.1 fusion.81
  187.6 16.4 %collective-permute-done.31 = bf16[4,3,64,256]{3,2,1,0:T(8,128)(2,1)S(1)} collective-permute-done((bf16[4,3,64,256]{3,2,1,0:T(8,128)(2,1)}, bf16[4,3,64,256]{3,2,1,0:T(8,128)(2,1)S(1)}, u32[]{:S(2)}, u32[]{:S(2)}) %collective-permute-start.31) | collective-permute-done | bytes 393248 | tf_op jit(solution)/shard_map/ppermute | solution.py:499
  204.1 5.0 collective-permute-done.35
  217.0 12.2 %shard_map.263 = bf16[4,3,64,1024]{3,2,1,0:T(8,128)(2,1)S(1)} custom-call(s32[2]{0:T(128)S(1)} %pad_add_fusion.places_ref, f32[4,3,64,1024]{3,2,1,0:T(8,128)S(1)} %bitcast.525, bf16[4,4,3,64,256]{4,3,2,1,0:T(8,128)(2,1)S(1)} %pad_maximum_fusion.4.k_ref.v_ref, bf16[4,4,3,64,256]{4,3,2,1,0:T(8,128)(2,1)S(1)} %pad_maximum_fusion.4.k_ref.v_ref, ...), custom_call_target="tpu_custom_call" | custom-call | flops 3221225472 | bytes 8388608 | tf_op jit(solution)/shard_map/pallas_call | solution.py:768
  252.2 12.0 %collective-permute-done.44 = bf16[192,2048]{1,0:T(8,128)(2,1)} collective-permute-done((bf16[192,2048]{1,0:T(8,128)(2,1)}, bf16[192,2048]{1,0:T(8,128)(2,1)}, u32[]{:S(2)}, u32[]{:S(2)}) %collective-permute-start.44) | collective-permute-done | bytes 786464 | tf_op jit(solution)/shard_map/ppermute | solution.py:503
  266.4 3.9 collective-permute-done.41
  294.9 15.8 %collective-permute-done.45.refs_1_ = bf16[192,2048]{1,0:T(8,128)(2,1)} collective-permute-done((bf16[192,2048]{1,0:T(8,128)(2,1)S(1)}, bf16[192,2048]{1,0:T(8,128)(2,1)}, u32[]{:S(2)}, u32[]{:S(2)}) %collective-permute-start.45) | collective-permute-done | bytes 786464 | tf_op jit(solution)/shard_map/ppermute | solution.py:499
  310.7 3.5 collective-permute-start.50
  323.3 15.9 %collective-permute-done.51 = bf16[96,2048]{1,0:T(8,128)(2,1)} collective-permute-done((bf16[96,2048]{1,0:T(8,128)(2,1)S(1)}, bf16[96,2048]{1,0:T(8,128)(2,1)}, u32[]{:S(2)}, u32[]{:S(2)}) %collective-permute-start.51) | collective-permute-done | bytes 393248 | tf_op jit(solution)/shard_map/ppermute | solution.py:499
  350.4 23.4 %shard_map.264 = (bf16[4,4,128,2048]{3,2,1,0:T(8,128)(2,1)}, bf16[4,4,128,768]{3,2,1,0:T(8,128)(2,1)}, bf16[4,4,128,2048]{3,2,1,0:T(8,128)(2,1)}, bf16[4,4,128,7...) custom-call(s32[2]{0:T(128)} %get-tuple-element.1379.refs_0_, ...), custom_call_target="tpu_custom_call" | custom-call | flops 9663676416 | bytes 41943040 | tf_op jit(solution)/shard_map/pallas_call | solution.py:919
  383.0 23.5 %shard_map.265 = (bf16[4,4,128,2048]{3,2,1,0:T(8,128)(2,1)}, bf16[4,4,128,768]{3,2,1,0:T(8,128)(2,1)}, bf16[4,4,128,2048]{3,2,1,0:T(8,128)(2,1)}, bf16[4,4,128,7...) custom-call(s32[2]{0:T(128)} %get-tuple-element.1380.refs_0_, ...), custom_call_target="tpu_custom_call", output_to_operand_aliasing={{0}: (15, {}), {1}: (16, {}), {2}: (17, {}), {3}: (18, {}),... | custom-call | flops 9663676416 | bytes 41943040 | tf_op jit(solution)/shard_map/pallas_call | solution.py:919
  417.9 23.6 %shard_map.266 = (bf16[4,4,128,2048]{3,2,1,0:T(8,128)(2,1)}, bf16[4,4,128,768]{3,2,1,0:T(8,128)(2,1)}, bf16[4,4,128,2048]{3,2,1,0:T(8,128)(2,1)}, bf16[4,4,128,7...) custom-call(s32[2]{0:T(128)} %get-tuple-element.1381.refs_0_, ...), custom_call_target="tpu_custom_call", output_to_operand_aliasing={{0}: (15, {}), {1}: (16, {}), {2}: (17, {}), {3}: (18, {}),... | custom-call | flops 9663676416 | bytes 41943040 | tf_op jit(solution)/shard_map/pallas_call | solution.py:919
  446.6 7.0 collective-permute-done.74
  460.0 24.0 %shard_map.267 = (bf16[4,4,128,2048]{3,2,1,0:T(8,128)(2,1)}, bf16[4,4,128,768]{3,2,1,0:T(8,128)(2,1)}, bf16[4,4,128,2048]{3,2,1,0:T(8,128)(2,1)}, bf16[4,4,128,7...) custom-call(s32[2]{0:T(128)} %get-tuple-element.1382.refs_0_, ...), custom_call_target="tpu_custom_call", output_to_operand_aliasing={{0}: (15, {}), {1}: (16, {}), {2}: (17, {}), {3}: (18, {}),... | custom-call | flops 9663676416 | bytes 41943040 | tf_op jit(solution)/shard_map/pallas_call | solution.py:919
  488.3 7.4 collective-permute-done.79
  501.9 9.3 %fusion.83 = f32[768,2048]{1,0:T(8,128)S(1)} fusion(bf16[2048,768]{1,0:T(8,128)(2,1)S(1)} %bitcast.537, bf16[2048,2048]{1,0:T(8,128)(2,1)} %bitcast.536), kind=kOutput, calls=%fused_computation.380 | convolution fusion | flops 6442450944 | bytes 17825792 | tf_op jit(solution)/shard_map/sf,sd->fd/dot_general | solution.py:936
  525.5 7.4 fusion.84
  539.0 6.4 collective-permute-done.86
  554.3 7.4 fusion.85
  568.4 3.4 collective-permute-done.92
  577.4 3.8 convolution_convert_fusion.1
  585.7 3.5 convolution_convert_fusion.4
  589.1 20.8 %shard_map.268 = (bf16[4,3,64,1024]{3,2,1,0:T(8,128)(2,1)S(1)}, f32[4,4,3,64,256]{4,3,2,1,0:T(8,128)S(1)}, f32[8,128]{1,0:T(8,128)S(1)}) custom-call(s32[2]{0:T(128)S(1)} %pad_add_fusion.places_ref, f32[4,3,64,1024]{3,2,1,0:T(8,128)S(1)} %bitcast.526, bf16[4,3,64,1024]{3,2,1,0:T(8,128)(2,1)S(1)} %bitcast.531, ...), custom_call_target="tpu_custom_call" | custom-call | flops 8053063680 | bytes 16777216 | tf_op jit(solution)/shard_map/pallas_call | solution.py:788
  610.0 3.7 convolution_convert_fusion
  614.2 6.0 collective-permute-done.95
  623.7 3.5 collective-permute-start.100
  628.7 5.4 fusion.86
  639.5 5.7 collective-permute-done.98
  645.3 15.3 %collective-permute-done.99 = bf16[4,3,64,256]{3,2,1,0:T(8,128)(2,1)S(1)} collective-permute-done((bf16[4,3,64,256]{3,2,1,0:T(8,128)(2,1)S(1)}, bf16[4,3,64,256]{3,2,1,0:T(8,128)(2,1)S(1)}, u32[]{:S(2)}, u32[]{:S(2)}) %collective-permute-start.99) | collective-permute-done | bytes 393248 | tf_op jit(solution)/shard_map/ppermute | solution.py:499
  673.0 17.8 %collective-permute-done.103 = bf16[4,64,1024]{2,1,0:T(8,128)(2,1)S(1)} collective-permute-done((bf16[4,64,1024]{2,1,0:T(8,128)(2,1)S(1)}, bf16[4,64,1024]{2,1,0:T(8,128)(2,1)S(1)}, u32[]{:S(2)}, u32[]{:S(2)}) %collective-permute-start.103) | collective-permute-done | bytes 524320 | tf_op jit(solution)/shard_map/ppermute | solution.py:499
  694.5 3.8 collective-permute-start.107
  701.1 10.3 %collective-permute-done.106 = bf16[4,64,1024]{2,1,0:T(8,128)(2,1)S(1)} collective-permute-done((bf16[4,64,1024]{2,1,0:T(8,128)(2,1)}, bf16[4,64,1024]{2,1,0:T(8,128)(2,1)S(1)}, u32[]{:S(2)}, u32[]{:S(2)}) %collective-permute-start.106) | collective-permute-done | bytes 524320 | tf_op jit(solution)/shard_map/ppermute | solution.py:499
  711.4 8.6 %collective-permute-done.107 = bf16[4,64,1024]{2,1,0:T(8,128)(2,1)S(1)} collective-permute-done((bf16[4,64,1024]{2,1,0:T(8,128)(2,1)}, bf16[4,64,1024]{2,1,0:T(8,128)(2,1)S(1)}, u32[]{:S(2)}, u32[]{:S(2)}) %collective-permute-start.107) | collective-permute-done | bytes 524320 | tf_op jit(solution)/shard_map/ppermute | solution.py:499
  724.8 3.8 collective-permute-start.112
  729.5 12.0 %collective-permute-done.111 = bf16[128,2048]{1,0:T(8,128)(2,1)S(1)} collective-permute-done((bf16[128,2048]{1,0:T(8,128)(2,1)S(1)}, bf16[128,2048]{1,0:T(8,128)(2,1)S(1)}, u32[]{:S(2)}, u32[]{:S(2)}) %collective-permute-start.111) | collective-permute-done | bytes 524320 | tf_op jit(solution)/shard_map/ppermute | solution.py:499
  741.5 7.2 collective-permute-done.112
  761.9 4.3 collective-permute-done.117
  777.3 14.5 %collective-permute-done.121 = bf16[128,2048]{1,0:T(8,128)(2,1)S(1)} collective-permute-done((bf16[128,2048]{1,0:T(8,128)(2,1)S(1)}, bf16[128,2048]{1,0:T(8,128)(2,1)S(1)}, u32[]{:S(2)}, u32[]{:S(2)}) %collective-permute-start.121) | collective-permute-done | bytes 524320 | tf_op jit(solution)/shard_map/ppermute | solution.py:499
  798.7 6.8 collective-permute-done.127
  805.5 7.4 collective-permute-done.126
  (801 shorter events, 327.6 us)
Async XLA Ops:
  54.5 32.4 %collective-permute-start.13 = (bf16[192,2048]{1,0:T(8,128)(2,1)}, bf16[192,2048]{1,0:T(8,128)(2,1)S(1)}, u32[]{:S(2)}, u32[]{:S(2)}) collective-permute-start(bf16[192,2048]{1,0:T(8,128)(2,1)} %copy-done.76), channel_id=1, source_target_pairs={{0,2},{2,0},{1,3},{3,1},{4,6},{6,4},{5,7},{7,5},{8,10},{10,8},{9,1... | collective-permute-start | bytes 2359304 | tf_op jit(solution)/shard_map/ppermute | solution.py:503
  54.5 32.3 %collective-permute-start.11 = (bf16[4,64,1280]{2,1,0:T(8,128)(2,1)}, bf16[4,64,1280]{2,1,0:T(8,128)(2,1)S(1)}, u32[]{:S(2)}, u32[]{:S(2)}) collective-permute-start(bf16[4,64,1280]{2,1,0:T(8,128)(2,1)} %copy-done.41), channel_id=1, source_target_pairs={{0,16},{8,24},{16,0},{24,8},{1,17},{9,25},{17,1},{25,9},{2,18},{10... | collective-permute-start | bytes 1966088 | tf_op jit(solution)/shard_map/ppermute | solution.py:499
  56.8 30.0 %collective-permute-start.12 = (bf16[4,64,1280]{2,1,0:T(8,128)(2,1)}, bf16[4,64,1280]{2,1,0:T(8,128)(2,1)S(1)}, u32[]{:S(2)}, u32[]{:S(2)}) collective-permute-start(bf16[4,64,1280]{2,1,0:T(8,128)(2,1)} %copy-done.99), channel_id=1, source_target_pairs={{0,1},{1,0},{2,3},{3,2},{4,5},{5,4},{6,7},{7,6},{8,9},{9,8},{10,11... | collective-permute-start | bytes 1966088 | tf_op jit(solution)/shard_map/ppermute | solution.py:503
  58.3 26.8 %collective-permute-start.15 = (bf16[128,2048]{1,0:T(8,128)(2,1)}, bf16[128,2048]{1,0:T(8,128)(2,1)S(1)}, u32[]{:S(2)}, u32[]{:S(2)}) collective-permute-start(bf16[128,2048]{1,0:T(8,128)(2,1)} %get-tuple-element.651), channel_id=1, source_target_pairs={{0,1},{1,0},{2,3},{3,2},{4,5},{5,4},{6,7},{7,6},{8,9},{9,8},{10,11... | collective-permute-start | bytes 1572872 | tf_op jit(solution)/shard_map/ppermute | solution.py:503
  107.6 30.6 %collective-permute-start.22 = (bf16[192,2048]{1,0:T(8,128)(2,1)S(1)}, bf16[192,2048]{1,0:T(8,128)(2,1)S(1)}, u32[]{:S(2)}, u32[]{:S(2)}) collective-permute-start(bf16[192,2048]{1,0:T(8,128)(2,1)S(1)} %copy-done.20), channel_id=1, source_target_pairs={{0,4},{4,0},{1,5},{5,1},{2,6},{6,2},{3,7},{7,3},{8,12},{12,8},{9,1... | collective-permute-start | bytes 2359304 | tf_op jit(solution)/shard_map/ppermute | solution.py:503
  109.1 29.1 %collective-permute-start.20 = (bf16[4,64,1280]{2,1,0:T(8,128)(2,1)S(1)}, bf16[4,64,1280]{2,1,0:T(8,128)(2,1)S(1)}, u32[]{:S(2)}, u32[]{:S(2)}) collective-permute-start(bf16[4,64,1280]{2,1,0:T(8,128)(2,1)S(1)} %collective-permute-done.16), channel_id=1, source_target_pairs={{0,1},{1,0},{2,3},{3,2},{4,5},{5,4},{6,7},{7,6},{8,9},{9,8},{10,11... | collective-permute-start | bytes 1966088 | tf_op jit(solution)/shard_map/ppermute | solution.py:503
  110.6 27.5 %collective-permute-start.21 = (bf16[128,2048]{1,0:T(8,128)(2,1)S(1)}, bf16[128,2048]{1,0:T(8,128)(2,1)S(1)}, u32[]{:S(2)}, u32[]{:S(2)}) collective-permute-start(bf16[128,2048]{1,0:T(8,128)(2,1)S(1)} %copy-done.105), channel_id=1, source_target_pairs={{0,16},{8,24},{16,0},{24,8},{1,17},{9,25},{17,1},{25,9},{2,18},{10... | collective-permute-start | bytes 1572872 | tf_op jit(solution)/shard_map/ppermute | solution.py:499
  110.6 27.5 %collective-permute-start.23 = (bf16[128,2048]{1,0:T(8,128)(2,1)S(1)}, bf16[128,2048]{1,0:T(8,128)(2,1)S(1)}, u32[]{:S(2)}, u32[]{:S(2)}) collective-permute-start(bf16[128,2048]{1,0:T(8,128)(2,1)S(1)} %copy-done.113), channel_id=1, source_target_pairs={{0,1},{1,0},{2,3},{3,2},{4,5},{5,4},{6,7},{7,6},{8,9},{9,8},{10,11... | collective-permute-start | bytes 1572872 | tf_op jit(solution)/shard_map/ppermute | solution.py:503
  111.2 26.9 %collective-permute-start.24 = (bf16[4,2,2,20,128]{4,3,2,1,0:T(8,128)(2,1)S(1)}, bf16[4,2,2,20,128]{4,3,2,1,0:T(8,128)(2,1)S(1)}, u32[]{:S(2)}, u32[]{:S(2)}) collective-permute-start(bf16[4,2,2,20,128]{4,3,2,1,0:T(8,128)(2,1)S(1)} %get-tuple-element.666), channel_id=1, source_target_pairs={{0,1},{1,0},{2,3},{3,2},{4,5},{5,4},{6,7},{7,6},{8,9},{9,8},{10,11... | collective-permute-start | bytes 245768 | tf_op jit(solution)/shard_map/ppermute | solution.py:503
  142.8 26.4 %collective-permute-start.25 = (bf16[2,128,2048]{2,1,0:T(8,128)(2,1)S(1)}, bf16[2,128,2048]{2,1,0:T(8,128)(2,1)S(1)}, u32[]{:S(2)}, u32[]{:S(2)}) collective-permute-start(bf16[2,128,2048]{2,1,0:T(8,128)(2,1)S(1)} %pad_maximum_fusion.5), channel_id=1, source_target_pairs={{0,4},{4,0},{1,5},{5,1},{2,6},{6,2},{3,7},{7,3},{8,12},{12,8},{9,1... | collective-permute-start | bytes 3145736 | tf_op jit(solution)/shard_map/ppermute | solution.py:503
  172.1 32.0 %collective-permute-start.33 = (bf16[2,128,2048]{2,1,0:T(8,128)(2,1)}, bf16[2,128,2048]{2,1,0:T(8,128)(2,1)S(1)}, u32[]{:S(2)}, u32[]{:S(2)}) collective-permute-start(bf16[2,128,2048]{2,1,0:T(8,128)(2,1)} %pad_maximum_fusion.6), channel_id=1, source_target_pairs={{0,1},{1,0},{2,3},{3,2},{4,5},{5,4},{6,7},{7,6},{8,9},{9,8},{10,11... | collective-permute-start | bytes 3145736 | tf_op jit(solution)/shard_map/ppermute | solution.py:503
  174.0 30.1 %collective-permute-start.31 = (bf16[4,3,64,256]{3,2,1,0:T(8,128)(2,1)}, bf16[4,3,64,256]{3,2,1,0:T(8,128)(2,1)S(1)}, u32[]{:S(2)}, u32[]{:S(2)}) collective-permute-start(bf16[4,3,64,256]{3,2,1,0:T(8,128)(2,1)} %pad_maximum_fusion.13), channel_id=1, source_target_pairs={{0,16},{8,24},{16,0},{24,8},{1,17},{9,25},{17,1},{25,9},{2,18},{10... | collective-permute-start | bytes 1179656 | tf_op jit(solution)/shard_map/ppermute | solution.py:499
  179.9 29.2 %collective-permute-start.35 = (bf16[128,2048]{1,0:T(8,128)(2,1)S(1)}, bf16[128,2048]{1,0:T(8,128)(2,1)S(1)}, u32[]{:S(2)}, u32[]{:S(2)}) collective-permute-start(bf16[128,2048]{1,0:T(8,128)(2,1)S(1)} %slice_bitcast_fusion.2), channel_id=1, source_target_pairs={{0,1},{1,0},{2,3},{3,2},{4,5},{5,4},{6,7},{7,6},{8,9},{9,8},{10,11... | collective-permute-start | bytes 1572872 | tf_op jit(solution)/shard_map/ppermute | solution.py:503
  272.9 37.8 %collective-permute-start.46 = (bf16[1024,768]{1,0:T(8,128)(2,1)}, bf16[1024,768]{1,0:T(8,128)(2,1)}, u32[]{:S(2)}, u32[]{:S(2)}) collective-permute-start(bf16[1024,768]{1,0:T(8,128)(2,1)} %bitcast.93), channel_id=1, source_target_pairs={{0,1},{1,0},{2,3},{3,2},{4,5},{5,4},{6,7},{7,6},{8,9},{9,8},{10,11... | collective-permute-start | bytes 4718600 | tf_op jit(solution)/shard_map/ppermute | solution.py:503
  273.9 36.7 %collective-permute-start.45 = (bf16[192,2048]{1,0:T(8,128)(2,1)S(1)}, bf16[192,2048]{1,0:T(8,128)(2,1)}, u32[]{:S(2)}, u32[]{:S(2)}) collective-permute-start(bf16[192,2048]{1,0:T(8,128)(2,1)S(1)} %multiply_convert_fusion.refs_1_), channel_id=1, source_target_pairs={{0,16},{8,24},{16,0},{24,8},{1,17},{9,25},{17,1},{25,9},{2,18},{10... | collective-permute-start | bytes 2359304 | tf_op jit(solution)/shard_map/ppermute | solution.py:499
  274.1 36.5 %collective-permute-start.47 = (bf16[192,2048]{1,0:T(8,128)(2,1)}, bf16[192,2048]{1,0:T(8,128)(2,1)}, u32[]{:S(2)}, u32[]{:S(2)}) collective-permute-start(bf16[192,2048]{1,0:T(8,128)(2,1)} %copy-done.127), channel_id=1, source_target_pairs={{0,4},{4,0},{1,5},{5,1},{2,6},{6,2},{3,7},{7,3},{8,12},{12,8},{9,1... | collective-permute-start | bytes 2359304 | tf_op jit(solution)/shard_map/ppermute | solution.py:503
  275.6 35.1 %collective-permute-start.48 = (bf16[192,2048]{1,0:T(8,128)(2,1)S(1)}, bf16[192,2048]{1,0:T(8,128)(2,1)}, u32[]{:S(2)}, u32[]{:S(2)}) collective-permute-start(bf16[192,2048]{1,0:T(8,128)(2,1)S(1)} %multiply_convert_fusion.refs_1_), channel_id=1, source_target_pairs={{0,4},{4,0},{1,5},{5,1},{2,6},{6,2},{3,7},{7,3},{8,12},{12,8},{9,1... | collective-permute-start | bytes 2359304 | tf_op jit(solution)/shard_map/ppermute | solution.py:503
  276.2 34.5 %collective-permute-start.49 = (bf16[192,2048]{1,0:T(8,128)(2,1)}, bf16[192,2048]{1,0:T(8,128)(2,1)}, u32[]{:S(2)}, u32[]{:S(2)}) collective-permute-start(bf16[192,2048]{1,0:T(8,128)(2,1)} %copy-done.127), channel_id=1, source_target_pairs={{0,2},{2,0},{1,3},{3,1},{4,6},{6,4},{5,7},{7,5},{8,10},{10,8},{9,1... | collective-permute-start | bytes 2359304 | tf_op jit(solution)/shard_map/ppermute | solution.py:503
  310.7 28.5 %collective-permute-start.50 = (bf16[192,2048]{1,0:T(8,128)(2,1)S(1)}, bf16[192,2048]{1,0:T(8,128)(2,1)S(1)}, u32[]{:S(2)}, u32[]{:S(2)}) collective-permute-start(bf16[192,2048]{1,0:T(8,128)(2,1)S(1)} %multiply_convert_fusion.refs_1_), channel_id=1, source_target_pairs={{0,8},{8,16},{16,24},{24,0},{1,9},{9,17},{17,25},{25,1},{2,10},{10... | collective-permute-start | bytes 2359304 | tf_op jit(solution)/shard_map/ppermute | solution.py:499
  345.0 31.0 %collective-permute-start.59 = (bf16[192,2048]{1,0:T(8,128)(2,1)S(1)}, bf16[192,2048]{1,0:T(8,128)(2,1)}, u32[]{:S(2)}, u32[]{:S(2)}) collective-permute-start(bf16[192,2048]{1,0:T(8,128)(2,1)S(1)} %multiply_convert_fusion.refs_1_), channel_id=1, source_target_pairs={{0,24},{8,0},{16,8},{24,16},{1,25},{9,1},{17,9},{25,17},{2,26},{10... | collective-permute-start | bytes 2359304 | tf_op jit(solution)/shard_map/ppermute | solution.py:499
  348.3 27.7 %collective-permute-start.61 = (bf16[192,2048]{1,0:T(8,128)(2,1)S(1)}, bf16[192,2048]{1,0:T(8,128)(2,1)S(1)}, u32[]{:S(2)}, u32[]{:S(2)}) collective-permute-start(bf16[192,2048]{1,0:T(8,128)(2,1)S(1)} %collective-permute-done.50.refs_1_), channel_id=1, source_target_pairs={{0,4},{4,0},{1,5},{5,1},{2,6},{6,2},{3,7},{7,3},{8,12},{12,8},{9,1... | collective-permute-start | bytes 2359304 | tf_op jit(solution)/shard_map/ppermute | solution.py:503
  348.9 27.1 %collective-permute-start.63 = (bf16[192,2048]{1,0:T(8,128)(2,1)S(1)}, bf16[192,2048]{1,0:T(8,128)(2,1)}, u32[]{:S(2)}, u32[]{:S(2)}) collective-permute-start(bf16[192,2048]{1,0:T(8,128)(2,1)S(1)} %collective-permute-done.50.refs_1_), channel_id=1, source_target_pairs={{0,2},{2,0},{1,3},{3,1},{4,6},{6,4},{5,7},{7,5},{8,10},{10,8},{9,1... | collective-permute-start | bytes 2359304 | tf_op jit(solution)/shard_map/ppermute | solution.py:503
  349.0 27.0 %collective-permute-start.62 = (bf16[96,2048]{1,0:T(8,128)(2,1)}, bf16[96,2048]{1,0:T(8,128)(2,1)S(1)}, u32[]{:S(2)}, u32[]{:S(2)}) collective-permute-start(bf16[96,2048]{1,0:T(8,128)(2,1)} %collective-permute-done.51), channel_id=1, source_target_pairs={{0,4},{4,0},{1,5},{5,1},{2,6},{6,2},{3,7},{7,3},{8,12},{12,8},{9,1... | collective-permute-start | bytes 1179656 | tf_op jit(solution)/shard_map/ppermute | solution.py:503
  379.7 26.8 %collective-permute-start.70 = (bf16[2,192,2048]{2,1,0:T(8,128)(2,1)}, bf16[2,192,2048]{2,1,0:T(8,128)(2,1)}, u32[]{:S(2)}, u32[]{:S(2)}) collective-permute-start(bf16[2,192,2048]{2,1,0:T(8,128)(2,1)} %get-tuple-element.838), channel_id=1, source_target_pairs={{0,2},{2,0},{1,3},{3,1},{4,6},{6,4},{5,7},{7,5},{8,10},{10,8},{9,1... | collective-permute-start | bytes 4718600 | tf_op jit(solution)/shard_map/ppermute | solution.py:503
  380.6 28.6 %collective-permute-start.69 = (bf16[2,192,2176]{2,1,0:T(8,128)(2,1)}, bf16[2,192,2176]{2,1,0:T(8,128)(2,1)}, u32[]{:S(2)}, u32[]{:S(2)}) collective-permute-start(bf16[2,192,2176]{2,1,0:T(8,128)(2,1)} %get-tuple-element.837), channel_id=1, source_target_pairs={{0,2},{2,0},{1,3},{3,1},{4,6},{6,4},{5,7},{7,5},{8,10},{10,8},{9,1... | collective-permute-start | bytes 5013512 | tf_op jit(solution)/shard_map/ppermute | solution.py:503
  380.8 29.8 %collective-permute-start.66 = (bf16[192,2048]{1,0:T(8,128)(2,1)}, bf16[192,2048]{1,0:T(8,128)(2,1)}, u32[]{:S(2)}, u32[]{:S(2)}) collective-permute-start(bf16[192,2048]{1,0:T(8,128)(2,1)} %collective-permute-done.59.refs_1_), channel_id=1, source_target_pairs={{0,4},{4,0},{1,5},{5,1},{2,6},{6,2},{3,7},{7,3},{8,12},{12,8},{9,1... | collective-permute-start | bytes 2359304 | tf_op jit(solution)/shard_map/ppermute | solution.py:503
  381.5 29.2 %collective-permute-start.68 = (bf16[192,2048]{1,0:T(8,128)(2,1)S(1)}, bf16[192,2048]{1,0:T(8,128)(2,1)}, u32[]{:S(2)}, u32[]{:S(2)}) collective-permute-start(bf16[192,2048]{1,0:T(8,128)(2,1)S(1)} %pad_maximum_fusion.11.refs_5_), channel_id=1, source_target_pairs={{0,2},{2,0},{1,3},{3,1},{4,6},{6,4},{5,7},{7,5},{8,10},{10,8},{9,1... | collective-permute-start | bytes 2359304 | tf_op jit(solution)/shard_map/ppermute | solution.py:503
  381.5 29.1 %collective-permute-start.67 = (bf16[96,2048]{1,0:T(8,128)(2,1)}, bf16[96,2048]{1,0:T(8,128)(2,1)S(1)}, u32[]{:S(2)}, u32[]{:S(2)}) collective-permute-start(bf16[96,2048]{1,0:T(8,128)(2,1)} %collective-permute-done.60), channel_id=1, source_target_pairs={{0,4},{4,0},{1,5},{5,1},{2,6},{6,2},{3,7},{7,3},{8,12},{12,8},{9,1... | collective-permute-start | bytes 1179656 | tf_op jit(solution)/shard_map/ppermute | solution.py:503
  414.1 27.4 %collective-permute-start.76 = (bf16[2,192,2048]{2,1,0:T(8,128)(2,1)}, bf16[2,192,2048]{2,1,0:T(8,128)(2,1)}, u32[]{:S(2)}, u32[]{:S(2)}) collective-permute-start(bf16[2,192,2048]{2,1,0:T(8,128)(2,1)} %get-tuple-element.890), channel_id=1, source_target_pairs={{0,2},{2,0},{1,3},{3,1},{4,6},{6,4},{5,7},{7,5},{8,10},{10,8},{9,1... | collective-permute-start | bytes 4718600 | tf_op jit(solution)/shard_map/ppermute | solution.py:503
  415.0 29.2 %collective-permute-start.75 = (bf16[2,192,2176]{2,1,0:T(8,128)(2,1)}, bf16[2,192,2176]{2,1,0:T(8,128)(2,1)}, u32[]{:S(2)}, u32[]{:S(2)}) collective-permute-start(bf16[2,192,2176]{2,1,0:T(8,128)(2,1)} %get-tuple-element.889), channel_id=1, source_target_pairs={{0,2},{2,0},{1,3},{3,1},{4,6},{6,4},{5,7},{7,5},{8,10},{10,8},{9,1... | collective-permute-start | bytes 5013512 | tf_op jit(solution)/shard_map/ppermute | solution.py:503
  415.8 37.7 %collective-permute-start.73 = (bf16[192,2176]{1,0:T(8,128)(2,1)S(1)}, bf16[192,2176]{1,0:T(8,128)(2,1)}, u32[]{:S(2)}, u32[]{:S(2)}) collective-permute-start(bf16[192,2176]{1,0:T(8,128)(2,1)S(1)} %fusion.33), channel_id=1, source_target_pairs={{0,4},{4,0},{1,5},{5,1},{2,6},{6,2},{3,7},{7,3},{8,12},{12,8},{9,1... | collective-permute-start | bytes 2506760 | tf_op jit(solution)/shard_map/ppermute | solution.py:503
  416.4 37.1 %collective-permute-start.74 = (bf16[192,2048]{1,0:T(8,128)(2,1)}, bf16[192,2048]{1,0:T(8,128)(2,1)S(1)}, u32[]{:S(2)}, u32[]{:S(2)}) collective-permute-start(bf16[192,2048]{1,0:T(8,128)(2,1)} %fusion.38), channel_id=1, source_target_pairs={{0,4},{4,0},{1,5},{5,1},{2,6},{6,2},{3,7},{7,3},{8,12},{12,8},{9,1... | collective-permute-start | bytes 2359304 | tf_op jit(solution)/shard_map/ppermute | solution.py:503
  456.5 27.6 %collective-permute-start.81 = (bf16[2,192,2048]{2,1,0:T(8,128)(2,1)}, bf16[2,192,2048]{2,1,0:T(8,128)(2,1)}, u32[]{:S(2)}, u32[]{:S(2)}) collective-permute-start(bf16[2,192,2048]{2,1,0:T(8,128)(2,1)} %get-tuple-element.938), channel_id=1, source_target_pairs={{0,2},{2,0},{1,3},{3,1},{4,6},{6,4},{5,7},{7,5},{8,10},{10,8},{9,1... | collective-permute-start | bytes 4718600 | tf_op jit(solution)/shard_map/ppermute | solution.py:503
  456.6 30.1 %collective-permute-start.80 = (bf16[2,192,2176]{2,1,0:T(8,128)(2,1)}, bf16[2,192,2176]{2,1,0:T(8,128)(2,1)}, u32[]{:S(2)}, u32[]{:S(2)}) collective-permute-start(bf16[2,192,2176]{2,1,0:T(8,128)(2,1)} %get-tuple-element.937), channel_id=1, source_target_pairs={{0,2},{2,0},{1,3},{3,1},{4,6},{6,4},{5,7},{7,5},{8,10},{10,8},{9,1... | collective-permute-start | bytes 5013512 | tf_op jit(solution)/shard_map/ppermute | solution.py:503
  457.9 39.2 %collective-permute-start.77 = (bf16[192,2176]{1,0:T(8,128)(2,1)}, bf16[192,2176]{1,0:T(8,128)(2,1)S(1)}, u32[]{:S(2)}, u32[]{:S(2)}) collective-permute-start(bf16[192,2176]{1,0:T(8,128)(2,1)} %fusion.11), channel_id=1, source_target_pairs={{0,16},{8,24},{16,0},{24,8},{1,17},{9,25},{17,1},{25,9},{2,18},{10... | collective-permute-start | bytes 2506760 | tf_op jit(solution)/shard_map/ppermute | solution.py:499
  457.9 39.1 %collective-permute-start.78 = (bf16[192,2176]{1,0:T(8,128)(2,1)}, bf16[192,2176]{1,0:T(8,128)(2,1)}, u32[]{:S(2)}, u32[]{:S(2)}) collective-permute-start(bf16[192,2176]{1,0:T(8,128)(2,1)} %fusion.34), channel_id=1, source_target_pairs={{0,4},{4,0},{1,5},{5,1},{2,6},{6,2},{3,7},{7,3},{8,12},{12,8},{9,1... | collective-permute-start | bytes 2506760 | tf_op jit(solution)/shard_map/ppermute | solution.py:503
  458.6 37.1 %collective-permute-start.79 = (bf16[192,2048]{1,0:T(8,128)(2,1)}, bf16[192,2048]{1,0:T(8,128)(2,1)}, u32[]{:S(2)}, u32[]{:S(2)}) collective-permute-start(bf16[192,2048]{1,0:T(8,128)(2,1)} %fusion.39), channel_id=1, source_target_pairs={{0,4},{4,0},{1,5},{5,1},{2,6},{6,2},{3,7},{7,3},{8,12},{12,8},{9,1... | collective-permute-start | bytes 2359304 | tf_op jit(solution)/shard_map/ppermute | solution.py:503
  581.5 38.7 %collective-permute-start.94 = (bf16[3,128,2048]{2,1,0:T(8,128)(2,1)S(1)}, bf16[3,128,2048]{2,1,0:T(8,128)(2,1)S(1)}, u32[]{:S(2)}, u32[]{:S(2)}) collective-permute-start(bf16[3,128,2048]{2,1,0:T(8,128)(2,1)S(1)} %dynamic-slice_bitcast_fusion.1), channel_id=1, source_target_pairs={{0,1},{1,0},{2,3},{3,2},{4,5},{5,4},{6,7},{7,6},{8,9},{9,8},{10,11... | collective-permute-start | bytes 4718600 | tf_op jit(solution)/shard_map/ppermute | solution.py:503
  582.4 37.7 %collective-permute-start.95 = (bf16[192,2048]{1,0:T(8,128)(2,1)}, bf16[192,2048]{1,0:T(8,128)(2,1)}, u32[]{:S(2)}, u32[]{:S(2)}) collective-permute-start(bf16[192,2048]{1,0:T(8,128)(2,1)} %fusion.24), channel_id=1, source_target_pairs={{0,16},{8,24},{16,0},{24,8},{1,17},{9,25},{17,1},{25,9},{2,18},{10... | collective-permute-start | bytes 2359304 | tf_op jit(solution)/shard_map/ppermute | solution.py:499
  583.6 36.5 %collective-permute-start.96 = (bf16[192,2048]{1,0:T(8,128)(2,1)}, bf16[192,2048]{1,0:T(8,128)(2,1)}, u32[]{:S(2)}, u32[]{:S(2)}) collective-permute-start(bf16[192,2048]{1,0:T(8,128)(2,1)} %fusion.40), channel_id=1, source_target_pairs={{0,4},{4,0},{1,5},{5,1},{2,6},{6,2},{3,7},{7,3},{8,12},{12,8},{9,1... | collective-permute-start | bytes 2359304 | tf_op jit(solution)/shard_map/ppermute | solution.py:503
  585.1 35.1 %collective-permute-start.97 = (bf16[192,2048]{1,0:T(8,128)(2,1)}, bf16[192,2048]{1,0:T(8,128)(2,1)}, u32[]{:S(2)}, u32[]{:S(2)}) collective-permute-start(bf16[192,2048]{1,0:T(8,128)(2,1)} %fusion.41), channel_id=1, source_target_pairs={{0,4},{4,0},{1,5},{5,1},{2,6},{6,2},{3,7},{7,3},{8,12},{12,8},{9,1... | collective-permute-start | bytes 2359304 | tf_op jit(solution)/shard_map/ppermute | solution.py:503
  621.0 39.6 %collective-permute-start.101 = (bf16[512,1024]{1,0:T(8,128)(2,1)S(1)}, bf16[512,1024]{1,0:T(8,128)(2,1)S(1)}, u32[]{:S(2)}, u32[]{:S(2)}) collective-permute-start(bf16[512,1024]{1,0:T(8,128)(2,1)S(1)} %pad_maximum_fusion.8), channel_id=1, source_target_pairs={{0,1},{1,0},{2,3},{3,2},{4,5},{5,4},{6,7},{7,6},{8,9},{9,8},{10,11... | collective-permute-start | bytes 3145736 | tf_op jit(solution)/shard_map/ppermute | solution.py:503
  622.3 38.4 %collective-permute-start.102 = (bf16[2,128,2048]{2,1,0:T(8,128)(2,1)S(1)}, bf16[2,128,2048]{2,1,0:T(8,128)(2,1)S(1)}, u32[]{:S(2)}, u32[]{:S(2)}) collective-permute-start(bf16[2,128,2048]{2,1,0:T(8,128)(2,1)S(1)} %fusion.1), channel_id=1, source_target_pairs={{0,4},{4,0},{1,5},{5,1},{2,6},{6,2},{3,7},{7,3},{8,12},{12,8},{9,1... | collective-permute-start | bytes 3145736 | tf_op jit(solution)/shard_map/ppermute | solution.py:503
  627.5 33.1 %collective-permute-start.99 = (bf16[4,3,64,256]{3,2,1,0:T(8,128)(2,1)S(1)}, bf16[4,3,64,256]{3,2,1,0:T(8,128)(2,1)S(1)}, u32[]{:S(2)}, u32[]{:S(2)}) collective-permute-start(bf16[4,3,64,256]{3,2,1,0:T(8,128)(2,1)S(1)} %get-tuple-element.1056), channel_id=1, source_target_pairs={{0,16},{8,24},{16,0},{24,8},{1,17},{9,25},{17,1},{25,9},{2,18},{10... | collective-permute-start | bytes 1179656 | tf_op jit(solution)/shard_map/ppermute | solution.py:499
  664.0 26.8 %collective-permute-start.104 = (bf16[2,4,64,1024]{3,2,1,0:T(8,128)(2,1)S(1)}, bf16[2,4,64,1024]{3,2,1,0:T(8,128)(2,1)S(1)}, u32[]{:S(2)}, u32[]{:S(2)}) collective-permute-start(bf16[2,4,64,1024]{3,2,1,0:T(8,128)(2,1)S(1)} %pad_maximum_fusion.9), channel_id=1, source_target_pairs={{0,1},{1,0},{2,3},{3,2},{4,5},{5,4},{6,7},{7,6},{8,9},{9,8},{10,11... | collective-permute-start | bytes 3145736 | tf_op jit(solution)/shard_map/ppermute | solution.py:503
  693.3 28.6 %collective-permute-start.110 = (bf16[2,192,2048]{2,1,0:T(8,128)(2,1)}, bf16[2,192,2048]{2,1,0:T(8,128)(2,1)S(1)}, u32[]{:S(2)}, u32[]{:S(2)}) collective-permute-start(bf16[2,192,2048]{2,1,0:T(8,128)(2,1)} %bitcast.161), channel_id=1, source_target_pairs={{0,2},{2,0},{1,3},{3,1},{4,6},{6,4},{5,7},{7,5},{8,10},{10,8},{9,1... | collective-permute-start | bytes 4718600 | tf_op jit(solution)/shard_map/ppermute | solution.py:503
  693.4 28.5 %collective-permute-start.109 = (bf16[4,4,80,256]{3,2,1,0:T(8,128)(2,1)}, bf16[4,4,80,256]{3,2,1,0:T(8,128)(2,1)S(1)}, u32[]{:S(2)}, u32[]{:S(2)}) collective-permute-start(bf16[4,4,80,256]{3,2,1,0:T(8,128)(2,1)} %get-tuple-element.1094), channel_id=1, source_target_pairs={{0,1},{1,0},{2,3},{3,2},{4,5},{5,4},{6,7},{7,6},{8,9},{9,8},{10,11... | collective-permute-start | bytes 1966088 | tf_op jit(solution)/shard_map/ppermute | solution.py:503
  722.1 27.9 %collective-permute-start.113 = (bf16[192,2048]{1,0:T(8,128)(2,1)S(1)}, bf16[192,2048]{1,0:T(8,128)(2,1)S(1)}, u32[]{:S(2)}, u32[]{:S(2)}) collective-permute-start(bf16[192,2048]{1,0:T(8,128)(2,1)S(1)} %fusion.42), channel_id=1, source_target_pairs={{0,4},{4,0},{1,5},{5,1},{2,6},{6,2},{3,7},{7,3},{8,12},{12,8},{9,1... | collective-permute-start | bytes 2359304 | tf_op jit(solution)/shard_map/ppermute | solution.py:503
  (238 other events, 3021.1 us)
